TPU v7x, 32 devices: a whole 2x2x4 slice. The times are simulated.
32 devices in a mesh: head: 2 (over y), leaf: 16 (over z, x, core).
Axes of the slice: x: 2, y: 2, z: 4, core: 2. Of those that a mesh axis runs over, the one named last changes fastest.
Arguments:
- queries: bfloat16 [32, 128, 8192], P('leaf', None, 'head'), may hold values from -6 to 6
- keys: bfloat16 [32, 128, 1024], P('leaf', 'head'), may hold values from -6 to 6
- values: bfloat16 [32, 128, 1024], P('leaf', 'head'), may hold values from -6 to 6
- output_gradient: bfloat16 [32, 128, 8192], P('leaf', None, 'head'), may hold values from -6 to 6
- parents: int32 [32], P('leaf'), may hold values from -1 to 31, as said below
Outputs:
- grad_queries: bfloat16 [32, 128, 8192], P('leaf', None, 'head')
- key_gradient: bfloat16 [32, 128, 1024], P('leaf', 'head')
- value_gradient: bfloat16 [32, 128, 1024], P('leaf', 'head')
Inputs may be any that keep to these rules, and one draw needn't show every extreme that they name: `parents`: block b is in tree b % 2 and its parent is in the same tree. In the tree of even blocks the parent lies below b and only block 0 is a root; in the tree of odd blocks the parent lies above b and only block 31 is a root. Every block has at most 2 ancestors, and some block has exactly 2.
All inputs are finite; a program needn't handle non-finite values.
Results may differ from a plain program's by a relative error of at most 0.012.
Values may be sent and summed in bfloat16 or wider, within the bound.
No kernel may reach another device: no remote copies, remote signals or barrier semaphores. Data moves between devices by JAX's collectives and lax.ppermute only.
A program may use at most 64 MiB of HBM per device.

v0:
```python
import jax
import jax.numpy as jnp
from jax import lax
from jax.sharding import PartitionSpec as P

QUERY_HEAD_COUNT = 64
KEY_VALUE_HEADS = 8
HEAD_DIM = 128


masked_score = -1e30


def follow_links(parent_table, chain_len):

    def extend(link_no, carry_in):
        current, ancestry = carry_in
        ancestry = ancestry.at[:, link_no].set(current)
        upward = jnp.where(current >= 0, parent_table[jnp.maximum(current, 0)], -1)
        return (upward, ancestry)

    start = jnp.full((parent_table.shape[0], chain_len), -1, jnp.int32)
    return lax.fori_loop(0, chain_len, extend, (parent_table, start))[1]


def pick_rows(paired, need_left, need_right):
    left_tile = paired[0][None]
    right_tile = paired[1][None]
    array_shape = (need_left.shape[0],) + (1,) * (paired.ndim - 1)
    return jnp.where(
        need_left.reshape(array_shape),
        left_tile,
        jnp.where(need_right.reshape(array_shape), right_tile, jnp.zeros_like(left_tile)),
    )


def attend_block(
    query_rows, grad_rows, self_keys, self_values, chain_row, incoming, back_keys, back_values
):
    row_count = query_rows.shape[0]
    groups = self_keys.shape[1] // HEAD_DIM
    heads_per_group = QUERY_HEAD_COUNT // KEY_VALUE_HEADS
    softmax_scale = HEAD_DIM ** (-0.5)
    query_heads = query_rows.reshape(row_count, groups, heads_per_group, HEAD_DIM)
    grad_heads = grad_rows.reshape(row_count, groups, heads_per_group, HEAD_DIM)
    causal = lax.broadcasted_iota(jnp.int32, (row_count, row_count), 0) >= lax.broadcasted_iota(
        jnp.int32, (row_count, row_count), 1
    )

    def scores_of(block_keys):
        return (
            jnp.einsum(
                "igrd,jgd->grij",
                query_heads,
                block_keys.reshape(-1, groups, HEAD_DIM),
                preferred_element_type=jnp.float32,
            )
            * softmax_scale
        )

    def slopes_of(block_values):
        return jnp.einsum(
            "igrd,jgd->grij",
            grad_heads,
            block_values.reshape(-1, groups, HEAD_DIM),
            preferred_element_type=jnp.float32,
        )

    def fetch_tile(anc_block):
        tile = lax.dynamic_index_in_dim(incoming, anc_block // 2, 0, keepdims=False)
        return (tile[0], tile[1])

    scores = jnp.where(causal, scores_of(self_keys), masked_score)
    row_peak = jnp.max(scores, -1)
    shifted = jnp.exp(scores - row_peak[..., None])
    row_total = jnp.sum(shifted, -1)
    weighted = jnp.sum(shifted * slopes_of(self_values), -1)

    def first_sweep(link_no, carry_in):
        anc_block = chain_row[link_no]

        def first_active(status):
            old_peak, old_total, old_weighted = status
            block_keys, block_values = fetch_tile(anc_block)
            fresh = scores_of(block_keys)
            new_peak = jnp.maximum(old_peak, jnp.max(fresh, -1))
            factor = jnp.exp(old_peak - new_peak)
            shifted_here = jnp.exp(fresh - new_peak[..., None])
            return (
                new_peak,
                old_total * factor + jnp.sum(shifted_here, -1),
                old_weighted * factor + jnp.sum(shifted_here * slopes_of(block_values), -1),
            )

        return lax.cond(anc_block >= 0, first_active, lambda status: status, carry_in)

    row_peak, row_total, weighted = lax.fori_loop(
        0, chain_row.shape[0], first_sweep, (row_peak, row_total, weighted)
    )
    row_level = row_peak + jnp.log(row_total)
    row_mean = weighted / row_total

    def partials(block_keys, block_values, mask_on):
        fresh = scores_of(block_keys)
        if mask_on:
            fresh = jnp.where(causal, fresh, masked_score)
        weights = jnp.exp(fresh - row_level[..., None])
        dscore = (weights * (slopes_of(block_values) - row_mean[..., None])).astype(jnp.bfloat16)
        rounded = weights.astype(jnp.bfloat16)
        query_part = jnp.einsum(
            "grij,jgd->igrd",
            dscore,
            block_keys.reshape(-1, groups, HEAD_DIM),
            preferred_element_type=jnp.float32,
        )
        key_portion = (
            jnp.einsum("grij,igrd->jgd", dscore, query_heads, preferred_element_type=jnp.float32)
            * softmax_scale
        )
        value_portion = jnp.einsum(
            "grij,igrd->jgd", rounded, grad_heads, preferred_element_type=jnp.float32
        )
        return (
            query_part,
            key_portion.reshape(row_count, -1),
            value_portion.reshape(row_count, -1),
        )

    query_acc, key_self, value_self = partials(self_keys, self_values, True)

    def second(link_no, carry_in):
        anc_block = chain_row[link_no]

        def second_active(status):
            query_sum, keys_out, values_out = status
            block_keys, block_values = fetch_tile(anc_block)
            query_part, key_portion, value_portion = partials(block_keys, block_values, False)
            source = anc_block // 2
            keys_out = lax.dynamic_update_index_in_dim(
                keys_out,
                lax.dynamic_index_in_dim(keys_out, source, 0, keepdims=False) + key_portion,
                source,
                0,
            )
            values_out = lax.dynamic_update_index_in_dim(
                values_out,
                lax.dynamic_index_in_dim(values_out, source, 0, keepdims=False) + value_portion,
                source,
                0,
            )
            return (query_sum + query_part, keys_out, values_out)

        return lax.cond(anc_block >= 0, second_active, lambda status: status, carry_in)

    query_acc, back_keys, back_values = lax.fori_loop(
        0, chain_row.shape[0], second, (query_acc, back_keys, back_values)
    )
    query_grad = (query_acc * softmax_scale).astype(jnp.bfloat16).reshape(row_count, -1)
    return (query_grad, key_self, value_self, back_keys, back_values)


def body(queries, keys, values, output_gradient, parents):
    leaf_count = lax.axis_size("leaf")
    leaf_rank = lax.axis_index("leaf")
    chain_len = leaf_count // 4 - 2
    all_parents = lax.all_gather(parents, "leaf", axis=0, tiled=True)
    ancestry = follow_links(all_parents, chain_len)
    need_left = jnp.any(ancestry[0::2] == 2 * leaf_rank, axis=1)
    need_right = jnp.any(ancestry[1::2] == 2 * leaf_rank + 1, axis=1)
    group_keys, group_values = (
        lax.all_to_all(keys, "head", split_axis=2, concat_axis=1, tiled=True),
        lax.all_to_all(values, "head", split_axis=2, concat_axis=1, tiled=True),
    )
    outgoing = pick_rows(jnp.stack([group_keys, group_values], 1), need_left, need_right)
    incoming = lax.all_to_all(outgoing, "leaf", split_axis=0, concat_axis=0, tiled=True)
    kv_width = group_keys.shape[2]
    back_keys = jnp.zeros((leaf_count, group_keys.shape[1], kv_width), jnp.float32)
    back_values = jnp.zeros((leaf_count, group_keys.shape[1], kv_width), jnp.float32)
    query_grads = []
    key_selfs = []
    value_selfs = []
    for tree_no in range(2):
        chain_row = lax.dynamic_index_in_dim(ancestry, 2 * leaf_rank + tree_no, 0, keepdims=False)
        query_grad, key_self, value_self, back_keys, back_values = attend_block(
            queries[tree_no],
            output_gradient[tree_no],
            group_keys[tree_no],
            group_values[tree_no],
            chain_row,
            incoming,
            back_keys,
            back_values,
        )
        query_grads.append(query_grad)
        key_selfs.append(key_self)
        value_selfs.append(value_self)
    returned_keys, returned_values = (
        lax.all_to_all(
            back_keys.astype(jnp.bfloat16), "leaf", split_axis=0, concat_axis=0, tiled=True
        ).astype(back_keys.dtype),
        lax.all_to_all(
            back_values.astype(jnp.bfloat16), "leaf", split_axis=0, concat_axis=0, tiled=True
        ).astype(back_values.dtype),
    )
    mask_left = need_left[:, None, None]
    mask_right = need_right[:, None, None]
    key_left = key_selfs[0] + jnp.sum(jnp.where(mask_left, returned_keys, 0.0), 0)
    key_right = key_selfs[1] + jnp.sum(jnp.where(mask_right, returned_keys, 0.0), 0)
    value_left = value_selfs[0] + jnp.sum(jnp.where(mask_left, returned_values, 0.0), 0)
    value_right = value_selfs[1] + jnp.sum(jnp.where(mask_right, returned_values, 0.0), 0)
    local_keys = jnp.stack([key_left, key_right]).astype(jnp.bfloat16)
    local_values = jnp.stack([value_left, value_right]).astype(jnp.bfloat16)
    key_gradient, value_gradient = (
        lax.all_to_all(local_keys, "head", split_axis=1, concat_axis=2, tiled=True),
        lax.all_to_all(local_values, "head", split_axis=1, concat_axis=2, tiled=True),
    )
    return (jnp.stack(query_grads), key_gradient, value_gradient)


def solution(mesh):
    in_specs = (
        P("leaf", None, "head"),
        P("leaf", "head", None),
        P("leaf", "head", None),
        P("leaf", None, "head"),
        P("leaf"),
    )
    out_specs = (P("leaf", None, "head"), P("leaf", "head", None), P("leaf", "head", None))
    return jax.shard_map(body, mesh=mesh, in_specs=in_specs, out_specs=out_specs, check_vma=False)
```

profile of v0, /device:TPU:0, one launch (start us, length us, event | category | flops | bytes accessed | tf_op | source)
XLA Modules:
  0.0 361.2 jit_solution(5367131213451872014)
XLA Ops:
  0.7 1.3 copy.170
  2.0 1.1 reshape.231
  3.1 4.2 %all-to-all-start = ((bf16[2,2,32768]{2,1,0:T(2,128)(2,1)}), bf16[2,2,32768]{2,1,0:T(2,128)(2,1)S(1)}, u32[]{:S(2)}, u32[]{:S(2)}) async-start(bf16[2,2,32768]{2,1,0:T(2,128)(2,1)} %reshape.231), calls=%async_computation | async-start | bytes 524288 | tf_op jit(solution)/shard_map/all_to_all | solution.py:171
  8.8 12.9 %all-reduce = s32[32]{0:T(128)S(1)} all-reduce(s32[32]{0:T(128)S(1)} %dynamic-update-slice.7), channel_id=1, replica_groups=mesh['head'=2,'leaf'=16] {'leaf'}, use_global_device_ids=true, to_apply=%add | all-reduce | flops 32 | bytes 256
  22.2 1.1 reshape.229
  23.3 3.4 all-to-all-start.1
  26.7 4.5 %while.84 = (s32[]{:T(128)}, s32[32]{0:T(128)S(1)}, s32[32,2]{0,1:T(2,128)S(1)}, s32[32]{0:T(128)S(1)}, s32[]{:T(128)}, /*index=5*/s32[1]{0:T(128)}, s32[]{:T(128)}) while((s32[]{:T(128)}, s32[32]{0:T(128)S(1)}, s32[32,2]{0,1:T(2,128)S(1)}, s32[32]{0:T(128)S(1)}, s32[]{:T(128)}, /*index=5*/s32[1]{0:T(128)}, s32[]{:T(128)}) %tuple.227), condition=%wide.region_5.6_spmd, body=%wide.region_3.0_spmd.sunk | while | flops 1163 | bytes 5991 | solution.py:23
  33.5 2.5 select_select_fusion
  36.0 4.7 %all-to-all-start.2 = ((bf16[16,2,128,512]{2,3,1,0:T(8,128)(2,1)}), bf16[16,2,128,512]{2,3,1,0:T(8,128)(2,1)}, u32[]{:S(2)}, u32[]{:S(2)}) async-start(bf16[16,2,128,512]{2,3,1,0:T(8,128)(2,1)} %select_select_fusion), calls=%async_computation.2 | async-start | bytes 8388608 | tf_op jit(solution)/shard_map/all_to_all | solution.py:175
  40.7 1.8 fusion.65
  43.2 1.3 copy.182
  45.1 1.3 copy.194
  46.4 3.2 fusion.66
  49.6 1.6 copy.285
  51.2 1.3 copy.183
  52.6 2.3 copy.287
  54.8 2.3 copy.195
  59.6 1.7 fusion.68
  61.2 1.6 reshape_squeeze.32
  62.8 1.6 reshape_squeeze.36
  65.4 1.5 copy-done
  67.0 1.8 fusion.32
  68.8 1.9 fusion.35
  70.8 47.4 %all-to-all-done.2 = bf16[16,2,128,512]{2,3,1,0:T(8,128)(2,1)} async-done(((bf16[16,2,128,512]{2,3,1,0:T(8,128)(2,1)}), bf16[16,2,128,512]{2,3,1,0:T(8,128)(2,1)}, u32[]{:S(2)}, u32[]{:S(2)}) %all-to-all-start.2) | async-done | bytes 4194336 | tf_op jit(solution)/shard_map/all_to_all | solution.py:175
  118.2 9.1 %while.87 = (s32[]{:T(128)}, f32[4,8,128]{2,1,0:T(8,128)S(1)}, f32[4,8,128]{2,1,0:T(8,128)S(1)}, f32[4,8,128]{2,1,0:T(8,128)S(1)}, s32[2]{0:T(128)S(1)}, /*index...) while((s32[]{:T(128)}, f32[4,8,128]{2,1,0:T(8,128)S(1)}, ...), condition=%wide.region_28.29_spmd, body=%wide.region_22.28_spmd.sunk | while | flops 273166336 | bytes 13664735 | solution.py:97
  119.4 6.6 %conditional.10 = ((f32[4,8,128]{2,1,0:T(8,128)S(1)}, f32[4,8,128]{2,1,0:T(8,128)S(1)}, f32[4,8,128]{2,1,0:T(8,128)S(1)})) conditional(s32[]{:T(128)} %convert_element_type.114, (f32[4,8,128]{2,1,0:T(8,128)S(1)}, f32[4,8,128]{2,1,0:T(8,128)S(1)}, f32[4,8,128]{2,1,0:T(8,128)S(1)}) %tuple.214, (s32[]{:T(128)}, bf16[16,2,128,512]{2,3,1,0:T(8,128)(2,1)}, ...), branch_computations={%region_23.23_spmd, %region_24.27_spmd} | conditional | flops 273166336 | bytes 13664520 | solution.py:95
  122.0 1.1 constant_dynamic-slice_fusion.5
  123.1 1.7 bitcast_reduce_fusion.1
  127.3 2.6 while.85
  129.9 2.8 fusion.34
  133.7 1.9 convolution_bitcast_fusion.2
  135.5 2.9 copy.198
  138.4 2.8 fusion.37
  142.2 1.9 convolution_bitcast_fusion.3
  144.0 2.9 copy.186
  147.0 2.4 broadcast.110.clone
  149.4 2.4 broadcast.110
  151.8 2.5 while.86
  154.3 13.4 %while.88 = (s32[]{:T(128)}, f32[128,4,8,128]{0,3,2,1:T(8,128)}, f32[16,128,512]{1,2,0:T(8,128)}, f32[16,128,512]{1,2,0:T(8,128)}, s32[2]{0:T(128)S(1)}, /*index...) while((s32[]{:T(128)}, f32[128,4,8,128]{0,3,2,1:T(8,128)}, ...), condition=%wide.region_32.33_spmd, body=%wide.region_29.32_spmd.sunk | while | flops 676003840 | bytes 41861688 | solution.py:155
  155.6 10.9 %conditional.11 = ((f32[128,4,8,128]{0,3,2,1:T(8,128)}, f32[16,128,512]{1,2,0:T(8,128)}, f32[16,128,512]{1,2,0:T(8,128)})) conditional(s32[]{:T(128)} %convert_element_type.115, (f32[128,4,8,128]{0,3,2,1:T(8,128)}, f32[16,128,512]{1,2,0:T(8,128)}, f32[16,128,512]{1,2,0:T(8,128)}) %tuple.217, (s32[]{:T(128)}, bf16[16,2,128,512]{2,3,1,0:T(8,128)(2,1)}, ...), branch_computations={%region_30.30_spmd, %region_31.31_spmd} | conditional | flops 676003840 | bytes 41861444 | solution.py:153
  158.2 1.1 constant_dynamic-slice_fusion.7
  161.5 1.1 copy-done.3
  163.3 1.3 copy-done.4
  164.6 1.9 fusion.26
  167.7 3.9 %convert_element_type.79 = bf16[16,128,512]{1,2,0:T(8,128)(2,1)} convert(f32[16,128,512]{1,2,0:T(8,128)} %get-tuple-element.896) | non-fusion elementwise | flops 1048576 | bytes 6291456 | tf_op jit(solution)/shard_map/convert_element_type | solution.py:202
  171.6 71.0 %all-to-all-start.5 = ((bf16[16,128,512]{1,2,0:T(8,128)(2,1)}), bf16[16,128,512]{1,2,0:T(8,128)(2,1)}, u32[]{:S(2)}, u32[]{:S(2)}) async-start(bf16[16,128,512]{1,2,0:T(8,128)(2,1)} %convert_element_type.79), calls=%async_computation.5 | async-start | bytes 4194304 | tf_op jit(solution)/shard_map/all_to_all | solution.py:201
  242.6 3.9 %convert_element_type.76 = bf16[16,128,512]{1,2,0:T(8,128)(2,1)} convert(f32[16,128,512]{1,2,0:T(8,128)} %get-tuple-element.895) | non-fusion elementwise | flops 1048576 | bytes 6291456 | tf_op jit(solution)/shard_map/convert_element_type | solution.py:199
  246.5 37.3 %all-to-all-done.5 = bf16[16,128,512]{1,2,0:T(8,128)(2,1)} async-done(((bf16[16,128,512]{1,2,0:T(8,128)(2,1)}), bf16[16,128,512]{1,2,0:T(8,128)(2,1)}, u32[]{:S(2)}, u32[]{:S(2)}) %all-to-all-start.5) | async-done | bytes 2097184 | tf_op jit(solution)/shard_map/all_to_all | solution.py:201
  283.8 11.3 %all-to-all-start.3 = ((bf16[16,128,512]{1,2,0:T(8,128)(2,1)}), bf16[16,128,512]{1,2,0:T(8,128)(2,1)}, u32[]{:S(2)}, u32[]{:S(2)}) async-start(bf16[16,128,512]{1,2,0:T(8,128)(2,1)} %convert_element_type.76), calls=%async_computation.3 | async-start | bytes 4194304 | tf_op jit(solution)/shard_map/all_to_all | solution.py:198
  295.1 2.9 multiply_convert_fusion
  297.9 2.3 copy.283
  300.2 2.9 multiply_convert_fusion.1
  303.1 2.3 copy.276
  305.3 1.8 fusion.43
  307.1 2.4 fusion.42
  309.5 1.2 fusion.44
  311.2 1.2 fusion.46
  312.4 23.9 %all-to-all-done.3 = bf16[16,128,512]{1,2,0:T(8,128)(2,1)} async-done(((bf16[16,128,512]{1,2,0:T(8,128)(2,1)}), bf16[16,128,512]{1,2,0:T(8,128)(2,1)}, u32[]{:S(2)}, u32[]{:S(2)}) %all-to-all-start.3) | async-done | bytes 2097184 | tf_op jit(solution)/shard_map/all_to_all | solution.py:198
  336.2 4.0 %fusion.28 = (f32[128,512]{0,1:T(8,128)S(1)}, f32[128,512]{0,1:T(8,128)S(1)}, f32[128,512]{0,1:T(8,128)S(1)}, f32[128,512]{0,1:T(8,128)S(1)}) fusion(bf16[16,128,512]{1,2,0:T(8,128)(2,1)} %all-to-all-done.3, pred[16]{0:T(512)(128)(4,1)S(1)} %copy-done.25, pred[16]{0:T(512)(128)(4,1)S(1)} %copy-done.23, bf16[16,128,512]{1,2,0:T(8,128)(2,1)} %all-to-all-done.5), kind=kLoop, calls=%fused_computation.68 | loop fusion | flops 10223616 | bytes 5242912 | tf_op jit(solution)/shard_map/reduce_sum | solution.py:207
  341.3 3.4 all-to-all-start.4
  347.6 3.6 %all-to-all-done.4 = bf16[2,128,512]{2,0,1:T(2,128)(2,1)S(1)} async-done(((bf16[2,128,512]{2,0,1:T(2,128)(2,1)}), bf16[2,128,512]{2,0,1:T(2,128)(2,1)S(1)}, u32[]{:S(2)}, u32[]{:S(2)}) %all-to-all-start.4) | async-done | bytes 262176 | tf_op jit(solution)/shard_map/all_to_all | solution.py:214
  351.2 3.4 all-to-all-start.6
  354.7 1.5 pad_maximum_fusion
  357.0 3.4 all-to-all-done.6
  (130 shorter events, 29.1 us)
Async XLA Ops:
  0.6 6.7 %copy-start.29 = (u32[32]{0:T(128)S(1)}, u32[32]{0:T(128)}, u32[]{:S(2)}) copy-start(u32[32]{0:T(128)} %constant.310) | copy-start | bytes 388
  0.6 7.9 %copy-start.28 = (s32[2]{0:T(128)S(1)}, s32[2]{0:T(128)}, u32[]{:S(2)}) copy-start(s32[2]{0:T(128)} %param.29) | copy-start | bytes 28
  0.7 21.1 %copy-start.21 = (bf16[2,64,1024]{2,1,0:T(8,128)(2,1)S(1)}, bf16[2,64,1024]{2,1,0:T(8,128)(2,1)}, u32[]{:S(2)}) copy-start(bf16[2,64,1024]{2,1,0:T(8,128)(2,1)} %param.27) | copy-start | bytes 786436
  3.1 20.2 %all-to-all-start = ((bf16[2,2,32768]{2,1,0:T(2,128)(2,1)}), bf16[2,2,32768]{2,1,0:T(2,128)(2,1)S(1)}, u32[]{:S(2)}, u32[]{:S(2)}) async-start(bf16[2,2,32768]{2,1,0:T(2,128)(2,1)} %reshape.231), calls=%async_computation | async-start | bytes 524288 | tf_op jit(solution)/shard_map/all_to_all | solution.py:171
  23.3 9.2 %all-to-all-start.1 = ((bf16[2,2,32768]{2,1,0:T(2,128)(2,1)}), bf16[2,2,32768]{2,1,0:T(2,128)(2,1)S(1)}, u32[]{:S(2)}, u32[]{:S(2)}) async-start(bf16[2,2,32768]{2,1,0:T(2,128)(2,1)} %reshape.229), calls=%async_computation.1 | async-start | bytes 524288 | tf_op jit(solution)/shard_map/all_to_all | solution.py:172
  31.5 2.0 copy-start.22
  31.5 2.0 copy-start.24
  33.2 2.8 copy-start.17
  36.0 82.1 %all-to-all-start.2 = ((bf16[16,2,128,512]{2,3,1,0:T(8,128)(2,1)}), bf16[16,2,128,512]{2,3,1,0:T(8,128)(2,1)}, u32[]{:S(2)}, u32[]{:S(2)}) async-start(bf16[16,2,128,512]{2,3,1,0:T(8,128)(2,1)} %select_select_fusion), calls=%async_computation.2 | async-start | bytes 8388608 | tf_op jit(solution)/shard_map/all_to_all | solution.py:175
  64.9 4.0 %copy-start.11 = (f32[4,8,128,128]{2,3,1,0:T(8,128)}, f32[4,8,128,128]{2,3,1,0:T(8,128)S(1)}, u32[]{:S(2)}) copy-start(f32[4,8,128,128]{2,3,1,0:T(8,128)S(1)} %get-tuple-element.1152) | copy-start | bytes 6291460
  64.9 2.0 copy-start
  64.9 2.1 copy-start.20
  65.4 3.5 copy-start.9
  67.0 1.9 copy-start.19
  68.8 49.3 %copy-start.26 = (s32[2]{0:T(128)S(1)}, s32[2]{0:T(128)}, u32[]{:S(2)}) copy-start(s32[2]{0:T(128)} %get-tuple-element.1573) | copy-start | bytes 28
  118.2 9.1 %copy-start.27 = (s32[2]{0:T(128)S(1)}, s32[2]{0:T(128)}, u32[]{:S(2)}) copy-start(s32[2]{0:T(128)} %get-tuple-element.1537) | copy-start | bytes 28
  122.0 2.8 copy-start.8
  132.6 1.0 copy-start.13
  141.2 1.0 copy-start.14
  158.2 1.6 copy-start.1
  161.0 1.6 copy-start.3
  163.3 1.3 copy-start.4
  171.6 112.2 %all-to-all-start.5 = ((bf16[16,128,512]{1,2,0:T(8,128)(2,1)}), bf16[16,128,512]{1,2,0:T(8,128)(2,1)}, u32[]{:S(2)}, u32[]{:S(2)}) async-start(bf16[16,128,512]{1,2,0:T(8,128)(2,1)} %convert_element_type.79), calls=%async_computation.5 | async-start | bytes 4194304 | tf_op jit(solution)/shard_map/all_to_all | solution.py:201
  283.8 52.4 %all-to-all-start.3 = ((bf16[16,128,512]{1,2,0:T(8,128)(2,1)}), bf16[16,128,512]{1,2,0:T(8,128)(2,1)}, u32[]{:S(2)}, u32[]{:S(2)}) async-start(bf16[16,128,512]{1,2,0:T(8,128)(2,1)} %convert_element_type.76), calls=%async_computation.3 | async-start | bytes 4194304 | tf_op jit(solution)/shard_map/all_to_all | solution.py:198
  305.3 4.2 %copy-start.2 = (bf16[128,4,8,128]{0,3,2,1:T(8,128)(2,1)S(1)}, bf16[128,4,8,128]{0,3,2,1:T(8,128)(2,1)}, u32[]{:S(2)}) copy-start(bf16[128,4,8,128]{0,3,2,1:T(8,128)(2,1)} %get-tuple-element.1612) | copy-start | bytes 3145732
  305.3 4.2 %copy-start.12 = (f32[4,8,128,128]{2,3,1,0:T(8,128)S(1)}, f32[4,8,128,128]{2,3,1,0:T(8,128)}, u32[]{:S(2)}) copy-start(f32[4,8,128,128]{2,3,1,0:T(8,128)} %copy-done.11) | copy-start | bytes 6291460
  309.5 1.7 copy-start.10
  311.2 25.0 %copy-start.23 = (pred[16]{0:T(512)(128)(4,1)S(1)}, pred[16]{0:T(512)(128)(4,1)}, u32[]{:S(2)}) copy-start(pred[16]{0:T(512)(128)(4,1)} %copy-done.22) | copy-start | bytes 52
  311.2 25.0 %copy-start.25 = (pred[16]{0:T(512)(128)(4,1)S(1)}, pred[16]{0:T(512)(128)(4,1)}, u32[]{:S(2)}) copy-start(pred[16]{0:T(512)(128)(4,1)} %copy-done.24) | copy-start | bytes 52
  312.4 27.9 %copy-start.18 = (f32[4,128,128]{1,2,0:T(8,128)S(1)}, f32[4,128,128]{1,2,0:T(8,128)}, u32[]{:S(2)}) copy-start(f32[4,128,128]{1,2,0:T(8,128)} %fusion.42) | copy-start | bytes 786436
  340.4 14.3 %copy-start.15 = (bf16[1,128,4096]{2,1,0:T(8,128)(2,1)S(1)}, bf16[1,128,4096]{2,1,0:T(8,128)(2,1)}, u32[]{:S(2)}) copy-start(bf16[1,128,4096]{2,1,0:T(8,128)(2,1)} %copy.283) | copy-start | bytes 3145732
  340.4 14.3 %copy-start.16 = (bf16[1,128,4096]{2,1,0:T(8,128)(2,1)S(1)}, bf16[1,128,4096]{2,1,0:T(8,128)(2,1)}, u32[]{:S(2)}) copy-start(bf16[1,128,4096]{2,1,0:T(8,128)(2,1)} %copy.276) | copy-start | bytes 3145732
  341.3 10.0 %all-to-all-start.4 = ((bf16[2,128,512]{2,0,1:T(2,128)(2,1)}), bf16[2,128,512]{2,0,1:T(2,128)(2,1)S(1)}, u32[]{:S(2)}, u32[]{:S(2)}) async-start(bf16[2,128,512]{2,0,1:T(2,128)(2,1)} %copy.202), calls=%async_computation.4 | async-start | bytes 524288 | tf_op jit(solution)/shard_map/all_to_all | solution.py:214
  351.2 9.2 %all-to-all-start.6 = ((bf16[2,128,512]{2,0,1:T(2,128)(2,1)}), bf16[2,128,512]{2,0,1:T(2,128)(2,1)S(1)}, u32[]{:S(2)}, u32[]{:S(2)}) async-start(bf16[2,128,512]{2,0,1:T(2,128)(2,1)} %copy.207), calls=%async_computation.6 | async-start | bytes 524288 | tf_op jit(solution)/shard_map/all_to_all | solution.py:215
where the time goes:
time: 368 us; the launch traced here: 361 us
  waiting for transfers between devices  116 us (32%)
  starting transfers between devices  102 us (28%)
  local copies, waits for them, and re-layouts  63.8 us (17%)
  other arithmetic  34.6 us (9%)
  matrix products  20 us (5%)
  blocking collectives  12.9 us (4%)
  loops' own time  10.9 us (3%)
    all_to_all x1, starting transfers between devices, body(): lax.all_to_all(back_values.astype(jnp.bfloat16), 'leaf', split_axis=0, co...  71 us
    all_to_all x1, waiting for transfers between devices, body(): lax.all_to_all(outgoing, 'leaf', split_axis=0, concat_axis=0, tiled=True)  47.4 us
    all_to_all x1, waiting for transfers between devices, body(): lax.all_to_all(back_values.astype(jnp.bfloat16), 'leaf', split_axis=0, co...  37.3 us
    all_to_all x1, waiting for transfers between devices, body(): lax.all_to_all(back_keys.astype(jnp.bfloat16), 'leaf', split_axis=0, conc...  23.9 us
    unnamed x60, local copies, waits for them, and re-layouts  14.8 us
    unnamed x1, blocking collectives  12.9 us
    all_to_all x1, starting transfers between devices, body(): lax.all_to_all(back_keys.astype(jnp.bfloat16), 'leaf', split_axis=0, conc...  11.3 us
  transfers between devices with their start and end apart: 7, of which 5 were waited for; matrix products, arithmetic and copies ran while one was open for 17% of the time, Pallas kernels for 0%

commit v1 on v0

v1 whole, which is shorter than its diff:
```python
import functools
import math

import jax
import jax.numpy as jnp
from jax import lax
from jax.experimental import pallas as pl
from jax.experimental.pallas import tpu as pltpu
from jax.sharding import PartitionSpec as P

QUERY_HEAD_COUNT = 64
KEY_VALUE_HEADS = 8
HEAD_DIM = 128

NT = (((1,), (1,)), ((), ()))
F32 = jnp.float32
BF16 = jnp.bfloat16


def dot(a, b, dims=(((1,), (0,)), ((), ()))):
    return lax.dot_general(a, b, dims, preferred_element_type=F32)


def attend_kernel(parents, rank, q_ref, do_ref, self_ref, anc_ref, dq_ref, dself_ref, danc_ref, qs, dos, ps, ds):
    depth = anc_ref.shape[1]
    rows = q_ref.shape[1]
    heads = q_ref.shape[2] // HEAD_DIM
    scale = HEAD_DIM ** (-0.5)
    c = scale * math.log2(math.e)
    block = 2 * rank[0] + pl.program_id(0)
    valid = []
    for _ in range(depth):
        block = jnp.where(block >= 0, parents[jnp.maximum(block, 0)], -1)
        valid.append(block >= 0)

    def whole(ref, *at):
        tile = ref[(slice(None),) + at]
        return tile.reshape(rows, HEAD_DIM)

    keys = jnp.concatenate([whole(self_ref, 0, 0)] + [whole(anc_ref, k, 0) for k in range(depth)], 0)
    values = jnp.concatenate([whole(self_ref, 1, 0)] + [whole(anc_ref, k, 1) for k in range(depth)], 0)
    keys_t = keys.T
    for h in range(heads):
        qs[h * rows : (h + 1) * rows, :] = q_ref[0, :, h * HEAD_DIM : (h + 1) * HEAD_DIM]
        dos[h * rows : (h + 1) * rows, :] = do_ref[0, :, h * HEAD_DIM : (h + 1) * HEAD_DIM]
    hidden = lax.broadcasted_iota(jnp.int32, (rows, rows), 0) > lax.broadcasted_iota(jnp.int32, (rows, rows), 1)
    for h in range(heads):
        part = slice(h * rows, (h + 1) * rows)
        scores = dot(keys, qs[part, :], NT)
        slopes = dot(values, dos[part, :], NT)
        s = [scores[k * rows : (k + 1) * rows] for k in range(depth + 1)]
        d = [slopes[k * rows : (k + 1) * rows] for k in range(depth + 1)]
        s[0] = jnp.where(hidden, -1e30, s[0])
        peak = jnp.max(s[0], 0, keepdims=True)
        for k in range(depth):
            peak = jnp.maximum(peak, jnp.where(valid[k], jnp.max(s[k + 1], 0, keepdims=True), -1e30))
        peak = peak * c
        e = [jnp.exp2(s[0] * c - peak)]
        for k in range(depth):
            e.append(jnp.exp2(s[k + 1] * c - jnp.where(valid[k], peak, 1e30)))
        total = functools.reduce(jnp.add, [jnp.sum(x, 0, keepdims=True) for x in e])
        weighted = functools.reduce(jnp.add, [jnp.sum(x * y, 0, keepdims=True) for x, y in zip(e, d)])
        inverse = 1.0 / total
        mean = weighted * inverse
        for k in range(depth + 1):
            p = e[k] * inverse
            ps[k * rows : (k + 1) * rows, part] = p.astype(BF16)
            ds[k * rows : (k + 1) * rows, part] = (p * (d[k] - mean)).astype(BF16)
        dq_t = dot(keys_t, ds[:, part])
        dq_ref[0, :, h * HEAD_DIM : (h + 1) * HEAD_DIM] = (dq_t * scale).T.astype(BF16)
    dkey = (dot(ds[...], qs[...]) * scale).astype(BF16)
    dvalue = dot(ps[...], dos[...]).astype(BF16)
    hubs, pieces = self_ref.shape[0], self_ref.shape[3]

    def piece(x, k):
        return x[k * rows : (k + 1) * rows].reshape(hubs, pieces, HEAD_DIM)

    dself_ref[:, 0, 0] = piece(dkey, 0)
    dself_ref[:, 1, 0] = piece(dvalue, 0)
    for k in range(depth):
        danc_ref[:, k, 0] = piece(dkey, k + 1)
        danc_ref[:, k, 1] = piece(dvalue, k + 1)


def attend(parents, rank, queries, output_gradient, own, foreign):
    trees, rows, width = queries.shape
    hubs, _, _, pieces, kv_width = own.shape
    depth = foreign.shape[1] // trees
    groups = kv_width // HEAD_DIM
    heads = width // groups // HEAD_DIM
    span = (depth + 1) * rows
    smem = pl.BlockSpec(memory_space=pltpu.SMEM)
    q_spec = pl.BlockSpec((1, rows, heads * HEAD_DIM), lambda t, g: (t, 0, g))
    own_spec = pl.BlockSpec((hubs, 2, 1, pieces, HEAD_DIM), lambda t, g: (0, 0, t, 0, g))
    anc_spec = pl.BlockSpec((hubs, depth, 2, pieces, HEAD_DIM), lambda t, g: (0, t, 0, 0, g))
    return pl.pallas_call(
        attend_kernel,
        grid=(trees, groups),
        in_specs=[smem, smem, q_spec, q_spec, own_spec, anc_spec],
        out_specs=[q_spec, own_spec, anc_spec],
        out_shape=[
            jax.ShapeDtypeStruct(queries.shape, BF16),
            jax.ShapeDtypeStruct(own.shape, BF16),
            jax.ShapeDtypeStruct(foreign.shape, BF16),
        ],
        scratch_shapes=[
            pltpu.VMEM((heads * rows, HEAD_DIM), BF16),
            pltpu.VMEM((heads * rows, HEAD_DIM), BF16),
            pltpu.VMEM((span, heads * rows), BF16),
            pltpu.VMEM((span, heads * rows), BF16),
        ],
        compiler_params=pltpu.CompilerParams(vmem_limit_bytes=40 * 1024 * 1024),
    )(parents, rank, queries, output_gradient, own, foreign)


def each_need(parents, rank, half, depth, act):
    base = (rank[0] // half) * half

    def leaf(d, _):
        for t in range(2):
            block = 2 * (base + d) + t
            for k in range(depth):
                block = jnp.where(block >= 0, parents[jnp.maximum(block, 0)], -1)
                p = block // 2
                here = (p >= base) & (p < base + half)
                act(d, t * depth + k, block >= 0, here, p % half, t)
        return 0

    lax.fori_loop(0, half, leaf, 0)


def pick_kernel(depth, parents, rank, own_ref, cross_ref, out_ref):
    half = own_ref.shape[0]

    def act(d, slot, valid, here, p, t):
        @pl.when(here | ~valid)
        def _():
            out_ref[d, slot] = own_ref[p, :, t]

        @pl.when(valid & ~here)
        def _():
            out_ref[d, slot] = cross_ref[p]

    each_need(parents, rank, half, depth, act)


def collect_kernel(depth, parents, rank, in_ref, own_ref, cross_ref, cross_sum):
    half = own_ref.shape[0]
    own_ref[...] = jnp.zeros_like(own_ref)
    cross_sum[...] = jnp.zeros_like(cross_sum)

    def act(d, slot, valid, here, p, t):
        @pl.when(valid & here)
        def _():
            own_ref[p, :, t] += in_ref[d, slot].astype(F32)

        @pl.when(valid & ~here)
        def _():
            cross_sum[p] += in_ref[d, slot].astype(F32)

    each_need(parents, rank, half, depth, act)
    cross_ref[...] = cross_sum[...].astype(BF16)


def body(queries, keys, values, output_gradient, parents):
    leaf_count = lax.axis_size("leaf")
    head_count = lax.axis_size("head")
    half = leaf_count // 2
    depth = leaf_count // 4 - 2
    leaf_rank = lax.axis_index("leaf")
    rank = leaf_rank.astype(jnp.int32).reshape(1)
    upper = leaf_rank >= half
    groups = [[half * i + j for j in range(half)] for i in range(2)]
    swap = [(i, (i + half) % leaf_count) for i in range(leaf_count)]
    trees, part_rows, kv_all = keys.shape
    kv_width = kv_all // head_count
    rows = part_rows * head_count
    pieces = rows // half
    share = half // head_count
    vmem = pl.BlockSpec(memory_space=pltpu.VMEM)
    smem = pl.BlockSpec(memory_space=pltpu.SMEM)
    params = pltpu.CompilerParams(vmem_limit_bytes=40 * 1024 * 1024)

    def exchange(x):
        return lax.all_to_all(x, "leaf", 0, 0, tiled=True, axis_index_groups=groups)

    all_parents = lax.all_gather(parents, "leaf", axis=0, tiled=True)

    pair = jnp.stack([keys, values]).reshape(2, trees, share, pieces, head_count, kv_width)
    pair = pair.transpose(4, 2, 0, 1, 3, 5)
    if head_count > 1:
        pair = lax.all_to_all(pair, "head", 0, 0, tiled=True)
    mine = pair.reshape(half, 2, trees, pieces, kv_width)
    hub_own = exchange(mine)
    hub_cross = lax.ppermute(jnp.where(upper, hub_own[:, :, 1], hub_own[:, :, 0]), "leaf", swap)
    picked = pl.pallas_call(
        functools.partial(pick_kernel, depth),
        in_specs=[smem, smem, vmem, vmem],
        out_specs=vmem,
        out_shape=jax.ShapeDtypeStruct((half, trees * depth, 2, pieces, kv_width), BF16),
        compiler_params=params,
    )(all_parents, rank, hub_own, hub_cross)
    foreign = exchange(picked)

    if pieces % 16:
        mine_rows = mine.transpose(1, 2, 0, 3, 4).reshape(1, 2, trees, rows, kv_width)
        foreign_rows = foreign.transpose(1, 2, 0, 3, 4).reshape(1, trees * depth, 2, rows, kv_width)
    else:
        mine_rows, foreign_rows = mine, foreign
    query_grad, self_grad, foreign_grad = attend(
        all_parents, rank, queries, output_gradient, mine_rows, foreign_rows
    )
    if pieces % 16:
        def split(x):
            return x.reshape(x.shape[1:3] + (half, pieces, kv_width)).transpose(2, 0, 1, 3, 4)
        self_grad, foreign_grad = split(self_grad), split(foreign_grad)

    back = exchange(foreign_grad)
    own_sum, cross_sum = pl.pallas_call(
        functools.partial(collect_kernel, depth),
        in_specs=[smem, smem, vmem],
        out_specs=[vmem, vmem],
        out_shape=[
            jax.ShapeDtypeStruct((half, 2, trees, pieces, kv_width), F32),
            jax.ShapeDtypeStruct((half, 2, pieces, kv_width), BF16),
        ],
        scratch_shapes=[pltpu.VMEM((half, 2, pieces, kv_width), F32)],
        compiler_params=params,
    )(all_parents, rank, back)
    crossed = lax.ppermute(cross_sum, "leaf", swap).astype(F32)
    is_left = (jnp.arange(trees) == jnp.where(upper, 1, 0))[None, None, :, None, None]
    hub_total = (own_sum + jnp.where(is_left, crossed[:, :, None], 0.0)).astype(BF16)
    returned = exchange(hub_total)
    total = (returned.astype(F32) + self_grad.astype(F32)).astype(BF16)
    total = total.reshape(head_count, share, 2, trees, pieces, kv_width)
    if head_count > 1:
        total = lax.all_to_all(total, "head", 0, 0, tiled=True)
    total = total.transpose(2, 3, 1, 4, 0, 5).reshape(2, trees, part_rows, kv_all)
    return query_grad, total[0], total[1]


def solution(mesh):
    in_specs = (
        P("leaf", None, "head"),
        P("leaf", "head", None),
        P("leaf", "head", None),
        P("leaf", None, "head"),
        P("leaf"),
    )
    out_specs = (P("leaf", None, "head"), P("leaf", "head", None), P("leaf", "head", None))
    return jax.shard_map(body, mesh=mesh, in_specs=in_specs, out_specs=out_specs, check_vma=False)
```

time: 368 us -> 152 us (0.41); the launches traced: 361 us -> 152 us
  waiting for transfers between devices: 116 us -> 20.7 us
  starting transfers between devices: 102 us -> 9.28 us
  blocking collectives: 12.9 us -> 79.3 us
  local copies, waits for them, and re-layouts: 63.8 us -> 7.13 us
  other arithmetic: 34.6 us -> 0.58 us
  Pallas kernels: 0 us -> 33.1 us
  matrix products: 20 us -> 0 us
  loops' own time: 10.9 us -> 0 us
    all_to_all x7 -> x1, waiting for transfers between devices: 116 us -> 8.84 us  [exchange(): return lax.all_to_all(x, 'leaf', 0, 0, tiled=True, axis_index_groups=groups)]
    all_to_all x7 -> x1, starting transfers between devices: 102 us -> 3.98 us  [exchange(): return lax.all_to_all(x, 'leaf', 0, 0, tiled=True, axis_index_groups=groups)]
    all_to_all x0 -> x5, blocking collectives: none -> 68.8 us  [the longest x3 45.6 us: exchange(): return lax.all_to_all(x, 'leaf', 0, 0, tiled=True, axis_index_groups=groups)]
    pallas_call x0 -> x3, Pallas kernels: none -> 33.1 us  [the longest x1 30.2 us: attend(): pl.pallas_call(attend_kernel, grid=(trees, groups), in_specs=[smem, smem,...]
    dot_general x17 -> x0, matrix products: 20 us -> none  [the longest x4 5.12 us: slopes_of(): jnp.einsum('igrd,jgd->grij', grad_heads, block_values.reshape(-1, groups,...]
    convert_element_type x6 -> x3, other arithmetic: 19 us -> 0.49 us  [the longest x1 0.25 us: body(): (own_sum + jnp.where(is_left, crossed[:, :, None], 0.0)).astype(BF16)]
    another operation x12 -> x4, local copies, waits for them, and re-layouts: 15.6 us -> 2.36 us  [body(): jnp.stack([keys, values])]
    unnamed x60 -> x11, local copies, waits for them, and re-layouts: 14.8 us -> 2.44 us
  transfers between devices with their start and end apart: 7 -> 3, of which waited for: 5 -> 2; matrix products, arithmetic and copies ran while one was open for 17% -> 1% of each run, Pallas kernels for 0% -> 0%
where the time goes in v1:
time: 152 us
  blocking collectives  79.3 us (52%)
  Pallas kernels  33.1 us (22%)
  waiting for transfers between devices  20.7 us (14%)
  starting transfers between devices  9.28 us (6%)
  local copies, waits for them, and re-layouts  7.13 us (5%)
    all_to_all x3, blocking collectives, exchange(): return lax.all_to_all(x, 'leaf', 0, 0, tiled=True, axis_index_groups=groups)  45.6 us
    pallas_call x1, Pallas kernels, attend(): pl.pallas_call(attend_kernel, grid=(trees, groups), in_specs=[smem, smem,...  30.2 us
    all_to_all x1, blocking collectives, body(): pair = lax.all_to_all(pair, 'head', 0, 0, tiled=True)  12.6 us
    ppermute x1, waiting for transfers between devices, body(): crossed = lax.ppermute(cross_sum, 'leaf', swap).astype(F32)  11.9 us
    all_to_all x1, blocking collectives, body(): total = lax.all_to_all(total, 'head', 0, 0, tiled=True)  10.6 us
    unnamed x1, blocking collectives  10.5 us
    all_to_all x1, waiting for transfers between devices, exchange(): return lax.all_to_all(x, 'leaf', 0, 0, tiled=True, axis_index_groups=groups)  8.84 us
    all_to_all x1, starting transfers between devices, exchange(): return lax.all_to_all(x, 'leaf', 0, 0, tiled=True, axis_index_groups=groups)  3.98 us
  transfers between devices with their start and end apart: 3, of which 2 were waited for; matrix products, arithmetic and copies ran while one was open for 1% of the time, Pallas kernels for 0%

profile of v1, /device:TPU:0, one launch (start us, length us, event | category | flops | bytes accessed | tf_op | source)
XLA Modules:
  0.0 151.6 jit_solution(11085504209208391363)
XLA Ops:
  0.6 1.1 stack.9
  1.8 1.2 stack.10
  3.0 0.0 copy-start.3
  3.0 0.0 copy-start.2
  3.0 0.1 maximum_bitcast_fusion
  3.1 12.6 %all_to_all.30 = bf16[2,4,2,2,16,512]{5,4,3,2,1,0:T(8,128)(2,1)} all-to-all(bf16[2,4,2,2,16,512]{5,4,3,2,1,0:T(8,128)(2,1)S(1)} %maximum_bitcast_fusion), channel_id=1, replica_groups=mesh['head'=2,'leaf'=16] {'head'}, dimensions={0} | all-to-all | bytes 1048576 | tf_op jit(solution)/shard_map/all_to_all | solution.py:192
  15.7 4.0 %all-to-all-start.1 = ((bf16[8,2,2,16,512]{4,3,2,1,0:T(8,128)(2,1)}), bf16[8,2,2,16,512]{4,3,2,1,0:T(8,128)(2,1)S(1)}, u32[]{:S(2)}, u32[]{:S(2)}) async-start(bf16[8,2,2,16,512]{4,3,2,1,0:T(8,128)(2,1)} %bitcast.3.self_ref), calls=%async_computation.1 | async-start | bytes 1048576 | tf_op jit(solution)/shard_map/all_to_all | solution.py:185
  19.7 8.8 %all-to-all-done.1.own_ref = bf16[8,2,2,16,512]{4,3,2,1,0:T(8,128)(2,1)S(1)} async-done(((bf16[8,2,2,16,512]{4,3,2,1,0:T(8,128)(2,1)}), bf16[8,2,2,16,512]{4,3,2,1,0:T(8,128)(2,1)S(1)}, u32[]{:S(2)}, u32[]{:S(2)}) %all-to-all-start.1) | async-done | bytes 524320 | tf_op jit(solution)/shard_map/all_to_all | solution.py:185
  28.6 0.0 copy-start
  28.6 2.7 %collective-permute-start = (bf16[8,2,16,512]{3,2,1,0:T(8,128)(2,1)S(1)}, bf16[8,2,16,512]{3,2,1,0:T(8,128)(2,1)S(1)}, u32[]{:S(2)}, u32[]{:S(2)}) collective-permute-start(bf16[8,2,16,512]{3,2,1,0:T(8,128)(2,1)S(1)} %fusion), channel_id=1, source_target_pairs={{0,8},{1,9},{2,10},{3,11},{4,12},{5,13},{6,14},{7,15},{8,0},{9,1},... | collective-permute-start | bytes 786440 | tf_op jit(solution)/shard_map/ppermute | solution.py:195
  31.3 0.0 copy-done.3
  31.3 0.6 dynamic-slice
  32.5 0.0 copy-done.2
  32.5 0.2 dynamic-update-slice
  32.7 10.5 %all-reduce.parents = s32[32]{0:T(128)S(1)} all-reduce(s32[32]{0:T(128)S(1)} %dynamic-update-slice), channel_id=1, replica_groups=mesh['head'=2,'leaf'=16] {'leaf'}, use_global_device_ids=true, to_apply=%add | all-reduce | flops 32 | bytes 256
  43.2 0.0 collective-permute-done.cross_ref
  43.2 1.4 shard_map.76
  44.6 17.1 %all_to_all.31.anc_ref = bf16[8,4,2,16,512]{4,3,2,1,0:T(8,128)(2,1)S(1)} all-to-all(bf16[8,4,2,16,512]{4,3,2,1,0:T(8,128)(2,1)S(1)} %shard_map.76), channel_id=1, replica_groups={{0,1,2,3,4,5,6,7},{8,9,10,11,12,13,14,15},{16,17,18,19,20,21,22,23},{24..., dimensions={0} | all-to-all | bytes 2097152 | tf_op jit(solution)/shard_map/all_to_all | solution.py:185
  61.7 0.0 copy-done
  61.7 0.0 copy-start.1
  61.7 1.6 %copy-done.1 = bf16[2,128,4096]{2,1,0:T(8,128)(2,1)S(1)} copy-done((bf16[2,128,4096]{2,1,0:T(8,128)(2,1)S(1)}, bf16[2,128,4096]{2,1,0:T(8,128)(2,1)}, u32[]{:S(2)}) %copy-start.1) | copy-done | bytes 2097176
  63.3 30.2 %shard_map.77 = (bf16[2,128,4096]{2,1,0:T(8,128)(2,1)}, bf16[8,2,2,16,512]{4,3,2,1,0:T(8,128)(2,1)S(1)}, bf16[8,4,2,16,512]{4,3,2,1,0:T(8,128)(2,1)S(1)}) custom-call(s32[32]{0:T(128)S(1)} %all-reduce.parents, s32[1]{0:T(128)} %bitcast.1.rank, bf16[2,128,4096]{2,1,0:T(8,128)(2,1)S(1)} %copy-done, bf16[2,128,4096]{2,1,0:T(8,128)(2,1)S(1)} %copy-done.1, ...), custom_call_target="tpu_custom_call" | custom-call | tf_op jit(solution)/shard_map/pallas_call | solution.py:96
  93.5 17.2 %all_to_all.32.in_ref = bf16[8,4,2,16,512]{4,3,2,1,0:T(8,128)(2,1)S(1)} all-to-all(bf16[8,4,2,16,512]{4,3,2,1,0:T(8,128)(2,1)S(1)} %get-tuple-element.9), channel_id=1, replica_groups={{0,1,2,3,4,5,6,7},{8,9,10,11,12,13,14,15},{16,17,18,19,20,21,22,23},{24..., dimensions={0} | all-to-all | bytes 2097152 | tf_op jit(solution)/shard_map/all_to_all | solution.py:185
  110.7 1.6 %shard_map.78 = (f32[8,2,2,16,512]{4,3,2,1,0:T(8,128)S(1)}, bf16[8,2,16,512]{3,2,1,0:T(8,128)(2,1)S(1)}) custom-call(s32[32]{0:T(128)S(1)} %all-reduce.parents, s32[1]{0:T(128)} %bitcast.1.rank, bf16[8,4,2,16,512]{4,3,2,1,0:T(8,128)(2,1)S(1)} %all_to_all.32.in_ref), custom_call_target="tpu_custom_call" | custom-call | tf_op jit(solution)/shard_map/pallas_call | solution.py:219
  112.2 2.7 %collective-permute-start.1 = (bf16[8,2,16,512]{3,2,1,0:T(8,128)(2,1)S(1)}, bf16[8,2,16,512]{3,2,1,0:T(8,128)(2,1)S(1)}, u32[]{:S(2)}, u32[]{:S(2)}) collective-permute-start(bf16[8,2,16,512]{3,2,1,0:T(8,128)(2,1)S(1)} %get-tuple-element.11), channel_id=1, source_target_pairs={{0,8},{1,9},{2,10},{3,11},{4,12},{5,13},{6,14},{7,15},{8,0},{9,1},... | collective-permute-start | bytes 786440 | tf_op jit(solution)/shard_map/ppermute | solution.py:230
  114.9 11.9 %collective-permute-done.1 = bf16[8,2,16,512]{3,2,1,0:T(8,128)(2,1)S(1)} collective-permute-done((bf16[8,2,16,512]{3,2,1,0:T(8,128)(2,1)S(1)}, bf16[8,2,16,512]{3,2,1,0:T(8,128)(2,1)S(1)}, u32[]{:S(2)}, u32[]{:S(2)}) %collective-permute-start.1) | collective-permute-done | bytes 262176 | tf_op jit(solution)/shard_map/ppermute | solution.py:230
  126.9 0.2 add_convert_fusion.1
  127.1 11.3 %all_to_all.33 = bf16[8,2,2,16,512]{4,3,2,1,0:T(8,128)(2,1)S(1)} all-to-all(bf16[8,2,2,16,512]{4,3,2,1,0:T(8,128)(2,1)S(1)} %add_convert_fusion.1), channel_id=1, replica_groups={{0,1,2,3,4,5,6,7},{8,9,10,11,12,13,14,15},{16,17,18,19,20,21,22,23},{24..., dimensions={0} | all-to-all | bytes 1048576 | tf_op jit(solution)/shard_map/all_to_all | solution.py:185
  138.4 0.2 add_convert_fusion
  138.6 10.6 %all_to_all.34 = bf16[2,4,2,2,16,512]{5,4,3,2,1,0:T(8,128)(2,1)S(1)} all-to-all(bf16[2,4,2,2,16,512]{5,4,3,2,1,0:T(8,128)(2,1)S(1)} %bitcast.9), channel_id=1, replica_groups=mesh['head'=2,'leaf'=16] {'head'}, dimensions={0} | all-to-all | bytes 1048576 | tf_op jit(solution)/shard_map/all_to_all | solution.py:237
  149.3 0.3 copy.11
  149.5 0.9 squeeze.9
  150.4 0.3 copy.10
  150.7 0.9 squeeze.8
  (7 shorter events, 0.2 us)
Async XLA Ops:
  3.0 28.2 %copy-start.3 = (u32[32]{0:T(128)S(1)}, u32[32]{0:T(128)}, u32[]{:S(2)}) copy-start(u32[32]{0:T(128)} %constant.19) | copy-start | bytes 388
  3.0 29.5 %copy-start.2 = (s32[2]{0:T(128)S(1)}, s32[2]{0:T(128)}, u32[]{:S(2)}) copy-start(s32[2]{0:T(128)} %param.9) | copy-start | bytes 28
  15.7 12.8 %all-to-all-start.1 = ((bf16[8,2,2,16,512]{4,3,2,1,0:T(8,128)(2,1)}), bf16[8,2,2,16,512]{4,3,2,1,0:T(8,128)(2,1)S(1)}, u32[]{:S(2)}, u32[]{:S(2)}) async-start(bf16[8,2,2,16,512]{4,3,2,1,0:T(8,128)(2,1)} %bitcast.3.self_ref), calls=%async_computation.1 | async-start | bytes 1048576 | tf_op jit(solution)/shard_map/all_to_all | solution.py:185
  28.6 33.1 %copy-start = (bf16[2,128,4096]{2,1,0:T(8,128)(2,1)S(1)}, bf16[2,128,4096]{2,1,0:T(8,128)(2,1)}, u32[]{:S(2)}) copy-start(bf16[2,128,4096]{2,1,0:T(8,128)(2,1)} %q_ref.1) | copy-start | bytes 6291460
  28.6 14.6 %collective-permute-start = (bf16[8,2,16,512]{3,2,1,0:T(8,128)(2,1)S(1)}, bf16[8,2,16,512]{3,2,1,0:T(8,128)(2,1)S(1)}, u32[]{:S(2)}, u32[]{:S(2)}) collective-permute-start(bf16[8,2,16,512]{3,2,1,0:T(8,128)(2,1)S(1)} %fusion), channel_id=1, source_target_pairs={{0,8},{1,9},{2,10},{3,11},{4,12},{5,13},{6,14},{7,15},{8,0},{9,1},... | collective-permute-start | bytes 786440 | tf_op jit(solution)/shard_map/ppermute | solution.py:195
  61.7 1.6 %copy-start.1 = (bf16[2,128,4096]{2,1,0:T(8,128)(2,1)S(1)}, bf16[2,128,4096]{2,1,0:T(8,128)(2,1)}, u32[]{:S(2)}) copy-start(bf16[2,128,4096]{2,1,0:T(8,128)(2,1)} %do_ref.1) | copy-start | bytes 6291460
  112.2 14.6 %collective-permute-start.1 = (bf16[8,2,16,512]{3,2,1,0:T(8,128)(2,1)S(1)}, bf16[8,2,16,512]{3,2,1,0:T(8,128)(2,1)S(1)}, u32[]{:S(2)}, u32[]{:S(2)}) collective-permute-start(bf16[8,2,16,512]{3,2,1,0:T(8,128)(2,1)S(1)} %get-tuple-element.11), channel_id=1, source_target_pairs={{0,8},{1,9},{2,10},{3,11},{4,12},{5,13},{6,14},{7,15},{8,0},{9,1},... | collective-permute-start | bytes 786440 | tf_op jit(solution)/shard_map/ppermute | solution.py:230

commit v2 on v1

v2 whole, which is shorter than its diff:
```python
import functools
import math

import jax
import jax.numpy as jnp
from jax import lax
from jax.experimental import pallas as pl
from jax.experimental.pallas import tpu as pltpu
from jax.sharding import PartitionSpec as P

HEAD_DIM = 128

NT = (((1,), (1,)), ((), ()))
NN = (((1,), (0,)), ((), ()))
F32 = jnp.float32
BF16 = jnp.bfloat16
VMEM = pl.BlockSpec(memory_space=pltpu.VMEM)
SMEM = pl.BlockSpec(memory_space=pltpu.SMEM)
PARAMS = pltpu.CompilerParams(vmem_limit_bytes=40 * 1024 * 1024)


def dot(a, b, dims=NN):
    return lax.dot_general(a, b, dims, preferred_element_type=F32)


def attend_kernel(
    place, parents, q_ref, do_ref, self_ref, anc_ref, _, dq_ref, dself_ref, danc_ref, qs, dos, ps, ds
):
    hubs, depth, _, pieces, _ = anc_ref.shape
    rows = q_ref.shape[1]
    heads = q_ref.shape[2] // HEAD_DIM
    scale = HEAD_DIM ** (-0.5)
    c = scale * math.log2(math.e)
    block = 2 * place[0] + place[1]
    valid = []
    for _ in range(depth):
        block = jnp.where(block >= 0, parents[jnp.maximum(block, 0)], -1)
        valid.append(block >= 0)

    def seen(which):
        tiles = [anc_ref[:, k, which].reshape(rows, HEAD_DIM) for k in range(depth)]
        return jnp.concatenate([self_ref[which, 0]] + tiles, 0)

    keys, values = seen(0), seen(1)
    for h in range(heads):
        qs[h * rows : (h + 1) * rows, :] = q_ref[0, :, h * HEAD_DIM : (h + 1) * HEAD_DIM]
        dos[h * rows : (h + 1) * rows, :] = do_ref[0, :, h * HEAD_DIM : (h + 1) * HEAD_DIM]
    hidden = lax.broadcasted_iota(jnp.int32, (rows, rows), 0) > lax.broadcasted_iota(jnp.int32, (rows, rows), 1)
    scores = dot(keys, qs[...], NT)
    slopes = dot(values, dos[...], NT)
    for h in range(heads):
        part = slice(h * rows, (h + 1) * rows)
        s = [scores[k * rows : (k + 1) * rows, part] for k in range(depth + 1)]
        d = [slopes[k * rows : (k + 1) * rows, part] for k in range(depth + 1)]
        s[0] = jnp.where(hidden, -1e30, s[0])
        peak = jnp.max(s[0], 0, keepdims=True)
        for k in range(depth):
            peak = jnp.maximum(peak, jnp.where(valid[k], jnp.max(s[k + 1], 0, keepdims=True), -1e30))
        peak = peak * c
        e = [jnp.exp2(s[0] * c - peak)]
        for k in range(depth):
            e.append(jnp.exp2(s[k + 1] * c - jnp.where(valid[k], peak, 1e30)))
        total = functools.reduce(jnp.add, [jnp.sum(x, 0, keepdims=True) for x in e])
        weighted = functools.reduce(jnp.add, [jnp.sum(x * y, 0, keepdims=True) for x, y in zip(e, d)])
        inverse = 1.0 / total
        mean = weighted * inverse
        for k in range(depth + 1):
            p = e[k] * inverse
            ps[k * rows : (k + 1) * rows, part] = p.astype(BF16)
            ds[k * rows : (k + 1) * rows, part] = (p * (d[k] - mean)).astype(BF16)
    dq_t = dot(keys.T, ds[...]) * scale
    for h in range(heads):
        dq_ref[0, :, h * HEAD_DIM : (h + 1) * HEAD_DIM] = dq_t[:, h * rows : (h + 1) * rows].T.astype(BF16)
    grads = [dot(ds[...], qs[...]) * scale, dot(ps[...], dos[...])]
    for which in range(2):
        dself_ref[which] = grads[which][:rows].astype(BF16)
        for k in range(depth):
            grad = grads[which][(k + 1) * rows : (k + 2) * rows].astype(BF16)
            danc_ref[:, k, which] = grad.reshape(hubs, pieces, HEAD_DIM)


def attend(place, parents, queries, output_gradient, own, foreign, query_grad):
    _, rows, width = queries.shape
    hubs, depth, _, pieces, kv_width = foreign.shape
    groups = kv_width // HEAD_DIM
    heads = width // groups // HEAD_DIM
    span = (depth + 1) * rows
    q_spec = pl.BlockSpec((1, rows, heads * HEAD_DIM), lambda g, place, _: (place[1], 0, g))
    own_spec = pl.BlockSpec((2, 1, rows, HEAD_DIM), lambda g, place, _: (0, place[1], 0, g))
    dself_spec = pl.BlockSpec((2, rows, HEAD_DIM), lambda g, place, _: (0, 0, g))
    anc_spec = pl.BlockSpec((hubs, depth, 2, pieces, HEAD_DIM), lambda g, place, _: (0, 0, 0, 0, g))
    hbm = pl.BlockSpec(memory_space=pl.ANY)
    first = query_grad is None
    return pl.pallas_call(
        attend_kernel,
        grid_spec=pltpu.PrefetchScalarGridSpec(
            num_scalar_prefetch=2,
            grid=(groups,),
            in_specs=[q_spec, q_spec, own_spec, anc_spec, SMEM if first else hbm],
            out_specs=[q_spec, dself_spec, anc_spec],
            scratch_shapes=[
                pltpu.VMEM((heads * rows, HEAD_DIM), BF16),
                pltpu.VMEM((heads * rows, HEAD_DIM), BF16),
                pltpu.VMEM((span, heads * rows), BF16),
                pltpu.VMEM((span, heads * rows), BF16),
            ],
        ),
        out_shape=[
            jax.ShapeDtypeStruct(queries.shape, BF16),
            jax.ShapeDtypeStruct((2, rows, kv_width), BF16),
            jax.ShapeDtypeStruct(foreign.shape, BF16),
        ],
        input_output_aliases={} if first else {6: 0},
        compiler_params=PARAMS,
        cost_estimate=pl.CostEstimate(
            flops=10 * groups * heads * span * rows * HEAD_DIM,
            bytes_accessed=6 * rows * width,
            transcendentals=groups * heads * span * rows,
        ),
    )(place, parents, queries, output_gradient, own, foreign, place if first else query_grad)


def each_need(place, parents, half, depth, which, act):
    base = (place[0] // half) * half
    t = place[1 + which]

    def leaf(d, _):
        block = 2 * (base + d) + t
        for k in range(depth):
            block = jnp.where(block >= 0, parents[jnp.maximum(block, 0)], -1)
            p = block // 2
            act(d, k, block >= 0, (p >= base) & (p < base + half), p % half, t)
        return 0

    lax.fori_loop(0, half, leaf, 0)


def pick_near_kernel(place, parents, own_ref, out_ref):
    half, depth = out_ref.shape[:2]

    def act(d, slot, valid, here, p, t):
        out_ref[d, slot] = own_ref[p, :, t]

    each_need(place, parents, half, depth, 0, act)


def pick_far_kernel(place, parents, own_ref, cross_ref, out_ref):
    half, depth = out_ref.shape[:2]

    def act(d, slot, valid, here, p, t):
        @pl.when(here | ~valid)
        def _():
            out_ref[d, slot] = own_ref[p, :, t]

        @pl.when(valid & ~here)
        def _():
            out_ref[d, slot] = cross_ref[p]

    each_need(place, parents, half, depth, 1, act)


def collect_near_kernel(place, parents, in_ref, own_ref):
    half, depth = in_ref.shape[:2]
    own_ref[...] = jnp.zeros_like(own_ref)

    def act(d, slot, valid, here, p, t):
        @pl.when(valid)
        def _():
            own_ref[p] += in_ref[d, slot].astype(F32)

    each_need(place, parents, half, depth, 0, act)


def collect_far_kernel(place, parents, in_ref, own_ref, cross_ref, sums):
    half, depth = in_ref.shape[:2]
    sums[...] = jnp.zeros_like(sums)

    def act(d, slot, valid, here, p, t):
        @pl.when(valid)
        def _():
            sums[jnp.where(here, 0, half) + p] += in_ref[d, slot].astype(F32)

    each_need(place, parents, half, depth, 1, act)
    own_ref[...] = sums[:half].astype(BF16)
    cross_ref[...] = sums[half:].astype(BF16)


def body(queries, keys, values, output_gradient, parents):
    leaf_count = lax.axis_size("leaf")
    head_count = lax.axis_size("head")
    half = leaf_count // 2
    depth = leaf_count // 4 - 2
    leaf_rank = lax.axis_index("leaf")
    head_rank = lax.axis_index("head")
    upper = leaf_rank >= half
    near = jnp.where(upper, 1, 0)
    place = jnp.stack([leaf_rank, near, 1 - near]).astype(jnp.int32)
    far_place = jnp.stack([leaf_rank, 1 - near]).astype(jnp.int32)
    sides = [[half * i + j for j in range(half)] for i in range(2)]
    both = [[leaf_count * h + j for h in range(head_count) for j in side] for side in sides]
    swap = [(i, (i + half) % leaf_count) for i in range(leaf_count)]
    trees, part_rows, kv_all = keys.shape
    kv_width = kv_all // head_count
    rows = part_rows * head_count
    pieces = rows // half
    merged = head_count == 2 and part_rows % half == 0
    bits = part_rows // half if merged else 0

    def exchange(x):
        return lax.all_to_all(x, "leaf", 0, 0, tiled=True, axis_index_groups=sides)

    def exchange_both(x):
        return lax.all_to_all(x, ("head", "leaf"), 0, 0, tiled=True, axis_index_groups=both)

    def to_other_head(x):
        return lax.ppermute(x, "head", [(0, 1), (1, 0)])

    def other(x, axis):
        return lax.dynamic_index_in_dim(x, 1 - head_rank, axis, keepdims=False)

    def this(x, axis):
        return lax.dynamic_index_in_dim(x, head_rank, axis, keepdims=False)

    def by_head(mine, theirs, axis):
        low = jnp.where(head_rank == 0, mine, theirs)
        high = jnp.where(head_rank == 0, theirs, mine)
        return jnp.stack([low, high], axis)

    all_parents = lax.all_gather(parents, "leaf", axis=0, tiled=True)

    pair = jnp.stack([keys, values]).reshape(2, trees, part_rows, head_count, kv_width)
    if merged:
        pair = jnp.moveaxis(pair, 3, 0)
        send = pair.reshape(2, 2, trees, half, bits, kv_width).transpose(0, 3, 1, 2, 4, 5)
        arrived = exchange_both(send.reshape(2 * half, 2, trees, bits, kv_width))
        arrived = arrived.reshape(2, half, 2, trees, bits, kv_width).transpose(1, 2, 3, 0, 4, 5)
        hub_own = arrived.reshape(half, 2, trees, pieces, kv_width)
        theirs = to_other_head(other(pair, 0))
        mine = by_head(this(pair, 0), theirs, 2).reshape(2, trees, rows, kv_width)
    else:
        pair = jnp.moveaxis(pair, 3, 0)
        if head_count > 1:
            pair = lax.all_to_all(pair, "head", 0, 0, tiled=True)
        mine = pair.transpose(1, 2, 0, 3, 4).reshape(2, trees, rows, kv_width)
        hub_own = exchange(mine.reshape(2, trees, half, pieces, kv_width).transpose(2, 0, 1, 3, 4))

    hub_cross = lax.ppermute(jnp.where(upper, hub_own[:, :, 1], hub_own[:, :, 0]), "leaf", swap)
    picked_shape = jax.ShapeDtypeStruct((half, depth, 2, pieces, kv_width), BF16)
    picked_near = pl.pallas_call(
        pick_near_kernel,
        in_specs=[SMEM, SMEM, VMEM],
        out_specs=VMEM,
        out_shape=picked_shape,
        compiler_params=PARAMS,
    )(place, all_parents, hub_own)
    foreign_near = exchange(picked_near)
    picked_far = pl.pallas_call(
        pick_far_kernel,
        in_specs=[SMEM, SMEM, VMEM, VMEM],
        out_specs=VMEM,
        out_shape=picked_shape,
        compiler_params=PARAMS,
    )(place, all_parents, hub_own, hub_cross)
    foreign_far = exchange(picked_far)

    def gather_rows(x):
        if pieces % 16 == 0:
            return x
        return x.transpose(1, 2, 0, 3, 4).reshape(1, depth, 2, rows, kv_width)

    def spread_rows(x):
        if pieces % 16 == 0:
            return x
        return x.reshape(depth, 2, half, pieces, kv_width).transpose(2, 0, 1, 3, 4)

    query_grad, self_near, grad_near = attend(
        place, all_parents, queries, output_gradient, mine, gather_rows(foreign_near), None
    )
    query_grad, self_far, grad_far = attend(
        far_place, all_parents, queries, output_gradient, mine, gather_rows(foreign_far), query_grad
    )
    back_near = exchange(spread_rows(grad_near))
    back_far = exchange(spread_rows(grad_far))

    sum_shape = (half, 2, pieces, kv_width)
    far_sum, cross_sum = pl.pallas_call(
        collect_far_kernel,
        in_specs=[SMEM, SMEM, VMEM],
        out_specs=[VMEM, VMEM],
        out_shape=[jax.ShapeDtypeStruct(sum_shape, BF16)] * 2,
        scratch_shapes=[pltpu.VMEM((2 * half,) + sum_shape[1:], F32)],
        compiler_params=PARAMS,
    )(place, all_parents, back_far)
    near_sum = pl.pallas_call(
        collect_near_kernel,
        in_specs=[SMEM, SMEM, VMEM],
        out_specs=VMEM,
        out_shape=jax.ShapeDtypeStruct(sum_shape, F32),
        compiler_params=PARAMS,
    )(place, all_parents, back_near)
    crossed = lax.ppermute(cross_sum, "leaf", swap)
    near_sum = (near_sum + crossed.astype(F32)).astype(BF16)
    hub_sum = jnp.stack([near_sum, far_sum], 1)
    self_sum = jnp.stack([self_near, self_far])
    if merged:
        hub_sum = hub_sum.reshape(half, 2, 2, 2, bits, kv_width).transpose(3, 0, 1, 2, 4, 5)
        returned = exchange_both(hub_sum.reshape(2 * half, 2, 2, bits, kv_width))
        returned = returned.reshape(2, half, 2, 2, bits, kv_width).transpose(0, 2, 3, 1, 4, 5)
        returned = returned.reshape(2, 2, 2, part_rows, kv_width)
        self_sum = self_sum.reshape(2, 2, 2, part_rows, kv_width)
        theirs = to_other_head(other(self_sum, 2))
        total = returned.astype(F32) + by_head(this(self_sum, 2), theirs, 0).astype(F32)
        total = total.astype(BF16)
    else:
        returned = exchange(hub_sum).transpose(1, 2, 0, 3, 4).reshape(2, 2, rows, kv_width)
        total = (returned.astype(F32) + self_sum.astype(F32)).astype(BF16)
        total = jnp.moveaxis(total.reshape(2, 2, head_count, part_rows, kv_width), 2, 0)
        if head_count > 1:
            total = lax.all_to_all(total, "head", 0, 0, tiled=True)
    total = total.transpose(2, 1, 3, 0, 4).reshape(2, 2, part_rows, kv_all)
    total = jnp.where(upper, total[:, ::-1], total)
    return query_grad, total[0], total[1]


def solution(mesh):
    in_specs = (
        P("leaf", None, "head"),
        P("leaf", "head", None),
        P("leaf", "head", None),
        P("leaf", None, "head"),
        P("leaf"),
    )
    out_specs = (P("leaf", None, "head"), P("leaf", "head", None), P("leaf", "head", None))
    return jax.shard_map(body, mesh=mesh, in_specs=in_specs, out_specs=out_specs, check_vma=False)
```

time: 152 us -> 144 us (0.947)
  blocking collectives: 79.3 us -> 27.1 us
  waiting for transfers between devices: 20.7 us -> 48.1 us
  starting transfers between devices: 9.28 us -> 25.1 us
  local copies, waits for them, and re-layouts: 7.13 us -> 14.6 us
  Pallas kernels: 33.1 us -> 25.7 us
    all_to_all x5 -> x1, blocking collectives: 68.8 us -> 12.5 us  [exchange(): return lax.all_to_all(x, 'leaf', 0, 0, tiled=True, axis_index_groups=sides)]
    all_to_all x1 -> x5, starting transfers between devices: 3.98 us -> 20.7 us  [the longest x3 10.5 us: exchange(): return lax.all_to_all(x, 'leaf', 0, 0, tiled=True, axis_index_groups=sides)]
    ppermute x1, waiting for transfers between devices: 0.01 us -> 14.9 us  [body(): lax.ppermute(jnp.where(upper, hub_own[:, :, 1], hub_own[:, :, 0]), 'leaf'...]
    ppermute x1 -> x3, waiting for transfers between devices: 11.9 us -> 22.4 us  [the longest x2 19.4 us: to_other_head(): return lax.ppermute(x, 'head', [(0, 1), (1, 0)])]
    pallas_call x3 -> x6, Pallas kernels: 33.1 us -> 25.7 us  [the longest x2 20.2 us: attend(): pl.pallas_call(attend_kernel, grid_spec=pltpu.PrefetchScalarGridSpec(num_...]
    unnamed x11 -> x17, local copies, waits for them, and re-layouts: 2.44 us -> 7.43 us
    unnamed x1, blocking collectives: 10.5 us -> 14.6 us
    ppermute x1, starting transfers between devices: 2.65 us -> 0.41 us  [body(): lax.ppermute(jnp.where(upper, hub_own[:, :, 1], hub_own[:, :, 0]), 'leaf'...]
  transfers between devices with their start and end apart: 3 -> 9, of which waited for: 2 -> 5; matrix products, arithmetic and copies ran while one was open for 1% -> 2% of each run, Pallas kernels for 0% -> 10%
where the time goes in v2:
time: 144 us; the launch traced here: 143 us
  waiting for transfers between devices  48.1 us (33%)
  blocking collectives  27.1 us (19%)
  Pallas kernels  25.7 us (18%)
  starting transfers between devices  25.1 us (17%)
  local copies, waits for them, and re-layouts  14.6 us (10%)
  between operations  1.52 us (1%)
    pallas_call x2, Pallas kernels, attend(): pl.pallas_call(attend_kernel, grid_spec=pltpu.PrefetchScalarGridSpec(num_...  20.2 us
    ppermute x2, waiting for transfers between devices, to_other_head(): return lax.ppermute(x, 'head', [(0, 1), (1, 0)])  19.4 us
    ppermute x1, waiting for transfers between devices, body(): lax.ppermute(jnp.where(upper, hub_own[:, :, 1], hub_own[:, :, 0]), 'leaf'...  14.9 us
    unnamed x1, blocking collectives  14.6 us
    all_to_all x1, blocking collectives, exchange(): return lax.all_to_all(x, 'leaf', 0, 0, tiled=True, axis_index_groups=sides)  12.5 us
    all_to_all x3, waiting for transfers between devices, exchange(): return lax.all_to_all(x, 'leaf', 0, 0, tiled=True, axis_index_groups=sides)  10.8 us
    all_to_all x3, starting transfers between devices, exchange(): return lax.all_to_all(x, 'leaf', 0, 0, tiled=True, axis_index_groups=sides)  10.5 us
    all_to_all x2, starting transfers between devices, exchange_both(): lax.all_to_all(x, ('head', 'leaf'), 0, 0, tiled=True, axis_index_groups=b...  10.2 us
  transfers between devices with their start and end apart: 9, of which 5 were waited for; matrix products, arithmetic and copies ran while one was open for 2% of the time, Pallas kernels for 10%

profile of v2, /device:TPU:0, one launch (start us, length us, event | category | flops | bytes accessed | tf_op | source)
XLA Modules:
  0.0 142.9 jit_solution(14380441640215953927)
XLA Ops:
  0.6 0.0 copy-start.5
  0.6 0.0 copy-start.4
  0.7 1.2 stack.65
  1.8 0.2 constant_dynamic-update-slice_fusion.1
  2.0 1.2 stack.66
  3.2 0.2 constant_dynamic-update-slice_fusion
  3.4 0.9 copy.18
  4.2 6.3 %all-to-all-start = ((bf16[16,2,2,8,512]{4,3,2,1,0:T(8,128)(2,1)}), bf16[16,2,2,8,512]{4,3,2,1,0:T(8,128)(2,1)S(1)}, u32[]{:S(2)}, u32[]{:S(2)}) async-start(bf16[16,2,2,8,512]{4,3,2,1,0:T(8,128)(2,1)} %bitcast.10), calls=%async_computation | async-start | bytes 1048576 | tf_op jit(solution)/shard_map/all_to_all | solution.py:213
  10.6 0.0 copy-done.5
  10.6 0.6 dynamic-slice.8
  11.8 0.0 copy-done.4
  11.8 0.2 dynamic-update-slice
  12.1 14.6 %all-reduce.parents = s32[32]{0:T(128)S(1)} all-reduce(s32[32]{0:T(128)S(1)} %dynamic-update-slice), channel_id=1, replica_groups=mesh['head'=2,'leaf'=16] {'leaf'}, use_global_device_ids=true, to_apply=%add | all-reduce | flops 32 | bytes 256
  26.6 0.1 pad_add_fusion.1.place._
  26.7 0.0 all-to-all-done
  26.7 0.1 copy.34
  26.8 1.6 %shard_map.77 = bf16[8,2,2,16,512]{4,3,2,1,0:T(8,128)(2,1)} custom-call(s32[3]{0:T(128)S(1)} %pad_add_fusion.1.place._, s32[32]{0:T(128)S(1)} %all-reduce.parents, bf16[8,2,2,16,512]{4,3,2,1,0:T(8,128)(2,1)S(1)} %bitcast.70), custom_call_target="tpu_custom_call" | custom-call | tf_op jit(solution)/shard_map/pallas_call | solution.py:249
  28.4 3.5 %all-to-all-start.2 = ((bf16[8,2,2,16,512]{4,3,2,1,0:T(8,128)(2,1)}), bf16[8,2,2,16,512]{4,3,2,1,0:T(8,128)(2,1)S(1)}, u32[]{:S(2)}, u32[]{:S(2)}) async-start(bf16[8,2,2,16,512]{4,3,2,1,0:T(8,128)(2,1)} %shard_map.77), calls=%async_computation.2 | async-start | bytes 1048576 | tf_op jit(solution)/shard_map/all_to_all | solution.py:210
  31.9 0.4 collective-permute-start.1
  32.3 14.9 %collective-permute-done.1.cross_ref = bf16[8,2,16,512]{3,2,1,0:T(8,128)(2,1)S(1)} collective-permute-done((bf16[8,2,16,512]{3,2,1,0:T(8,128)(2,1)S(1)}, bf16[8,2,16,512]{3,2,1,0:T(8,128)(2,1)S(1)}, u32[]{:S(2)}, u32[]{:S(2)}) %collective-permute-start.1) | collective-permute-done | bytes 262176 | tf_op jit(solution)/shard_map/ppermute | solution.py:247
  47.2 1.8 %shard_map.76 = bf16[8,2,2,16,512]{4,3,2,1,0:T(8,128)(2,1)} custom-call(s32[3]{0:T(128)S(1)} %pad_add_fusion.1.place._, s32[32]{0:T(128)S(1)} %all-reduce.parents, bf16[8,2,2,16,512]{4,3,2,1,0:T(8,128)(2,1)S(1)} %bitcast.72, bf16[8,2,16,512]{3,2,1,0:T(8,128)(2,1)S(1)} %collective-permute-done.1.cross_ref), custom_call_target="tpu_custom_call" | custom-call | tf_op jit(solution)/shard_map/pallas_call | solution.py:257
  49.0 0.0 all-to-all-done.2.anc_ref
  49.0 3.5 %all-to-all-start.1 = ((bf16[8,2,2,16,512]{4,3,2,1,0:T(8,128)(2,1)}), bf16[8,2,2,16,512]{4,3,2,1,0:T(8,128)(2,1)S(1)}, u32[]{:S(2)}, u32[]{:S(2)}) async-start(bf16[8,2,2,16,512]{4,3,2,1,0:T(8,128)(2,1)} %shard_map.76), calls=%async_computation.1 | async-start | bytes 1048576 | tf_op jit(solution)/shard_map/all_to_all | solution.py:210
  52.5 1.1 constant_dynamic-slice_fusion.1
  53.6 1.5 %collective-permute-start = (bf16[2,2,64,512]{3,2,1,0:T(8,128)(2,1)S(1)}, bf16[2,2,64,512]{3,2,1,0:T(8,128)(2,1)S(1)}, u32[]{:S(2)}, u32[]{:S(2)}) collective-permute-start(bf16[2,2,64,512]{3,2,1,0:T(8,128)(2,1)S(1)} %bitcast.83), channel_id=1, source_target_pairs={{0,16},{16,0},{1,17},{17,1},{2,18},{18,2},{3,19},{19,3},{4,20},{20... | collective-permute-start | bytes 786440 | tf_op jit(solution)/shard_map/ppermute | solution.py:216
  55.2 0.1 pad_add_fusion.place
  55.2 7.1 %collective-permute-done = bf16[2,2,64,512]{3,2,1,0:T(8,128)(2,1)S(1)} collective-permute-done((bf16[2,2,64,512]{3,2,1,0:T(8,128)(2,1)S(1)}, bf16[2,2,64,512]{3,2,1,0:T(8,128)(2,1)S(1)}, u32[]{:S(2)}, u32[]{:S(2)}) %collective-permute-start) | collective-permute-done | bytes 262176 | tf_op jit(solution)/shard_map/ppermute | solution.py:216
  62.4 0.1 pad_maximum_fusion
  62.5 0.0 copy-start
  62.5 1.6 %copy-done = bf16[2,128,4096]{2,1,0:T(8,128)(2,1)S(1)} copy-done((bf16[2,128,4096]{2,1,0:T(8,128)(2,1)S(1)}, bf16[2,128,4096]{2,1,0:T(8,128)(2,1)}, u32[]{:S(2)}) %copy-start) | copy-done | bytes 2097176
  64.1 0.0 copy-start.2
  64.1 1.6 %copy-done.2 = bf16[2,128,4096]{2,1,0:T(8,128)(2,1)S(1)} copy-done((bf16[2,128,4096]{2,1,0:T(8,128)(2,1)S(1)}, bf16[2,128,4096]{2,1,0:T(8,128)(2,1)}, u32[]{:S(2)}) %copy-start.2) | copy-done | bytes 2097176
  65.7 10.4 %shard_map.78 = (bf16[2,128,4096]{2,1,0:T(8,128)(2,1)}, bf16[2,128,512]{2,1,0:T(8,128)(2,1)S(1)}, bf16[8,2,2,16,512]{4,3,2,1,0:T(8,128)(2,1)}) custom-call(s32[3]{0:T(128)S(1)} %pad_add_fusion.1.place._, s32[32]{0:T(128)S(1)} %all-reduce.parents, bf16[2,128,4096]{2,1,0:T(8,128)(2,1)S(1)} %copy-done, bf16[2,128,4096]{2,1,0:T(8,128)(2,1)S(1)} %copy-done.2, ...), custom_call_target="tpu_custom_call" | custom-call | flops 2013265920 | bytes 3145728 | tf_op jit(solution)/shard_map/pallas_call | solution.py:94
  76.1 0.0 all-to-all-done.1.anc_ref
  76.1 0.0 copy-start.1
  76.1 1.6 %copy-done.1 = bf16[2,128,4096]{2,1,0:T(8,128)(2,1)S(1)} copy-done((bf16[2,128,4096]{2,1,0:T(8,128)(2,1)S(1)}, bf16[2,128,4096]{2,1,0:T(8,128)(2,1)}, u32[]{:S(2)}) %copy-start.1) | copy-done | bytes 2097176
  77.6 0.0 copy-start.3
  77.6 1.6 %copy-done.3 = bf16[2,128,4096]{2,1,0:T(8,128)(2,1)S(1)} copy-done((bf16[2,128,4096]{2,1,0:T(8,128)(2,1)S(1)}, bf16[2,128,4096]{2,1,0:T(8,128)(2,1)}, u32[]{:S(2)}) %copy-start.3) | copy-done | bytes 2097176
  79.2 9.9 %shard_map.79 = (bf16[2,128,4096]{2,1,0:T(8,128)(2,1)}, bf16[2,128,512]{2,1,0:T(8,128)(2,1)S(1)}, bf16[8,2,2,16,512]{4,3,2,1,0:T(8,128)(2,1)S(1)}) custom-call(s32[2]{0:T(128)S(1)} %pad_add_fusion.place, s32[32]{0:T(128)S(1)} %all-reduce.parents, bf16[2,128,4096]{2,1,0:T(8,128)(2,1)S(1)} %copy-done.1, ...), custom_call_target="tpu_custom_call", output_to_operand_aliasing={{0}: (6, {})} | custom-call | flops 2013265920 | bytes 3145728 | tf_op jit(solution)/shard_map/pallas_call | solution.py:94
  89.1 12.5 %all_to_all.30.in_ref = bf16[8,2,2,16,512]{4,3,2,1,0:T(8,128)(2,1)S(1)} all-to-all(bf16[8,2,2,16,512]{4,3,2,1,0:T(8,128)(2,1)S(1)} %get-tuple-element.14), channel_id=1, replica_groups={{0,1,2,3,4,5,6,7},{8,9,10,11,12,13,14,15},{16,17,18,19,20,21,22,23},{24..., dimensions={0} | all-to-all | bytes 1048576 | tf_op jit(solution)/shard_map/all_to_all | solution.py:210
  101.6 3.5 %all-to-all-start.3 = ((bf16[8,2,2,16,512]{4,3,2,1,0:T(8,128)(2,1)}), bf16[8,2,2,16,512]{4,3,2,1,0:T(8,128)(2,1)S(1)}, u32[]{:S(2)}, u32[]{:S(2)}) async-start(bf16[8,2,2,16,512]{4,3,2,1,0:T(8,128)(2,1)} %get-tuple-element.13), calls=%async_computation.3 | async-start | bytes 1048576 | tf_op jit(solution)/shard_map/all_to_all | solution.py:210
  105.1 1.1 shard_map.81
  106.2 0.5 collective-permute-start.2
  106.7 10.8 %all-to-all-done.3.in_ref = bf16[8,2,2,16,512]{4,3,2,1,0:T(8,128)(2,1)S(1)} async-done(((bf16[8,2,2,16,512]{4,3,2,1,0:T(8,128)(2,1)}), bf16[8,2,2,16,512]{4,3,2,1,0:T(8,128)(2,1)S(1)}, u32[]{:S(2)}, u32[]{:S(2)}) %all-to-all-start.3) | async-done | bytes 524320 | tf_op jit(solution)/shard_map/all_to_all | solution.py:210
  117.5 0.9 shard_map.80
  118.5 3.0 %collective-permute-done.2 = bf16[8,2,16,512]{3,2,1,0:T(8,128)(2,1)S(1)} collective-permute-done((bf16[8,2,16,512]{3,2,1,0:T(8,128)(2,1)S(1)}, bf16[8,2,16,512]{3,2,1,0:T(8,128)(2,1)S(1)}, u32[]{:S(2)}, u32[]{:S(2)}) %collective-permute-start.2) | collective-permute-done | bytes 262176 | tf_op jit(solution)/shard_map/ppermute | solution.py:301
  121.5 0.1 fusion.2
  121.5 0.1 pad_maximum_fusion.1
  121.6 0.9 copy.24
  122.5 3.9 %all-to-all-start.5 = ((bf16[16,2,2,8,512]{4,3,2,1,0:T(8,128)(2,1)}), bf16[16,2,2,8,512]{4,3,2,1,0:T(8,128)(2,1)S(1)}, u32[]{:S(2)}, u32[]{:S(2)}) async-start(bf16[16,2,2,8,512]{4,3,2,1,0:T(8,128)(2,1)} %bitcast.18), calls=%async_computation.5 | async-start | bytes 1048576 | tf_op jit(solution)/shard_map/all_to_all | solution.py:213
  126.5 2.0 %collective-permute-start.3 = (bf16[2,2,64,512]{3,2,1,0:T(8,128)(2,1)S(1)}, bf16[2,2,64,512]{3,2,1,0:T(8,128)(2,1)S(1)}, u32[]{:S(2)}, u32[]{:S(2)}) collective-permute-start(bf16[2,2,64,512]{3,2,1,0:T(8,128)(2,1)S(1)} %fusion.4), channel_id=1, source_target_pairs={{0,16},{16,0},{1,17},{17,1},{2,18},{18,2},{3,19},{19,3},{4,20},{20... | collective-permute-start | bytes 786440 | tf_op jit(solution)/shard_map/ppermute | solution.py:216
  128.4 12.3 %collective-permute-done.3 = bf16[2,2,64,512]{3,2,1,0:T(8,128)(2,1)S(1)} collective-permute-done((bf16[2,2,64,512]{3,2,1,0:T(8,128)(2,1)S(1)}, bf16[2,2,64,512]{3,2,1,0:T(8,128)(2,1)S(1)}, u32[]{:S(2)}, u32[]{:S(2)}) %collective-permute-start.3) | collective-permute-done | bytes 262176 | tf_op jit(solution)/shard_map/ppermute | solution.py:216
  140.8 0.0 all-to-all-done.5
  140.8 0.1 fusion.1
  141.0 0.5 copy.23
  141.5 0.4 reshape.60
  141.9 0.1 reverse_select_fusion
  142.0 0.8 slice_bitcast_fusion
  (7 shorter events, 0.2 us)
Async XLA Ops:
  0.6 9.9 %copy-start.5 = (u32[32]{0:T(128)S(1)}, u32[32]{0:T(128)}, u32[]{:S(2)}) copy-start(u32[32]{0:T(128)} %constant.37) | copy-start | bytes 388
  0.6 11.2 %copy-start.4 = (s32[2]{0:T(128)S(1)}, s32[2]{0:T(128)}, u32[]{:S(2)}) copy-start(s32[2]{0:T(128)} %param.9) | copy-start | bytes 28
  4.2 22.4 %all-to-all-start = ((bf16[16,2,2,8,512]{4,3,2,1,0:T(8,128)(2,1)}), bf16[16,2,2,8,512]{4,3,2,1,0:T(8,128)(2,1)S(1)}, u32[]{:S(2)}, u32[]{:S(2)}) async-start(bf16[16,2,2,8,512]{4,3,2,1,0:T(8,128)(2,1)} %bitcast.10), calls=%async_computation | async-start | bytes 1048576 | tf_op jit(solution)/shard_map/all_to_all | solution.py:213
  28.4 20.6 %all-to-all-start.2 = ((bf16[8,2,2,16,512]{4,3,2,1,0:T(8,128)(2,1)}), bf16[8,2,2,16,512]{4,3,2,1,0:T(8,128)(2,1)S(1)}, u32[]{:S(2)}, u32[]{:S(2)}) async-start(bf16[8,2,2,16,512]{4,3,2,1,0:T(8,128)(2,1)} %shard_map.77), calls=%async_computation.2 | async-start | bytes 1048576 | tf_op jit(solution)/shard_map/all_to_all | solution.py:210
  31.9 15.3 %collective-permute-start.1 = (bf16[8,2,16,512]{3,2,1,0:T(8,128)(2,1)S(1)}, bf16[8,2,16,512]{3,2,1,0:T(8,128)(2,1)S(1)}, u32[]{:S(2)}, u32[]{:S(2)}) collective-permute-start(bf16[8,2,16,512]{3,2,1,0:T(8,128)(2,1)S(1)} %fusion.7), channel_id=1, source_target_pairs={{0,8},{1,9},{2,10},{3,11},{4,12},{5,13},{6,14},{7,15},{8,0},{9,1},... | collective-permute-start | bytes 786440 | tf_op jit(solution)/shard_map/ppermute | solution.py:247
  49.0 27.1 %all-to-all-start.1 = ((bf16[8,2,2,16,512]{4,3,2,1,0:T(8,128)(2,1)}), bf16[8,2,2,16,512]{4,3,2,1,0:T(8,128)(2,1)S(1)}, u32[]{:S(2)}, u32[]{:S(2)}) async-start(bf16[8,2,2,16,512]{4,3,2,1,0:T(8,128)(2,1)} %shard_map.76), calls=%async_computation.1 | async-start | bytes 1048576 | tf_op jit(solution)/shard_map/all_to_all | solution.py:210
  53.6 8.7 %collective-permute-start = (bf16[2,2,64,512]{3,2,1,0:T(8,128)(2,1)S(1)}, bf16[2,2,64,512]{3,2,1,0:T(8,128)(2,1)S(1)}, u32[]{:S(2)}, u32[]{:S(2)}) collective-permute-start(bf16[2,2,64,512]{3,2,1,0:T(8,128)(2,1)S(1)} %bitcast.83), channel_id=1, source_target_pairs={{0,16},{16,0},{1,17},{17,1},{2,18},{18,2},{3,19},{19,3},{4,20},{20... | collective-permute-start | bytes 786440 | tf_op jit(solution)/shard_map/ppermute | solution.py:216
  62.5 1.6 %copy-start = (bf16[2,128,4096]{2,1,0:T(8,128)(2,1)S(1)}, bf16[2,128,4096]{2,1,0:T(8,128)(2,1)}, u32[]{:S(2)}) copy-start(bf16[2,128,4096]{2,1,0:T(8,128)(2,1)} %q_ref.3) | copy-start | bytes 6291460
  64.1 1.6 %copy-start.2 = (bf16[2,128,4096]{2,1,0:T(8,128)(2,1)S(1)}, bf16[2,128,4096]{2,1,0:T(8,128)(2,1)}, u32[]{:S(2)}) copy-start(bf16[2,128,4096]{2,1,0:T(8,128)(2,1)} %do_ref.3) | copy-start | bytes 6291460
  76.1 1.6 %copy-start.1 = (bf16[2,128,4096]{2,1,0:T(8,128)(2,1)S(1)}, bf16[2,128,4096]{2,1,0:T(8,128)(2,1)}, u32[]{:S(2)}) copy-start(bf16[2,128,4096]{2,1,0:T(8,128)(2,1)} %q_ref.3) | copy-start | bytes 6291460
  77.6 1.6 %copy-start.3 = (bf16[2,128,4096]{2,1,0:T(8,128)(2,1)S(1)}, bf16[2,128,4096]{2,1,0:T(8,128)(2,1)}, u32[]{:S(2)}) copy-start(bf16[2,128,4096]{2,1,0:T(8,128)(2,1)} %do_ref.3) | copy-start | bytes 6291460
  101.6 15.9 %all-to-all-start.3 = ((bf16[8,2,2,16,512]{4,3,2,1,0:T(8,128)(2,1)}), bf16[8,2,2,16,512]{4,3,2,1,0:T(8,128)(2,1)S(1)}, u32[]{:S(2)}, u32[]{:S(2)}) async-start(bf16[8,2,2,16,512]{4,3,2,1,0:T(8,128)(2,1)} %get-tuple-element.13), calls=%async_computation.3 | async-start | bytes 1048576 | tf_op jit(solution)/shard_map/all_to_all | solution.py:210
  106.2 15.3 %collective-permute-start.2 = (bf16[8,2,16,512]{3,2,1,0:T(8,128)(2,1)S(1)}, bf16[8,2,16,512]{3,2,1,0:T(8,128)(2,1)S(1)}, u32[]{:S(2)}, u32[]{:S(2)}) collective-permute-start(bf16[8,2,16,512]{3,2,1,0:T(8,128)(2,1)S(1)} %get-tuple-element.15), channel_id=1, source_target_pairs={{0,8},{1,9},{2,10},{3,11},{4,12},{5,13},{6,14},{7,15},{8,0},{9,1},... | collective-permute-start | bytes 786440 | tf_op jit(solution)/shard_map/ppermute | solution.py:301
  122.5 18.4 %all-to-all-start.5 = ((bf16[16,2,2,8,512]{4,3,2,1,0:T(8,128)(2,1)}), bf16[16,2,2,8,512]{4,3,2,1,0:T(8,128)(2,1)S(1)}, u32[]{:S(2)}, u32[]{:S(2)}) async-start(bf16[16,2,2,8,512]{4,3,2,1,0:T(8,128)(2,1)} %bitcast.18), calls=%async_computation.5 | async-start | bytes 1048576 | tf_op jit(solution)/shard_map/all_to_all | solution.py:213
  126.5 14.3 %collective-permute-start.3 = (bf16[2,2,64,512]{3,2,1,0:T(8,128)(2,1)S(1)}, bf16[2,2,64,512]{3,2,1,0:T(8,128)(2,1)S(1)}, u32[]{:S(2)}, u32[]{:S(2)}) collective-permute-start(bf16[2,2,64,512]{3,2,1,0:T(8,128)(2,1)S(1)} %fusion.4), channel_id=1, source_target_pairs={{0,16},{16,0},{1,17},{17,1},{2,18},{18,2},{3,19},{19,3},{4,20},{20... | collective-permute-start | bytes 786440 | tf_op jit(solution)/shard_map/ppermute | solution.py:216

commit v3 on v2

--- a/solution.py
+++ b/solution.py
@@ -23,9 +23,11 @@
     return lax.dot_general(a, b, dims, preferred_element_type=F32)
 
 
-def attend_kernel(
-    place, parents, q_ref, do_ref, self_ref, anc_ref, _, dq_ref, dself_ref, danc_ref, qs, dos, ps, ds
-):
+def attend_kernel(parts, first, place, parents, q_ref, do_ref, *refs):
+    own_refs, anc_ref = refs[:parts], refs[parts]
+    refs = refs[parts + (1 if first else 2) :]
+    dq_ref, dself_refs, danc_ref = refs[0], refs[1 : 1 + parts], refs[1 + parts]
+    qs, dos, ps, ds = refs[2 + parts :]
     hubs, depth, _, pieces, _ = anc_ref.shape
     rows = q_ref.shape[1]
     heads = q_ref.shape[2] // HEAD_DIM
@@ -39,13 +41,14 @@
 
     def seen(which):
         tiles = [anc_ref[:, k, which].reshape(rows, HEAD_DIM) for k in range(depth)]
-        return jnp.concatenate([self_ref[which, 0]] + tiles, 0)
+        return jnp.concatenate([ref[which, 0] for ref in own_refs] + tiles, 0)
 
     keys, values = seen(0), seen(1)
     for h in range(heads):
         qs[h * rows : (h + 1) * rows, :] = q_ref[0, :, h * HEAD_DIM : (h + 1) * HEAD_DIM]
         dos[h * rows : (h + 1) * rows, :] = do_ref[0, :, h * HEAD_DIM : (h + 1) * HEAD_DIM]
-    hidden = lax.broadcasted_iota(jnp.int32, (rows, rows), 0) > lax.broadcasted_iota(jnp.int32, (rows, rows), 1)
+    token = lax.rem(lax.broadcasted_iota(jnp.int32, (rows, rows), 0) + place[2], rows)
+    hidden = token > lax.broadcasted_iota(jnp.int32, (rows, rows), 1)
     scores = dot(keys, qs[...], NT)
     slopes = dot(values, dos[...], NT)
     for h in range(heads):
@@ -73,31 +76,33 @@
         dq_ref[0, :, h * HEAD_DIM : (h + 1) * HEAD_DIM] = dq_t[:, h * rows : (h + 1) * rows].T.astype(BF16)
     grads = [dot(ds[...], qs[...]) * scale, dot(ps[...], dos[...])]
     for which in range(2):
-        dself_ref[which] = grads[which][:rows].astype(BF16)
+        start = 0
+        for ref in dself_refs:
+            ref[which] = grads[which][start : start + ref.shape[1]].astype(BF16)
+            start += ref.shape[1]
         for k in range(depth):
             grad = grads[which][(k + 1) * rows : (k + 2) * rows].astype(BF16)
             danc_ref[:, k, which] = grad.reshape(hubs, pieces, HEAD_DIM)
 
 
-def attend(place, parents, queries, output_gradient, own, foreign, query_grad):
+def attend(place, parents, queries, output_gradient, owns, foreign, query_grad):
     _, rows, width = queries.shape
     hubs, depth, _, pieces, kv_width = foreign.shape
     groups = kv_width // HEAD_DIM
     heads = width // groups // HEAD_DIM
     span = (depth + 1) * rows
     q_spec = pl.BlockSpec((1, rows, heads * HEAD_DIM), lambda g, place, _: (place[1], 0, g))
-    own_spec = pl.BlockSpec((2, 1, rows, HEAD_DIM), lambda g, place, _: (0, place[1], 0, g))
-    dself_spec = pl.BlockSpec((2, rows, HEAD_DIM), lambda g, place, _: (0, 0, g))
+    own_specs = [pl.BlockSpec((2, 1, x.shape[2], HEAD_DIM), lambda g, place, _: (0, place[1], 0, g)) for x in owns]
+    dself_specs = [pl.BlockSpec((2, x.shape[2], HEAD_DIM), lambda g, place, _: (0, 0, g)) for x in owns]
     anc_spec = pl.BlockSpec((hubs, depth, 2, pieces, HEAD_DIM), lambda g, place, _: (0, 0, 0, 0, g))
-    hbm = pl.BlockSpec(memory_space=pl.ANY)
     first = query_grad is None
     return pl.pallas_call(
-        attend_kernel,
+        functools.partial(attend_kernel, len(owns), first),
         grid_spec=pltpu.PrefetchScalarGridSpec(
             num_scalar_prefetch=2,
             grid=(groups,),
-            in_specs=[q_spec, q_spec, own_spec, anc_spec, SMEM if first else hbm],
-            out_specs=[q_spec, dself_spec, anc_spec],
+            in_specs=[q_spec, q_spec, *own_specs, anc_spec] + ([] if first else [pl.BlockSpec(memory_space=pl.ANY)]),
+            out_specs=[q_spec, *dself_specs, anc_spec],
             scratch_shapes=[
                 pltpu.VMEM((heads * rows, HEAD_DIM), BF16),
                 pltpu.VMEM((heads * rows, HEAD_DIM), BF16),
@@ -107,17 +112,48 @@
         ),
         out_shape=[
             jax.ShapeDtypeStruct(queries.shape, BF16),
-            jax.ShapeDtypeStruct((2, rows, kv_width), BF16),
+            *[jax.ShapeDtypeStruct((2, x.shape[2], kv_width), BF16) for x in owns],
             jax.ShapeDtypeStruct(foreign.shape, BF16),
         ],
-        input_output_aliases={} if first else {6: 0},
-        compiler_params=PARAMS,
+        input_output_aliases={} if first else {5 + len(owns): 0},
+        compiler_params=pltpu.CompilerParams(vmem_limit_bytes=56 * 1024 * 1024),
         cost_estimate=pl.CostEstimate(
             flops=10 * groups * heads * span * rows * HEAD_DIM,
             bytes_accessed=6 * rows * width,
             transcendentals=groups * heads * span * rows,
         ),
-    )(place, parents, queries, output_gradient, own, foreign, place if first else query_grad)
+    )(place, parents, queries, output_gradient, *owns, foreign, *([] if first else [query_grad]))
+
+
+def pack_kernel(place, keys_ref, values_ref, send_ref, keep_ref, give_ref):
+    heads, width = send_ref.shape[0] // (keys_ref.shape[1] // 8), keep_ref.shape[3]
+    leaves = send_ref.shape[0] // heads
+    for kv, ref in enumerate((keys_ref, values_ref)):
+        for h in range(heads):
+            for j in range(0, leaves, 2):
+                tiles = [ref[t, 8 * j : 8 * j + 16, h * width : (h + 1) * width] for t in range(2)]
+                send_ref[h * leaves + j, kv] = jnp.concatenate([x[:8] for x in tiles], 0)
+                send_ref[h * leaves + j + 1, kv] = jnp.concatenate([x[8:] for x in tiles], 0)
+        keep_ref[kv] = ref[:, :, pl.ds(pl.multiple_of(place[3] * width, width), width)]
+        give_ref[kv] = ref[:, :, pl.ds(pl.multiple_of((1 - place[3]) * width, width), width)]
+
+
+def finish_kernel(place, got_ref, near_ref, near_got_ref, far_ref, far_got_ref, keys_ref, values_ref):
+    width = near_ref.shape[2]
+    leaves = near_ref.shape[1] // 8
+    upper = place[1] == 1
+    for kv, out_ref in enumerate((keys_ref, values_ref)):
+        for own in range(2):
+            h = place[3] if own else 1 - place[3]
+            refs = (near_ref, far_ref) if own else (near_got_ref, far_got_ref)
+            lanes = pl.ds(pl.multiple_of(h * width, width), width)
+            for j in range(0, leaves, 2):
+                rows = slice(8 * j, 8 * j + 16)
+                a, b = got_ref[h * leaves + j, kv], got_ref[h * leaves + j + 1, kv]
+                near = jnp.concatenate([a[:8], b[:8]], 0).astype(F32) + refs[0][kv, rows].astype(F32)
+                far = jnp.concatenate([a[8:], b[8:]], 0).astype(F32) + refs[1][kv, rows].astype(F32)
+                out_ref[0, rows, lanes] = jnp.where(upper, far, near).astype(BF16)
+                out_ref[1, rows, lanes] = jnp.where(upper, near, far).astype(BF16)
 
 
 def each_need(place, parents, half, depth, which, act):
@@ -194,8 +230,10 @@
     head_rank = lax.axis_index("head")
     upper = leaf_rank >= half
     near = jnp.where(upper, 1, 0)
-    place = jnp.stack([leaf_rank, near, 1 - near]).astype(jnp.int32)
-    far_place = jnp.stack([leaf_rank, 1 - near]).astype(jnp.int32)
+    token = head_rank * keys.shape[1] if head_count == 2 else 0
+    place = jnp.stack([leaf_rank, near, 1 - near, head_rank]).astype(jnp.int32)
+    near_place = jnp.stack([leaf_rank, near, token]).astype(jnp.int32)
+    far_place = jnp.stack([leaf_rank, 1 - near, token]).astype(jnp.int32)
     sides = [[half * i + j for j in range(half)] for i in range(2)]
     both = [[leaf_count * h + j for h in range(head_count) for j in side] for side in sides]
     swap = [(i, (i + half) % leaf_count) for i in range(leaf_count)]
@@ -203,8 +241,7 @@
     kv_width = kv_all // head_count
     rows = part_rows * head_count
     pieces = rows // half
-    merged = head_count == 2 and part_rows % half == 0
-    bits = part_rows // half if merged else 0
+    merged = head_count == 2 and part_rows == 8 * half and half % 2 == 0
 
     def exchange(x):
         return lax.all_to_all(x, "leaf", 0, 0, tiled=True, axis_index_groups=sides)
@@ -215,34 +252,33 @@
     def to_other_head(x):
         return lax.ppermute(x, "head", [(0, 1), (1, 0)])
 
-    def other(x, axis):
-        return lax.dynamic_index_in_dim(x, 1 - head_rank, axis, keepdims=False)
-
-    def this(x, axis):
-        return lax.dynamic_index_in_dim(x, head_rank, axis, keepdims=False)
-
-    def by_head(mine, theirs, axis):
-        low = jnp.where(head_rank == 0, mine, theirs)
-        high = jnp.where(head_rank == 0, theirs, mine)
-        return jnp.stack([low, high], axis)
-
     all_parents = lax.all_gather(parents, "leaf", axis=0, tiled=True)
 
-    pair = jnp.stack([keys, values]).reshape(2, trees, part_rows, head_count, kv_width)
     if merged:
-        pair = jnp.moveaxis(pair, 3, 0)
-        send = pair.reshape(2, 2, trees, half, bits, kv_width).transpose(0, 3, 1, 2, 4, 5)
-        arrived = exchange_both(send.reshape(2 * half, 2, trees, bits, kv_width))
-        arrived = arrived.reshape(2, half, 2, trees, bits, kv_width).transpose(1, 2, 3, 0, 4, 5)
+        send, keep, give = pl.pallas_call(
+            pack_kernel,
+            in_specs=[SMEM, VMEM, VMEM],
+            out_specs=[VMEM, VMEM, VMEM],
+            out_shape=[
+                jax.ShapeDtypeStruct((2 * half, 2, 16, kv_width), BF16),
+                *[jax.ShapeDtypeStruct((2, trees, part_rows, kv_width), BF16)] * 2,
+            ],
+            compiler_params=PARAMS,
+        )(place, keys, values)
+        arrived, theirs, all_parents = lax.optimization_barrier(
+            (exchange_both(send), to_other_head(give), all_parents)
+        )
+        arrived = arrived.reshape(2, half, 2, trees, 8, kv_width).transpose(1, 2, 3, 0, 4, 5)
         hub_own = arrived.reshape(half, 2, trees, pieces, kv_width)
-        theirs = to_other_head(other(pair, 0))
-        mine = by_head(this(pair, 0), theirs, 2).reshape(2, trees, rows, kv_width)
+        owns = [keep, theirs]
     else:
+        pair = jnp.stack([keys, values]).reshape(2, trees, part_rows, head_count, kv_width)
         pair = jnp.moveaxis(pair, 3, 0)
         if head_count > 1:
             pair = lax.all_to_all(pair, "head", 0, 0, tiled=True)
         mine = pair.transpose(1, 2, 0, 3, 4).reshape(2, trees, rows, kv_width)
         hub_own = exchange(mine.reshape(2, trees, half, pieces, kv_width).transpose(2, 0, 1, 3, 4))
+        owns = [mine]
 
     hub_cross = lax.ppermute(jnp.where(upper, hub_own[:, :, 1], hub_own[:, :, 0]), "leaf", swap)
     picked_shape = jax.ShapeDtypeStruct((half, depth, 2, pieces, kv_width), BF16)
@@ -273,13 +309,13 @@
             return x
         return x.reshape(depth, 2, half, pieces, kv_width).transpose(2, 0, 1, 3, 4)
 
-    query_grad, self_near, grad_near = attend(
-        place, all_parents, queries, output_gradient, mine, gather_rows(foreign_near), None
+    query_grad, *self_near, grad_near = attend(
+        near_place, all_parents, queries, output_gradient, owns, gather_rows(foreign_near), None
     )
-    query_grad, self_far, grad_far = attend(
-        far_place, all_parents, queries, output_gradient, mine, gather_rows(foreign_far), query_grad
+    query_grad, *self_far, grad_far = attend(
+        far_place, all_parents, queries, output_gradient, owns, gather_rows(foreign_far), query_grad
     )
-    back_near = exchange(spread_rows(grad_near))
+    back_near, grad_far = lax.optimization_barrier((exchange(spread_rows(grad_near)), grad_far))
     back_far = exchange(spread_rows(grad_far))
 
     sum_shape = (half, 2, pieces, kv_width)
@@ -301,22 +337,24 @@
     crossed = lax.ppermute(cross_sum, "leaf", swap)
     near_sum = (near_sum + crossed.astype(F32)).astype(BF16)
     hub_sum = jnp.stack([near_sum, far_sum], 1)
-    self_sum = jnp.stack([self_near, self_far])
     if merged:
-        hub_sum = hub_sum.reshape(half, 2, 2, 2, bits, kv_width).transpose(3, 0, 1, 2, 4, 5)
-        returned = exchange_both(hub_sum.reshape(2 * half, 2, 2, bits, kv_width))
-        returned = returned.reshape(2, half, 2, 2, bits, kv_width).transpose(0, 2, 3, 1, 4, 5)
-        returned = returned.reshape(2, 2, 2, part_rows, kv_width)
-        self_sum = self_sum.reshape(2, 2, 2, part_rows, kv_width)
-        theirs = to_other_head(other(self_sum, 2))
-        total = returned.astype(F32) + by_head(this(self_sum, 2), theirs, 0).astype(F32)
-        total = total.astype(BF16)
-    else:
-        returned = exchange(hub_sum).transpose(1, 2, 0, 3, 4).reshape(2, 2, rows, kv_width)
-        total = (returned.astype(F32) + self_sum.astype(F32)).astype(BF16)
-        total = jnp.moveaxis(total.reshape(2, 2, head_count, part_rows, kv_width), 2, 0)
-        if head_count > 1:
-            total = lax.all_to_all(total, "head", 0, 0, tiled=True)
+        hub_sum = hub_sum.reshape(half, 2, 2, 2, 8, kv_width).transpose(3, 0, 2, 1, 4, 5)
+        returned = exchange_both(hub_sum.reshape(2 * half, 2, 16, kv_width))
+        near_got, far_got = to_other_head(self_near[1]), to_other_head(self_far[1])
+        key_gradient, value_gradient = pl.pallas_call(
+            finish_kernel,
+            in_specs=[SMEM] + [VMEM] * 5,
+            out_specs=[VMEM, VMEM],
+            out_shape=[jax.ShapeDtypeStruct(keys.shape, BF16)] * 2,
+            compiler_params=PARAMS,
+        )(place, returned, self_near[0], near_got, self_far[0], far_got)
+        return query_grad, key_gradient, value_gradient
+    self_sum = jnp.stack([self_near[0], self_far[0]])
+    returned = exchange(hub_sum).transpose(1, 2, 0, 3, 4).reshape(2, 2, rows, kv_width)
+    total = (returned.astype(F32) + self_sum.astype(F32)).astype(BF16)
+    total = jnp.moveaxis(total.reshape(2, 2, head_count, part_rows, kv_width), 2, 0)
+    if head_count > 1:
+        total = lax.all_to_all(total, "head", 0, 0, tiled=True)
     total = total.transpose(2, 1, 3, 0, 4).reshape(2, 2, part_rows, kv_all)
     total = jnp.where(upper, total[:, ::-1], total)
     return query_grad, total[0], total[1]

time: 144 us -> 130 us (0.903)
  local copies, waits for them, and re-layouts: 14.6 us -> 5.68 us
  waiting for transfers between devices: 48.1 us -> 40.1 us
  Pallas kernels: 25.7 us -> 30.2 us
  blocking collectives: 27.1 us -> 25.2 us
    unnamed x1 -> x0, blocking collectives: 14.6 us -> none
    optimization_barrier x0 -> x1, blocking collectives: none -> 12.1 us  [body(): lax.optimization_barrier((exchange_both(send), to_other_head(give), all_p...]
    all_to_all x3, waiting for transfers between devices: 10.8 us -> 0.01 us  [exchange(): return lax.all_to_all(x, 'leaf', 0, 0, tiled=True, axis_index_groups=sides)]
    ppermute x1, waiting for transfers between devices: 2.96 us -> 13 us  [body(): crossed = lax.ppermute(cross_sum, 'leaf', swap)]
    ppermute x2 -> x3, waiting for transfers between devices: 19.4 us -> 12.2 us  [to_other_head(): return lax.ppermute(x, 'head', [(0, 1), (1, 0)])]
    pallas_call x2 -> x4, Pallas kernels: 20.2 us -> 24.7 us  [the longest x2 21.8 us: attend(): pl.pallas_call(functools.partial(attend_kernel, len(owns), first), grid_s...]
    another operation x5 -> x0, local copies, waits for them, and re-layouts: 3.64 us -> none  [the longest x3 2.52 us: body(): jnp.stack([keys, values]).reshape(2, trees, part_rows, head_count, kv_width)]
    unnamed x17 -> x27, local copies, waits for them, and re-layouts: 7.43 us -> 4.74 us
  transfers between devices with their start and end apart: 9 -> 10, of which waited for: 5 -> 4; matrix products, arithmetic and copies ran while one was open for 2% -> 2% of each run, Pallas kernels for 10% -> 19%
where the time goes in v3:
time: 130 us; the launch traced here: 129 us
  waiting for transfers between devices  40.1 us (31%)
  Pallas kernels  30.2 us (23%)
  starting transfers between devices  25.9 us (20%)
  blocking collectives  25.2 us (19%)
  local copies, waits for them, and re-layouts  5.68 us (4%)
  between operations  1.5 us (1%)
    pallas_call x2, Pallas kernels, attend(): pl.pallas_call(functools.partial(attend_kernel, len(owns), first), grid_s...  21.8 us
    ppermute x1, waiting for transfers between devices, body(): lax.ppermute(jnp.where(upper, hub_own[:, :, 1], hub_own[:, :, 0]), 'leaf'...  14.9 us
    all_to_all x1, blocking collectives, exchange(): return lax.all_to_all(x, 'leaf', 0, 0, tiled=True, axis_index_groups=sides)  13.1 us
    ppermute x1, waiting for transfers between devices, body(): crossed = lax.ppermute(cross_sum, 'leaf', swap)  13 us
    ppermute x3, waiting for transfers between devices, to_other_head(): return lax.ppermute(x, 'head', [(0, 1), (1, 0)])  12.2 us
    optimization_barrier x1, blocking collectives, body(): lax.optimization_barrier((exchange_both(send), to_other_head(give), all_p...  12.1 us
    all_to_all x3, starting transfers between devices, exchange(): return lax.all_to_all(x, 'leaf', 0, 0, tiled=True, axis_index_groups=sides)  11.1 us
    all_to_all x2, starting transfers between devices, exchange_both(): lax.all_to_all(x, ('head', 'leaf'), 0, 0, tiled=True, axis_index_groups=b...  9.86 us
  transfers between devices with their start and end apart: 10, of which 4 were waited for; matrix products, arithmetic and copies ran while one was open for 2% of the time, Pallas kernels for 19%

profile of v3, /device:TPU:0, one launch (start us, length us, event | category | flops | bytes accessed | tf_op | source)
XLA Modules:
  0.0 129.5 jit_solution(7037795234506292728)
XLA Ops:
  0.6 0.1 pad_add_fusion.place
  0.7 0.0 copy-start
  0.7 0.9 copy-done
  1.7 0.0 copy-start.1
  1.7 0.9 copy-done.1
  2.6 1.4 %shard_map.76 = (bf16[16,2,16,512]{3,2,1,0:T(8,128)(2,1)}, bf16[2,2,64,512]{3,2,1,0:T(8,128)(2,1)S(1)}, bf16[2,2,64,512]{3,2,1,0:T(8,128)(2,1)S(1)}) custom-call(s32[4]{0:T(128)S(1)} %pad_add_fusion.place, bf16[2,64,1024]{2,1,0:T(8,128)(2,1)S(1)} %copy-done, bf16[2,64,1024]{2,1,0:T(8,128)(2,1)S(1)} %copy-done.1), custom_call_target="tpu_custom_call" | custom-call | tf_op jit(solution)/shard_map/pallas_call | solution.py:258
  4.0 0.0 copy-start.6
  4.0 0.7 copy-done.6
  4.8 6.3 %all-to-all-start = ((bf16[16,2,16,512]{3,2,1,0:T(8,128)(2,1)}), bf16[16,2,16,512]{3,2,1,0:T(8,128)(2,1)S(1)}, u32[]{:S(2)}, u32[]{:S(2)}) async-start(bf16[16,2,16,512]{3,2,1,0:T(8,128)(2,1)} %get-tuple-element.23), calls=%async_computation | async-start | bytes 1048576 | tf_op jit(solution)/shard_map/all_to_all | solution.py:250
  11.0 1.9 %collective-permute-start = (bf16[2,2,64,512]{3,2,1,0:T(8,128)(2,1)S(1)}, bf16[2,2,64,512]{3,2,1,0:T(8,128)(2,1)S(1)}, u32[]{:S(2)}, u32[]{:S(2)}) collective-permute-start(bf16[2,2,64,512]{3,2,1,0:T(8,128)(2,1)S(1)} %get-tuple-element.24), channel_id=1, source_target_pairs={{0,16},{16,0},{1,17},{17,1},{2,18},{18,2},{3,19},{19,3},{4,20},{20... | collective-permute-start | bytes 786440 | tf_op jit(solution)/shard_map/ppermute | solution.py:253
  13.0 1.2 dynamic-slice
  14.9 0.9 dynamic-update-slice
  15.7 12.1 %all-reduce.parents = s32[32]{0:T(128)S(1)} all-reduce(s32[32]{0:T(128)S(1)} %dynamic-update-slice), channel_id=1, replica_groups=mesh['head'=2,'leaf'=16] {'leaf'}, use_global_device_ids=true, to_apply=%add | all-reduce | flops 32 | bytes 256 | tf_op jit(solution)/shard_map/optimization_barrier | solution.py:268
  27.8 0.0 copy-start.4
  27.9 0.0 collective-permute-done.refs_1_
  27.9 0.0 copy-start.9
  27.9 0.0 all-to-all-done
  27.9 0.1 copy.14
  27.9 1.6 %shard_map.78 = bf16[8,2,2,16,512]{4,3,2,1,0:T(8,128)(2,1)} custom-call(s32[4]{0:T(128)S(1)} %pad_add_fusion.place, s32[32]{0:T(128)S(1)} %all-reduce.parents, bf16[8,2,2,16,512]{4,3,2,1,0:T(8,128)(2,1)S(1)} %bitcast.20), custom_call_target="tpu_custom_call" | custom-call | tf_op jit(solution)/shard_map/pallas_call | solution.py:285
  29.5 3.5 %all-to-all-start.2 = ((bf16[8,2,2,16,512]{4,3,2,1,0:T(8,128)(2,1)}), bf16[8,2,2,16,512]{4,3,2,1,0:T(8,128)(2,1)S(1)}, u32[]{:S(2)}, u32[]{:S(2)}) async-start(bf16[8,2,2,16,512]{4,3,2,1,0:T(8,128)(2,1)} %shard_map.78), calls=%async_computation.2 | async-start | bytes 1048576 | tf_op jit(solution)/shard_map/all_to_all | solution.py:247
  33.1 0.4 collective-permute-start.1
  33.5 14.9 %collective-permute-done.1.cross_ref = bf16[8,2,16,512]{3,2,1,0:T(8,128)(2,1)S(1)} collective-permute-done((bf16[8,2,16,512]{3,2,1,0:T(8,128)(2,1)S(1)}, bf16[8,2,16,512]{3,2,1,0:T(8,128)(2,1)S(1)}, u32[]{:S(2)}, u32[]{:S(2)}) %collective-permute-start.1) | collective-permute-done | bytes 262176 | tf_op jit(solution)/shard_map/ppermute | solution.py:283
  48.4 1.8 %shard_map.77 = bf16[8,2,2,16,512]{4,3,2,1,0:T(8,128)(2,1)} custom-call(s32[4]{0:T(128)S(1)} %pad_add_fusion.place, s32[32]{0:T(128)S(1)} %all-reduce.parents, bf16[8,2,2,16,512]{4,3,2,1,0:T(8,128)(2,1)S(1)} %bitcast.22, bf16[8,2,16,512]{3,2,1,0:T(8,128)(2,1)S(1)} %collective-permute-done.1.cross_ref), custom_call_target="tpu_custom_call" | custom-call | tf_op jit(solution)/shard_map/pallas_call | solution.py:293
  50.2 0.0 copy-done.4
  50.2 0.0 copy-done.9
  50.2 0.0 all-to-all-done.2.refs_2_
  50.2 0.0 copy-start.7
  50.2 3.5 %all-to-all-start.1 = ((bf16[8,2,2,16,512]{4,3,2,1,0:T(8,128)(2,1)}), bf16[8,2,2,16,512]{4,3,2,1,0:T(8,128)(2,1)S(1)}, u32[]{:S(2)}, u32[]{:S(2)}) async-start(bf16[8,2,2,16,512]{4,3,2,1,0:T(8,128)(2,1)} %shard_map.77), calls=%async_computation.1 | async-start | bytes 1048576 | tf_op jit(solution)/shard_map/all_to_all | solution.py:247
  53.7 0.6 add_add_fusion
  54.3 0.0 copy-done.7
  54.3 10.9 %shard_map.79 = (bf16[2,128,4096]{2,1,0:T(8,128)(2,1)}, bf16[2,64,512]{2,1,0:T(8,128)(2,1)}, bf16[2,64,512]{2,1,0:T(8,128)(2,1)}, bf16[8,2,2,16,512]{4,3,2,1,0:T(8,128)(2,1)}) custom-call(s32[3]{0:T(128)} %get-tuple-element.44.place, s32[32]{0:T(128)} %copy-done.4, bf16[2,128,4096]{2,1,0:T(8,128)(2,1)} %q_ref.3, bf16[2,128,4096]{2,1,0:T(8,128)(2,1)} %do_ref.3, ...), custom_call_target="tpu_custom_call" | custom-call | flops 2013265920 | bytes 3145728 | tf_op jit(solution)/shard_map/pallas_call | solution.py:99
  65.2 0.0 all-to-all-done.1.refs_2_
  65.2 0.0 copy-start.8
  65.2 4.1 %all-to-all-start.3 = ((bf16[8,2,2,16,512]{4,3,2,1,0:T(8,128)(2,1)}), bf16[8,2,2,16,512]{4,3,2,1,0:T(8,128)(2,1)S(1)}, u32[]{:S(2)}, u32[]{:S(2)}) async-start(bf16[8,2,2,16,512]{4,3,2,1,0:T(8,128)(2,1)} %get-tuple-element.31), calls=%async_computation.3 | async-start | bytes 1048576 | tf_op jit(solution)/shard_map/all_to_all | solution.py:247
  69.4 0.0 copy-done.8
  69.4 0.0 copy-start.5
  69.4 10.9 %shard_map.80 = (bf16[2,128,4096]{2,1,0:T(8,128)(2,1)}, bf16[2,64,512]{2,1,0:T(8,128)(2,1)}, bf16[2,64,512]{2,1,0:T(8,128)(2,1)}, bf16[8,2,2,16,512]{4,3,2,1,0:T(8,128)(2,1)}) custom-call(s32[3]{0:T(128)} %get-tuple-element.43.place, s32[32]{0:T(128)} %copy-done.4, bf16[2,128,4096]{2,1,0:T(8,128)(2,1)} %q_ref.3, ...), custom_call_target="tpu_custom_call", output_to_operand_aliasing={{0}: (7, {})} | custom-call | flops 2013265920 | bytes 3145728 | tf_op jit(solution)/shard_map/pallas_call | solution.py:99
  80.3 0.0 all-to-all-done.3.in_ref
  80.3 13.1 %all_to_all.30.in_ref = bf16[8,2,2,16,512]{4,3,2,1,0:T(8,128)(2,1)S(1)} all-to-all(bf16[8,2,2,16,512]{4,3,2,1,0:T(8,128)(2,1)} %get-tuple-element.34), channel_id=1, replica_groups={{0,1,2,3,4,5,6,7},{8,9,10,11,12,13,14,15},{16,17,18,19,20,21,22,23},{24..., dimensions={0} | all-to-all | bytes 1048576 | tf_op jit(solution)/shard_map/all_to_all | solution.py:247
  93.4 0.0 copy-done.5
  93.4 1.1 shard_map.82
  94.5 0.5 collective-permute-start.2
  95.0 0.9 shard_map.81
  96.0 0.0 copy-start.10
  96.0 0.0 copy-start.11
  96.0 0.0 copy-start.2
  96.0 0.0 copy-start.3
  96.0 13.0 %collective-permute-done.2 = bf16[8,2,16,512]{3,2,1,0:T(8,128)(2,1)S(1)} collective-permute-done((bf16[8,2,16,512]{3,2,1,0:T(8,128)(2,1)S(1)}, bf16[8,2,16,512]{3,2,1,0:T(8,128)(2,1)S(1)}, u32[]{:S(2)}, u32[]{:S(2)}) %collective-permute-start.2) | collective-permute-done | bytes 262176 | tf_op jit(solution)/shard_map/ppermute | solution.py:337
  109.1 0.1 fusion
  109.1 0.1 pad_maximum_fusion
  109.2 0.9 copy.12
  110.1 3.6 %all-to-all-start.5 = ((bf16[16,2,16,512]{3,2,1,0:T(8,128)(2,1)}), bf16[16,2,16,512]{3,2,1,0:T(8,128)(2,1)S(1)}, u32[]{:S(2)}, u32[]{:S(2)}) async-start(bf16[16,2,16,512]{3,2,1,0:T(8,128)(2,1)} %bitcast.14), calls=%async_computation.5 | async-start | bytes 1048576 | tf_op jit(solution)/shard_map/all_to_all | solution.py:250
  113.7 0.0 copy-done.10
  113.7 1.9 %collective-permute-start.3 = (bf16[2,64,512]{2,1,0:T(8,128)(2,1)S(1)}, bf16[2,64,512]{2,1,0:T(8,128)(2,1)S(1)}, u32[]{:S(2)}, u32[]{:S(2)}) collective-permute-start(bf16[2,64,512]{2,1,0:T(8,128)(2,1)S(1)} %copy-done.10), channel_id=1, source_target_pairs={{0,16},{16,0},{1,17},{17,1},{2,18},{18,2},{3,19},{19,3},{4,20},{20... | collective-permute-start | bytes 393224 | tf_op jit(solution)/shard_map/ppermute | solution.py:253
  115.6 0.0 copy-done.11
  115.6 0.2 collective-permute-start.4
  115.8 9.8 %collective-permute-done.3.near_got_ref = bf16[2,64,512]{2,1,0:T(8,128)(2,1)S(1)} collective-permute-done((bf16[2,64,512]{2,1,0:T(8,128)(2,1)S(1)}, bf16[2,64,512]{2,1,0:T(8,128)(2,1)S(1)}, u32[]{:S(2)}, u32[]{:S(2)}) %collective-permute-start.3) | collective-permute-done | bytes 131104 | tf_op jit(solution)/shard_map/ppermute | solution.py:253
  125.6 2.3 %collective-permute-done.4.far_got_ref = bf16[2,64,512]{2,1,0:T(8,128)(2,1)S(1)} collective-permute-done((bf16[2,64,512]{2,1,0:T(8,128)(2,1)S(1)}, bf16[2,64,512]{2,1,0:T(8,128)(2,1)S(1)}, u32[]{:S(2)}, u32[]{:S(2)}) %collective-permute-start.4) | collective-permute-done | bytes 131104 | tf_op jit(solution)/shard_map/ppermute | solution.py:253
  128.0 0.0 all-to-all-done.5.got_ref
  128.0 0.0 copy-done.2
  128.0 0.0 copy-done.3
  128.0 1.5 %shard_map.83 = (bf16[2,64,1024]{2,1,0:T(8,128)(2,1)}, bf16[2,64,1024]{2,1,0:T(8,128)(2,1)}) custom-call(s32[4]{0:T(128)S(1)} %pad_add_fusion.place, bf16[16,2,16,512]{3,2,1,0:T(8,128)(2,1)S(1)} %all-to-all-done.5.got_ref, bf16[2,64,512]{2,1,0:T(8,128)(2,1)S(1)} %copy-done.2, bf16[2,64,512]{2,1,0:T(8,128)(2,1)S(1)} %collective-permute-done.3.near_got_ref, ...), custom_call_target="tpu_custom_call" | custom-call | tf_op jit(solution)/shard_map/pallas_call | solution.py:344
  (2 shorter events, 0.0 us)
Async XLA Ops:
  0.7 1.0 copy-start
  1.7 0.9 copy-start.1
  4.0 0.7 copy-start.6
  4.8 23.1 %all-to-all-start = ((bf16[16,2,16,512]{3,2,1,0:T(8,128)(2,1)}), bf16[16,2,16,512]{3,2,1,0:T(8,128)(2,1)S(1)}, u32[]{:S(2)}, u32[]{:S(2)}) async-start(bf16[16,2,16,512]{3,2,1,0:T(8,128)(2,1)} %get-tuple-element.23), calls=%async_computation | async-start | bytes 1048576 | tf_op jit(solution)/shard_map/all_to_all | solution.py:250
  11.0 16.8 %collective-permute-start = (bf16[2,2,64,512]{3,2,1,0:T(8,128)(2,1)S(1)}, bf16[2,2,64,512]{3,2,1,0:T(8,128)(2,1)S(1)}, u32[]{:S(2)}, u32[]{:S(2)}) collective-permute-start(bf16[2,2,64,512]{3,2,1,0:T(8,128)(2,1)S(1)} %get-tuple-element.24), channel_id=1, source_target_pairs={{0,16},{16,0},{1,17},{17,1},{2,18},{18,2},{3,19},{19,3},{4,20},{20... | collective-permute-start | bytes 786440 | tf_op jit(solution)/shard_map/ppermute | solution.py:253
  27.8 22.3 %copy-start.4 = (s32[32]{0:T(128)}, s32[32]{0:T(128)S(1)}, u32[]{:S(2)}) copy-start(s32[32]{0:T(128)S(1)} %all-reduce.parents) | copy-start | bytes 388
  27.9 22.3 %copy-start.9 = (bf16[2,2,64,512]{3,2,1,0:T(8,128)(2,1)}, bf16[2,2,64,512]{3,2,1,0:T(8,128)(2,1)S(1)}, u32[]{:S(2)}) copy-start(bf16[2,2,64,512]{3,2,1,0:T(8,128)(2,1)S(1)} %collective-permute-done.refs_1_) | copy-start | bytes 786436
  29.5 20.6 %all-to-all-start.2 = ((bf16[8,2,2,16,512]{4,3,2,1,0:T(8,128)(2,1)}), bf16[8,2,2,16,512]{4,3,2,1,0:T(8,128)(2,1)S(1)}, u32[]{:S(2)}, u32[]{:S(2)}) async-start(bf16[8,2,2,16,512]{4,3,2,1,0:T(8,128)(2,1)} %shard_map.78), calls=%async_computation.2 | async-start | bytes 1048576 | tf_op jit(solution)/shard_map/all_to_all | solution.py:247
  33.1 15.3 %collective-permute-start.1 = (bf16[8,2,16,512]{3,2,1,0:T(8,128)(2,1)S(1)}, bf16[8,2,16,512]{3,2,1,0:T(8,128)(2,1)S(1)}, u32[]{:S(2)}, u32[]{:S(2)}) collective-permute-start(bf16[8,2,16,512]{3,2,1,0:T(8,128)(2,1)S(1)} %fusion.1), channel_id=1, source_target_pairs={{0,8},{1,9},{2,10},{3,11},{4,12},{5,13},{6,14},{7,15},{8,0},{9,1},... | collective-permute-start | bytes 786440 | tf_op jit(solution)/shard_map/ppermute | solution.py:283
  50.2 4.2 %copy-start.7 = (bf16[8,2,2,16,512]{4,3,2,1,0:T(8,128)(2,1)}, bf16[8,2,2,16,512]{4,3,2,1,0:T(8,128)(2,1)S(1)}, u32[]{:S(2)}) copy-start(bf16[8,2,2,16,512]{4,3,2,1,0:T(8,128)(2,1)S(1)} %all-to-all-done.2.refs_2_) | copy-start | bytes 1572868
  50.2 15.0 %all-to-all-start.1 = ((bf16[8,2,2,16,512]{4,3,2,1,0:T(8,128)(2,1)}), bf16[8,2,2,16,512]{4,3,2,1,0:T(8,128)(2,1)S(1)}, u32[]{:S(2)}, u32[]{:S(2)}) async-start(bf16[8,2,2,16,512]{4,3,2,1,0:T(8,128)(2,1)} %shard_map.77), calls=%async_computation.1 | async-start | bytes 1048576 | tf_op jit(solution)/shard_map/all_to_all | solution.py:247
  65.2 4.1 %copy-start.8 = (bf16[8,2,2,16,512]{4,3,2,1,0:T(8,128)(2,1)}, bf16[8,2,2,16,512]{4,3,2,1,0:T(8,128)(2,1)S(1)}, u32[]{:S(2)}) copy-start(bf16[8,2,2,16,512]{4,3,2,1,0:T(8,128)(2,1)S(1)} %all-to-all-done.1.refs_2_) | copy-start | bytes 1572868
  65.2 15.1 %all-to-all-start.3 = ((bf16[8,2,2,16,512]{4,3,2,1,0:T(8,128)(2,1)}), bf16[8,2,2,16,512]{4,3,2,1,0:T(8,128)(2,1)S(1)}, u32[]{:S(2)}, u32[]{:S(2)}) async-start(bf16[8,2,2,16,512]{4,3,2,1,0:T(8,128)(2,1)} %get-tuple-element.31), calls=%async_computation.3 | async-start | bytes 1048576 | tf_op jit(solution)/shard_map/all_to_all | solution.py:247
  69.4 24.1 %copy-start.5 = (s32[32]{0:T(128)S(1)}, s32[32]{0:T(128)}, u32[]{:S(2)}) copy-start(s32[32]{0:T(128)} %copy-done.4) | copy-start | bytes 388
  94.5 14.5 %collective-permute-start.2 = (bf16[8,2,16,512]{3,2,1,0:T(8,128)(2,1)S(1)}, bf16[8,2,16,512]{3,2,1,0:T(8,128)(2,1)S(1)}, u32[]{:S(2)}, u32[]{:S(2)}) collective-permute-start(bf16[8,2,16,512]{3,2,1,0:T(8,128)(2,1)S(1)} %get-tuple-element.35), channel_id=1, source_target_pairs={{0,8},{1,9},{2,10},{3,11},{4,12},{5,13},{6,14},{7,15},{8,0},{9,1},... | collective-permute-start | bytes 786440 | tf_op jit(solution)/shard_map/ppermute | solution.py:337
  96.0 17.7 %copy-start.10 = (bf16[2,64,512]{2,1,0:T(8,128)(2,1)S(1)}, bf16[2,64,512]{2,1,0:T(8,128)(2,1)}, u32[]{:S(2)}) copy-start(bf16[2,64,512]{2,1,0:T(8,128)(2,1)} %get-tuple-element.38) | copy-start | bytes 393220
  96.0 19.6 %copy-start.11 = (bf16[2,64,512]{2,1,0:T(8,128)(2,1)S(1)}, bf16[2,64,512]{2,1,0:T(8,128)(2,1)}, u32[]{:S(2)}) copy-start(bf16[2,64,512]{2,1,0:T(8,128)(2,1)} %get-tuple-element.40) | copy-start | bytes 393220
  96.0 32.0 %copy-start.2 = (bf16[2,64,512]{2,1,0:T(8,128)(2,1)S(1)}, bf16[2,64,512]{2,1,0:T(8,128)(2,1)}, u32[]{:S(2)}) copy-start(bf16[2,64,512]{2,1,0:T(8,128)(2,1)} %get-tuple-element.37.near_ref) | copy-start | bytes 393220
  96.0 31.9 %copy-start.3 = (bf16[2,64,512]{2,1,0:T(8,128)(2,1)S(1)}, bf16[2,64,512]{2,1,0:T(8,128)(2,1)}, u32[]{:S(2)}) copy-start(bf16[2,64,512]{2,1,0:T(8,128)(2,1)} %get-tuple-element.39.far_ref) | copy-start | bytes 393220
  110.1 17.9 %all-to-all-start.5 = ((bf16[16,2,16,512]{3,2,1,0:T(8,128)(2,1)}), bf16[16,2,16,512]{3,2,1,0:T(8,128)(2,1)S(1)}, u32[]{:S(2)}, u32[]{:S(2)}) async-start(bf16[16,2,16,512]{3,2,1,0:T(8,128)(2,1)} %bitcast.14), calls=%async_computation.5 | async-start | bytes 1048576 | tf_op jit(solution)/shard_map/all_to_all | solution.py:250
  113.7 11.9 %collective-permute-start.3 = (bf16[2,64,512]{2,1,0:T(8,128)(2,1)S(1)}, bf16[2,64,512]{2,1,0:T(8,128)(2,1)S(1)}, u32[]{:S(2)}, u32[]{:S(2)}) collective-permute-start(bf16[2,64,512]{2,1,0:T(8,128)(2,1)S(1)} %copy-done.10), channel_id=1, source_target_pairs={{0,16},{16,0},{1,17},{17,1},{2,18},{18,2},{3,19},{19,3},{4,20},{20... | collective-permute-start | bytes 393224 | tf_op jit(solution)/shard_map/ppermute | solution.py:253
  115.6 12.4 %collective-permute-start.4 = (bf16[2,64,512]{2,1,0:T(8,128)(2,1)S(1)}, bf16[2,64,512]{2,1,0:T(8,128)(2,1)S(1)}, u32[]{:S(2)}, u32[]{:S(2)}) collective-permute-start(bf16[2,64,512]{2,1,0:T(8,128)(2,1)S(1)} %copy-done.11), channel_id=1, source_target_pairs={{0,16},{16,0},{1,17},{17,1},{2,18},{18,2},{3,19},{19,3},{4,20},{20... | collective-permute-start | bytes 393224 | tf_op jit(solution)/shard_map/ppermute | solution.py:253

commit v4 on v3

--- a/solution.py
+++ b/solution.py
@@ -27,7 +27,6 @@
     own_refs, anc_ref = refs[:parts], refs[parts]
     refs = refs[parts + (1 if first else 2) :]
     dq_ref, dself_refs, danc_ref = refs[0], refs[1 : 1 + parts], refs[1 + parts]
-    qs, dos, ps, ds = refs[2 + parts :]
     hubs, depth, _, pieces, _ = anc_ref.shape
     rows = q_ref.shape[1]
     heads = q_ref.shape[2] // HEAD_DIM
@@ -44,17 +43,20 @@
         return jnp.concatenate([ref[which, 0] for ref in own_refs] + tiles, 0)
 
     keys, values = seen(0), seen(1)
-    for h in range(heads):
-        qs[h * rows : (h + 1) * rows, :] = q_ref[0, :, h * HEAD_DIM : (h + 1) * HEAD_DIM]
-        dos[h * rows : (h + 1) * rows, :] = do_ref[0, :, h * HEAD_DIM : (h + 1) * HEAD_DIM]
+    keys_t = keys.T
     token = lax.rem(lax.broadcasted_iota(jnp.int32, (rows, rows), 0) + place[2], rows)
     hidden = token > lax.broadcasted_iota(jnp.int32, (rows, rows), 1)
-    scores = dot(keys, qs[...], NT)
-    slopes = dot(values, dos[...], NT)
-    for h in range(heads):
-        part = slice(h * rows, (h + 1) * rows)
-        s = [scores[k * rows : (k + 1) * rows, part] for k in range(depth + 1)]
-        d = [slopes[k * rows : (k + 1) * rows, part] for k in range(depth + 1)]
+
+    def products(h):
+        q, do = (
+            jnp.concatenate([ref[0, :, i * HEAD_DIM : (i + 1) * HEAD_DIM] for i in range(h, h + 2)], 0)
+            for ref in (q_ref, do_ref)
+        )
+        return h, q, do, dot(keys, q, NT), dot(values, do, NT)
+
+    def soften(scores, slopes):
+        s = [scores[k * rows : (k + 1) * rows] for k in range(depth + 1)]
+        d = [slopes[k * rows : (k + 1) * rows] for k in range(depth + 1)]
         s[0] = jnp.where(hidden, -1e30, s[0])
         peak = jnp.max(s[0], 0, keepdims=True)
         for k in range(depth):
@@ -67,14 +69,32 @@
         weighted = functools.reduce(jnp.add, [jnp.sum(x * y, 0, keepdims=True) for x, y in zip(e, d)])
         inverse = 1.0 / total
         mean = weighted * inverse
-        for k in range(depth + 1):
-            p = e[k] * inverse
-            ps[k * rows : (k + 1) * rows, part] = p.astype(BF16)
-            ds[k * rows : (k + 1) * rows, part] = (p * (d[k] - mean)).astype(BF16)
-    dq_t = dot(keys.T, ds[...]) * scale
-    for h in range(heads):
-        dq_ref[0, :, h * HEAD_DIM : (h + 1) * HEAD_DIM] = dq_t[:, h * rows : (h + 1) * rows].T.astype(BF16)
-    grads = [dot(ds[...], qs[...]) * scale, dot(ps[...], dos[...])]
+        p = [x * inverse for x in e]
+        ds = [(x * (y - mean)).astype(BF16) for x, y in zip(p, d)]
+        return jnp.concatenate([x.astype(BF16) for x in p], 0), jnp.concatenate(ds, 0)
+
+    def gradients(h, q, do, ps, ds):
+        dq_t = dot(keys_t, ds) * scale
+        for i in range(2):
+            lanes = slice((h + i) * HEAD_DIM, (h + i + 1) * HEAD_DIM)
+            dq_ref[0, :, lanes] = dq_t[:, i * rows : (i + 1) * rows].T.astype(BF16)
+        return dot(ds, q), dot(ps, do)
+
+    grads = None
+    stage = products(0)
+    ready = None
+    for h in range(0, heads + 2, 2):
+        following = products(h + 2) if h + 2 < heads else None
+        soft = None
+        if stage is not None:
+            i, q, do, scores, slopes = stage
+            halves = [soften(scores[:, x * rows : (x + 1) * rows], slopes[:, x * rows : (x + 1) * rows]) for x in range(2)]
+            soft = (i, q, do, jnp.concatenate([x[0] for x in halves], 1), jnp.concatenate([x[1] for x in halves], 1))
+        if ready is not None:
+            more = gradients(*ready)
+            grads = more if grads is None else (grads[0] + more[0], grads[1] + more[1])
+        stage, ready = following, soft
+    grads = (grads[0] * scale, grads[1])
     for which in range(2):
         start = 0
         for ref in dself_refs:
@@ -103,12 +123,6 @@
             grid=(groups,),
             in_specs=[q_spec, q_spec, *own_specs, anc_spec] + ([] if first else [pl.BlockSpec(memory_space=pl.ANY)]),
             out_specs=[q_spec, *dself_specs, anc_spec],
-            scratch_shapes=[
-                pltpu.VMEM((heads * rows, HEAD_DIM), BF16),
-                pltpu.VMEM((heads * rows, HEAD_DIM), BF16),
-                pltpu.VMEM((span, heads * rows), BF16),
-                pltpu.VMEM((span, heads * rows), BF16),
-            ],
         ),
         out_shape=[
             jax.ShapeDtypeStruct(queries.shape, BF16),
@@ -265,12 +279,9 @@
             ],
             compiler_params=PARAMS,
         )(place, keys, values)
-        arrived, theirs, all_parents = lax.optimization_barrier(
-            (exchange_both(send), to_other_head(give), all_parents)
-        )
+        arrived, all_parents, give = lax.optimization_barrier((exchange_both(send), all_parents, give))
         arrived = arrived.reshape(2, half, 2, trees, 8, kv_width).transpose(1, 2, 3, 0, 4, 5)
         hub_own = arrived.reshape(half, 2, trees, pieces, kv_width)
-        owns = [keep, theirs]
     else:
         pair = jnp.stack([keys, values]).reshape(2, trees, part_rows, head_count, kv_width)
         pair = jnp.moveaxis(pair, 3, 0)
@@ -280,7 +291,6 @@
         hub_own = exchange(mine.reshape(2, trees, half, pieces, kv_width).transpose(2, 0, 1, 3, 4))
         owns = [mine]
 
-    hub_cross = lax.ppermute(jnp.where(upper, hub_own[:, :, 1], hub_own[:, :, 0]), "leaf", swap)
     picked_shape = jax.ShapeDtypeStruct((half, depth, 2, pieces, kv_width), BF16)
     picked_near = pl.pallas_call(
         pick_near_kernel,
@@ -290,6 +300,13 @@
         compiler_params=PARAMS,
     )(place, all_parents, hub_own)
     foreign_near = exchange(picked_near)
+    crossing = jnp.where(upper, hub_own[:, :, 1], hub_own[:, :, 0])
+    if merged:
+        foreign_near, theirs, crossing = lax.optimization_barrier((foreign_near, to_other_head(give), crossing))
+        owns = [keep, theirs]
+    else:
+        foreign_near, crossing = lax.optimization_barrier((foreign_near, crossing))
+    hub_cross = lax.ppermute(crossing, "leaf", swap)
     picked_far = pl.pallas_call(
         pick_far_kernel,
         in_specs=[SMEM, SMEM, VMEM, VMEM],
@@ -315,8 +332,14 @@
     query_grad, *self_far, grad_far = attend(
         far_place, all_parents, queries, output_gradient, owns, gather_rows(foreign_far), query_grad
     )
-    back_near, grad_far = lax.optimization_barrier((exchange(spread_rows(grad_near)), grad_far))
-    back_far = exchange(spread_rows(grad_far))
+    if merged:
+        back_near, near_got, grad_far, give = lax.optimization_barrier(
+            (exchange(grad_near), to_other_head(self_near[1]), grad_far, self_far[1])
+        )
+        back_far, far_got = lax.optimization_barrier((exchange(grad_far), to_other_head(give)))
+    else:
+        back_near, grad_far = lax.optimization_barrier((exchange(spread_rows(grad_near)), grad_far))
+        back_far = exchange(spread_rows(grad_far))
 
     sum_shape = (half, 2, pieces, kv_width)
     far_sum, cross_sum = pl.pallas_call(
@@ -340,7 +363,6 @@
     if merged:
         hub_sum = hub_sum.reshape(half, 2, 2, 2, 8, kv_width).transpose(3, 0, 2, 1, 4, 5)
         returned = exchange_both(hub_sum.reshape(2 * half, 2, 16, kv_width))
-        near_got, far_got = to_other_head(self_near[1]), to_other_head(self_far[1])
         key_gradient, value_gradient = pl.pallas_call(
             finish_kernel,
             in_specs=[SMEM] + [VMEM] * 5,

time: 130 us -> 129 us (level)
  Pallas kernels: 30.2 us -> 25.7 us
  waiting for transfers between devices: 40.1 us -> 42.5 us
  blocking collectives: 25.2 us -> 26.5 us
    pallas_call x2, Pallas kernels: 21.8 us -> 17.3 us  [attend(): pl.pallas_call(functools.partial(attend_kernel, len(owns), first), grid_s...]
    all_to_all x3 -> x4, starting transfers between devices: 11.1 us -> 15.3 us  [exchange(): return lax.all_to_all(x, 'leaf', 0, 0, tiled=True, axis_index_groups=sides)]
    all_to_all x2 -> x1, starting transfers between devices: 9.86 us -> 6.29 us  [exchange_both(): lax.all_to_all(x, ('head', 'leaf'), 0, 0, tiled=True, axis_index_groups=b...]
    all_to_all x3 -> x4, waiting for transfers between devices: 0.01 us -> 2.88 us  [exchange(): return lax.all_to_all(x, 'leaf', 0, 0, tiled=True, axis_index_groups=sides)]
    unnamed x27 -> x23, local copies, waits for them, and re-layouts: 4.74 us -> 4.73 us
  transfers between devices with their start and end apart: 10 -> 10, of which waited for: 4 -> 6; matrix products, arithmetic and copies ran while one was open for 2% -> 3% of each run, Pallas kernels for 19% -> 14%
where the time goes in v4:
time: 129 us; the launch traced here: 128 us
  waiting for transfers between devices  42.5 us (33%)
  blocking collectives  26.5 us (21%)
  starting transfers between devices  26 us (20%)
  Pallas kernels  25.7 us (20%)
  local copies, waits for them, and re-layouts  4.89 us (4%)
  between operations  1.45 us (1%)
  other arithmetic  1.41 us (1%)
    pallas_call x2, Pallas kernels, attend(): pl.pallas_call(functools.partial(attend_kernel, len(owns), first), grid_s...  17.3 us
    all_to_all x4, starting transfers between devices, exchange(): return lax.all_to_all(x, 'leaf', 0, 0, tiled=True, axis_index_groups=sides)  15.3 us
    ppermute x1, waiting for transfers between devices, body(): hub_cross = lax.ppermute(crossing, 'leaf', swap)  14 us
    optimization_barrier x1, blocking collectives, body(): lax.optimization_barrier((exchange_both(send), all_parents, give))  13.3 us
    all_to_all x1, blocking collectives, exchange_both(): lax.all_to_all(x, ('head', 'leaf'), 0, 0, tiled=True, axis_index_groups=b...  13.2 us
    ppermute x1, waiting for transfers between devices, body(): crossed = lax.ppermute(cross_sum, 'leaf', swap)  13 us
    ppermute x3, waiting for transfers between devices, to_other_head(): return lax.ppermute(x, 'head', [(0, 1), (1, 0)])  12.6 us
    all_to_all x1, starting transfers between devices, exchange_both(): lax.all_to_all(x, ('head', 'leaf'), 0, 0, tiled=True, axis_index_groups=b...  6.29 us
  transfers between devices with their start and end apart: 10, of which 6 were waited for; matrix products, arithmetic and copies ran while one was open for 3% of the time, Pallas kernels for 14%

profile of v4, /device:TPU:0, one launch (start us, length us, event | category | flops | bytes accessed | tf_op | source)
XLA Modules:
  0.0 128.4 jit_solution(4307946824320094326)
XLA Ops:
  0.6 0.1 pad_add_fusion.place
  0.7 0.0 copy-start
  0.7 0.9 copy-done
  1.7 0.0 copy-start.1
  1.7 0.9 copy-done.1
  2.6 1.4 %shard_map.76 = (bf16[16,2,16,512]{3,2,1,0:T(8,128)(2,1)}, bf16[2,2,64,512]{3,2,1,0:T(8,128)(2,1)S(1)}, bf16[2,2,64,512]{3,2,1,0:T(8,128)(2,1)S(1)}) custom-call(s32[4]{0:T(128)S(1)} %pad_add_fusion.place, bf16[2,64,1024]{2,1,0:T(8,128)(2,1)S(1)} %copy-done, bf16[2,64,1024]{2,1,0:T(8,128)(2,1)S(1)} %copy-done.1), custom_call_target="tpu_custom_call" | custom-call | tf_op jit(solution)/shard_map/pallas_call | solution.py:272
  4.0 0.0 copy-start.6
  4.0 0.7 copy-done.6
  4.8 6.3 %all-to-all-start = ((bf16[16,2,16,512]{3,2,1,0:T(8,128)(2,1)}), bf16[16,2,16,512]{3,2,1,0:T(8,128)(2,1)S(1)}, u32[]{:S(2)}, u32[]{:S(2)}) async-start(bf16[16,2,16,512]{3,2,1,0:T(8,128)(2,1)} %get-tuple-element.30), calls=%async_computation | async-start | bytes 1048576 | tf_op jit(solution)/shard_map/all_to_all | solution.py:264
  11.1 1.2 dynamic-slice
  13.0 0.9 dynamic-update-slice
  13.8 13.3 %all-reduce.parents = s32[32]{0:T(128)S(1)} all-reduce(s32[32]{0:T(128)S(1)} %dynamic-update-slice), channel_id=1, replica_groups=mesh['head'=2,'leaf'=16] {'leaf'}, use_global_device_ids=true, to_apply=%add | all-reduce | flops 32 | bytes 256 | tf_op jit(solution)/shard_map/optimization_barrier | solution.py:282
  27.1 0.0 copy-start.4
  27.1 0.0 all-to-all-done
  27.1 0.1 copy.16
  27.2 1.6 %shard_map.77 = bf16[8,2,2,16,512]{4,3,2,1,0:T(8,128)(2,1)} custom-call(s32[4]{0:T(128)S(1)} %pad_add_fusion.place, s32[32]{0:T(128)S(1)} %all-reduce.parents, bf16[8,2,2,16,512]{4,3,2,1,0:T(8,128)(2,1)S(1)} %copy.10.own_ref), custom_call_target="tpu_custom_call" | custom-call | tf_op jit(solution)/shard_map/pallas_call | solution.py:295
  28.8 3.5 %all-to-all-start.1 = ((bf16[8,2,2,16,512]{4,3,2,1,0:T(8,128)(2,1)}), bf16[8,2,2,16,512]{4,3,2,1,0:T(8,128)(2,1)S(1)}, u32[]{:S(2)}, u32[]{:S(2)}) async-start(bf16[8,2,2,16,512]{4,3,2,1,0:T(8,128)(2,1)} %shard_map.77), calls=%async_computation.1 | async-start | bytes 1048576 | tf_op jit(solution)/shard_map/all_to_all | solution.py:261
  32.4 1.5 %collective-permute-start = (bf16[2,2,64,512]{3,2,1,0:T(8,128)(2,1)S(1)}, bf16[2,2,64,512]{3,2,1,0:T(8,128)(2,1)S(1)}, u32[]{:S(2)}, u32[]{:S(2)}) collective-permute-start(bf16[2,2,64,512]{3,2,1,0:T(8,128)(2,1)S(1)} %get-tuple-element.35), channel_id=1, source_target_pairs={{0,16},{16,0},{1,17},{17,1},{2,18},{18,2},{3,19},{19,3},{4,20},{20... | collective-permute-start | bytes 786440 | tf_op jit(solution)/shard_map/ppermute | solution.py:267
  33.9 7.1 %collective-permute-done.refs_1_ = bf16[2,2,64,512]{3,2,1,0:T(8,128)(2,1)S(1)} collective-permute-done((bf16[2,2,64,512]{3,2,1,0:T(8,128)(2,1)S(1)}, bf16[2,2,64,512]{3,2,1,0:T(8,128)(2,1)S(1)}, u32[]{:S(2)}, u32[]{:S(2)}) %collective-permute-start) | collective-permute-done | bytes 262176 | tf_op jit(solution)/shard_map/ppermute | solution.py:267
  41.0 0.0 copy-start.9
  41.0 0.1 all-to-all-done.1.refs_2_
  41.1 0.0 copy-start.7
  41.1 0.3 collective-permute-start.1
  41.5 14.0 %collective-permute-done.1.cross_ref = bf16[8,2,16,512]{3,2,1,0:T(8,128)(2,1)S(1)} collective-permute-done((bf16[8,2,16,512]{3,2,1,0:T(8,128)(2,1)S(1)}, bf16[8,2,16,512]{3,2,1,0:T(8,128)(2,1)S(1)}, u32[]{:S(2)}, u32[]{:S(2)}) %collective-permute-start.1) | collective-permute-done | bytes 262176 | tf_op jit(solution)/shard_map/ppermute | solution.py:309
  55.5 0.0 copy-done.4
  55.5 1.8 %shard_map.78 = bf16[8,2,2,16,512]{4,3,2,1,0:T(8,128)(2,1)} custom-call(s32[4]{0:T(128)S(1)} %pad_add_fusion.place, s32[32]{0:T(128)S(1)} %all-reduce.parents, bf16[8,2,2,16,512]{4,3,2,1,0:T(8,128)(2,1)S(1)} %copy.10.own_ref, bf16[8,2,16,512]{3,2,1,0:T(8,128)(2,1)S(1)} %collective-permute-done.1.cross_ref), custom_call_target="tpu_custom_call" | custom-call | tf_op jit(solution)/shard_map/pallas_call | solution.py:310
  57.3 3.5 %all-to-all-start.2 = ((bf16[8,2,2,16,512]{4,3,2,1,0:T(8,128)(2,1)}), bf16[8,2,2,16,512]{4,3,2,1,0:T(8,128)(2,1)S(1)}, u32[]{:S(2)}, u32[]{:S(2)}) async-start(bf16[8,2,2,16,512]{4,3,2,1,0:T(8,128)(2,1)} %shard_map.78), calls=%async_computation.2 | async-start | bytes 1048576 | tf_op jit(solution)/shard_map/all_to_all | solution.py:261
  60.8 0.6 add_add_fusion.1.place
  61.4 0.0 copy-done.9
  61.4 0.0 copy-done.7
  61.4 8.6 %shard_map.79 = (bf16[2,128,4096]{2,1,0:T(8,128)(2,1)}, bf16[2,64,512]{2,1,0:T(8,128)(2,1)}, bf16[2,64,512]{2,1,0:T(8,128)(2,1)}, bf16[8,2,2,16,512]{4,3,2,1,0:T(8,128)(2,1)}) custom-call(s32[3]{0:T(128)} %add_add_fusion.1.place, s32[32]{0:T(128)} %copy-done.4, bf16[2,128,4096]{2,1,0:T(8,128)(2,1)} %q_ref.3, bf16[2,128,4096]{2,1,0:T(8,128)(2,1)} %do_ref.3, ...), custom_call_target="tpu_custom_call" | custom-call | flops 2013265920 | bytes 3145728 | tf_op jit(solution)/shard_map/pallas_call | solution.py:119
  70.0 0.0 all-to-all-done.2.refs_2_
  70.0 0.0 copy-start.8
  70.0 4.1 %all-to-all-start.3 = ((bf16[8,2,2,16,512]{4,3,2,1,0:T(8,128)(2,1)}), bf16[8,2,2,16,512]{4,3,2,1,0:T(8,128)(2,1)S(1)}, u32[]{:S(2)}, u32[]{:S(2)}) async-start(bf16[8,2,2,16,512]{4,3,2,1,0:T(8,128)(2,1)} %get-tuple-element.41), calls=%async_computation.3 | async-start | bytes 1048576 | tf_op jit(solution)/shard_map/all_to_all | solution.py:261
  74.1 0.6 add_add_fusion.place
  74.7 1.5 %collective-permute-start.2 = (bf16[2,64,512]{2,1,0:T(8,128)(2,1)}, bf16[2,64,512]{2,1,0:T(8,128)(2,1)S(1)}, u32[]{:S(2)}, u32[]{:S(2)}) collective-permute-start(bf16[2,64,512]{2,1,0:T(8,128)(2,1)} %get-tuple-element.42), channel_id=1, source_target_pairs={{0,16},{16,0},{1,17},{17,1},{2,18},{18,2},{3,19},{19,3},{4,20},{20... | collective-permute-start | bytes 393224 | tf_op jit(solution)/shard_map/ppermute | solution.py:267
  76.2 0.0 copy-done.8
  76.2 0.0 copy-start.5
  76.2 8.7 %shard_map.80 = (bf16[2,128,4096]{2,1,0:T(8,128)(2,1)}, bf16[2,64,512]{2,1,0:T(8,128)(2,1)}, bf16[2,64,512]{2,1,0:T(8,128)(2,1)}, bf16[8,2,2,16,512]{4,3,2,1,0:T(8,128)(2,1)}) custom-call(s32[3]{0:T(128)} %add_add_fusion.place, s32[32]{0:T(128)} %copy-done.4, bf16[2,128,4096]{2,1,0:T(8,128)(2,1)} %q_ref.3, ...), custom_call_target="tpu_custom_call", output_to_operand_aliasing={{0}: (7, {})} | custom-call | flops 2013265920 | bytes 3145728 | tf_op jit(solution)/shard_map/pallas_call | solution.py:119
  84.9 0.0 collective-permute-done.2.near_got_ref
  84.9 0.0 all-to-all-done.3.in_ref
  84.9 4.2 %all-to-all-start.4 = ((bf16[8,2,2,16,512]{4,3,2,1,0:T(8,128)(2,1)}), bf16[8,2,2,16,512]{4,3,2,1,0:T(8,128)(2,1)S(1)}, u32[]{:S(2)}, u32[]{:S(2)}) async-start(bf16[8,2,2,16,512]{4,3,2,1,0:T(8,128)(2,1)} %get-tuple-element.46), calls=%async_computation.4 | async-start | bytes 1048576 | tf_op jit(solution)/shard_map/all_to_all | solution.py:261
  89.1 0.6 collective-permute-start.3
  89.7 5.6 %collective-permute-done.3.far_got_ref = bf16[2,64,512]{2,1,0:T(8,128)(2,1)S(1)} collective-permute-done((bf16[2,64,512]{2,1,0:T(8,128)(2,1)}, bf16[2,64,512]{2,1,0:T(8,128)(2,1)S(1)}, u32[]{:S(2)}, u32[]{:S(2)}) %collective-permute-start.3) | collective-permute-done | bytes 131104 | tf_op jit(solution)/shard_map/ppermute | solution.py:267
  95.3 2.7 %all-to-all-done.4.in_ref = bf16[8,2,2,16,512]{4,3,2,1,0:T(8,128)(2,1)S(1)} async-done(((bf16[8,2,2,16,512]{4,3,2,1,0:T(8,128)(2,1)}), bf16[8,2,2,16,512]{4,3,2,1,0:T(8,128)(2,1)S(1)}, u32[]{:S(2)}, u32[]{:S(2)}) %all-to-all-start.4) | async-done | bytes 524320 | tf_op jit(solution)/shard_map/all_to_all | solution.py:261
  98.0 0.0 copy-done.5
  98.0 1.1 shard_map.82
  99.1 0.4 collective-permute-start.4
  99.5 0.9 shard_map.81
  100.5 0.0 copy-start.2
  100.5 0.0 copy-start.3
  100.5 13.0 %collective-permute-done.4 = bf16[8,2,16,512]{3,2,1,0:T(8,128)(2,1)S(1)} collective-permute-done((bf16[8,2,16,512]{3,2,1,0:T(8,128)(2,1)S(1)}, bf16[8,2,16,512]{3,2,1,0:T(8,128)(2,1)S(1)}, u32[]{:S(2)}, u32[]{:S(2)}) %collective-permute-start.4) | collective-permute-done | bytes 262176 | tf_op jit(solution)/shard_map/ppermute | solution.py:360
  113.5 0.1 fusion
  113.6 0.1 pad_maximum_fusion
  113.6 0.1 copy.14
  113.7 13.2 %all_to_all.30.got_ref = bf16[16,2,16,512]{3,2,1,0:T(8,128)(2,1)S(1)} all-to-all(bf16[16,2,16,512]{3,2,1,0:T(8,128)(2,1)S(1)} %bitcast.24), channel_id=1, replica_groups={{0,1,2,3,4,5,6,7,16,17,18,19,20,21,22,23},{8,9,10,11,12,13,14,15,24,25,..., dimensions={0} | all-to-all | bytes 1048576 | tf_op jit(solution)/shard_map/all_to_all | solution.py:264
  126.9 0.0 copy-done.2
  126.9 0.0 copy-done.3
  126.9 1.5 %shard_map.83 = (bf16[2,64,1024]{2,1,0:T(8,128)(2,1)}, bf16[2,64,1024]{2,1,0:T(8,128)(2,1)}) custom-call(s32[4]{0:T(128)S(1)} %pad_add_fusion.place, bf16[16,2,16,512]{3,2,1,0:T(8,128)(2,1)S(1)} %all_to_all.30.got_ref, bf16[2,64,512]{2,1,0:T(8,128)(2,1)S(1)} %copy-done.2, bf16[2,64,512]{2,1,0:T(8,128)(2,1)S(1)} %collective-permute-done.2.near_got_ref, ...), custom_call_target="tpu_custom_call" | custom-call | tf_op jit(solution)/shard_map/pallas_call | solution.py:366
  (3 shorter events, 0.1 us)
Async XLA Ops:
  0.7 1.0 copy-start
  1.7 0.9 copy-start.1
  4.0 0.7 copy-start.6
  4.8 22.4 %all-to-all-start = ((bf16[16,2,16,512]{3,2,1,0:T(8,128)(2,1)}), bf16[16,2,16,512]{3,2,1,0:T(8,128)(2,1)S(1)}, u32[]{:S(2)}, u32[]{:S(2)}) async-start(bf16[16,2,16,512]{3,2,1,0:T(8,128)(2,1)} %get-tuple-element.30), calls=%async_computation | async-start | bytes 1048576 | tf_op jit(solution)/shard_map/all_to_all | solution.py:264
  27.1 28.4 %copy-start.4 = (s32[32]{0:T(128)}, s32[32]{0:T(128)S(1)}, u32[]{:S(2)}) copy-start(s32[32]{0:T(128)S(1)} %all-reduce.parents) | copy-start | bytes 388
  28.8 12.3 %all-to-all-start.1 = ((bf16[8,2,2,16,512]{4,3,2,1,0:T(8,128)(2,1)}), bf16[8,2,2,16,512]{4,3,2,1,0:T(8,128)(2,1)S(1)}, u32[]{:S(2)}, u32[]{:S(2)}) async-start(bf16[8,2,2,16,512]{4,3,2,1,0:T(8,128)(2,1)} %shard_map.77), calls=%async_computation.1 | async-start | bytes 1048576 | tf_op jit(solution)/shard_map/all_to_all | solution.py:261
  32.4 8.6 %collective-permute-start = (bf16[2,2,64,512]{3,2,1,0:T(8,128)(2,1)S(1)}, bf16[2,2,64,512]{3,2,1,0:T(8,128)(2,1)S(1)}, u32[]{:S(2)}, u32[]{:S(2)}) collective-permute-start(bf16[2,2,64,512]{3,2,1,0:T(8,128)(2,1)S(1)} %get-tuple-element.35), channel_id=1, source_target_pairs={{0,16},{16,0},{1,17},{17,1},{2,18},{18,2},{3,19},{19,3},{4,20},{20... | collective-permute-start | bytes 786440 | tf_op jit(solution)/shard_map/ppermute | solution.py:267
  41.0 20.4 %copy-start.9 = (bf16[2,2,64,512]{3,2,1,0:T(8,128)(2,1)}, bf16[2,2,64,512]{3,2,1,0:T(8,128)(2,1)S(1)}, u32[]{:S(2)}) copy-start(bf16[2,2,64,512]{3,2,1,0:T(8,128)(2,1)S(1)} %collective-permute-done.refs_1_) | copy-start | bytes 786436
  41.1 20.3 %copy-start.7 = (bf16[8,2,2,16,512]{4,3,2,1,0:T(8,128)(2,1)}, bf16[8,2,2,16,512]{4,3,2,1,0:T(8,128)(2,1)S(1)}, u32[]{:S(2)}) copy-start(bf16[8,2,2,16,512]{4,3,2,1,0:T(8,128)(2,1)S(1)} %all-to-all-done.1.refs_2_) | copy-start | bytes 1572868
  41.1 14.4 %collective-permute-start.1 = (bf16[8,2,16,512]{3,2,1,0:T(8,128)(2,1)S(1)}, bf16[8,2,16,512]{3,2,1,0:T(8,128)(2,1)S(1)}, u32[]{:S(2)}, u32[]{:S(2)}) collective-permute-start(bf16[8,2,16,512]{3,2,1,0:T(8,128)(2,1)S(1)} %fusion.1), channel_id=1, source_target_pairs={{0,8},{1,9},{2,10},{3,11},{4,12},{5,13},{6,14},{7,15},{8,0},{9,1},... | collective-permute-start | bytes 786440 | tf_op jit(solution)/shard_map/ppermute | solution.py:309
  57.3 12.7 %all-to-all-start.2 = ((bf16[8,2,2,16,512]{4,3,2,1,0:T(8,128)(2,1)}), bf16[8,2,2,16,512]{4,3,2,1,0:T(8,128)(2,1)S(1)}, u32[]{:S(2)}, u32[]{:S(2)}) async-start(bf16[8,2,2,16,512]{4,3,2,1,0:T(8,128)(2,1)} %shard_map.78), calls=%async_computation.2 | async-start | bytes 1048576 | tf_op jit(solution)/shard_map/all_to_all | solution.py:261
  70.0 6.2 %copy-start.8 = (bf16[8,2,2,16,512]{4,3,2,1,0:T(8,128)(2,1)}, bf16[8,2,2,16,512]{4,3,2,1,0:T(8,128)(2,1)S(1)}, u32[]{:S(2)}) copy-start(bf16[8,2,2,16,512]{4,3,2,1,0:T(8,128)(2,1)S(1)} %all-to-all-done.2.refs_2_) | copy-start | bytes 1572868
  70.0 14.9 %all-to-all-start.3 = ((bf16[8,2,2,16,512]{4,3,2,1,0:T(8,128)(2,1)}), bf16[8,2,2,16,512]{4,3,2,1,0:T(8,128)(2,1)S(1)}, u32[]{:S(2)}, u32[]{:S(2)}) async-start(bf16[8,2,2,16,512]{4,3,2,1,0:T(8,128)(2,1)} %get-tuple-element.41), calls=%async_computation.3 | async-start | bytes 1048576 | tf_op jit(solution)/shard_map/all_to_all | solution.py:261
  74.7 10.2 %collective-permute-start.2 = (bf16[2,64,512]{2,1,0:T(8,128)(2,1)}, bf16[2,64,512]{2,1,0:T(8,128)(2,1)S(1)}, u32[]{:S(2)}, u32[]{:S(2)}) collective-permute-start(bf16[2,64,512]{2,1,0:T(8,128)(2,1)} %get-tuple-element.42), channel_id=1, source_target_pairs={{0,16},{16,0},{1,17},{17,1},{2,18},{18,2},{3,19},{19,3},{4,20},{20... | collective-permute-start | bytes 393224 | tf_op jit(solution)/shard_map/ppermute | solution.py:267
  76.2 21.8 %copy-start.5 = (s32[32]{0:T(128)S(1)}, s32[32]{0:T(128)}, u32[]{:S(2)}) copy-start(s32[32]{0:T(128)} %copy-done.4) | copy-start | bytes 388
  84.9 13.1 %all-to-all-start.4 = ((bf16[8,2,2,16,512]{4,3,2,1,0:T(8,128)(2,1)}), bf16[8,2,2,16,512]{4,3,2,1,0:T(8,128)(2,1)S(1)}, u32[]{:S(2)}, u32[]{:S(2)}) async-start(bf16[8,2,2,16,512]{4,3,2,1,0:T(8,128)(2,1)} %get-tuple-element.46), calls=%async_computation.4 | async-start | bytes 1048576 | tf_op jit(solution)/shard_map/all_to_all | solution.py:261
  89.1 6.1 %collective-permute-start.3 = (bf16[2,64,512]{2,1,0:T(8,128)(2,1)}, bf16[2,64,512]{2,1,0:T(8,128)(2,1)S(1)}, u32[]{:S(2)}, u32[]{:S(2)}) collective-permute-start(bf16[2,64,512]{2,1,0:T(8,128)(2,1)} %get-tuple-element.47), channel_id=1, source_target_pairs={{0,16},{16,0},{1,17},{17,1},{2,18},{18,2},{3,19},{19,3},{4,20},{20... | collective-permute-start | bytes 393224 | tf_op jit(solution)/shard_map/ppermute | solution.py:267
  99.1 14.4 %collective-permute-start.4 = (bf16[8,2,16,512]{3,2,1,0:T(8,128)(2,1)S(1)}, bf16[8,2,16,512]{3,2,1,0:T(8,128)(2,1)S(1)}, u32[]{:S(2)}, u32[]{:S(2)}) collective-permute-start(bf16[8,2,16,512]{3,2,1,0:T(8,128)(2,1)S(1)} %get-tuple-element.49), channel_id=1, source_target_pairs={{0,8},{1,9},{2,10},{3,11},{4,12},{5,13},{6,14},{7,15},{8,0},{9,1},... | collective-permute-start | bytes 786440 | tf_op jit(solution)/shard_map/ppermute | solution.py:360
  100.5 26.4 %copy-start.2 = (bf16[2,64,512]{2,1,0:T(8,128)(2,1)S(1)}, bf16[2,64,512]{2,1,0:T(8,128)(2,1)}, u32[]{:S(2)}) copy-start(bf16[2,64,512]{2,1,0:T(8,128)(2,1)} %get-tuple-element.51.near_ref) | copy-start | bytes 393220
  100.5 26.4 %copy-start.3 = (bf16[2,64,512]{2,1,0:T(8,128)(2,1)S(1)}, bf16[2,64,512]{2,1,0:T(8,128)(2,1)}, u32[]{:S(2)}) copy-start(bf16[2,64,512]{2,1,0:T(8,128)(2,1)} %get-tuple-element.53.far_ref) | copy-start | bytes 393220

commit v5 on v4

v5 whole, which is shorter than its diff:
```python
import functools
import math

import jax
import jax.numpy as jnp
from jax import lax
from jax.experimental import pallas as pl
from jax.experimental.pallas import tpu as pltpu
from jax.sharding import PartitionSpec as P

HEAD_DIM = 128

NT = (((1,), (1,)), ((), ()))
NN = (((1,), (0,)), ((), ()))
F32 = jnp.float32
BF16 = jnp.bfloat16
SMEM = pl.BlockSpec(memory_space=pltpu.SMEM)
PARAMS = pltpu.CompilerParams(vmem_limit_bytes=40 * 1024 * 1024)


def dot(a, b, dims=NN):
    return lax.dot_general(a, b, dims, preferred_element_type=F32)


def attend_kernel(parts, place, parents, q_ref, do_ref, *refs):
    own_refs, anc_ref, dq_ref = refs[:parts], refs[parts], refs[parts + 1]
    dself_refs, danc_ref = refs[parts + 2 : 2 * parts + 2], refs[2 * parts + 2]
    hubs, depth, _, pieces, _ = anc_ref.shape
    rows = q_ref.shape[1]
    heads = q_ref.shape[2] // HEAD_DIM
    scale = HEAD_DIM ** (-0.5)
    c = scale * math.log2(math.e)
    block = 2 * place[0] + pl.program_id(0)
    valid = []
    for _ in range(depth):
        block = above(parents, block)
        valid.append(block >= 0)

    def seen(which):
        tiles = [anc_ref[:, k, which].reshape(rows, HEAD_DIM) for k in range(depth)]
        return jnp.concatenate([ref[which, 0] for ref in own_refs] + tiles, 0)

    keys, values = seen(0), seen(1)
    keys_t = keys.T
    token = lax.rem(lax.broadcasted_iota(jnp.int32, (rows, rows), 0) + place[2], rows)
    hidden = token > lax.broadcasted_iota(jnp.int32, (rows, rows), 1)

    def products(h):
        q, do = (
            jnp.concatenate([ref[0, :, i * HEAD_DIM : (i + 1) * HEAD_DIM] for i in range(h, h + 2)], 0)
            for ref in (q_ref, do_ref)
        )
        return h, q, do, dot(keys, q, NT), dot(values, do, NT)

    def soften(scores, slopes):
        s = [scores[k * rows : (k + 1) * rows] for k in range(depth + 1)]
        d = [slopes[k * rows : (k + 1) * rows] for k in range(depth + 1)]
        s[0] = jnp.where(hidden, -1e30, s[0])
        peak = jnp.max(s[0], 0, keepdims=True)
        for k in range(depth):
            peak = jnp.maximum(peak, jnp.where(valid[k], jnp.max(s[k + 1], 0, keepdims=True), -1e30))
        peak = peak * c
        e = [jnp.exp2(s[0] * c - peak)]
        for k in range(depth):
            e.append(jnp.exp2(s[k + 1] * c - jnp.where(valid[k], peak, 1e30)))
        total = functools.reduce(jnp.add, [jnp.sum(x, 0, keepdims=True) for x in e])
        weighted = functools.reduce(jnp.add, [jnp.sum(x * y, 0, keepdims=True) for x, y in zip(e, d)])
        inverse = 1.0 / total
        mean = weighted * inverse
        p = [x * inverse for x in e]
        ds = [(x * (y - mean)).astype(BF16) for x, y in zip(p, d)]
        return jnp.concatenate([x.astype(BF16) for x in p], 0), jnp.concatenate(ds, 0)

    def gradients(h, q, do, ps, ds):
        dq_t = dot(keys_t, ds) * scale
        for i in range(2):
            lanes = slice((h + i) * HEAD_DIM, (h + i + 1) * HEAD_DIM)
            dq_ref[0, :, lanes] = dq_t[:, i * rows : (i + 1) * rows].T.astype(BF16)
        return dot(ds, q), dot(ps, do)

    grads = None
    stage = products(0)
    ready = None
    for h in range(0, heads + 2, 2):
        following = products(h + 2) if h + 2 < heads else None
        soft = None
        if stage is not None:
            i, q, do, scores, slopes = stage
            halves = [soften(scores[:, x * rows : (x + 1) * rows], slopes[:, x * rows : (x + 1) * rows]) for x in range(2)]
            soft = (i, q, do, jnp.concatenate([x[0] for x in halves], 1), jnp.concatenate([x[1] for x in halves], 1))
        if ready is not None:
            more = gradients(*ready)
            grads = more if grads is None else (grads[0] + more[0], grads[1] + more[1])
        stage, ready = following, soft
    grads = (grads[0] * scale, grads[1])
    for which in range(2):
        start = 0
        for ref in dself_refs:
            ref[which, 0] = grads[which][start : start + ref.shape[2]].astype(BF16)
            start += ref.shape[2]
        for k in range(depth):
            grad = grads[which][(k + 1) * rows : (k + 2) * rows].astype(BF16)
            danc_ref[:, k, which] = grad.reshape(hubs, pieces, HEAD_DIM)


def attend(place, parents, queries, output_gradient, owns, foreign):
    trees, rows, width = queries.shape
    hubs, slots, _, pieces, kv_width = foreign.shape
    depth = slots // trees
    groups = kv_width // HEAD_DIM
    heads = width // groups // HEAD_DIM
    q_spec = pl.BlockSpec((1, rows, heads * HEAD_DIM), lambda t, g: (t, 0, g))
    own_specs = [pl.BlockSpec((2, 1, x.shape[2], HEAD_DIM), lambda t, g: (0, t, 0, g)) for x in owns]
    anc_spec = pl.BlockSpec((hubs, depth, 2, pieces, HEAD_DIM), lambda t, g: (0, t, 0, 0, g))
    return pl.pallas_call(
        functools.partial(attend_kernel, len(owns)),
        grid=(trees, groups),
        in_specs=[SMEM, SMEM, q_spec, q_spec, *own_specs, anc_spec],
        out_specs=[q_spec, *own_specs, anc_spec],
        out_shape=[jax.ShapeDtypeStruct(x.shape, BF16) for x in (queries, *owns, foreign)],
        compiler_params=pltpu.CompilerParams(vmem_limit_bytes=56 * 1024 * 1024),
        cost_estimate=pl.CostEstimate(
            flops=10 * trees * groups * heads * (depth + 1) * rows * rows * HEAD_DIM,
            bytes_accessed=12 * rows * width,
            transcendentals=trees * groups * heads * (depth + 1) * rows * rows,
        ),
    )(place, parents, queries, output_gradient, *owns, foreign)


def pack_kernel(place, parents, keys_ref, values_ref, send_ref, keep_ref, give_ref, table_ref):
    heads, width = send_ref.shape[0] // (keys_ref.shape[1] // 8), keep_ref.shape[3]
    leaves = send_ref.shape[0] // heads
    for kv, ref in enumerate((keys_ref, values_ref)):
        for h in range(heads):
            for j in range(0, leaves, 2):
                tiles = [ref[t, 8 * j : 8 * j + 16, h * width : (h + 1) * width] for t in range(2)]
                send_ref[h * leaves + j, kv] = jnp.concatenate([x[:8] for x in tiles], 0)
                send_ref[h * leaves + j + 1, kv] = jnp.concatenate([x[8:] for x in tiles], 0)
        keep_ref[kv] = ref[:, :, pl.ds(pl.multiple_of(place[1] * width, width), width)]
        give_ref[kv] = ref[:, :, pl.ds(pl.multiple_of((1 - place[1]) * width, width), width)]
    block = lax.broadcasted_iota(jnp.int32, table_ref.shape, 1)
    table = jnp.zeros(table_ref.shape, jnp.int32)
    for t in range(2):
        table = jnp.where(block == 2 * place[0] + t, parents[t], table)
    table_ref[...] = table


def above(parents, block):
    return jnp.where(block >= 0, parents[0, jnp.maximum(block, 0)], -1)


def far_slots(place, parents, half, depth, sending, slots):
    base = (place[0] // half) * half
    source = base if sending else half - base
    target = half - source
    t = jnp.where(source == 0, 0, 1)

    def clear(p, _):
        slots[p] = -1
        return 0

    def mark(d, _):
        block = 2 * (target + d) + t
        for _ in range(depth):
            block = above(parents, block)
            p = block // 2 - source

            @pl.when((block >= 0) & (p >= 0) & (p < half))
            def _():
                slots[p] = 0

        return 0

    def number(p, count):
        needed = slots[p] >= 0
        slots[p] = jnp.where(needed, count, -1)
        return count + needed.astype(jnp.int32)

    lax.fori_loop(0, half, clear, 0)
    lax.fori_loop(0, half, mark, 0)
    return lax.fori_loop(0, half, number, 0)


def each_need(place, parents, half, depth, act):
    base = (place[0] // half) * half

    def leaf(d, _):
        for t in range(2):
            block = 2 * (base + d) + t
            for k in range(depth):
                block = above(parents, block)
                p = block // 2
                act(d, t * depth + k, block >= 0, (p >= base) & (p < base + half), p % half, t)
        return 0

    lax.fori_loop(0, half, leaf, 0)


def cross_kernel(depth, place, parents, own_ref, cross_ref, count_ref, slots):
    half = own_ref.shape[0]
    other = far_slots(place, parents, half, depth, False, slots)
    mine = far_slots(place, parents, half, depth, True, slots)
    count_ref[0] = jnp.maximum(mine, other)
    t = place[0] // half

    def copy(p, _):
        @pl.when(slots[p] >= 0)
        def _():
            cross_ref[slots[p]] = own_ref[p, :, t]

        return 0

    lax.fori_loop(0, half, copy, 0)


def pick_kernel(depth, place, parents, own_ref, cross_ref, out_ref, slots):
    half = own_ref.shape[0]
    far_slots(place, parents, half, depth, False, slots)

    def act(d, slot, valid, here, p, t):
        @pl.when(here | ~valid)
        def _():
            out_ref[d, slot] = own_ref[p, :, t]

        @pl.when(valid & ~here)
        def _():
            out_ref[d, slot] = cross_ref[slots[p]]

    each_need(place, parents, half, depth, act)


def collect_kernel(depth, place, parents, in_ref, own_ref, cross_ref, sums, slots):
    half = own_ref.shape[0]
    far_slots(place, parents, half, depth, False, slots)
    own_ref[...] = jnp.zeros_like(own_ref)
    sums[...] = jnp.zeros_like(sums)

    def act(d, slot, valid, here, p, t):
        @pl.when(valid & here)
        def _():
            own_ref[p, :, t] += in_ref[d, slot].astype(F32)

        @pl.when(valid & ~here)
        def _():
            sums[slots[p]] += in_ref[d, slot].astype(F32)

    each_need(place, parents, half, depth, act)
    cross_ref[...] = sums[...].astype(BF16)


def merge_kernel(depth, spread, place, parents, own_ref, cross_ref, out_ref, slots):
    half = own_ref.shape[0]
    far_slots(place, parents, half, depth, True, slots)
    t = place[0] // half

    def add(p, _):
        needed = slots[p] >= 0
        far = cross_ref[jnp.maximum(slots[p], 0)].astype(F32)
        for kv in range(2):
            sums = [own_ref[p, kv, i] + jnp.where(needed & (i == t), far[kv], 0.0) for i in range(2)]
            if spread:
                for h in range(2):
                    tiles = [x[8 * h : 8 * h + 8] for x in sums]
                    out_ref[h * half + p, kv] = jnp.concatenate(tiles, 0).astype(BF16)
            else:
                for i in range(2):
                    out_ref[p, kv, i] = sums[i].astype(BF16)
        return 0

    lax.fori_loop(0, half, add, 0)


def finish_kernel(place, got_ref, own_ref, own_got_ref, keys_ref, values_ref):
    width = own_ref.shape[3]
    leaves = own_ref.shape[2] // 8
    for kv, out_ref in enumerate((keys_ref, values_ref)):
        for own in range(2):
            h = place[1] if own else 1 - place[1]
            ref = own_ref if own else own_got_ref
            lanes = pl.ds(pl.multiple_of(h * width, width), width)
            for j in range(0, leaves, 2):
                rows = slice(8 * j, 8 * j + 16)
                a, b = (got_ref[h * leaves + j + i, kv].astype(F32) for i in range(2))
                for t in range(2):
                    part = slice(8 * t, 8 * t + 8)
                    total = jnp.concatenate([a[part], b[part]], 0) + ref[kv, t, rows].astype(F32)
                    out_ref[t, rows, lanes] = total.astype(BF16)


def whole(shape):
    return pl.BlockSpec(shape, lambda i: (0,) * len(shape))


def simple(kernel, place, parents, arrays, outs, scratch=(), count=False):
    out_specs = [whole(x.shape) for x in outs] + ([SMEM] if count else [])
    outs = list(outs) + ([jax.ShapeDtypeStruct((1,), jnp.int32)] if count else [])
    return pl.pallas_call(
        kernel,
        grid=(1,),
        in_specs=[SMEM, SMEM] + [whole(x.shape) for x in arrays],
        out_specs=out_specs,
        out_shape=outs,
        scratch_shapes=list(scratch),
        compiler_params=PARAMS,
    )(place, parents, *arrays)


def body(queries, keys, values, output_gradient, parents):
    leaf_count = lax.axis_size("leaf")
    head_count = lax.axis_size("head")
    half = leaf_count // 2
    depth = leaf_count // 4 - 2
    leaf_rank = lax.axis_index("leaf")
    head_rank = lax.axis_index("head")
    token = head_rank * keys.shape[1] if head_count == 2 else 0
    place = jnp.stack([leaf_rank, head_rank, token]).astype(jnp.int32)
    sides = [[half * i + j for j in range(half)] for i in range(2)]
    both = [[leaf_count * h + j for h in range(head_count) for j in side] for side in sides]
    swap = [(i, (i + half) % leaf_count) for i in range(leaf_count)]
    trees, part_rows, kv_all = keys.shape
    kv_width = kv_all // head_count
    rows = part_rows * head_count
    pieces = rows // half
    merged = head_count == 2 and part_rows == 8 * half and half % 2 == 0

    def exchange(x):
        return lax.all_to_all(x, "leaf", 0, 0, tiled=True, axis_index_groups=sides)

    def exchange_both(x):
        return lax.all_to_all(x, ("head", "leaf"), 0, 0, tiled=True, axis_index_groups=both)

    def to_other_head(x):
        return lax.ppermute(x, "head", [(0, 1), (1, 0)])

    def like(*shape, dtype=BF16):
        return jax.ShapeDtypeStruct(shape, dtype)

    blocks = trees * leaf_count
    if merged:
        send, keep, give, table = simple(
            pack_kernel,
            place,
            parents,
            (keys, values),
            [
                like(2 * half, 2, 16, kv_width),
                like(2, trees, part_rows, kv_width),
                like(2, trees, part_rows, kv_width),
                like(1, blocks, dtype=jnp.int32),
            ],
        )
        arrived, all_parents, give = lax.optimization_barrier((exchange_both(send), lax.psum(table, "leaf"), give))
        arrived = arrived.reshape(2, half, 2, trees, 8, kv_width).transpose(1, 2, 3, 0, 4, 5)
        hub_own = arrived.reshape(half, 2, trees, pieces, kv_width)
    else:
        all_parents = lax.all_gather(parents, "leaf", axis=0, tiled=True).reshape(1, blocks)
        pair = jnp.stack([keys, values]).reshape(2, trees, part_rows, head_count, kv_width)
        pair = jnp.moveaxis(pair, 3, 0)
        if head_count > 1:
            pair = lax.all_to_all(pair, "head", 0, 0, tiled=True)
        mine = pair.transpose(1, 2, 0, 3, 4).reshape(2, trees, rows, kv_width)
        hub_own = exchange(mine.reshape(2, trees, half, pieces, kv_width).transpose(2, 0, 1, 3, 4))

    piece = (2, pieces, kv_width)
    slots = pltpu.SMEM((half,), jnp.int32)
    few = min(2, half)

    def cross(x, count):
        def short():
            return jnp.concatenate([lax.ppermute(x[:few], "leaf", swap), x[few:]])

        return lax.cond(count[0] <= few, short, lambda: lax.ppermute(x, "leaf", swap))

    crossing, count = simple(
        functools.partial(cross_kernel, depth),
        place,
        all_parents,
        (hub_own,),
        [like(half, *piece)],
        [slots],
        count=True,
    )
    hub_cross = cross(crossing, count)
    (picked,) = simple(
        functools.partial(pick_kernel, depth),
        place,
        all_parents,
        (hub_own, hub_cross),
        [like(half, trees * depth, *piece)],
        [slots],
    )
    if merged:
        foreign, theirs = lax.optimization_barrier((exchange(picked), to_other_head(give)))
        owns = [keep, theirs]
    else:
        foreign = exchange(picked)
        owns = [mine]
    if pieces % 16:
        foreign = foreign.transpose(1, 2, 0, 3, 4).reshape(1, trees * depth, 2, rows, kv_width)

    query_grad, *self_grads, foreign_grad = attend(place, all_parents, queries, output_gradient, owns, foreign)
    if pieces % 16:
        foreign_grad = foreign_grad.reshape(trees * depth, 2, half, pieces, kv_width).transpose(2, 0, 1, 3, 4)
    back = exchange(foreign_grad)
    if merged:
        back, own_got = lax.optimization_barrier((back, to_other_head(self_grads[1])))

    own_sum, cross_sum = simple(
        functools.partial(collect_kernel, depth),
        place,
        all_parents,
        (back,),
        [like(half, 2, trees, pieces, kv_width, dtype=F32), like(half, *piece)],
        [pltpu.VMEM((half,) + piece, F32), slots],
    )
    (hub_sum,) = simple(
        functools.partial(merge_kernel, depth, merged),
        place,
        all_parents,
        (own_sum, cross(cross_sum, count)),
        [like(2 * half, 2, 16, kv_width) if merged else like(half, 2, trees, pieces, kv_width)],
        [slots],
    )
    if merged:
        returned = exchange_both(hub_sum)
        return query_grad, *pl.pallas_call(
            finish_kernel,
            grid=(1,),
            in_specs=[SMEM] + [whole(x.shape) for x in (returned, self_grads[0], own_got)],
            out_specs=[whole(keys.shape)] * 2,
            out_shape=[like(*keys.shape)] * 2,
            compiler_params=PARAMS,
        )(place, returned, self_grads[0], own_got)
    returned = exchange(hub_sum).transpose(1, 2, 0, 3, 4).reshape(2, trees, rows, kv_width)
    total = (returned.astype(F32) + self_grads[0].astype(F32)).astype(BF16)
    total = jnp.moveaxis(total.reshape(2, trees, head_count, part_rows, kv_width), 2, 0)
    if head_count > 1:
        total = lax.all_to_all(total, "head", 0, 0, tiled=True)
    total = total.transpose(1, 2, 3, 0, 4).reshape(2, trees, part_rows, kv_all)
    return query_grad, total[0], total[1]


def solution(mesh):
    in_specs = (
        P("leaf", None, "head"),
        P("leaf", "head", None),
        P("leaf", "head", None),
        P("leaf", None, "head"),
        P("leaf"),
    )
    out_specs = (P("leaf", None, "head"), P("leaf", "head", None), P("leaf", "head", None))
    return jax.shard_map(body, mesh=mesh, in_specs=in_specs, out_specs=out_specs, check_vma=False)
```

time: 129 us -> 115 us (0.89)
  starting transfers between devices: 26 us -> 17.4 us
  waiting for transfers between devices: 42.5 us -> 35.4 us
  blocking collectives: 26.5 us -> 30.9 us
  Pallas kernels: 25.7 us -> 24.4 us
    ppermute x2, waiting for transfers between devices: 27 us -> 9.69 us  [short(): return jnp.concatenate([lax.ppermute(x[:few], 'leaf', swap), x[few:]])]
    psum x0 -> x1, blocking collectives: none -> 16.1 us  [body(): lax.psum(table, 'leaf')]
    optimization_barrier x1 -> x0, blocking collectives: 13.3 us -> none  [body(): lax.optimization_barrier((exchange_both(send), all_parents, give))]
    all_to_all x4 -> x2, waiting for transfers between devices: 2.88 us -> 11.5 us  [exchange(): return lax.all_to_all(x, 'leaf', 0, 0, tiled=True, axis_index_groups=sides)]
    all_to_all x4 -> x2, starting transfers between devices: 15.3 us -> 7.26 us  [exchange(): return lax.all_to_all(x, 'leaf', 0, 0, tiled=True, axis_index_groups=sides)]
    all_to_all x1, blocking collectives: 13.2 us -> 14.8 us  [exchange_both(): lax.all_to_all(x, ('head', 'leaf'), 0, 0, tiled=True, axis_index_groups=b...]
    ppermute x3 -> x2, waiting for transfers between devices: 12.6 us -> 14.2 us  [to_other_head(): return lax.ppermute(x, 'head', [(0, 1), (1, 0)])]
    another operation x5 -> x1, other arithmetic: 1.38 us -> 0.08 us  [body(): place = jnp.stack([leaf_rank, head_rank, token]).astype(jnp.int32)]
  transfers between devices with their start and end apart: 10 -> 7, of which waited for: 6 -> 6; matrix products, arithmetic and copies ran while one was open for 3% -> 0% of each run, Pallas kernels for 14% -> 0%
where the time goes in v5:
time: 115 us; the launch traced here: 114 us
  waiting for transfers between devices  35.4 us (31%)
  blocking collectives  30.9 us (27%)
  Pallas kernels  24.4 us (21%)
  starting transfers between devices  17.4 us (15%)
  local copies, waits for them, and re-layouts  4.39 us (4%)
  between operations  1.41 us (1%)
    psum x1, blocking collectives, body(): lax.psum(table, 'leaf')  16.1 us
    all_to_all x1, blocking collectives, exchange_both(): lax.all_to_all(x, ('head', 'leaf'), 0, 0, tiled=True, axis_index_groups=b...  14.8 us
    ppermute x2, waiting for transfers between devices, to_other_head(): return lax.ppermute(x, 'head', [(0, 1), (1, 0)])  14.2 us
    pallas_call x1, Pallas kernels, attend(): pl.pallas_call(functools.partial(attend_kernel, len(owns)), grid=(trees,...  14 us
    all_to_all x2, waiting for transfers between devices, exchange(): return lax.all_to_all(x, 'leaf', 0, 0, tiled=True, axis_index_groups=sides)  11.5 us
    ppermute x2, waiting for transfers between devices, short(): return jnp.concatenate([lax.ppermute(x[:few], 'leaf', swap), x[few:]])  9.69 us
    pallas_call x5, Pallas kernels, simple(): pl.pallas_call(kernel, grid=(1,), in_specs=[SMEM, SMEM] + [whole(x.shape)...  8.98 us
    all_to_all x2, starting transfers between devices, exchange(): return lax.all_to_all(x, 'leaf', 0, 0, tiled=True, axis_index_groups=sides)  7.26 us
  transfers between devices with their start and end apart: 7, of which 6 were waited for; matrix products, arithmetic and copies ran while one was open for 0% of the time, Pallas kernels for 0%

profile of v5, /device:TPU:0, one launch (start us, length us, event | category | flops | bytes accessed | tf_op | source)
XLA Modules:
  0.0 114.0 jit_solution(15670316132167225892)
XLA Ops:
  0.6 0.1 pad_add_fusion.place
  0.7 0.0 copy-start
  0.7 0.9 copy-done
  1.7 0.0 copy-start.1
  1.7 0.9 copy-done.1
  2.6 0.0 copy-start.7
  2.6 0.7 copy-done.7
  3.3 0.0 copy-start.3
  3.3 1.4 %shard_map.76 = (bf16[16,2,16,512]{3,2,1,0:T(8,128)(2,1)}, bf16[2,2,64,512]{3,2,1,0:T(8,128)(2,1)S(1)}, bf16[2,2,64,512]{3,2,1,0:T(8,128)(2,1)S(1)}, s32[1,32]{1,0:T(1,128)S(1)}) custom-call(s32[3]{0:T(128)S(1)} %pad_add_fusion.place, s32[2]{0:T(128)S(1)} %copy-done.7, bf16[2,64,1024]{2,1,0:T(8,128)(2,1)S(1)} %copy-done, bf16[2,64,1024]{2,1,0:T(8,128)(2,1)S(1)} %copy-done.1), custom_call_target="tpu_custom_call" | custom-call | tf_op jit(solution)/shard_map/pallas_call | solution.py:297
  4.7 0.0 copy-start.8
  4.7 0.7 copy-done.8
  5.4 6.3 %all-to-all-start = ((bf16[16,2,16,512]{3,2,1,0:T(8,128)(2,1)}), bf16[16,2,16,512]{3,2,1,0:T(8,128)(2,1)S(1)}, u32[]{:S(2)}, u32[]{:S(2)}) async-start(bf16[16,2,16,512]{3,2,1,0:T(8,128)(2,1)} %get-tuple-element.34), calls=%async_computation | async-start | bytes 1048576 | tf_op jit(solution)/shard_map/all_to_all | solution.py:330
  11.7 16.1 %psum.7.parents = s32[1,32]{1,0:T(1,128)S(1)} all-reduce(s32[1,32]{1,0:T(1,128)S(1)} %get-tuple-element.35), channel_id=1, replica_groups=mesh['head'=2,'leaf'=16] {'leaf'}, use_global_device_ids=true, to_apply=%region_0.0 | all-reduce | flops 32 | bytes 256 | tf_op jit(solution)/shard_map/psum | solution.py:352
  27.8 0.0 copy-start.5
  27.8 0.0 all-to-all-done
  27.8 0.1 copy.10
  27.8 1.9 %shard_map.77 = (bf16[8,2,16,512]{3,2,1,0:T(8,128)(2,1)S(1)}, s32[1]{0:T(128)}) custom-call(s32[3]{0:T(128)S(1)} %pad_add_fusion.place, s32[1,32]{1,0:T(1,128)S(1)} %psum.7.parents, bf16[8,2,2,16,512]{4,3,2,1,0:T(8,128)(2,1)S(1)} %bitcast.10), custom_call_target="tpu_custom_call" | custom-call | tf_op jit(solution)/shard_map/pallas_call | solution.py:297
  30.4 5.3 %conditional.2 = (bf16[8,2,16,512]{3,2,1,0:T(8,128)(2,1)S(1)}) conditional(s32[]{:T(128)} %bitcast.7, bf16[8,2,16,512]{3,2,1,0:T(8,128)(2,1)S(1)} %get-tuple-element.41, bf16[8,2,16,512]{3,2,1,0:T(8,128)(2,1)S(1)} %get-tuple-element.41), branch_computations={%region_1.0_spmd, %region_2.0_spmd} | conditional | flops 131072 | bytes 1310768 | solution.py:372
  30.4 0.4 collective-permute-start.2
  30.8 4.8 %collective-permute-done.2 = bf16[2,2,16,512]{3,2,1,0:T(8,128)(2,1)S(1)} collective-permute-done((bf16[2,2,16,512]{3,2,1,0:T(8,128)(2,1)S(1)}, bf16[2,2,16,512]{3,2,1,0:T(8,128)(2,1)S(1)}, u32[]{:S(2)}, u32[]{:S(2)}) %collective-permute-start.2) | collective-permute-done | bytes 65568 | tf_op jit(solution)/shard_map/cond/branch_1_fun/ppermute | solution.py:370
  35.6 0.0 copy-done.3
  35.7 2.7 %shard_map.78 = bf16[8,4,2,16,512]{4,3,2,1,0:T(8,128)(2,1)} custom-call(s32[3]{0:T(128)S(1)} %pad_add_fusion.place, s32[1,32]{1,0:T(1,128)S(1)} %psum.7.parents, bf16[8,2,2,16,512]{4,3,2,1,0:T(8,128)(2,1)S(1)} %bitcast.11, bf16[8,2,16,512]{3,2,1,0:T(8,128)(2,1)S(1)} %get-tuple-element.55.cross_ref), custom_call_target="tpu_custom_call" | custom-call | tf_op jit(solution)/shard_map/pallas_call | solution.py:297
  38.4 0.0 copy-done.5
  38.4 3.6 %all-to-all-start.1 = ((bf16[8,4,2,16,512]{4,3,2,1,0:T(8,128)(2,1)}), bf16[8,4,2,16,512]{4,3,2,1,0:T(8,128)(2,1)S(1)}, u32[]{:S(2)}, u32[]{:S(2)}) async-start(bf16[8,4,2,16,512]{4,3,2,1,0:T(8,128)(2,1)} %shard_map.78), calls=%async_computation.1 | async-start | bytes 2097152 | tf_op jit(solution)/shard_map/all_to_all | solution.py:327
  41.9 1.5 %collective-permute-start.4 = (bf16[2,2,64,512]{3,2,1,0:T(8,128)(2,1)S(1)}, bf16[2,2,64,512]{3,2,1,0:T(8,128)(2,1)S(1)}, u32[]{:S(2)}, u32[]{:S(2)}) collective-permute-start(bf16[2,2,64,512]{3,2,1,0:T(8,128)(2,1)S(1)} %get-tuple-element.42), channel_id=1, source_target_pairs={{0,16},{16,0},{1,17},{17,1},{2,18},{18,2},{3,19},{19,3},{4,20},{20... | collective-permute-start | bytes 786440 | tf_op jit(solution)/shard_map/ppermute | solution.py:333
  43.5 7.1 %collective-permute-done.4.refs_1_ = bf16[2,2,64,512]{3,2,1,0:T(8,128)(2,1)S(1)} collective-permute-done((bf16[2,2,64,512]{3,2,1,0:T(8,128)(2,1)S(1)}, bf16[2,2,64,512]{3,2,1,0:T(8,128)(2,1)S(1)}, u32[]{:S(2)}, u32[]{:S(2)}) %collective-permute-start.4) | collective-permute-done | bytes 262176 | tf_op jit(solution)/shard_map/ppermute | solution.py:333
  50.5 0.0 copy-start.10
  50.5 5.8 %all-to-all-done.1.refs_2_ = bf16[8,4,2,16,512]{4,3,2,1,0:T(8,128)(2,1)S(1)} async-done(((bf16[8,4,2,16,512]{4,3,2,1,0:T(8,128)(2,1)}), bf16[8,4,2,16,512]{4,3,2,1,0:T(8,128)(2,1)S(1)}, u32[]{:S(2)}, u32[]{:S(2)}) %all-to-all-start.1) | async-done | bytes 1048608 | tf_op jit(solution)/shard_map/all_to_all | solution.py:327
  56.3 0.0 copy-start.9
  56.3 0.0 copy-done.10
  56.3 1.0 copy-done.9
  57.3 14.0 %shard_map.79 = (bf16[2,128,4096]{2,1,0:T(8,128)(2,1)}, bf16[2,2,64,512]{3,2,1,0:T(8,128)(2,1)}, bf16[2,2,64,512]{3,2,1,0:T(8,128)(2,1)}, bf16[8,4,2,16,512]{4,3,2,1,0:T(8,128)(2,1)}) custom-call(s32[3]{0:T(128)} %copy-done.3, s32[1,32]{1,0:T(1,128)} %copy-done.5, bf16[2,128,4096]{2,1,0:T(8,128)(2,1)} %q_ref.1, bf16[2,128,4096]{2,1,0:T(8,128)(2,1)} %do_ref.1, ...), custom_call_target="tpu_custom_call" | custom-call | flops 4026531840 | bytes 6291456 | tf_op jit(solution)/shard_map/pallas_call | solution.py:115
  71.3 0.0 copy-start.11
  71.3 0.0 copy-start.4
  71.3 0.0 copy-start.6
  71.3 3.7 %all-to-all-start.2 = ((bf16[8,4,2,16,512]{4,3,2,1,0:T(8,128)(2,1)}), bf16[8,4,2,16,512]{4,3,2,1,0:T(8,128)(2,1)S(1)}, u32[]{:S(2)}, u32[]{:S(2)}) async-start(bf16[8,4,2,16,512]{4,3,2,1,0:T(8,128)(2,1)} %get-tuple-element.46), calls=%async_computation.2 | async-start | bytes 2097152 | tf_op jit(solution)/shard_map/all_to_all | solution.py:327
  75.0 0.0 copy-done.11
  75.0 1.5 %collective-permute-start.5 = (bf16[2,2,64,512]{3,2,1,0:T(8,128)(2,1)S(1)}, bf16[2,2,64,512]{3,2,1,0:T(8,128)(2,1)S(1)}, u32[]{:S(2)}, u32[]{:S(2)}) collective-permute-start(bf16[2,2,64,512]{3,2,1,0:T(8,128)(2,1)S(1)} %copy-done.11), channel_id=1, source_target_pairs={{0,16},{16,0},{1,17},{17,1},{2,18},{18,2},{3,19},{19,3},{4,20},{20... | collective-permute-start | bytes 786440 | tf_op jit(solution)/shard_map/ppermute | solution.py:333
  76.6 7.1 %collective-permute-done.5.own_got_ref = bf16[2,2,64,512]{3,2,1,0:T(8,128)(2,1)S(1)} collective-permute-done((bf16[2,2,64,512]{3,2,1,0:T(8,128)(2,1)S(1)}, bf16[2,2,64,512]{3,2,1,0:T(8,128)(2,1)S(1)}, u32[]{:S(2)}, u32[]{:S(2)}) %collective-permute-start.5) | collective-permute-done | bytes 262176 | tf_op jit(solution)/shard_map/ppermute | solution.py:333
  83.6 5.8 %all-to-all-done.2.in_ref = bf16[8,4,2,16,512]{4,3,2,1,0:T(8,128)(2,1)S(1)} async-done(((bf16[8,4,2,16,512]{4,3,2,1,0:T(8,128)(2,1)}), bf16[8,4,2,16,512]{4,3,2,1,0:T(8,128)(2,1)S(1)}, u32[]{:S(2)}, u32[]{:S(2)}) %all-to-all-start.2) | async-done | bytes 1048608 | tf_op jit(solution)/shard_map/all_to_all | solution.py:327
  89.4 0.0 copy-done.4
  89.4 0.0 copy-done.6
  89.4 1.9 %shard_map.80 = (f32[8,2,2,16,512]{4,3,2,1,0:T(8,128)S(1)}, bf16[8,2,16,512]{3,2,1,0:T(8,128)(2,1)S(1)}) custom-call(s32[3]{0:T(128)S(1)} %copy-done.4, s32[1,32]{1,0:T(1,128)S(1)} %copy-done.6, bf16[8,4,2,16,512]{4,3,2,1,0:T(8,128)(2,1)S(1)} %all-to-all-done.2.in_ref), custom_call_target="tpu_custom_call" | custom-call | tf_op jit(solution)/shard_map/pallas_call | solution.py:297
  91.4 0.0 copy-start.2
  91.4 5.4 %conditional.3 = (bf16[8,2,16,512]{3,2,1,0:T(8,128)(2,1)S(1)}) conditional(s32[]{:T(128)} %bitcast.7, bf16[8,2,16,512]{3,2,1,0:T(8,128)(2,1)S(1)} %get-tuple-element.50, bf16[8,2,16,512]{3,2,1,0:T(8,128)(2,1)S(1)} %get-tuple-element.50), branch_computations={%region_3.0_spmd, %region_4.0_spmd} | conditional | flops 131072 | bytes 1310768 | solution.py:372
  91.4 0.4 collective-permute-start.3
  91.8 4.9 %collective-permute-done.3 = bf16[2,2,16,512]{3,2,1,0:T(8,128)(2,1)S(1)} collective-permute-done((bf16[2,2,16,512]{3,2,1,0:T(8,128)(2,1)S(1)}, bf16[2,2,16,512]{3,2,1,0:T(8,128)(2,1)S(1)}, u32[]{:S(2)}, u32[]{:S(2)}) %collective-permute-start.3) | collective-permute-done | bytes 65568 | tf_op jit(solution)/shard_map/cond/branch_1_fun/ppermute | solution.py:370
  96.7 1.1 shard_map.81
  97.8 14.8 %all_to_all.20.got_ref = bf16[16,2,16,512]{3,2,1,0:T(8,128)(2,1)S(1)} all-to-all(bf16[16,2,16,512]{3,2,1,0:T(8,128)(2,1)S(1)} %shard_map.81), channel_id=1, replica_groups={{0,1,2,3,4,5,6,7,16,17,18,19,20,21,22,23},{8,9,10,11,12,13,14,15,24,25,..., dimensions={0} | all-to-all | bytes 1048576 | tf_op jit(solution)/shard_map/all_to_all | solution.py:330
  112.6 0.0 copy-done.2
  112.6 1.4 %shard_map.82 = (bf16[2,64,1024]{2,1,0:T(8,128)(2,1)}, bf16[2,64,1024]{2,1,0:T(8,128)(2,1)}) custom-call(s32[3]{0:T(128)S(1)} %copy-done.4, bf16[16,2,16,512]{3,2,1,0:T(8,128)(2,1)S(1)} %all_to_all.20.got_ref, bf16[2,2,64,512]{3,2,1,0:T(8,128)(2,1)S(1)} %copy-done.2, bf16[2,2,64,512]{3,2,1,0:T(8,128)(2,1)S(1)} %collective-permute-done.5.own_got_ref), custom_call_target="tpu_custom_call" | custom-call | tf_op jit(solution)/shard_map/pallas_call | solution.py:426
  (6 shorter events, 0.1 us)
Async XLA Ops:
  0.7 1.0 copy-start
  1.7 0.9 copy-start.1
  2.6 0.7 copy-start.7
  3.3 32.4 %copy-start.3 = (s32[3]{0:T(128)}, s32[3]{0:T(128)S(1)}, u32[]{:S(2)}) copy-start(s32[3]{0:T(128)S(1)} %pad_add_fusion.place) | copy-start | bytes 40
  4.7 0.7 copy-start.8
  5.4 22.4 %all-to-all-start = ((bf16[16,2,16,512]{3,2,1,0:T(8,128)(2,1)}), bf16[16,2,16,512]{3,2,1,0:T(8,128)(2,1)S(1)}, u32[]{:S(2)}, u32[]{:S(2)}) async-start(bf16[16,2,16,512]{3,2,1,0:T(8,128)(2,1)} %get-tuple-element.34), calls=%async_computation | async-start | bytes 1048576 | tf_op jit(solution)/shard_map/all_to_all | solution.py:330
  27.8 10.6 %copy-start.5 = (s32[1,32]{1,0:T(1,128)}, s32[1,32]{1,0:T(1,128)S(1)}, u32[]{:S(2)}) copy-start(s32[1,32]{1,0:T(1,128)S(1)} %psum.7.parents) | copy-start | bytes 388
  30.4 5.2 %collective-permute-start.2 = (bf16[2,2,16,512]{3,2,1,0:T(8,128)(2,1)S(1)}, bf16[2,2,16,512]{3,2,1,0:T(8,128)(2,1)S(1)}, u32[]{:S(2)}, u32[]{:S(2)}) collective-permute-start(bf16[2,2,16,512]{3,2,1,0:T(8,128)(2,1)S(1)} %slice.8), channel_id=1, source_target_pairs={{0,8},{1,9},{2,10},{3,11},{4,12},{5,13},{6,14},{7,15},{8,0},{9,1},... | collective-permute-start | bytes 196616 | tf_op jit(solution)/shard_map/cond/branch_1_fun/ppermute | solution.py:370
  38.4 17.9 %all-to-all-start.1 = ((bf16[8,4,2,16,512]{4,3,2,1,0:T(8,128)(2,1)}), bf16[8,4,2,16,512]{4,3,2,1,0:T(8,128)(2,1)S(1)}, u32[]{:S(2)}, u32[]{:S(2)}) async-start(bf16[8,4,2,16,512]{4,3,2,1,0:T(8,128)(2,1)} %shard_map.78), calls=%async_computation.1 | async-start | bytes 2097152 | tf_op jit(solution)/shard_map/all_to_all | solution.py:327
  41.9 8.6 %collective-permute-start.4 = (bf16[2,2,64,512]{3,2,1,0:T(8,128)(2,1)S(1)}, bf16[2,2,64,512]{3,2,1,0:T(8,128)(2,1)S(1)}, u32[]{:S(2)}, u32[]{:S(2)}) collective-permute-start(bf16[2,2,64,512]{3,2,1,0:T(8,128)(2,1)S(1)} %get-tuple-element.42), channel_id=1, source_target_pairs={{0,16},{16,0},{1,17},{17,1},{2,18},{18,2},{3,19},{19,3},{4,20},{20... | collective-permute-start | bytes 786440 | tf_op jit(solution)/shard_map/ppermute | solution.py:333
  50.5 5.8 %copy-start.10 = (bf16[2,2,64,512]{3,2,1,0:T(8,128)(2,1)}, bf16[2,2,64,512]{3,2,1,0:T(8,128)(2,1)S(1)}, u32[]{:S(2)}) copy-start(bf16[2,2,64,512]{3,2,1,0:T(8,128)(2,1)S(1)} %collective-permute-done.4.refs_1_) | copy-start | bytes 786436
  56.3 1.0 copy-start.9
  71.3 3.7 %copy-start.11 = (bf16[2,2,64,512]{3,2,1,0:T(8,128)(2,1)S(1)}, bf16[2,2,64,512]{3,2,1,0:T(8,128)(2,1)}, u32[]{:S(2)}) copy-start(bf16[2,2,64,512]{3,2,1,0:T(8,128)(2,1)} %get-tuple-element.47) | copy-start | bytes 786436
  71.3 18.1 %copy-start.4 = (s32[3]{0:T(128)S(1)}, s32[3]{0:T(128)}, u32[]{:S(2)}) copy-start(s32[3]{0:T(128)} %copy-done.3) | copy-start | bytes 40
  71.3 18.1 %copy-start.6 = (s32[1,32]{1,0:T(1,128)S(1)}, s32[1,32]{1,0:T(1,128)}, u32[]{:S(2)}) copy-start(s32[1,32]{1,0:T(1,128)} %copy-done.5) | copy-start | bytes 388
  71.3 18.1 %all-to-all-start.2 = ((bf16[8,4,2,16,512]{4,3,2,1,0:T(8,128)(2,1)}), bf16[8,4,2,16,512]{4,3,2,1,0:T(8,128)(2,1)S(1)}, u32[]{:S(2)}, u32[]{:S(2)}) async-start(bf16[8,4,2,16,512]{4,3,2,1,0:T(8,128)(2,1)} %get-tuple-element.46), calls=%async_computation.2 | async-start | bytes 2097152 | tf_op jit(solution)/shard_map/all_to_all | solution.py:327
  75.0 8.6 %collective-permute-start.5 = (bf16[2,2,64,512]{3,2,1,0:T(8,128)(2,1)S(1)}, bf16[2,2,64,512]{3,2,1,0:T(8,128)(2,1)S(1)}, u32[]{:S(2)}, u32[]{:S(2)}) collective-permute-start(bf16[2,2,64,512]{3,2,1,0:T(8,128)(2,1)S(1)} %copy-done.11), channel_id=1, source_target_pairs={{0,16},{16,0},{1,17},{17,1},{2,18},{18,2},{3,19},{19,3},{4,20},{20... | collective-permute-start | bytes 786440 | tf_op jit(solution)/shard_map/ppermute | solution.py:333
  91.4 21.2 %copy-start.2 = (bf16[2,2,64,512]{3,2,1,0:T(8,128)(2,1)S(1)}, bf16[2,2,64,512]{3,2,1,0:T(8,128)(2,1)}, u32[]{:S(2)}) copy-start(bf16[2,2,64,512]{3,2,1,0:T(8,128)(2,1)} %get-tuple-element.51.own_ref) | copy-start | bytes 786436
  91.4 5.3 %collective-permute-start.3 = (bf16[2,2,16,512]{3,2,1,0:T(8,128)(2,1)S(1)}, bf16[2,2,16,512]{3,2,1,0:T(8,128)(2,1)S(1)}, u32[]{:S(2)}, u32[]{:S(2)}) collective-permute-start(bf16[2,2,16,512]{3,2,1,0:T(8,128)(2,1)S(1)} %slice.10), channel_id=1, source_target_pairs={{0,8},{1,9},{2,10},{3,11},{4,12},{5,13},{6,14},{7,15},{8,0},{9,1},... | collective-permute-start | bytes 196616 | tf_op jit(solution)/shard_map/cond/branch_1_fun/ppermute | solution.py:370

commit v6 on v5

--- a/solution.py
+++ b/solution.py
@@ -16,6 +16,7 @@
 BF16 = jnp.bfloat16
 SMEM = pl.BlockSpec(memory_space=pltpu.SMEM)
 PARAMS = pltpu.CompilerParams(vmem_limit_bytes=40 * 1024 * 1024)
+WIDE = pltpu.CompilerParams(vmem_limit_bytes=60 * 1024 * 1024)
 
 
 def dot(a, b, dims=NN):
@@ -118,7 +119,7 @@
         in_specs=[SMEM, SMEM, q_spec, q_spec, *own_specs, anc_spec],
         out_specs=[q_spec, *own_specs, anc_spec],
         out_shape=[jax.ShapeDtypeStruct(x.shape, BF16) for x in (queries, *owns, foreign)],
-        compiler_params=pltpu.CompilerParams(vmem_limit_bytes=56 * 1024 * 1024),
+        compiler_params=pltpu.CompilerParams(vmem_limit_bytes=24 * 1024 * 1024),
         cost_estimate=pl.CostEstimate(
             flops=10 * trees * groups * heads * (depth + 1) * rows * rows * HEAD_DIM,
             bytes_accessed=12 * rows * width,
@@ -149,14 +150,14 @@
     return jnp.where(block >= 0, parents[0, jnp.maximum(block, 0)], -1)
 
 
-def far_slots(place, parents, half, depth, sending, slots):
+def far_slots(place, parents, half, depth, sending, slots, start):
     base = (place[0] // half) * half
     source = base if sending else half - base
     target = half - source
     t = jnp.where(source == 0, 0, 1)
 
     def clear(p, _):
-        slots[p] = -1
+        slots[start + p] = -1
         return 0
 
     def mark(d, _):
@@ -167,13 +168,13 @@
 
             @pl.when((block >= 0) & (p >= 0) & (p < half))
             def _():
-                slots[p] = 0
+                slots[start + p] = 0
 
         return 0
 
     def number(p, count):
-        needed = slots[p] >= 0
-        slots[p] = jnp.where(needed, count, -1)
+        needed = slots[start + p] >= 0
+        slots[start + p] = jnp.where(needed, count, -1)
         return count + needed.astype(jnp.int32)
 
     lax.fori_loop(0, half, clear, 0)
@@ -196,26 +197,27 @@
     lax.fori_loop(0, half, leaf, 0)
 
 
-def cross_kernel(depth, place, parents, own_ref, cross_ref, count_ref, slots):
+def cross_kernel(depth, place, parents, own_ref, cross_ref, slots):
     half = own_ref.shape[0]
-    other = far_slots(place, parents, half, depth, False, slots)
-    mine = far_slots(place, parents, half, depth, True, slots)
-    count_ref[0] = jnp.maximum(mine, other)
+    other = far_slots(place, parents, half, depth, False, slots, 0)
+    mine = far_slots(place, parents, half, depth, True, slots, half)
+    slots[2 * half] = jnp.maximum(mine, other)
     t = place[0] // half
 
     def copy(p, _):
-        @pl.when(slots[p] >= 0)
+        slot = slots[half + p]
+
+        @pl.when(slot >= 0)
         def _():
-            cross_ref[slots[p]] = own_ref[p, :, t]
+            cross_ref[slot] = own_ref[p, :, t]
 
         return 0
 
     lax.fori_loop(0, half, copy, 0)
 
 
-def pick_kernel(depth, place, parents, own_ref, cross_ref, out_ref, slots):
+def pick_kernel(depth, place, parents, slots, own_ref, cross_ref, out_ref):
     half = own_ref.shape[0]
-    far_slots(place, parents, half, depth, False, slots)
 
     def act(d, slot, valid, here, p, t):
         @pl.when(here | ~valid)
@@ -229,9 +231,8 @@
     each_need(place, parents, half, depth, act)
 
 
-def collect_kernel(depth, place, parents, in_ref, own_ref, cross_ref, sums, slots):
+def collect_kernel(depth, place, parents, slots, in_ref, own_ref, cross_ref, sums):
     half = own_ref.shape[0]
-    far_slots(place, parents, half, depth, False, slots)
     own_ref[...] = jnp.zeros_like(own_ref)
     sums[...] = jnp.zeros_like(sums)
 
@@ -248,16 +249,15 @@
     cross_ref[...] = sums[...].astype(BF16)
 
 
-def merge_kernel(depth, spread, place, parents, own_ref, cross_ref, out_ref, slots):
+def merge_kernel(spread, place, slots, own_ref, cross_ref, out_ref):
     half = own_ref.shape[0]
-    far_slots(place, parents, half, depth, True, slots)
     t = place[0] // half
 
     def add(p, _):
-        needed = slots[p] >= 0
-        far = cross_ref[jnp.maximum(slots[p], 0)].astype(F32)
+        slot = slots[half + p]
+        far = cross_ref[jnp.maximum(slot, 0)].astype(F32)
         for kv in range(2):
-            sums = [own_ref[p, kv, i] + jnp.where(needed & (i == t), far[kv], 0.0) for i in range(2)]
+            sums = [own_ref[p, kv, i] + jnp.where((slot >= 0) & (i == t), far[kv], 0.0) for i in range(2)]
             if spread:
                 for h in range(2):
                     tiles = [x[8 * h : 8 * h + 8] for x in sums]
@@ -291,18 +291,18 @@
     return pl.BlockSpec(shape, lambda i: (0,) * len(shape))
 
 
-def simple(kernel, place, parents, arrays, outs, scratch=(), count=False):
-    out_specs = [whole(x.shape) for x in outs] + ([SMEM] if count else [])
-    outs = list(outs) + ([jax.ShapeDtypeStruct((1,), jnp.int32)] if count else [])
+def simple(kernel, scalars, arrays, outs, scratch=(), slots=0, params=PARAMS):
+    out_specs = [whole(x.shape) for x in outs] + ([SMEM] if slots else [])
+    outs = list(outs) + ([jax.ShapeDtypeStruct((slots,), jnp.int32)] if slots else [])
     return pl.pallas_call(
         kernel,
         grid=(1,),
-        in_specs=[SMEM, SMEM] + [whole(x.shape) for x in arrays],
+        in_specs=[SMEM] * len(scalars) + [whole(x.shape) for x in arrays],
         out_specs=out_specs,
         out_shape=outs,
         scratch_shapes=list(scratch),
-        compiler_params=PARAMS,
-    )(place, parents, *arrays)
+        compiler_params=params,
+    )(*scalars, *arrays)
 
 
 def body(queries, keys, values, output_gradient, parents):
@@ -339,8 +339,7 @@
     if merged:
         send, keep, give, table = simple(
             pack_kernel,
-            place,
-            parents,
+            (place, parents),
             (keys, values),
             [
                 like(2 * half, 2, 16, kv_width),
@@ -348,8 +347,12 @@
                 like(2, trees, part_rows, kv_width),
                 like(1, blocks, dtype=jnp.int32),
             ],
+            params=WIDE,
         )
-        arrived, all_parents, give = lax.optimization_barrier((exchange_both(send), lax.psum(table, "leaf"), give))
+        arrived, all_parents, theirs = lax.optimization_barrier(
+            (exchange_both(send), lax.psum(table, "leaf"), to_other_head(give))
+        )
+        owns = [keep, theirs]
         arrived = arrived.reshape(2, half, 2, trees, 8, kv_width).transpose(1, 2, 3, 0, 4, 5)
         hub_own = arrived.reshape(half, 2, trees, pieces, kv_width)
     else:
@@ -360,41 +363,31 @@
             pair = lax.all_to_all(pair, "head", 0, 0, tiled=True)
         mine = pair.transpose(1, 2, 0, 3, 4).reshape(2, trees, rows, kv_width)
         hub_own = exchange(mine.reshape(2, trees, half, pieces, kv_width).transpose(2, 0, 1, 3, 4))
+        owns = [mine]
 
     piece = (2, pieces, kv_width)
-    slots = pltpu.SMEM((half,), jnp.int32)
     few = min(2, half)
 
-    def cross(x, count):
+    def cross(x):
         def short():
             return jnp.concatenate([lax.ppermute(x[:few], "leaf", swap), x[few:]])
 
-        return lax.cond(count[0] <= few, short, lambda: lax.ppermute(x, "leaf", swap))
-
-    crossing, count = simple(
+        return lax.cond(slots[2 * half] <= few, short, lambda: lax.ppermute(x, "leaf", swap))
+
+    crossing, slots = simple(
         functools.partial(cross_kernel, depth),
-        place,
-        all_parents,
+        (place, all_parents),
         (hub_own,),
         [like(half, *piece)],
-        [slots],
-        count=True,
+        slots=2 * half + 1,
     )
-    hub_cross = cross(crossing, count)
     (picked,) = simple(
         functools.partial(pick_kernel, depth),
-        place,
-        all_parents,
-        (hub_own, hub_cross),
+        (place, all_parents, slots),
+        (hub_own, cross(crossing)),
         [like(half, trees * depth, *piece)],
-        [slots],
     )
-    if merged:
-        foreign, theirs = lax.optimization_barrier((exchange(picked), to_other_head(give)))
-        owns = [keep, theirs]
-    else:
-        foreign = exchange(picked)
-        owns = [mine]
+    foreign = exchange(picked)
     if pieces % 16:
         foreign = foreign.transpose(1, 2, 0, 3, 4).reshape(1, trees * depth, 2, rows, kv_width)
 
@@ -407,30 +400,22 @@
 
     own_sum, cross_sum = simple(
         functools.partial(collect_kernel, depth),
-        place,
-        all_parents,
+        (place, all_parents, slots),
         (back,),
         [like(half, 2, trees, pieces, kv_width, dtype=F32), like(half, *piece)],
-        [pltpu.VMEM((half,) + piece, F32), slots],
+        [pltpu.VMEM((half,) + piece, F32)],
     )
     (hub_sum,) = simple(
-        functools.partial(merge_kernel, depth, merged),
-        place,
-        all_parents,
-        (own_sum, cross(cross_sum, count)),
+        functools.partial(merge_kernel, merged),
+        (place, slots),
+        (own_sum, cross(cross_sum)),
         [like(2 * half, 2, 16, kv_width) if merged else like(half, 2, trees, pieces, kv_width)],
-        [slots],
     )
     if merged:
         returned = exchange_both(hub_sum)
-        return query_grad, *pl.pallas_call(
-            finish_kernel,
-            grid=(1,),
-            in_specs=[SMEM] + [whole(x.shape) for x in (returned, self_grads[0], own_got)],
-            out_specs=[whole(keys.shape)] * 2,
-            out_shape=[like(*keys.shape)] * 2,
-            compiler_params=PARAMS,
-        )(place, returned, self_grads[0], own_got)
+        return query_grad, *simple(
+            finish_kernel, (place,), (returned, self_grads[0], own_got), [like(*keys.shape)] * 2
+        )
     returned = exchange(hub_sum).transpose(1, 2, 0, 3, 4).reshape(2, trees, rows, kv_width)
     total = (returned.astype(F32) + self_grads[0].astype(F32)).astype(BF16)
     total = jnp.moveaxis(total.reshape(2, trees, head_count, part_rows, kv_width), 2, 0)

time: 115 us -> 110 us (0.957)
  waiting for transfers between devices: 35.4 us -> 20.4 us
  blocking collectives: 30.9 us -> 44.9 us
  local copies, waits for them, and re-layouts: 4.39 us -> 2.28 us
  Pallas kernels: 24.4 us -> 22.9 us
    all_to_all x0 -> x1, blocking collectives: none -> 17 us  [exchange(): return lax.all_to_all(x, 'leaf', 0, 0, tiled=True, axis_index_groups=sides)]
    ppermute x2, waiting for transfers between devices: 14.2 us -> 7.09 us  [to_other_head(): return lax.ppermute(x, 'head', [(0, 1), (1, 0)])]
    all_to_all x2 -> x1, waiting for transfers between devices: 11.5 us -> 5.76 us  [exchange(): return lax.all_to_all(x, 'leaf', 0, 0, tiled=True, axis_index_groups=sides)]
    all_to_all x2 -> x1, starting transfers between devices: 7.26 us -> 3.56 us  [exchange(): return lax.all_to_all(x, 'leaf', 0, 0, tiled=True, axis_index_groups=sides)]
    ppermute x2, starting transfers between devices: 0.81 us -> 3.96 us  [short(): return jnp.concatenate([lax.ppermute(x[:few], 'leaf', swap), x[few:]])]
    unnamed x24 -> x8, local copies, waits for them, and re-layouts: 4.29 us -> 1.61 us
    ppermute x2, waiting for transfers between devices: 9.69 us -> 7.55 us  [short(): return jnp.concatenate([lax.ppermute(x[:few], 'leaf', swap), x[few:]])]
    psum x1, blocking collectives: 16.1 us -> 14.1 us  [body(): lax.psum(table, 'leaf')]
  transfers between devices with their start and end apart: 7 -> 6, of which waited for: 6 -> 4; matrix products, arithmetic and copies ran while one was open for 0% -> 0% of each run, Pallas kernels for 0% -> 0%
where the time goes in v6:
time: 110 us
  blocking collectives  44.9 us (41%)
  Pallas kernels  22.9 us (21%)
  waiting for transfers between devices  20.4 us (19%)
  starting transfers between devices  17.3 us (16%)
  local copies, waits for them, and re-layouts  2.28 us (2%)
  between operations  1.38 us (1%)
    all_to_all x1, blocking collectives, exchange(): return lax.all_to_all(x, 'leaf', 0, 0, tiled=True, axis_index_groups=sides)  17 us
    psum x1, blocking collectives, body(): lax.psum(table, 'leaf')  14.1 us
    all_to_all x1, blocking collectives, exchange_both(): lax.all_to_all(x, ('head', 'leaf'), 0, 0, tiled=True, axis_index_groups=b...  13.8 us
    pallas_call x1, Pallas kernels, attend(): pl.pallas_call(functools.partial(attend_kernel, len(owns)), grid=(trees,...  13.7 us
    pallas_call x6, Pallas kernels, simple(): pl.pallas_call(kernel, grid=(1,), in_specs=[SMEM] * len(scalars) + [whole...  9.17 us
    ppermute x2, waiting for transfers between devices, short(): return jnp.concatenate([lax.ppermute(x[:few], 'leaf', swap), x[few:]])  7.55 us
    ppermute x2, waiting for transfers between devices, to_other_head(): return lax.ppermute(x, 'head', [(0, 1), (1, 0)])  7.09 us
    all_to_all x1, starting transfers between devices, exchange_both(): lax.all_to_all(x, ('head', 'leaf'), 0, 0, tiled=True, axis_index_groups=b...  6.28 us
  transfers between devices with their start and end apart: 6, of which 4 were waited for; matrix products, arithmetic and copies ran while one was open for 0% of the time, Pallas kernels for 0%

profile of v6, /device:TPU:0, one launch (start us, length us, event | category | flops | bytes accessed | tf_op | source)
XLA Modules:
  0.0 109.9 jit_solution(12405833128109920082)
XLA Ops:
  0.6 0.7 pad_add_fusion.place
  1.3 0.0 copy-start
  1.3 2.0 %shard_map.76 = (bf16[16,2,16,512]{3,2,1,0:T(8,128)(2,1)}, bf16[2,2,64,512]{3,2,1,0:T(8,128)(2,1)}, bf16[2,2,64,512]{3,2,1,0:T(8,128)(2,1)}, s32[1,32]{1,0:T(1,128)}) custom-call(s32[3]{0:T(128)} %pad_add_fusion.place, s32[2]{0:T(128)} %parents.1, bf16[2,64,1024]{2,1,0:T(8,128)(2,1)} %keys_ref.1, bf16[2,64,1024]{2,1,0:T(8,128)(2,1)} %values_ref.1), custom_call_target="tpu_custom_call" | custom-call | tf_op jit(solution)/shard_map/pallas_call | solution.py:297
  3.3 6.3 %all-to-all-start = ((bf16[16,2,16,512]{3,2,1,0:T(8,128)(2,1)}), bf16[16,2,16,512]{3,2,1,0:T(8,128)(2,1)S(1)}, u32[]{:S(2)}, u32[]{:S(2)}) async-start(bf16[16,2,16,512]{3,2,1,0:T(8,128)(2,1)} %get-tuple-element.32), calls=%async_computation | async-start | bytes 1048576 | tf_op jit(solution)/shard_map/all_to_all | solution.py:330
  9.6 1.9 %collective-permute-start.4 = (bf16[2,2,64,512]{3,2,1,0:T(8,128)(2,1)}, bf16[2,2,64,512]{3,2,1,0:T(8,128)(2,1)S(1)}, u32[]{:S(2)}, u32[]{:S(2)}) collective-permute-start(bf16[2,2,64,512]{3,2,1,0:T(8,128)(2,1)} %get-tuple-element.34), channel_id=1, source_target_pairs={{0,16},{16,0},{1,17},{17,1},{2,18},{18,2},{3,19},{19,3},{4,20},{20... | collective-permute-start | bytes 786440 | tf_op jit(solution)/shard_map/ppermute | solution.py:333
  11.6 14.1 %psum.7.parents = s32[1,32]{1,0:T(1,128)S(1)} all-reduce(s32[1,32]{1,0:T(1,128)} %get-tuple-element.33), channel_id=1, replica_groups=mesh['head'=2,'leaf'=16] {'leaf'}, use_global_device_ids=true, to_apply=%region_0.0 | all-reduce | flops 32 | bytes 256 | tf_op jit(solution)/shard_map/psum | solution.py:353
  25.7 0.0 collective-permute-done.4.refs_1_
  25.7 0.0 all-to-all-done
  25.7 0.1 copy.10
  25.8 0.0 copy-done
  25.8 1.9 %shard_map.77 = (bf16[8,2,16,512]{3,2,1,0:T(8,128)(2,1)S(1)}, s32[17]{0:T(128)S(1)}) custom-call(s32[3]{0:T(128)S(1)} %copy-done, s32[1,32]{1,0:T(1,128)S(1)} %psum.7.parents, bf16[8,2,2,16,512]{4,3,2,1,0:T(8,128)(2,1)S(1)} %bitcast.10), custom_call_target="tpu_custom_call" | custom-call | tf_op jit(solution)/shard_map/pallas_call | solution.py:297
  27.7 0.6 slice.16
  29.0 5.3 %conditional.2 = (bf16[8,2,16,512]{3,2,1,0:T(8,128)(2,1)S(1)}) conditional(s32[]{:T(128)} %bitcast.6, bf16[8,2,16,512]{3,2,1,0:T(8,128)(2,1)S(1)} %get-tuple-element.40, bf16[8,2,16,512]{3,2,1,0:T(8,128)(2,1)S(1)} %get-tuple-element.40), branch_computations={%region_1.0_spmd, %region_2.0_spmd} | conditional | flops 131072 | bytes 1310768 | solution.py:375
  29.0 0.9 collective-permute-start.2
  30.0 4.3 %collective-permute-done.2 = bf16[2,2,16,512]{3,2,1,0:T(8,128)(2,1)S(1)} collective-permute-done((bf16[2,2,16,512]{3,2,1,0:T(8,128)(2,1)S(1)}, bf16[2,2,16,512]{3,2,1,0:T(8,128)(2,1)S(1)}, u32[]{:S(2)}, u32[]{:S(2)}) %collective-permute-start.2) | collective-permute-done | bytes 65568 | tf_op jit(solution)/shard_map/cond/branch_1_fun/ppermute | solution.py:373
  34.3 0.0 copy-start.3
  34.3 0.0 copy-start.1
  34.3 1.4 %shard_map.78 = bf16[8,4,2,16,512]{4,3,2,1,0:T(8,128)(2,1)S(1)} custom-call(s32[3]{0:T(128)S(1)} %copy-done, s32[1,32]{1,0:T(1,128)S(1)} %psum.7.parents, s32[17]{0:T(128)S(1)} %get-tuple-element.39.slots, bf16[8,2,2,16,512]{4,3,2,1,0:T(8,128)(2,1)S(1)} %bitcast.11, bf16[8,2,16,512]{3,2,1,0:T(8,128)(2,1)S(1)} %get-tuple-element.51.cross_ref), custom_call_target="tpu_custom_call" | custom-call | tf_op jit(solution)/shard_map/pallas_call | solution.py:297
  35.7 17.0 %all_to_all.20.refs_2_ = bf16[8,4,2,16,512]{4,3,2,1,0:T(8,128)(2,1)S(1)} all-to-all(bf16[8,4,2,16,512]{4,3,2,1,0:T(8,128)(2,1)S(1)} %shard_map.78), channel_id=1, replica_groups={{0,1,2,3,4,5,6,7},{8,9,10,11,12,13,14,15},{16,17,18,19,20,21,22,23},{24..., dimensions={0} | all-to-all | bytes 2097152 | tf_op jit(solution)/shard_map/all_to_all | solution.py:327
  52.7 0.0 copy-done.3
  52.7 0.0 copy-done.1
  52.7 0.0 copy-start.2
  52.7 1.6 %copy-done.2 = bf16[2,128,4096]{2,1,0:T(8,128)(2,1)S(1)} copy-done((bf16[2,128,4096]{2,1,0:T(8,128)(2,1)S(1)}, bf16[2,128,4096]{2,1,0:T(8,128)(2,1)}, u32[]{:S(2)}) %copy-start.2) | copy-done | bytes 2097176
  54.3 13.7 %shard_map.79 = (bf16[2,128,4096]{2,1,0:T(8,128)(2,1)}, bf16[2,2,64,512]{3,2,1,0:T(8,128)(2,1)S(1)}, bf16[2,2,64,512]{3,2,1,0:T(8,128)(2,1)S(1)}, bf16[8,4,2,16,512]{4,3,2,1,0:T(8,128)(2,1)}) custom-call(s32[3]{0:T(128)S(1)} %copy-done, s32[1,32]{1,0:T(1,128)S(1)} %psum.7.parents, bf16[2,128,4096]{2,1,0:T(8,128)(2,1)S(1)} %copy-done.1, ...), custom_call_target="tpu_custom_call" | custom-call | flops 4026531840 | bytes 6291456 | tf_op jit(solution)/shard_map/pallas_call | solution.py:116
  68.0 3.6 %all-to-all-start.2 = ((bf16[8,4,2,16,512]{4,3,2,1,0:T(8,128)(2,1)}), bf16[8,4,2,16,512]{4,3,2,1,0:T(8,128)(2,1)S(1)}, u32[]{:S(2)}, u32[]{:S(2)}) async-start(bf16[8,4,2,16,512]{4,3,2,1,0:T(8,128)(2,1)} %get-tuple-element.42), calls=%async_computation.2 | async-start | bytes 2097152 | tf_op jit(solution)/shard_map/all_to_all | solution.py:327
  71.6 1.5 %collective-permute-start.5 = (bf16[2,2,64,512]{3,2,1,0:T(8,128)(2,1)S(1)}, bf16[2,2,64,512]{3,2,1,0:T(8,128)(2,1)S(1)}, u32[]{:S(2)}, u32[]{:S(2)}) collective-permute-start(bf16[2,2,64,512]{3,2,1,0:T(8,128)(2,1)S(1)} %get-tuple-element.43), channel_id=1, source_target_pairs={{0,16},{16,0},{1,17},{17,1},{2,18},{18,2},{3,19},{19,3},{4,20},{20... | collective-permute-start | bytes 786440 | tf_op jit(solution)/shard_map/ppermute | solution.py:333
  73.1 7.1 %collective-permute-done.5.own_got_ref = bf16[2,2,64,512]{3,2,1,0:T(8,128)(2,1)S(1)} collective-permute-done((bf16[2,2,64,512]{3,2,1,0:T(8,128)(2,1)S(1)}, bf16[2,2,64,512]{3,2,1,0:T(8,128)(2,1)S(1)}, u32[]{:S(2)}, u32[]{:S(2)}) %collective-permute-start.5) | collective-permute-done | bytes 262176 | tf_op jit(solution)/shard_map/ppermute | solution.py:333
  80.2 5.8 %all-to-all-done.2.in_ref = bf16[8,4,2,16,512]{4,3,2,1,0:T(8,128)(2,1)S(1)} async-done(((bf16[8,4,2,16,512]{4,3,2,1,0:T(8,128)(2,1)}), bf16[8,4,2,16,512]{4,3,2,1,0:T(8,128)(2,1)S(1)}, u32[]{:S(2)}, u32[]{:S(2)}) %all-to-all-start.2) | async-done | bytes 1048608 | tf_op jit(solution)/shard_map/all_to_all | solution.py:327
  86.0 1.6 %shard_map.80 = (f32[8,2,2,16,512]{4,3,2,1,0:T(8,128)S(1)}, bf16[8,2,16,512]{3,2,1,0:T(8,128)(2,1)S(1)}) custom-call(s32[3]{0:T(128)S(1)} %copy-done, s32[1,32]{1,0:T(1,128)S(1)} %psum.7.parents, s32[17]{0:T(128)S(1)} %get-tuple-element.39.slots, bf16[8,4,2,16,512]{4,3,2,1,0:T(8,128)(2,1)S(1)} %all-to-all-done.2.in_ref), custom_call_target="tpu_custom_call" | custom-call | tf_op jit(solution)/shard_map/pallas_call | solution.py:297
  87.6 6.4 %conditional.3 = (bf16[8,2,16,512]{3,2,1,0:T(8,128)(2,1)S(1)}) conditional(s32[]{:T(128)} %bitcast.6, bf16[8,2,16,512]{3,2,1,0:T(8,128)(2,1)S(1)} %get-tuple-element.46, bf16[8,2,16,512]{3,2,1,0:T(8,128)(2,1)S(1)} %get-tuple-element.46), branch_computations={%region_3.0_spmd, %region_4.0_spmd} | conditional | flops 131072 | bytes 1310768 | solution.py:375
  87.7 3.0 %collective-permute-start.3 = (bf16[2,2,16,512]{3,2,1,0:T(8,128)(2,1)S(1)}, bf16[2,2,16,512]{3,2,1,0:T(8,128)(2,1)S(1)}, u32[]{:S(2)}, u32[]{:S(2)}) collective-permute-start(bf16[2,2,16,512]{3,2,1,0:T(8,128)(2,1)S(1)} %slice.13), channel_id=1, source_target_pairs={{0,8},{1,9},{2,10},{3,11},{4,12},{5,13},{6,14},{7,15},{8,0},{9,1},... | collective-permute-start | bytes 196616 | tf_op jit(solution)/shard_map/cond/branch_1_fun/ppermute | solution.py:373
  90.7 3.3 %collective-permute-done.3 = bf16[2,2,16,512]{3,2,1,0:T(8,128)(2,1)S(1)} collective-permute-done((bf16[2,2,16,512]{3,2,1,0:T(8,128)(2,1)S(1)}, bf16[2,2,16,512]{3,2,1,0:T(8,128)(2,1)S(1)}, u32[]{:S(2)}, u32[]{:S(2)}) %collective-permute-start.3) | collective-permute-done | bytes 65568 | tf_op jit(solution)/shard_map/cond/branch_1_fun/ppermute | solution.py:373
  94.0 0.7 shard_map.81
  94.7 13.8 %all_to_all.21.got_ref = bf16[16,2,16,512]{3,2,1,0:T(8,128)(2,1)S(1)} all-to-all(bf16[16,2,16,512]{3,2,1,0:T(8,128)(2,1)S(1)} %shard_map.81), channel_id=1, replica_groups={{0,1,2,3,4,5,6,7,16,17,18,19,20,21,22,23},{8,9,10,11,12,13,14,15,24,25,..., dimensions={0} | all-to-all | bytes 1048576 | tf_op jit(solution)/shard_map/all_to_all | solution.py:330
  108.5 1.4 %shard_map.82 = (bf16[2,64,1024]{2,1,0:T(8,128)(2,1)}, bf16[2,64,1024]{2,1,0:T(8,128)(2,1)}) custom-call(s32[3]{0:T(128)S(1)} %copy-done, bf16[16,2,16,512]{3,2,1,0:T(8,128)(2,1)S(1)} %all_to_all.21.got_ref, bf16[2,2,64,512]{3,2,1,0:T(8,128)(2,1)S(1)} %get-tuple-element.47.own_ref, bf16[2,2,64,512]{3,2,1,0:T(8,128)(2,1)S(1)} %collective-permute-done.5.own_got_ref), custom_call_target="tpu_custom_call" | custom-call | tf_op jit(solution)/shard_map/pallas_call | solution.py:297
  (6 shorter events, 0.1 us)
Async XLA Ops:
  1.3 24.5 %copy-start = (s32[3]{0:T(128)S(1)}, s32[3]{0:T(128)}, u32[]{:S(2)}) copy-start(s32[3]{0:T(128)} %pad_add_fusion.place) | copy-start | bytes 40
  3.3 22.4 %all-to-all-start = ((bf16[16,2,16,512]{3,2,1,0:T(8,128)(2,1)}), bf16[16,2,16,512]{3,2,1,0:T(8,128)(2,1)S(1)}, u32[]{:S(2)}, u32[]{:S(2)}) async-start(bf16[16,2,16,512]{3,2,1,0:T(8,128)(2,1)} %get-tuple-element.32), calls=%async_computation | async-start | bytes 1048576 | tf_op jit(solution)/shard_map/all_to_all | solution.py:330
  9.6 16.1 %collective-permute-start.4 = (bf16[2,2,64,512]{3,2,1,0:T(8,128)(2,1)}, bf16[2,2,64,512]{3,2,1,0:T(8,128)(2,1)S(1)}, u32[]{:S(2)}, u32[]{:S(2)}) collective-permute-start(bf16[2,2,64,512]{3,2,1,0:T(8,128)(2,1)} %get-tuple-element.34), channel_id=1, source_target_pairs={{0,16},{16,0},{1,17},{17,1},{2,18},{18,2},{3,19},{19,3},{4,20},{20... | collective-permute-start | bytes 786440 | tf_op jit(solution)/shard_map/ppermute | solution.py:333
  29.0 5.2 %collective-permute-start.2 = (bf16[2,2,16,512]{3,2,1,0:T(8,128)(2,1)S(1)}, bf16[2,2,16,512]{3,2,1,0:T(8,128)(2,1)S(1)}, u32[]{:S(2)}, u32[]{:S(2)}) collective-permute-start(bf16[2,2,16,512]{3,2,1,0:T(8,128)(2,1)S(1)} %slice.6), channel_id=1, source_target_pairs={{0,8},{1,9},{2,10},{3,11},{4,12},{5,13},{6,14},{7,15},{8,0},{9,1},... | collective-permute-start | bytes 196616 | tf_op jit(solution)/shard_map/cond/branch_1_fun/ppermute | solution.py:373
  34.3 18.5 %copy-start.3 = (bf16[2,2,64,512]{3,2,1,0:T(8,128)(2,1)S(1)}, bf16[2,2,64,512]{3,2,1,0:T(8,128)(2,1)}, u32[]{:S(2)}) copy-start(bf16[2,2,64,512]{3,2,1,0:T(8,128)(2,1)} %get-tuple-element.36.refs_0_) | copy-start | bytes 786436
  34.3 18.5 %copy-start.1 = (bf16[2,128,4096]{2,1,0:T(8,128)(2,1)S(1)}, bf16[2,128,4096]{2,1,0:T(8,128)(2,1)}, u32[]{:S(2)}) copy-start(bf16[2,128,4096]{2,1,0:T(8,128)(2,1)} %q_ref.1) | copy-start | bytes 6291460
  52.7 1.6 %copy-start.2 = (bf16[2,128,4096]{2,1,0:T(8,128)(2,1)S(1)}, bf16[2,128,4096]{2,1,0:T(8,128)(2,1)}, u32[]{:S(2)}) copy-start(bf16[2,128,4096]{2,1,0:T(8,128)(2,1)} %do_ref.1) | copy-start | bytes 6291460
  68.0 17.9 %all-to-all-start.2 = ((bf16[8,4,2,16,512]{4,3,2,1,0:T(8,128)(2,1)}), bf16[8,4,2,16,512]{4,3,2,1,0:T(8,128)(2,1)S(1)}, u32[]{:S(2)}, u32[]{:S(2)}) async-start(bf16[8,4,2,16,512]{4,3,2,1,0:T(8,128)(2,1)} %get-tuple-element.42), calls=%async_computation.2 | async-start | bytes 2097152 | tf_op jit(solution)/shard_map/all_to_all | solution.py:327
  71.6 8.6 %collective-permute-start.5 = (bf16[2,2,64,512]{3,2,1,0:T(8,128)(2,1)S(1)}, bf16[2,2,64,512]{3,2,1,0:T(8,128)(2,1)S(1)}, u32[]{:S(2)}, u32[]{:S(2)}) collective-permute-start(bf16[2,2,64,512]{3,2,1,0:T(8,128)(2,1)S(1)} %get-tuple-element.43), channel_id=1, source_target_pairs={{0,16},{16,0},{1,17},{17,1},{2,18},{18,2},{3,19},{19,3},{4,20},{20... | collective-permute-start | bytes 786440 | tf_op jit(solution)/shard_map/ppermute | solution.py:333
  87.7 6.3 %collective-permute-start.3 = (bf16[2,2,16,512]{3,2,1,0:T(8,128)(2,1)S(1)}, bf16[2,2,16,512]{3,2,1,0:T(8,128)(2,1)S(1)}, u32[]{:S(2)}, u32[]{:S(2)}) collective-permute-start(bf16[2,2,16,512]{3,2,1,0:T(8,128)(2,1)S(1)} %slice.13), channel_id=1, source_target_pairs={{0,8},{1,9},{2,10},{3,11},{4,12},{5,13},{6,14},{7,15},{8,0},{9,1},... | collective-permute-start | bytes 196616 | tf_op jit(solution)/shard_map/cond/branch_1_fun/ppermute | solution.py:373

commit v7 on v6

--- a/solution.py
+++ b/solution.py
@@ -28,7 +28,8 @@
     dself_refs, danc_ref = refs[parts + 2 : 2 * parts + 2], refs[2 * parts + 2]
     hubs, depth, _, pieces, _ = anc_ref.shape
     rows = q_ref.shape[1]
-    heads = q_ref.shape[2] // HEAD_DIM
+    step_groups = anc_ref.shape[4] // HEAD_DIM
+    heads = q_ref.shape[2] // HEAD_DIM // step_groups
     scale = HEAD_DIM ** (-0.5)
     c = scale * math.log2(math.e)
     block = 2 * place[0] + pl.program_id(0)
@@ -37,21 +38,24 @@
         block = above(parents, block)
         valid.append(block >= 0)
 
-    def seen(which):
-        tiles = [anc_ref[:, k, which].reshape(rows, HEAD_DIM) for k in range(depth)]
-        return jnp.concatenate([ref[which, 0] for ref in own_refs] + tiles, 0)
-
-    keys, values = seen(0), seen(1)
-    keys_t = keys.T
+    def lanes(group, count=1):
+        return slice(group * HEAD_DIM, (group + count) * HEAD_DIM)
+
+    def seen(which, group):
+        tiles = [anc_ref[:, k, which, :, lanes(group)].reshape(rows, HEAD_DIM) for k in range(depth)]
+        return jnp.concatenate([ref[which, 0, :, lanes(group)] for ref in own_refs] + tiles, 0)
+
+    held = [(seen(0, group), seen(1, group)) for group in range(step_groups)]
+    held = [(keys, values, keys.T) for keys, values in held]
     token = lax.rem(lax.broadcasted_iota(jnp.int32, (rows, rows), 0) + place[2], rows)
     hidden = token > lax.broadcasted_iota(jnp.int32, (rows, rows), 1)
 
-    def products(h):
+    def products(group, h):
         q, do = (
-            jnp.concatenate([ref[0, :, i * HEAD_DIM : (i + 1) * HEAD_DIM] for i in range(h, h + 2)], 0)
+            jnp.concatenate([ref[0, :, lanes(group * heads + i)] for i in range(h, h + 2)], 0)
             for ref in (q_ref, do_ref)
         )
-        return h, q, do, dot(keys, q, NT), dot(values, do, NT)
+        return group, h, q, do, dot(held[group][0], q, NT), dot(held[group][1], do, NT)
 
     def soften(scores, slopes):
         s = [scores[k * rows : (k + 1) * rows] for k in range(depth + 1)]
@@ -72,36 +76,38 @@
         ds = [(x * (y - mean)).astype(BF16) for x, y in zip(p, d)]
         return jnp.concatenate([x.astype(BF16) for x in p], 0), jnp.concatenate(ds, 0)
 
-    def gradients(h, q, do, ps, ds):
-        dq_t = dot(keys_t, ds) * scale
+    def gradients(group, h, q, do, ps, ds):
+        dq_t = dot(held[group][2], ds) * scale
         for i in range(2):
-            lanes = slice((h + i) * HEAD_DIM, (h + i + 1) * HEAD_DIM)
-            dq_ref[0, :, lanes] = dq_t[:, i * rows : (i + 1) * rows].T.astype(BF16)
+            dq_ref[0, :, lanes(group * heads + h + i)] = dq_t[:, i * rows : (i + 1) * rows].T.astype(BF16)
         return dot(ds, q), dot(ps, do)
 
-    grads = None
-    stage = products(0)
-    ready = None
-    for h in range(0, heads + 2, 2):
-        following = products(h + 2) if h + 2 < heads else None
+    def store(group, grads):
+        for which in range(2):
+            start = 0
+            for ref in dself_refs:
+                ref[which, 0, :, lanes(group)] = grads[which][start : start + ref.shape[2]].astype(BF16)
+                start += ref.shape[2]
+            for k in range(depth):
+                grad = grads[which][(k + 1) * rows : (k + 2) * rows].astype(BF16)
+                danc_ref[:, k, which, :, lanes(group)] = grad.reshape(hubs, pieces, HEAD_DIM)
+
+    pairs = [(group, h) for group in range(step_groups) for h in range(0, heads, 2)]
+    stage, ready, grads = products(*pairs[0]), None, None
+    for i in range(len(pairs) + 1):
+        following = products(*pairs[i + 1]) if i + 1 < len(pairs) else None
         soft = None
         if stage is not None:
-            i, q, do, scores, slopes = stage
+            group, h, q, do, scores, slopes = stage
             halves = [soften(scores[:, x * rows : (x + 1) * rows], slopes[:, x * rows : (x + 1) * rows]) for x in range(2)]
-            soft = (i, q, do, jnp.concatenate([x[0] for x in halves], 1), jnp.concatenate([x[1] for x in halves], 1))
+            soft = (group, h, q, do, *[jnp.concatenate(x, 1) for x in zip(*halves)])
         if ready is not None:
             more = gradients(*ready)
             grads = more if grads is None else (grads[0] + more[0], grads[1] + more[1])
+            if ready[1] == heads - 2:
+                store(ready[0], (grads[0] * scale, grads[1]))
+                grads = None
         stage, ready = following, soft
-    grads = (grads[0] * scale, grads[1])
-    for which in range(2):
-        start = 0
-        for ref in dself_refs:
-            ref[which, 0] = grads[which][start : start + ref.shape[2]].astype(BF16)
-            start += ref.shape[2]
-        for k in range(depth):
-            grad = grads[which][(k + 1) * rows : (k + 2) * rows].astype(BF16)
-            danc_ref[:, k, which] = grad.reshape(hubs, pieces, HEAD_DIM)
 
 
 def attend(place, parents, queries, output_gradient, owns, foreign):
@@ -110,16 +116,18 @@
     depth = slots // trees
     groups = kv_width // HEAD_DIM
     heads = width // groups // HEAD_DIM
-    q_spec = pl.BlockSpec((1, rows, heads * HEAD_DIM), lambda t, g: (t, 0, g))
-    own_specs = [pl.BlockSpec((2, 1, x.shape[2], HEAD_DIM), lambda t, g: (0, t, 0, g)) for x in owns]
-    anc_spec = pl.BlockSpec((hubs, depth, 2, pieces, HEAD_DIM), lambda t, g: (0, t, 0, 0, g))
+    step = 2 - groups % 2
+    lanes = step * HEAD_DIM
+    q_spec = pl.BlockSpec((1, rows, heads * lanes), lambda t, g: (t, 0, g))
+    own_specs = [pl.BlockSpec((2, 1, x.shape[2], lanes), lambda t, g: (0, t, 0, g)) for x in owns]
+    anc_spec = pl.BlockSpec((hubs, depth, 2, pieces, lanes), lambda t, g: (0, t, 0, 0, g))
     return pl.pallas_call(
         functools.partial(attend_kernel, len(owns)),
-        grid=(trees, groups),
+        grid=(trees, groups // step),
         in_specs=[SMEM, SMEM, q_spec, q_spec, *own_specs, anc_spec],
         out_specs=[q_spec, *own_specs, anc_spec],
         out_shape=[jax.ShapeDtypeStruct(x.shape, BF16) for x in (queries, *owns, foreign)],
-        compiler_params=pltpu.CompilerParams(vmem_limit_bytes=24 * 1024 * 1024),
+        compiler_params=pltpu.CompilerParams(vmem_limit_bytes=50 * 1024 * 1024),
         cost_estimate=pl.CostEstimate(
             flops=10 * trees * groups * heads * (depth + 1) * rows * rows * HEAD_DIM,
             bytes_accessed=12 * rows * width,
@@ -128,7 +136,7 @@
     )(place, parents, queries, output_gradient, *owns, foreign)
 
 
-def pack_kernel(place, parents, keys_ref, values_ref, send_ref, keep_ref, give_ref, table_ref):
+def pack_kernel(place, keys_ref, values_ref, send_ref, keep_ref, give_ref):
     heads, width = send_ref.shape[0] // (keys_ref.shape[1] // 8), keep_ref.shape[3]
     leaves = send_ref.shape[0] // heads
     for kv, ref in enumerate((keys_ref, values_ref)):
@@ -139,10 +147,16 @@
                 send_ref[h * leaves + j + 1, kv] = jnp.concatenate([x[8:] for x in tiles], 0)
         keep_ref[kv] = ref[:, :, pl.ds(pl.multiple_of(place[1] * width, width), width)]
         give_ref[kv] = ref[:, :, pl.ds(pl.multiple_of((1 - place[1]) * width, width), width)]
+
+
+def table_kernel(place, parents, partner_parents, table_ref):
+    blocks = table_ref.shape[1]
     block = lax.broadcasted_iota(jnp.int32, table_ref.shape, 1)
     table = jnp.zeros(table_ref.shape, jnp.int32)
     for t in range(2):
-        table = jnp.where(block == 2 * place[0] + t, parents[t], table)
+        own = 2 * place[0] + t
+        table = jnp.where(block == own, parents[t], table)
+        table = jnp.where(block == lax.rem(own + blocks // 2, blocks), partner_parents[t], table)
     table_ref[...] = table
 
 
@@ -197,11 +211,11 @@
     lax.fori_loop(0, half, leaf, 0)
 
 
-def cross_kernel(depth, place, parents, own_ref, cross_ref, slots):
+def cross_kernel(depth, place, parents, own_ref, cross_ref, slots, count):
     half = own_ref.shape[0]
     other = far_slots(place, parents, half, depth, False, slots, 0)
     mine = far_slots(place, parents, half, depth, True, slots, half)
-    slots[2 * half] = jnp.maximum(mine, other)
+    count[0] = jnp.maximum(mine, other)
     t = place[0] // half
 
     def copy(p, _):
@@ -291,9 +305,9 @@
     return pl.BlockSpec(shape, lambda i: (0,) * len(shape))
 
 
-def simple(kernel, scalars, arrays, outs, scratch=(), slots=0, params=PARAMS):
-    out_specs = [whole(x.shape) for x in outs] + ([SMEM] if slots else [])
-    outs = list(outs) + ([jax.ShapeDtypeStruct((slots,), jnp.int32)] if slots else [])
+def simple(kernel, scalars, arrays, outs, scratch=(), slots=(), params=PARAMS):
+    out_specs = [whole(x.shape) for x in outs] + [SMEM] * len(slots)
+    outs = list(outs) + [jax.ShapeDtypeStruct((x,), jnp.int32) for x in slots]
     return pl.pallas_call(
         kernel,
         grid=(1,),
@@ -329,34 +343,42 @@
     def exchange_both(x):
         return lax.all_to_all(x, ("head", "leaf"), 0, 0, tiled=True, axis_index_groups=both)
 
+    def gather_parents(x):
+        return lax.psum(x, "leaf", axis_index_groups=sides)
+
     def to_other_head(x):
         return lax.ppermute(x, "head", [(0, 1), (1, 0)])
 
     def like(*shape, dtype=BF16):
         return jax.ShapeDtypeStruct(shape, dtype)
 
-    blocks = trees * leaf_count
+    (table,) = simple(
+        table_kernel,
+        (place, parents, lax.ppermute(parents, "leaf", swap)),
+        (),
+        [like(1, trees * leaf_count, dtype=jnp.int32)],
+    )
     if merged:
-        send, keep, give, table = simple(
+        send, keep, give = simple(
             pack_kernel,
-            (place, parents),
+            (place,),
             (keys, values),
             [
                 like(2 * half, 2, 16, kv_width),
                 like(2, trees, part_rows, kv_width),
                 like(2, trees, part_rows, kv_width),
-                like(1, blocks, dtype=jnp.int32),
             ],
             params=WIDE,
         )
+        send, give, table = lax.optimization_barrier((send, give, table))
         arrived, all_parents, theirs = lax.optimization_barrier(
-            (exchange_both(send), lax.psum(table, "leaf"), to_other_head(give))
+            (exchange_both(send), gather_parents(table), to_other_head(give))
         )
         owns = [keep, theirs]
         arrived = arrived.reshape(2, half, 2, trees, 8, kv_width).transpose(1, 2, 3, 0, 4, 5)
         hub_own = arrived.reshape(half, 2, trees, pieces, kv_width)
     else:
-        all_parents = lax.all_gather(parents, "leaf", axis=0, tiled=True).reshape(1, blocks)
+        all_parents = gather_parents(table)
         pair = jnp.stack([keys, values]).reshape(2, trees, part_rows, head_count, kv_width)
         pair = jnp.moveaxis(pair, 3, 0)
         if head_count > 1:
@@ -372,14 +394,14 @@
         def short():
             return jnp.concatenate([lax.ppermute(x[:few], "leaf", swap), x[few:]])
 
-        return lax.cond(slots[2 * half] <= few, short, lambda: lax.ppermute(x, "leaf", swap))
-
-    crossing, slots = simple(
+        return lax.cond(count[0] <= few, short, lambda: lax.ppermute(x, "leaf", swap))
+
+    crossing, slots, count = simple(
         functools.partial(cross_kernel, depth),
         (place, all_parents),
         (hub_own,),
         [like(half, *piece)],
-        slots=2 * half + 1,
+        slots=(2 * half, 1),
     )
     (picked,) = simple(
         functools.partial(pick_kernel, depth),

time: 110 us -> 111 us (level)
  blocking collectives: 44.9 us -> 41.9 us
  starting transfers between devices: 17.3 us -> 19.6 us
  waiting for transfers between devices: 20.4 us -> 22.5 us
    psum x1, blocking collectives: 14.1 us -> 9.96 us  [gather_parents(): return lax.psum(x, 'leaf', axis_index_groups=sides)]
    ppermute x0 -> x1, starting transfers between devices: none -> 4.1 us  [body(): lax.ppermute(parents, 'leaf', swap)]
    ppermute x2, waiting for transfers between devices: 7.09 us -> 10.5 us  [to_other_head(): return lax.ppermute(x, 'head', [(0, 1), (1, 0)])]
    all_to_all x1, starting transfers between devices: 6.28 us -> 4.85 us  [exchange_both(): lax.all_to_all(x, ('head', 'leaf'), 0, 0, tiled=True, axis_index_groups=b...]
    ppermute x2, waiting for transfers between devices: 7.55 us -> 6.21 us  [short(): return jnp.concatenate([lax.ppermute(x[:few], 'leaf', swap), x[few:]])]
    pallas_call x6 -> x7, Pallas kernels: 9.17 us -> 9.73 us  [simple(): pl.pallas_call(kernel, grid=(1,), in_specs=[SMEM] * len(scalars) + [whole...]
  transfers between devices with their start and end apart: 6 -> 7, of which waited for: 4 -> 5; matrix products, arithmetic and copies ran while one was open for 0% -> 1% of each run, Pallas kernels for 0% -> 2%
where the time goes in v7:
time: 111 us; the launch traced here: 110 us
  blocking collectives  41.9 us (38%)
  Pallas kernels  22.6 us (20%)
  waiting for transfers between devices  22.5 us (20%)
  starting transfers between devices  19.6 us (18%)
  local copies, waits for them, and re-layouts  1.43 us (1%)
  between operations  1.38 us (1%)
    all_to_all x1, blocking collectives, exchange(): return lax.all_to_all(x, 'leaf', 0, 0, tiled=True, axis_index_groups=sides)  18.1 us
    all_to_all x1, blocking collectives, exchange_both(): lax.all_to_all(x, ('head', 'leaf'), 0, 0, tiled=True, axis_index_groups=b...  13.9 us
    pallas_call x1, Pallas kernels, attend(): pl.pallas_call(functools.partial(attend_kernel, len(owns)), grid=(trees,...  12.9 us
    ppermute x2, waiting for transfers between devices, to_other_head(): return lax.ppermute(x, 'head', [(0, 1), (1, 0)])  10.5 us
    psum x1, blocking collectives, gather_parents(): return lax.psum(x, 'leaf', axis_index_groups=sides)  9.96 us
    pallas_call x7, Pallas kernels, simple(): pl.pallas_call(kernel, grid=(1,), in_specs=[SMEM] * len(scalars) + [whole...  9.73 us
    ppermute x2, waiting for transfers between devices, short(): return jnp.concatenate([lax.ppermute(x[:few], 'leaf', swap), x[few:]])  6.21 us
    all_to_all x1, waiting for transfers between devices, exchange(): return lax.all_to_all(x, 'leaf', 0, 0, tiled=True, axis_index_groups=sides)  5.76 us
  transfers between devices with their start and end apart: 7, of which 5 were waited for; matrix products, arithmetic and copies ran while one was open for 1% of the time, Pallas kernels for 2%

profile of v7, /device:TPU:0, one launch (start us, length us, event | category | flops | bytes accessed | tf_op | source)
XLA Modules:
  0.0 110.2 jit_solution(14522699131759841537)
XLA Ops:
  0.6 4.1 %collective-permute-start.4 = (s32[2]{0:T(128)}, s32[2]{0:T(128)S(1)}, u32[]{:S(2)}, u32[]{:S(2)}) collective-permute-start(s32[2]{0:T(128)} %parents.1), channel_id=1, source_target_pairs={{0,8},{1,9},{2,10},{3,11},{4,12},{5,13},{6,14},{7,15},{8,0},{9,1},... | collective-permute-start | bytes 32 | tf_op jit(solution)/shard_map/ppermute | solution.py:357
  4.7 0.7 pad_add_fusion.place
  5.4 0.0 copy-start.1
  5.4 2.0 %shard_map.76 = (bf16[16,2,16,512]{3,2,1,0:T(8,128)(2,1)}, bf16[2,2,64,512]{3,2,1,0:T(8,128)(2,1)}, bf16[2,2,64,512]{3,2,1,0:T(8,128)(2,1)}) custom-call(s32[3]{0:T(128)} %pad_add_fusion.place, bf16[2,64,1024]{2,1,0:T(8,128)(2,1)} %keys_ref.1, bf16[2,64,1024]{2,1,0:T(8,128)(2,1)} %values_ref.1), custom_call_target="tpu_custom_call" | custom-call | tf_op jit(solution)/shard_map/pallas_call | solution.py:311
  7.4 0.0 collective-permute-done.4.partner_parents
  7.4 0.0 copy-start
  7.4 0.7 copy-done
  8.1 0.0 copy-start.2
  8.1 0.7 copy-done.2
  8.8 0.6 shard_map.77
  9.3 4.8 %all-to-all-start = ((bf16[16,2,16,512]{3,2,1,0:T(8,128)(2,1)}), bf16[16,2,16,512]{3,2,1,0:T(8,128)(2,1)S(1)}, u32[]{:S(2)}, u32[]{:S(2)}) async-start(bf16[16,2,16,512]{3,2,1,0:T(8,128)(2,1)} %get-tuple-element.37), calls=%async_computation | async-start | bytes 1048576 | tf_op jit(solution)/shard_map/all_to_all | solution.py:344
  14.2 1.9 %collective-permute-start.5 = (bf16[2,2,64,512]{3,2,1,0:T(8,128)(2,1)}, bf16[2,2,64,512]{3,2,1,0:T(8,128)(2,1)S(1)}, u32[]{:S(2)}, u32[]{:S(2)}) collective-permute-start(bf16[2,2,64,512]{3,2,1,0:T(8,128)(2,1)} %get-tuple-element.39), channel_id=1, source_target_pairs={{0,16},{16,0},{1,17},{17,1},{2,18},{18,2},{3,19},{19,3},{4,20},{20... | collective-permute-start | bytes 786440 | tf_op jit(solution)/shard_map/ppermute | solution.py:350
  16.1 10.0 %psum.7.parents = s32[1,32]{1,0:T(1,128)S(1)} all-reduce(s32[1,32]{1,0:T(1,128)S(1)} %shard_map.77), channel_id=1, replica_groups={{0,1,2,3,4,5,6,7},{8,9,10,11,12,13,14,15},{16,17,18,19,20,21,22,23},{24..., use_global_device_ids=true, to_apply=%region_0.0 | all-reduce | flops 32 | bytes 256 | tf_op jit(solution)/shard_map/psum | solution.py:347
  26.1 2.5 %collective-permute-done.5.refs_1_ = bf16[2,2,64,512]{3,2,1,0:T(8,128)(2,1)S(1)} collective-permute-done((bf16[2,2,64,512]{3,2,1,0:T(8,128)(2,1)}, bf16[2,2,64,512]{3,2,1,0:T(8,128)(2,1)S(1)}, u32[]{:S(2)}, u32[]{:S(2)}) %collective-permute-start.5) | collective-permute-done | bytes 262176 | tf_op jit(solution)/shard_map/ppermute | solution.py:350
  28.6 0.0 all-to-all-done
  28.6 0.1 copy.10
  28.6 0.0 copy-done.1
  28.6 1.9 %shard_map.78 = (bf16[8,2,16,512]{3,2,1,0:T(8,128)(2,1)S(1)}, s32[16]{0:T(128)S(1)}, s32[1]{0:T(128)}) custom-call(s32[3]{0:T(128)S(1)} %copy-done.1, s32[1,32]{1,0:T(1,128)S(1)} %psum.7.parents, bf16[8,2,2,16,512]{4,3,2,1,0:T(8,128)(2,1)S(1)} %bitcast.10), custom_call_target="tpu_custom_call" | custom-call | tf_op jit(solution)/shard_map/pallas_call | solution.py:311
  31.2 5.6 %conditional.2 = (bf16[8,2,16,512]{3,2,1,0:T(8,128)(2,1)S(1)}) conditional(s32[]{:T(128)} %bitcast.6, bf16[8,2,16,512]{3,2,1,0:T(8,128)(2,1)S(1)} %get-tuple-element.46, bf16[8,2,16,512]{3,2,1,0:T(8,128)(2,1)S(1)} %get-tuple-element.46), branch_computations={%region_1.0_spmd, %region_2.0_spmd} | conditional | flops 131072 | bytes 1310768 | solution.py:397
  31.3 1.9 %collective-permute-start.2 = (bf16[2,2,16,512]{3,2,1,0:T(8,128)(2,1)S(1)}, bf16[2,2,16,512]{3,2,1,0:T(8,128)(2,1)S(1)}, u32[]{:S(2)}, u32[]{:S(2)}) collective-permute-start(bf16[2,2,16,512]{3,2,1,0:T(8,128)(2,1)S(1)} %slice.8), channel_id=1, source_target_pairs={{0,8},{1,9},{2,10},{3,11},{4,12},{5,13},{6,14},{7,15},{8,0},{9,1},... | collective-permute-start | bytes 196616 | tf_op jit(solution)/shard_map/cond/branch_1_fun/ppermute | solution.py:395
  33.2 3.6 %collective-permute-done.2 = bf16[2,2,16,512]{3,2,1,0:T(8,128)(2,1)S(1)} collective-permute-done((bf16[2,2,16,512]{3,2,1,0:T(8,128)(2,1)S(1)}, bf16[2,2,16,512]{3,2,1,0:T(8,128)(2,1)S(1)}, u32[]{:S(2)}, u32[]{:S(2)}) %collective-permute-start.2) | collective-permute-done | bytes 65568 | tf_op jit(solution)/shard_map/cond/branch_1_fun/ppermute | solution.py:395
  36.8 0.0 copy-start.3
  36.8 1.4 %shard_map.79 = bf16[8,4,2,16,512]{4,3,2,1,0:T(8,128)(2,1)S(1)} custom-call(s32[3]{0:T(128)S(1)} %copy-done.1, s32[1,32]{1,0:T(1,128)S(1)} %psum.7.parents, s32[16]{0:T(128)S(1)} %get-tuple-element.44.slots, bf16[8,2,2,16,512]{4,3,2,1,0:T(8,128)(2,1)S(1)} %bitcast.11, bf16[8,2,16,512]{3,2,1,0:T(8,128)(2,1)S(1)} %get-tuple-element.57.cross_ref), custom_call_target="tpu_custom_call" | custom-call | tf_op jit(solution)/shard_map/pallas_call | solution.py:311
  38.2 18.1 %all_to_all.20.refs_2_ = bf16[8,4,2,16,512]{4,3,2,1,0:T(8,128)(2,1)S(1)} all-to-all(bf16[8,4,2,16,512]{4,3,2,1,0:T(8,128)(2,1)S(1)} %shard_map.79), channel_id=1, replica_groups={{0,1,2,3,4,5,6,7},{8,9,10,11,12,13,14,15},{16,17,18,19,20,21,22,23},{24..., dimensions={0} | all-to-all | bytes 2097152 | tf_op jit(solution)/shard_map/all_to_all | solution.py:341
  56.3 0.0 copy-done.3
  56.4 12.9 %shard_map.80 = (bf16[2,128,4096]{2,1,0:T(8,128)(2,1)}, bf16[2,2,64,512]{3,2,1,0:T(8,128)(2,1)S(1)}, bf16[2,2,64,512]{3,2,1,0:T(8,128)(2,1)S(1)}, bf16[8,4,2,16,512]{4,3,2,1,0:T(8,128)(2,1)}) custom-call(s32[3]{0:T(128)S(1)} %copy-done.1, s32[1,32]{1,0:T(1,128)S(1)} %psum.7.parents, bf16[2,128,4096]{2,1,0:T(8,128)(2,1)} %q_ref.1, ...), custom_call_target="tpu_custom_call" | custom-call | flops 4026531840 | bytes 6291456 | tf_op jit(solution)/shard_map/pallas_call | solution.py:124
  69.2 3.6 %all-to-all-start.2 = ((bf16[8,4,2,16,512]{4,3,2,1,0:T(8,128)(2,1)}), bf16[8,4,2,16,512]{4,3,2,1,0:T(8,128)(2,1)S(1)}, u32[]{:S(2)}, u32[]{:S(2)}) async-start(bf16[8,4,2,16,512]{4,3,2,1,0:T(8,128)(2,1)} %get-tuple-element.48), calls=%async_computation.2 | async-start | bytes 2097152 | tf_op jit(solution)/shard_map/all_to_all | solution.py:341
  72.8 0.6 collective-permute-start.6
  73.4 8.1 %collective-permute-done.6.own_got_ref = bf16[2,2,64,512]{3,2,1,0:T(8,128)(2,1)S(1)} collective-permute-done((bf16[2,2,64,512]{3,2,1,0:T(8,128)(2,1)S(1)}, bf16[2,2,64,512]{3,2,1,0:T(8,128)(2,1)S(1)}, u32[]{:S(2)}, u32[]{:S(2)}) %collective-permute-start.6) | collective-permute-done | bytes 262176 | tf_op jit(solution)/shard_map/ppermute | solution.py:350
  81.4 5.8 %all-to-all-done.2.in_ref = bf16[8,4,2,16,512]{4,3,2,1,0:T(8,128)(2,1)S(1)} async-done(((bf16[8,4,2,16,512]{4,3,2,1,0:T(8,128)(2,1)}), bf16[8,4,2,16,512]{4,3,2,1,0:T(8,128)(2,1)S(1)}, u32[]{:S(2)}, u32[]{:S(2)}) %all-to-all-start.2) | async-done | bytes 1048608 | tf_op jit(solution)/shard_map/all_to_all | solution.py:341
  87.2 1.6 %shard_map.81 = (f32[8,2,2,16,512]{4,3,2,1,0:T(8,128)S(1)}, bf16[8,2,16,512]{3,2,1,0:T(8,128)(2,1)S(1)}) custom-call(s32[3]{0:T(128)S(1)} %copy-done.1, s32[1,32]{1,0:T(1,128)S(1)} %psum.7.parents, s32[16]{0:T(128)S(1)} %get-tuple-element.44.slots, bf16[8,4,2,16,512]{4,3,2,1,0:T(8,128)(2,1)S(1)} %all-to-all-done.2.in_ref), custom_call_target="tpu_custom_call" | custom-call | tf_op jit(solution)/shard_map/pallas_call | solution.py:311
  88.8 5.4 %conditional.3 = (bf16[8,2,16,512]{3,2,1,0:T(8,128)(2,1)S(1)}) conditional(s32[]{:T(128)} %bitcast.6, bf16[8,2,16,512]{3,2,1,0:T(8,128)(2,1)S(1)} %get-tuple-element.52, bf16[8,2,16,512]{3,2,1,0:T(8,128)(2,1)S(1)} %get-tuple-element.52), branch_computations={%region_3.0_spmd, %region_4.0_spmd} | conditional | flops 131072 | bytes 1310768 | solution.py:397
  88.8 2.6 %collective-permute-start.3 = (bf16[2,2,16,512]{3,2,1,0:T(8,128)(2,1)S(1)}, bf16[2,2,16,512]{3,2,1,0:T(8,128)(2,1)S(1)}, u32[]{:S(2)}, u32[]{:S(2)}) collective-permute-start(bf16[2,2,16,512]{3,2,1,0:T(8,128)(2,1)S(1)} %slice.10), channel_id=1, source_target_pairs={{0,8},{1,9},{2,10},{3,11},{4,12},{5,13},{6,14},{7,15},{8,0},{9,1},... | collective-permute-start | bytes 196616 | tf_op jit(solution)/shard_map/cond/branch_1_fun/ppermute | solution.py:395
  91.5 2.6 %collective-permute-done.3 = bf16[2,2,16,512]{3,2,1,0:T(8,128)(2,1)S(1)} collective-permute-done((bf16[2,2,16,512]{3,2,1,0:T(8,128)(2,1)S(1)}, bf16[2,2,16,512]{3,2,1,0:T(8,128)(2,1)S(1)}, u32[]{:S(2)}, u32[]{:S(2)}) %collective-permute-start.3) | collective-permute-done | bytes 65568 | tf_op jit(solution)/shard_map/cond/branch_1_fun/ppermute | solution.py:395
  94.2 0.7 shard_map.82
  94.9 13.9 %all_to_all.21.got_ref = bf16[16,2,16,512]{3,2,1,0:T(8,128)(2,1)S(1)} all-to-all(bf16[16,2,16,512]{3,2,1,0:T(8,128)(2,1)S(1)} %shard_map.82), channel_id=1, replica_groups={{0,1,2,3,4,5,6,7,16,17,18,19,20,21,22,23},{8,9,10,11,12,13,14,15,24,25,..., dimensions={0} | all-to-all | bytes 1048576 | tf_op jit(solution)/shard_map/all_to_all | solution.py:344
  108.8 1.4 %shard_map.83 = (bf16[2,64,1024]{2,1,0:T(8,128)(2,1)}, bf16[2,64,1024]{2,1,0:T(8,128)(2,1)}) custom-call(s32[3]{0:T(128)S(1)} %copy-done.1, bf16[16,2,16,512]{3,2,1,0:T(8,128)(2,1)S(1)} %all_to_all.21.got_ref, bf16[2,2,64,512]{3,2,1,0:T(8,128)(2,1)S(1)} %get-tuple-element.53.own_ref, bf16[2,2,64,512]{3,2,1,0:T(8,128)(2,1)S(1)} %collective-permute-done.6.own_got_ref), custom_call_target="tpu_custom_call" | custom-call | tf_op jit(solution)/shard_map/pallas_call | solution.py:311
  (6 shorter events, 0.1 us)
Async XLA Ops:
  0.6 6.8 %collective-permute-start.4 = (s32[2]{0:T(128)}, s32[2]{0:T(128)S(1)}, u32[]{:S(2)}, u32[]{:S(2)}) collective-permute-start(s32[2]{0:T(128)} %parents.1), channel_id=1, source_target_pairs={{0,8},{1,9},{2,10},{3,11},{4,12},{5,13},{6,14},{7,15},{8,0},{9,1},... | collective-permute-start | bytes 32 | tf_op jit(solution)/shard_map/ppermute | solution.py:357
  5.4 23.2 %copy-start.1 = (s32[3]{0:T(128)S(1)}, s32[3]{0:T(128)}, u32[]{:S(2)}) copy-start(s32[3]{0:T(128)} %pad_add_fusion.place) | copy-start | bytes 40
  7.4 0.7 copy-start
  8.1 0.7 copy-start.2
  9.3 19.2 %all-to-all-start = ((bf16[16,2,16,512]{3,2,1,0:T(8,128)(2,1)}), bf16[16,2,16,512]{3,2,1,0:T(8,128)(2,1)S(1)}, u32[]{:S(2)}, u32[]{:S(2)}) async-start(bf16[16,2,16,512]{3,2,1,0:T(8,128)(2,1)} %get-tuple-element.37), calls=%async_computation | async-start | bytes 1048576 | tf_op jit(solution)/shard_map/all_to_all | solution.py:344
  14.2 14.4 %collective-permute-start.5 = (bf16[2,2,64,512]{3,2,1,0:T(8,128)(2,1)}, bf16[2,2,64,512]{3,2,1,0:T(8,128)(2,1)S(1)}, u32[]{:S(2)}, u32[]{:S(2)}) collective-permute-start(bf16[2,2,64,512]{3,2,1,0:T(8,128)(2,1)} %get-tuple-element.39), channel_id=1, source_target_pairs={{0,16},{16,0},{1,17},{17,1},{2,18},{18,2},{3,19},{19,3},{4,20},{20... | collective-permute-start | bytes 786440 | tf_op jit(solution)/shard_map/ppermute | solution.py:350
  31.3 5.5 %collective-permute-start.2 = (bf16[2,2,16,512]{3,2,1,0:T(8,128)(2,1)S(1)}, bf16[2,2,16,512]{3,2,1,0:T(8,128)(2,1)S(1)}, u32[]{:S(2)}, u32[]{:S(2)}) collective-permute-start(bf16[2,2,16,512]{3,2,1,0:T(8,128)(2,1)S(1)} %slice.8), channel_id=1, source_target_pairs={{0,8},{1,9},{2,10},{3,11},{4,12},{5,13},{6,14},{7,15},{8,0},{9,1},... | collective-permute-start | bytes 196616 | tf_op jit(solution)/shard_map/cond/branch_1_fun/ppermute | solution.py:395
  36.8 19.5 %copy-start.3 = (bf16[2,2,64,512]{3,2,1,0:T(8,128)(2,1)S(1)}, bf16[2,2,64,512]{3,2,1,0:T(8,128)(2,1)}, u32[]{:S(2)}) copy-start(bf16[2,2,64,512]{3,2,1,0:T(8,128)(2,1)} %get-tuple-element.41.refs_0_) | copy-start | bytes 786436
  69.2 17.9 %all-to-all-start.2 = ((bf16[8,4,2,16,512]{4,3,2,1,0:T(8,128)(2,1)}), bf16[8,4,2,16,512]{4,3,2,1,0:T(8,128)(2,1)S(1)}, u32[]{:S(2)}, u32[]{:S(2)}) async-start(bf16[8,4,2,16,512]{4,3,2,1,0:T(8,128)(2,1)} %get-tuple-element.48), calls=%async_computation.2 | async-start | bytes 2097152 | tf_op jit(solution)/shard_map/all_to_all | solution.py:341
  72.8 8.6 %collective-permute-start.6 = (bf16[2,2,64,512]{3,2,1,0:T(8,128)(2,1)S(1)}, bf16[2,2,64,512]{3,2,1,0:T(8,128)(2,1)S(1)}, u32[]{:S(2)}, u32[]{:S(2)}) collective-permute-start(bf16[2,2,64,512]{3,2,1,0:T(8,128)(2,1)S(1)} %get-tuple-element.49), channel_id=1, source_target_pairs={{0,16},{16,0},{1,17},{17,1},{2,18},{18,2},{3,19},{19,3},{4,20},{20... | collective-permute-start | bytes 786440 | tf_op jit(solution)/shard_map/ppermute | solution.py:350
  88.8 5.3 %collective-permute-start.3 = (bf16[2,2,16,512]{3,2,1,0:T(8,128)(2,1)S(1)}, bf16[2,2,16,512]{3,2,1,0:T(8,128)(2,1)S(1)}, u32[]{:S(2)}, u32[]{:S(2)}) collective-permute-start(bf16[2,2,16,512]{3,2,1,0:T(8,128)(2,1)S(1)} %slice.10), channel_id=1, source_target_pairs={{0,8},{1,9},{2,10},{3,11},{4,12},{5,13},{6,14},{7,15},{8,0},{9,1},... | collective-permute-start | bytes 196616 | tf_op jit(solution)/shard_map/cond/branch_1_fun/ppermute | solution.py:395

commit v8 on v7

--- a/solution.py
+++ b/solution.py
@@ -23,7 +23,7 @@
     return lax.dot_general(a, b, dims, preferred_element_type=F32)
 
 
-def attend_kernel(parts, place, parents, q_ref, do_ref, *refs):
+def attend_kernel(parts, parents, q_ref, do_ref, *refs):
     own_refs, anc_ref, dq_ref = refs[:parts], refs[parts], refs[parts + 1]
     dself_refs, danc_ref = refs[parts + 2 : 2 * parts + 2], refs[2 * parts + 2]
     hubs, depth, _, pieces, _ = anc_ref.shape
@@ -32,7 +32,7 @@
     heads = q_ref.shape[2] // HEAD_DIM // step_groups
     scale = HEAD_DIM ** (-0.5)
     c = scale * math.log2(math.e)
-    block = 2 * place[0] + pl.program_id(0)
+    block = 2 * leaf_rank() + pl.program_id(0)
     valid = []
     for _ in range(depth):
         block = above(parents, block)
@@ -47,7 +47,8 @@
 
     held = [(seen(0, group), seen(1, group)) for group in range(step_groups)]
     held = [(keys, values, keys.T) for keys, values in held]
-    token = lax.rem(lax.broadcasted_iota(jnp.int32, (rows, rows), 0) + place[2], rows)
+    first_token = lax.axis_index("head") * own_refs[0].shape[2] if parts == 2 else 0
+    token = lax.rem(lax.broadcasted_iota(jnp.int32, (rows, rows), 0) + first_token, rows)
     hidden = token > lax.broadcasted_iota(jnp.int32, (rows, rows), 1)
 
     def products(group, h):
@@ -110,7 +111,7 @@
         stage, ready = following, soft
 
 
-def attend(place, parents, queries, output_gradient, owns, foreign):
+def attend(parents, queries, output_gradient, owns, foreign):
     trees, rows, width = queries.shape
     hubs, slots, _, pieces, kv_width = foreign.shape
     depth = slots // trees
@@ -124,7 +125,7 @@
     return pl.pallas_call(
         functools.partial(attend_kernel, len(owns)),
         grid=(trees, groups // step),
-        in_specs=[SMEM, SMEM, q_spec, q_spec, *own_specs, anc_spec],
+        in_specs=[SMEM, q_spec, q_spec, *own_specs, anc_spec],
         out_specs=[q_spec, *own_specs, anc_spec],
         out_shape=[jax.ShapeDtypeStruct(x.shape, BF16) for x in (queries, *owns, foreign)],
         compiler_params=pltpu.CompilerParams(vmem_limit_bytes=50 * 1024 * 1024),
@@ -133,10 +134,10 @@
             bytes_accessed=12 * rows * width,
             transcendentals=trees * groups * heads * (depth + 1) * rows * rows,
         ),
-    )(place, parents, queries, output_gradient, *owns, foreign)
-
-
-def pack_kernel(place, keys_ref, values_ref, send_ref, keep_ref, give_ref):
+    )(parents, queries, output_gradient, *owns, foreign)
+
+
+def pack_kernel(parents, keys_ref, values_ref, send_ref, keep_ref, give_ref, table_ref):
     heads, width = send_ref.shape[0] // (keys_ref.shape[1] // 8), keep_ref.shape[3]
     leaves = send_ref.shape[0] // heads
     for kv, ref in enumerate((keys_ref, values_ref)):
@@ -145,27 +146,25 @@
                 tiles = [ref[t, 8 * j : 8 * j + 16, h * width : (h + 1) * width] for t in range(2)]
                 send_ref[h * leaves + j, kv] = jnp.concatenate([x[:8] for x in tiles], 0)
                 send_ref[h * leaves + j + 1, kv] = jnp.concatenate([x[8:] for x in tiles], 0)
-        keep_ref[kv] = ref[:, :, pl.ds(pl.multiple_of(place[1] * width, width), width)]
-        give_ref[kv] = ref[:, :, pl.ds(pl.multiple_of((1 - place[1]) * width, width), width)]
-
-
-def table_kernel(place, parents, partner_parents, table_ref):
-    blocks = table_ref.shape[1]
+        keep_ref[kv] = ref[:, :, pl.ds(pl.multiple_of(lax.axis_index("head") * width, width), width)]
+        give_ref[kv] = ref[:, :, pl.ds(pl.multiple_of((1 - lax.axis_index("head")) * width, width), width)]
     block = lax.broadcasted_iota(jnp.int32, table_ref.shape, 1)
     table = jnp.zeros(table_ref.shape, jnp.int32)
     for t in range(2):
-        own = 2 * place[0] + t
-        table = jnp.where(block == own, parents[t], table)
-        table = jnp.where(block == lax.rem(own + blocks // 2, blocks), partner_parents[t], table)
+        table = jnp.where(block == 2 * leaf_rank() + t, parents[t], table)
     table_ref[...] = table
+
+
+def leaf_rank():
+    return lax.axis_index("leaf")
 
 
 def above(parents, block):
     return jnp.where(block >= 0, parents[0, jnp.maximum(block, 0)], -1)
 
 
-def far_slots(place, parents, half, depth, sending, slots, start):
-    base = (place[0] // half) * half
+def far_slots(parents, half, depth, sending, slots, start):
+    base = (leaf_rank() // half) * half
     source = base if sending else half - base
     target = half - source
     t = jnp.where(source == 0, 0, 1)
@@ -196,8 +195,8 @@
     return lax.fori_loop(0, half, number, 0)
 
 
-def each_need(place, parents, half, depth, act):
-    base = (place[0] // half) * half
+def each_need(parents, half, depth, act):
+    base = (leaf_rank() // half) * half
 
     def leaf(d, _):
         for t in range(2):
@@ -211,12 +210,12 @@
     lax.fori_loop(0, half, leaf, 0)
 
 
-def cross_kernel(depth, place, parents, own_ref, cross_ref, slots, count):
+def cross_kernel(depth, parents, own_ref, cross_ref, slots, count):
     half = own_ref.shape[0]
-    other = far_slots(place, parents, half, depth, False, slots, 0)
-    mine = far_slots(place, parents, half, depth, True, slots, half)
+    other = far_slots(parents, half, depth, False, slots, 0)
+    mine = far_slots(parents, half, depth, True, slots, half)
     count[0] = jnp.maximum(mine, other)
-    t = place[0] // half
+    t = leaf_rank() // half
 
     def copy(p, _):
         slot = slots[half + p]
@@ -230,7 +229,7 @@
     lax.fori_loop(0, half, copy, 0)
 
 
-def pick_kernel(depth, place, parents, slots, own_ref, cross_ref, out_ref):
+def pick_kernel(depth, parents, slots, own_ref, cross_ref, out_ref):
     half = own_ref.shape[0]
 
     def act(d, slot, valid, here, p, t):
@@ -242,10 +241,10 @@
         def _():
             out_ref[d, slot] = cross_ref[slots[p]]
 
-    each_need(place, parents, half, depth, act)
-
-
-def collect_kernel(depth, place, parents, slots, in_ref, own_ref, cross_ref, sums):
+    each_need(parents, half, depth, act)
+
+
+def collect_kernel(depth, parents, slots, in_ref, own_ref, cross_ref, sums):
     half = own_ref.shape[0]
     own_ref[...] = jnp.zeros_like(own_ref)
     sums[...] = jnp.zeros_like(sums)
@@ -259,13 +258,13 @@
         def _():
             sums[slots[p]] += in_ref[d, slot].astype(F32)
 
-    each_need(place, parents, half, depth, act)
+    each_need(parents, half, depth, act)
     cross_ref[...] = sums[...].astype(BF16)
 
 
-def merge_kernel(spread, place, slots, own_ref, cross_ref, out_ref):
+def merge_kernel(spread, slots, own_ref, cross_ref, out_ref):
     half = own_ref.shape[0]
-    t = place[0] // half
+    t = leaf_rank() // half
 
     def add(p, _):
         slot = slots[half + p]
@@ -284,12 +283,12 @@
     lax.fori_loop(0, half, add, 0)
 
 
-def finish_kernel(place, got_ref, own_ref, own_got_ref, keys_ref, values_ref):
+def finish_kernel(got_ref, own_ref, own_got_ref, keys_ref, values_ref):
     width = own_ref.shape[3]
     leaves = own_ref.shape[2] // 8
     for kv, out_ref in enumerate((keys_ref, values_ref)):
         for own in range(2):
-            h = place[1] if own else 1 - place[1]
+            h = lax.axis_index("head") if own else 1 - lax.axis_index("head")
             ref = own_ref if own else own_got_ref
             lanes = pl.ds(pl.multiple_of(h * width, width), width)
             for j in range(0, leaves, 2):
@@ -324,10 +323,6 @@
     head_count = lax.axis_size("head")
     half = leaf_count // 2
     depth = leaf_count // 4 - 2
-    leaf_rank = lax.axis_index("leaf")
-    head_rank = lax.axis_index("head")
-    token = head_rank * keys.shape[1] if head_count == 2 else 0
-    place = jnp.stack([leaf_rank, head_rank, token]).astype(jnp.int32)
     sides = [[half * i + j for j in range(half)] for i in range(2)]
     both = [[leaf_count * h + j for h in range(head_count) for j in side] for side in sides]
     swap = [(i, (i + half) % leaf_count) for i in range(leaf_count)]
@@ -343,42 +338,33 @@
     def exchange_both(x):
         return lax.all_to_all(x, ("head", "leaf"), 0, 0, tiled=True, axis_index_groups=both)
 
-    def gather_parents(x):
-        return lax.psum(x, "leaf", axis_index_groups=sides)
-
     def to_other_head(x):
         return lax.ppermute(x, "head", [(0, 1), (1, 0)])
 
     def like(*shape, dtype=BF16):
         return jax.ShapeDtypeStruct(shape, dtype)
 
-    (table,) = simple(
-        table_kernel,
-        (place, parents, lax.ppermute(parents, "leaf", swap)),
-        (),
-        [like(1, trees * leaf_count, dtype=jnp.int32)],
-    )
     if merged:
-        send, keep, give = simple(
+        send, keep, give, table = simple(
             pack_kernel,
-            (place,),
+            (parents,),
             (keys, values),
             [
                 like(2 * half, 2, 16, kv_width),
                 like(2, trees, part_rows, kv_width),
                 like(2, trees, part_rows, kv_width),
+                like(1, trees * leaf_count, dtype=jnp.int32),
             ],
             params=WIDE,
         )
-        send, give, table = lax.optimization_barrier((send, give, table))
         arrived, all_parents, theirs = lax.optimization_barrier(
-            (exchange_both(send), gather_parents(table), to_other_head(give))
+            (exchange_both(send), lax.psum(table, "leaf"), to_other_head(give))
         )
         owns = [keep, theirs]
         arrived = arrived.reshape(2, half, 2, trees, 8, kv_width).transpose(1, 2, 3, 0, 4, 5)
         hub_own = arrived.reshape(half, 2, trees, pieces, kv_width)
     else:
-        all_parents = gather_parents(table)
+        all_parents = lax.all_gather(parents, "leaf", axis=0, tiled=True).reshape(1, trees * leaf_count)
         pair = jnp.stack([keys, values]).reshape(2, trees, part_rows, head_count, kv_width)
         pair = jnp.moveaxis(pair, 3, 0)
         if head_count > 1:
@@ -398,14 +384,14 @@
 
     crossing, slots, count = simple(
         functools.partial(cross_kernel, depth),
-        (place, all_parents),
+        (all_parents,),
         (hub_own,),
         [like(half, *piece)],
         slots=(2 * half, 1),
     )
     (picked,) = simple(
         functools.partial(pick_kernel, depth),
-        (place, all_parents, slots),
+        (all_parents, slots),
         (hub_own, cross(crossing)),
         [like(half, trees * depth, *piece)],
     )
@@ -413,7 +399,7 @@
     if pieces % 16:
         foreign = foreign.transpose(1, 2, 0, 3, 4).reshape(1, trees * depth, 2, rows, kv_width)
 
-    query_grad, *self_grads, foreign_grad = attend(place, all_parents, queries, output_gradient, owns, foreign)
+    query_grad, *self_grads, foreign_grad = attend(all_parents, queries, output_gradient, owns, foreign)
     if pieces % 16:
         foreign_grad = foreign_grad.reshape(trees * depth, 2, half, pieces, kv_width).transpose(2, 0, 1, 3, 4)
     back = exchange(foreign_grad)
@@ -422,21 +408,21 @@
 
     own_sum, cross_sum = simple(
         functools.partial(collect_kernel, depth),
-        (place, all_parents, slots),
+        (all_parents, slots),
         (back,),
         [like(half, 2, trees, pieces, kv_width, dtype=F32), like(half, *piece)],
         [pltpu.VMEM((half,) + piece, F32)],
     )
     (hub_sum,) = simple(
         functools.partial(merge_kernel, merged),
-        (place, slots),
+        (slots,),
         (own_sum, cross(cross_sum)),
         [like(2 * half, 2, 16, kv_width) if merged else like(half, 2, trees, pieces, kv_width)],
     )
     if merged:
         returned = exchange_both(hub_sum)
         return query_grad, *simple(
-            finish_kernel, (place,), (returned, self_grads[0], own_got), [like(*keys.shape)] * 2
+            finish_kernel, (), (returned, self_grads[0], own_got), [like(*keys.shape)] * 2
         )
     returned = exchange(hub_sum).transpose(1, 2, 0, 3, 4).reshape(2, trees, rows, kv_width)
     total = (returned.astype(F32) + self_grads[0].astype(F32)).astype(BF16)

time: 111 us -> 106 us (0.955)
  blocking collectives: 41.9 us -> 44.9 us
  starting transfers between devices: 19.6 us -> 17.3 us
  waiting for transfers between devices: 22.5 us -> 20.4 us
  local copies, waits for them, and re-layouts: 1.43 us -> 0.1 us
    psum x1, blocking collectives: 9.96 us -> 14.1 us  [body(): lax.psum(table, 'leaf')]
    ppermute x1 -> x0, starting transfers between devices: 4.1 us -> none  [body(): lax.ppermute(parents, 'leaf', swap)]
    ppermute x2, waiting for transfers between devices: 10.5 us -> 7.09 us  [to_other_head(): return lax.ppermute(x, 'head', [(0, 1), (1, 0)])]
    all_to_all x1, starting transfers between devices: 4.85 us -> 6.29 us  [exchange_both(): lax.all_to_all(x, ('head', 'leaf'), 0, 0, tiled=True, axis_index_groups=b...]
    ppermute x2, waiting for transfers between devices: 6.21 us -> 7.55 us  [short(): return jnp.concatenate([lax.ppermute(x[:few], 'leaf', swap), x[few:]])]
    unnamed x8 -> x2, local copies, waits for them, and re-layouts: 1.34 us -> 0.01 us
    pallas_call x7 -> x6, Pallas kernels: 9.73 us -> 8.65 us  [simple(): pl.pallas_call(kernel, grid=(1,), in_specs=[SMEM] * len(scalars) + [whole...]
  transfers between devices with their start and end apart: 7 -> 6, of which waited for: 5 -> 4; matrix products, arithmetic and copies ran while one was open for 1% -> 0% of each run, Pallas kernels for 2% -> 0%
where the time goes in v8:
time: 106 us
  blocking collectives  44.9 us (42%)
  Pallas kernels  21.5 us (20%)
  waiting for transfers between devices  20.4 us (19%)
  starting transfers between devices  17.3 us (16%)
  between operations  1.36 us (1%)
    all_to_all x1, blocking collectives, exchange(): return lax.all_to_all(x, 'leaf', 0, 0, tiled=True, axis_index_groups=sides)  17 us
    psum x1, blocking collectives, body(): lax.psum(table, 'leaf')  14.1 us
    all_to_all x1, blocking collectives, exchange_both(): lax.all_to_all(x, ('head', 'leaf'), 0, 0, tiled=True, axis_index_groups=b...  13.8 us
    pallas_call x1, Pallas kernels, attend(): pl.pallas_call(functools.partial(attend_kernel, len(owns)), grid=(trees,...  12.9 us
    pallas_call x6, Pallas kernels, simple(): pl.pallas_call(kernel, grid=(1,), in_specs=[SMEM] * len(scalars) + [whole...  8.65 us
    ppermute x2, waiting for transfers between devices, short(): return jnp.concatenate([lax.ppermute(x[:few], 'leaf', swap), x[few:]])  7.55 us
    ppermute x2, waiting for transfers between devices, to_other_head(): return lax.ppermute(x, 'head', [(0, 1), (1, 0)])  7.09 us
    all_to_all x1, starting transfers between devices, exchange_both(): lax.all_to_all(x, ('head', 'leaf'), 0, 0, tiled=True, axis_index_groups=b...  6.29 us
  transfers between devices with their start and end apart: 6, of which 4 were waited for; matrix products, arithmetic and copies ran while one was open for 0% of the time, Pallas kernels for 0%

profile of v8, /device:TPU:0, one launch (start us, length us, event | category | flops | bytes accessed | tf_op | source)
XLA Modules:
  0.0 105.7 jit_solution(9359846081841265080)
XLA Ops:
  0.6 2.1 %shard_map.76 = (bf16[16,2,16,512]{3,2,1,0:T(8,128)(2,1)}, bf16[2,2,64,512]{3,2,1,0:T(8,128)(2,1)}, bf16[2,2,64,512]{3,2,1,0:T(8,128)(2,1)}, s32[1,32]{1,0:T(1,128)}) custom-call(s32[2]{0:T(128)} %parents.1, bf16[2,64,1024]{2,1,0:T(8,128)(2,1)} %keys_ref.1, bf16[2,64,1024]{2,1,0:T(8,128)(2,1)} %values_ref.1), custom_call_target="tpu_custom_call" | custom-call | tf_op jit(solution)/shard_map/pallas_call | solution.py:310
  2.7 6.3 %all-to-all-start = ((bf16[16,2,16,512]{3,2,1,0:T(8,128)(2,1)}), bf16[16,2,16,512]{3,2,1,0:T(8,128)(2,1)S(1)}, u32[]{:S(2)}, u32[]{:S(2)}) async-start(bf16[16,2,16,512]{3,2,1,0:T(8,128)(2,1)} %get-tuple-element.33), calls=%async_computation | async-start | bytes 1048576 | tf_op jit(solution)/shard_map/all_to_all | solution.py:339
  9.0 1.9 %collective-permute-start.4 = (bf16[2,2,64,512]{3,2,1,0:T(8,128)(2,1)}, bf16[2,2,64,512]{3,2,1,0:T(8,128)(2,1)S(1)}, u32[]{:S(2)}, u32[]{:S(2)}) collective-permute-start(bf16[2,2,64,512]{3,2,1,0:T(8,128)(2,1)} %get-tuple-element.35), channel_id=1, source_target_pairs={{0,16},{16,0},{1,17},{17,1},{2,18},{18,2},{3,19},{19,3},{4,20},{20... | collective-permute-start | bytes 786440 | tf_op jit(solution)/shard_map/ppermute | solution.py:342
  10.9 14.1 %psum.7.parents = s32[1,32]{1,0:T(1,128)S(1)} all-reduce(s32[1,32]{1,0:T(1,128)} %get-tuple-element.34), channel_id=1, replica_groups=mesh['head'=2,'leaf'=16] {'leaf'}, use_global_device_ids=true, to_apply=%region_0.0 | all-reduce | flops 32 | bytes 256 | tf_op jit(solution)/shard_map/psum | solution.py:361
  25.1 0.0 collective-permute-done.4.refs_1_
  25.1 0.0 all-to-all-done
  25.1 0.1 copy.10
  25.1 1.9 %shard_map.77 = (bf16[8,2,16,512]{3,2,1,0:T(8,128)(2,1)S(1)}, s32[16]{0:T(128)S(1)}, s32[1]{0:T(128)}) custom-call(s32[1,32]{1,0:T(1,128)S(1)} %psum.7.parents, bf16[8,2,2,16,512]{4,3,2,1,0:T(8,128)(2,1)S(1)} %bitcast.7), custom_call_target="tpu_custom_call" | custom-call | tf_op jit(solution)/shard_map/pallas_call | solution.py:310
  27.7 5.3 %conditional.2 = (bf16[8,2,16,512]{3,2,1,0:T(8,128)(2,1)S(1)}) conditional(s32[]{:T(128)} %bitcast.3, bf16[8,2,16,512]{3,2,1,0:T(8,128)(2,1)S(1)} %get-tuple-element.42, bf16[8,2,16,512]{3,2,1,0:T(8,128)(2,1)S(1)} %get-tuple-element.42), branch_computations={%region_1.0_spmd, %region_2.0_spmd} | conditional | flops 131072 | bytes 1310768 | solution.py:383
  27.7 0.9 collective-permute-start.2
  28.7 4.3 %collective-permute-done.2 = bf16[2,2,16,512]{3,2,1,0:T(8,128)(2,1)S(1)} collective-permute-done((bf16[2,2,16,512]{3,2,1,0:T(8,128)(2,1)S(1)}, bf16[2,2,16,512]{3,2,1,0:T(8,128)(2,1)S(1)}, u32[]{:S(2)}, u32[]{:S(2)}) %collective-permute-start.2) | collective-permute-done | bytes 65568 | tf_op jit(solution)/shard_map/cond/branch_1_fun/ppermute | solution.py:381
  33.0 0.0 copy-start
  33.0 1.4 %shard_map.78 = bf16[8,4,2,16,512]{4,3,2,1,0:T(8,128)(2,1)S(1)} custom-call(s32[1,32]{1,0:T(1,128)S(1)} %psum.7.parents, s32[16]{0:T(128)S(1)} %get-tuple-element.40.slots, bf16[8,2,2,16,512]{4,3,2,1,0:T(8,128)(2,1)S(1)} %bitcast.8, bf16[8,2,16,512]{3,2,1,0:T(8,128)(2,1)S(1)} %get-tuple-element.53.cross_ref), custom_call_target="tpu_custom_call" | custom-call | tf_op jit(solution)/shard_map/pallas_call | solution.py:310
  34.4 17.0 %all_to_all.20.refs_2_ = bf16[8,4,2,16,512]{4,3,2,1,0:T(8,128)(2,1)S(1)} all-to-all(bf16[8,4,2,16,512]{4,3,2,1,0:T(8,128)(2,1)S(1)} %shard_map.78), channel_id=1, replica_groups={{0,1,2,3,4,5,6,7},{8,9,10,11,12,13,14,15},{16,17,18,19,20,21,22,23},{24..., dimensions={0} | all-to-all | bytes 2097152 | tf_op jit(solution)/shard_map/all_to_all | solution.py:336
  51.4 0.0 copy-done
  51.5 12.9 %shard_map.79 = (bf16[2,128,4096]{2,1,0:T(8,128)(2,1)}, bf16[2,2,64,512]{3,2,1,0:T(8,128)(2,1)S(1)}, bf16[2,2,64,512]{3,2,1,0:T(8,128)(2,1)S(1)}, bf16[8,4,2,16,512]{4,3,2,1,0:T(8,128)(2,1)}) custom-call(s32[1,32]{1,0:T(1,128)S(1)} %psum.7.parents, bf16[2,128,4096]{2,1,0:T(8,128)(2,1)} %q_ref.1, bf16[2,128,4096]{2,1,0:T(8,128)(2,1)} %do_ref.1, ...), custom_call_target="tpu_custom_call" | custom-call | flops 4026531840 | bytes 6291456 | tf_op jit(solution)/shard_map/pallas_call | solution.py:125
  64.4 3.6 %all-to-all-start.2 = ((bf16[8,4,2,16,512]{4,3,2,1,0:T(8,128)(2,1)}), bf16[8,4,2,16,512]{4,3,2,1,0:T(8,128)(2,1)S(1)}, u32[]{:S(2)}, u32[]{:S(2)}) async-start(bf16[8,4,2,16,512]{4,3,2,1,0:T(8,128)(2,1)} %get-tuple-element.44), calls=%async_computation.2 | async-start | bytes 2097152 | tf_op jit(solution)/shard_map/all_to_all | solution.py:336
  67.9 1.5 %collective-permute-start.5 = (bf16[2,2,64,512]{3,2,1,0:T(8,128)(2,1)S(1)}, bf16[2,2,64,512]{3,2,1,0:T(8,128)(2,1)S(1)}, u32[]{:S(2)}, u32[]{:S(2)}) collective-permute-start(bf16[2,2,64,512]{3,2,1,0:T(8,128)(2,1)S(1)} %get-tuple-element.45), channel_id=1, source_target_pairs={{0,16},{16,0},{1,17},{17,1},{2,18},{18,2},{3,19},{19,3},{4,20},{20... | collective-permute-start | bytes 786440 | tf_op jit(solution)/shard_map/ppermute | solution.py:342
  69.4 7.1 %collective-permute-done.5.own_got_ref = bf16[2,2,64,512]{3,2,1,0:T(8,128)(2,1)S(1)} collective-permute-done((bf16[2,2,64,512]{3,2,1,0:T(8,128)(2,1)S(1)}, bf16[2,2,64,512]{3,2,1,0:T(8,128)(2,1)S(1)}, u32[]{:S(2)}, u32[]{:S(2)}) %collective-permute-start.5) | collective-permute-done | bytes 262176 | tf_op jit(solution)/shard_map/ppermute | solution.py:342
  76.5 5.8 %all-to-all-done.2.in_ref = bf16[8,4,2,16,512]{4,3,2,1,0:T(8,128)(2,1)S(1)} async-done(((bf16[8,4,2,16,512]{4,3,2,1,0:T(8,128)(2,1)}), bf16[8,4,2,16,512]{4,3,2,1,0:T(8,128)(2,1)S(1)}, u32[]{:S(2)}, u32[]{:S(2)}) %all-to-all-start.2) | async-done | bytes 1048608 | tf_op jit(solution)/shard_map/all_to_all | solution.py:336
  82.3 1.6 %shard_map.80 = (f32[8,2,2,16,512]{4,3,2,1,0:T(8,128)S(1)}, bf16[8,2,16,512]{3,2,1,0:T(8,128)(2,1)S(1)}) custom-call(s32[1,32]{1,0:T(1,128)S(1)} %psum.7.parents, s32[16]{0:T(128)S(1)} %get-tuple-element.40.slots, bf16[8,4,2,16,512]{4,3,2,1,0:T(8,128)(2,1)S(1)} %all-to-all-done.2.in_ref), custom_call_target="tpu_custom_call" | custom-call | tf_op jit(solution)/shard_map/pallas_call | solution.py:310
  83.9 6.4 %conditional.3 = (bf16[8,2,16,512]{3,2,1,0:T(8,128)(2,1)S(1)}) conditional(s32[]{:T(128)} %bitcast.3, bf16[8,2,16,512]{3,2,1,0:T(8,128)(2,1)S(1)} %get-tuple-element.48, bf16[8,2,16,512]{3,2,1,0:T(8,128)(2,1)S(1)} %get-tuple-element.48), branch_computations={%region_3.0_spmd, %region_4.0_spmd} | conditional | flops 131072 | bytes 1310768 | solution.py:383
  83.9 3.0 %collective-permute-start.3 = (bf16[2,2,16,512]{3,2,1,0:T(8,128)(2,1)S(1)}, bf16[2,2,16,512]{3,2,1,0:T(8,128)(2,1)S(1)}, u32[]{:S(2)}, u32[]{:S(2)}) collective-permute-start(bf16[2,2,16,512]{3,2,1,0:T(8,128)(2,1)S(1)} %slice.10), channel_id=1, source_target_pairs={{0,8},{1,9},{2,10},{3,11},{4,12},{5,13},{6,14},{7,15},{8,0},{9,1},... | collective-permute-start | bytes 196616 | tf_op jit(solution)/shard_map/cond/branch_1_fun/ppermute | solution.py:381
  87.0 3.3 %collective-permute-done.3 = bf16[2,2,16,512]{3,2,1,0:T(8,128)(2,1)S(1)} collective-permute-done((bf16[2,2,16,512]{3,2,1,0:T(8,128)(2,1)S(1)}, bf16[2,2,16,512]{3,2,1,0:T(8,128)(2,1)S(1)}, u32[]{:S(2)}, u32[]{:S(2)}) %collective-permute-start.3) | collective-permute-done | bytes 65568 | tf_op jit(solution)/shard_map/cond/branch_1_fun/ppermute | solution.py:381
  90.3 0.7 shard_map.81
  91.0 13.8 %all_to_all.21.got_ref = bf16[16,2,16,512]{3,2,1,0:T(8,128)(2,1)S(1)} all-to-all(bf16[16,2,16,512]{3,2,1,0:T(8,128)(2,1)S(1)} %shard_map.81), channel_id=1, replica_groups={{0,1,2,3,4,5,6,7,16,17,18,19,20,21,22,23},{8,9,10,11,12,13,14,15,24,25,..., dimensions={0} | all-to-all | bytes 1048576 | tf_op jit(solution)/shard_map/all_to_all | solution.py:339
  104.8 0.9 shard_map.82
  (6 shorter events, 0.1 us)
Async XLA Ops:
  2.7 22.4 %all-to-all-start = ((bf16[16,2,16,512]{3,2,1,0:T(8,128)(2,1)}), bf16[16,2,16,512]{3,2,1,0:T(8,128)(2,1)S(1)}, u32[]{:S(2)}, u32[]{:S(2)}) async-start(bf16[16,2,16,512]{3,2,1,0:T(8,128)(2,1)} %get-tuple-element.33), calls=%async_computation | async-start | bytes 1048576 | tf_op jit(solution)/shard_map/all_to_all | solution.py:339
  9.0 16.1 %collective-permute-start.4 = (bf16[2,2,64,512]{3,2,1,0:T(8,128)(2,1)}, bf16[2,2,64,512]{3,2,1,0:T(8,128)(2,1)S(1)}, u32[]{:S(2)}, u32[]{:S(2)}) collective-permute-start(bf16[2,2,64,512]{3,2,1,0:T(8,128)(2,1)} %get-tuple-element.35), channel_id=1, source_target_pairs={{0,16},{16,0},{1,17},{17,1},{2,18},{18,2},{3,19},{19,3},{4,20},{20... | collective-permute-start | bytes 786440 | tf_op jit(solution)/shard_map/ppermute | solution.py:342
  27.7 5.2 %collective-permute-start.2 = (bf16[2,2,16,512]{3,2,1,0:T(8,128)(2,1)S(1)}, bf16[2,2,16,512]{3,2,1,0:T(8,128)(2,1)S(1)}, u32[]{:S(2)}, u32[]{:S(2)}) collective-permute-start(bf16[2,2,16,512]{3,2,1,0:T(8,128)(2,1)S(1)} %slice.8), channel_id=1, source_target_pairs={{0,8},{1,9},{2,10},{3,11},{4,12},{5,13},{6,14},{7,15},{8,0},{9,1},... | collective-permute-start | bytes 196616 | tf_op jit(solution)/shard_map/cond/branch_1_fun/ppermute | solution.py:381
  33.0 18.4 %copy-start = (bf16[2,2,64,512]{3,2,1,0:T(8,128)(2,1)S(1)}, bf16[2,2,64,512]{3,2,1,0:T(8,128)(2,1)}, u32[]{:S(2)}) copy-start(bf16[2,2,64,512]{3,2,1,0:T(8,128)(2,1)} %get-tuple-element.37.refs_0_) | copy-start | bytes 786436
  64.4 17.9 %all-to-all-start.2 = ((bf16[8,4,2,16,512]{4,3,2,1,0:T(8,128)(2,1)}), bf16[8,4,2,16,512]{4,3,2,1,0:T(8,128)(2,1)S(1)}, u32[]{:S(2)}, u32[]{:S(2)}) async-start(bf16[8,4,2,16,512]{4,3,2,1,0:T(8,128)(2,1)} %get-tuple-element.44), calls=%async_computation.2 | async-start | bytes 2097152 | tf_op jit(solution)/shard_map/all_to_all | solution.py:336
  67.9 8.6 %collective-permute-start.5 = (bf16[2,2,64,512]{3,2,1,0:T(8,128)(2,1)S(1)}, bf16[2,2,64,512]{3,2,1,0:T(8,128)(2,1)S(1)}, u32[]{:S(2)}, u32[]{:S(2)}) collective-permute-start(bf16[2,2,64,512]{3,2,1,0:T(8,128)(2,1)S(1)} %get-tuple-element.45), channel_id=1, source_target_pairs={{0,16},{16,0},{1,17},{17,1},{2,18},{18,2},{3,19},{19,3},{4,20},{20... | collective-permute-start | bytes 786440 | tf_op jit(solution)/shard_map/ppermute | solution.py:342
  83.9 6.3 %collective-permute-start.3 = (bf16[2,2,16,512]{3,2,1,0:T(8,128)(2,1)S(1)}, bf16[2,2,16,512]{3,2,1,0:T(8,128)(2,1)S(1)}, u32[]{:S(2)}, u32[]{:S(2)}) collective-permute-start(bf16[2,2,16,512]{3,2,1,0:T(8,128)(2,1)S(1)} %slice.10), channel_id=1, source_target_pairs={{0,8},{1,9},{2,10},{3,11},{4,12},{5,13},{6,14},{7,15},{8,0},{9,1},... | collective-permute-start | bytes 196616 | tf_op jit(solution)/shard_map/cond/branch_1_fun/ppermute | solution.py:381

commit v9 on v8

--- a/solution.py
+++ b/solution.py
@@ -169,11 +169,10 @@
     target = half - source
     t = jnp.where(source == 0, 0, 1)
 
-    def clear(p, _):
+    def clear(p):
         slots[start + p] = -1
-        return 0
-
-    def mark(d, _):
+
+    def mark(d):
         block = 2 * (target + d) + t
         for _ in range(depth):
             block = above(parents, block)
@@ -183,31 +182,37 @@
             def _():
                 slots[start + p] = 0
 
-        return 0
-
     def number(p, count):
         needed = slots[start + p] >= 0
         slots[start + p] = jnp.where(needed, count, -1)
         return count + needed.astype(jnp.int32)
 
-    lax.fori_loop(0, half, clear, 0)
-    lax.fori_loop(0, half, mark, 0)
-    return lax.fori_loop(0, half, number, 0)
+    each(half, clear)
+    each(half, mark)
+    return lax.fori_loop(0, half, number, 0, unroll=half <= 8)
+
+
+def each(count, act):
+    def step(i, _):
+        act(i)
+        return 0
+
+    lax.fori_loop(0, count, step, 0, unroll=count <= 8)
 
 
 def each_need(parents, half, depth, act):
     base = (leaf_rank() // half) * half
 
-    def leaf(d, _):
+    def leaf(d):
         for t in range(2):
             block = 2 * (base + d) + t
             for k in range(depth):
                 block = above(parents, block)
-                p = block // 2
-                act(d, t * depth + k, block >= 0, (p >= base) & (p < base + half), p % half, t)
-        return 0
-
-    lax.fori_loop(0, half, leaf, 0)
+                p = jnp.maximum(block, 0) // 2
+                here = (p >= base) & (p < base + half)
+                act(d, t * depth + k, block >= 0, here, lax.rem(p, half), t)
+
+    each(half, leaf)
 
 
 def cross_kernel(depth, parents, own_ref, cross_ref, slots, count):
@@ -217,60 +222,45 @@
     count[0] = jnp.maximum(mine, other)
     t = leaf_rank() // half
 
-    def copy(p, _):
+    def copy(p):
         slot = slots[half + p]
 
         @pl.when(slot >= 0)
         def _():
             cross_ref[slot] = own_ref[p, :, t]
 
-        return 0
-
-    lax.fori_loop(0, half, copy, 0)
+    each(half, copy)
 
 
 def pick_kernel(depth, parents, slots, own_ref, cross_ref, out_ref):
-    half = own_ref.shape[0]
-
     def act(d, slot, valid, here, p, t):
-        @pl.when(here | ~valid)
-        def _():
-            out_ref[d, slot] = own_ref[p, :, t]
-
-        @pl.when(valid & ~here)
-        def _():
-            out_ref[d, slot] = cross_ref[slots[p]]
+        far = cross_ref[jnp.maximum(slots[p], 0)]
+        out_ref[d, slot] = jnp.where(here | ~valid, own_ref[p, :, t], far)
+
+    each_need(parents, own_ref.shape[0], depth, act)
+
+
+def collect_kernel(depth, parents, slots, in_ref, sums, cross_ref):
+    half = cross_ref.shape[0]
+    sums[...] = jnp.zeros_like(sums)
+
+    def act(d, slot, valid, here, p, t):
+        row = jnp.where(here, t * half + p, 2 * half + jnp.maximum(slots[p], 0))
+        sums[jnp.where(valid, row, 3 * half)] += in_ref[d, slot].astype(F32)
 
     each_need(parents, half, depth, act)
-
-
-def collect_kernel(depth, parents, slots, in_ref, own_ref, cross_ref, sums):
-    half = own_ref.shape[0]
-    own_ref[...] = jnp.zeros_like(own_ref)
-    sums[...] = jnp.zeros_like(sums)
-
-    def act(d, slot, valid, here, p, t):
-        @pl.when(valid & here)
-        def _():
-            own_ref[p, :, t] += in_ref[d, slot].astype(F32)
-
-        @pl.when(valid & ~here)
-        def _():
-            sums[slots[p]] += in_ref[d, slot].astype(F32)
-
-    each_need(parents, half, depth, act)
-    cross_ref[...] = sums[...].astype(BF16)
-
-
-def merge_kernel(spread, slots, own_ref, cross_ref, out_ref):
-    half = own_ref.shape[0]
+    cross_ref[...] = sums[2 * half : 3 * half].astype(BF16)
+
+
+def merge_kernel(spread, slots, sums_ref, cross_ref, out_ref):
+    half = cross_ref.shape[0]
     t = leaf_rank() // half
 
-    def add(p, _):
+    def add(p):
         slot = slots[half + p]
         far = cross_ref[jnp.maximum(slot, 0)].astype(F32)
         for kv in range(2):
-            sums = [own_ref[p, kv, i] + jnp.where((slot >= 0) & (i == t), far[kv], 0.0) for i in range(2)]
+            sums = [sums_ref[i * half + p, kv] + jnp.where((slot >= 0) & (i == t), far[kv], 0.0) for i in range(2)]
             if spread:
                 for h in range(2):
                     tiles = [x[8 * h : 8 * h + 8] for x in sums]
@@ -278,9 +268,8 @@
             else:
                 for i in range(2):
                     out_ref[p, kv, i] = sums[i].astype(BF16)
-        return 0
-
-    lax.fori_loop(0, half, add, 0)
+
+    each(half, add)
 
 
 def finish_kernel(got_ref, own_ref, own_got_ref, keys_ref, values_ref):
@@ -304,7 +293,7 @@
     return pl.BlockSpec(shape, lambda i: (0,) * len(shape))
 
 
-def simple(kernel, scalars, arrays, outs, scratch=(), slots=(), params=PARAMS):
+def simple(kernel, scalars, arrays, outs, slots=(), params=PARAMS):
     out_specs = [whole(x.shape) for x in outs] + [SMEM] * len(slots)
     outs = list(outs) + [jax.ShapeDtypeStruct((x,), jnp.int32) for x in slots]
     return pl.pallas_call(
@@ -313,7 +302,6 @@
         in_specs=[SMEM] * len(scalars) + [whole(x.shape) for x in arrays],
         out_specs=out_specs,
         out_shape=outs,
-        scratch_shapes=list(scratch),
         compiler_params=params,
     )(*scalars, *arrays)
 
@@ -406,17 +394,16 @@
     if merged:
         back, own_got = lax.optimization_barrier((back, to_other_head(self_grads[1])))
 
-    own_sum, cross_sum = simple(
+    sums, cross_sum = simple(
         functools.partial(collect_kernel, depth),
         (all_parents, slots),
         (back,),
-        [like(half, 2, trees, pieces, kv_width, dtype=F32), like(half, *piece)],
-        [pltpu.VMEM((half,) + piece, F32)],
+        [like(3 * half + 1, *piece, dtype=F32), like(half, *piece)],
     )
     (hub_sum,) = simple(
         functools.partial(merge_kernel, merged),
         (slots,),
-        (own_sum, cross(cross_sum)),
+        (sums, cross(cross_sum)),
         [like(2 * half, 2, 16, kv_width) if merged else like(half, 2, trees, pieces, kv_width)],
     )
     if merged:

time: 106 us -> 104 us (0.981)
  Pallas kernels: 21.5 us -> 19.9 us
    pallas_call x6, Pallas kernels: 8.65 us -> 7 us  [simple(): pl.pallas_call(kernel, grid=(1,), in_specs=[SMEM] * len(scalars) + [whole...]
where the time goes in v9:
time: 104 us
  blocking collectives  44.9 us (43%)
  waiting for transfers between devices  20.4 us (20%)
  Pallas kernels  19.9 us (19%)
  starting transfers between devices  17.3 us (17%)
  between operations  1.36 us (1%)
    all_to_all x1, blocking collectives, exchange(): return lax.all_to_all(x, 'leaf', 0, 0, tiled=True, axis_index_groups=sides)  17 us
    psum x1, blocking collectives, body(): lax.psum(table, 'leaf')  14.1 us
    all_to_all x1, blocking collectives, exchange_both(): lax.all_to_all(x, ('head', 'leaf'), 0, 0, tiled=True, axis_index_groups=b...  13.8 us
    pallas_call x1, Pallas kernels, attend(): pl.pallas_call(functools.partial(attend_kernel, len(owns)), grid=(trees,...  12.9 us
    ppermute x2, waiting for transfers between devices, short(): return jnp.concatenate([lax.ppermute(x[:few], 'leaf', swap), x[few:]])  7.55 us
    ppermute x2, waiting for transfers between devices, to_other_head(): return lax.ppermute(x, 'head', [(0, 1), (1, 0)])  7.09 us
    pallas_call x6, Pallas kernels, simple(): pl.pallas_call(kernel, grid=(1,), in_specs=[SMEM] * len(scalars) + [whole...  7 us
    all_to_all x1, starting transfers between devices, exchange_both(): lax.all_to_all(x, ('head', 'leaf'), 0, 0, tiled=True, axis_index_groups=b...  6.29 us
  transfers between devices with their start and end apart: 6, of which 4 were waited for; matrix products, arithmetic and copies ran while one was open for 0% of the time, Pallas kernels for 0%

profile of v9, /device:TPU:0, one launch (start us, length us, event | category | flops | bytes accessed | tf_op | source)
XLA Modules:
  0.0 104.1 jit_solution(8740476401374278222)
XLA Ops:
  0.6 2.1 %shard_map.76 = (bf16[16,2,16,512]{3,2,1,0:T(8,128)(2,1)}, bf16[2,2,64,512]{3,2,1,0:T(8,128)(2,1)}, bf16[2,2,64,512]{3,2,1,0:T(8,128)(2,1)}, s32[1,32]{1,0:T(1,128)}) custom-call(s32[2]{0:T(128)} %parents.1, bf16[2,64,1024]{2,1,0:T(8,128)(2,1)} %keys_ref.1, bf16[2,64,1024]{2,1,0:T(8,128)(2,1)} %values_ref.1), custom_call_target="tpu_custom_call" | custom-call | tf_op jit(solution)/shard_map/pallas_call | solution.py:299
  2.7 6.3 %all-to-all-start = ((bf16[16,2,16,512]{3,2,1,0:T(8,128)(2,1)}), bf16[16,2,16,512]{3,2,1,0:T(8,128)(2,1)S(1)}, u32[]{:S(2)}, u32[]{:S(2)}) async-start(bf16[16,2,16,512]{3,2,1,0:T(8,128)(2,1)} %get-tuple-element.33), calls=%async_computation | async-start | bytes 1048576 | tf_op jit(solution)/shard_map/all_to_all | solution.py:327
  9.0 1.9 %collective-permute-start.4 = (bf16[2,2,64,512]{3,2,1,0:T(8,128)(2,1)}, bf16[2,2,64,512]{3,2,1,0:T(8,128)(2,1)S(1)}, u32[]{:S(2)}, u32[]{:S(2)}) collective-permute-start(bf16[2,2,64,512]{3,2,1,0:T(8,128)(2,1)} %get-tuple-element.35), channel_id=1, source_target_pairs={{0,16},{16,0},{1,17},{17,1},{2,18},{18,2},{3,19},{19,3},{4,20},{20... | collective-permute-start | bytes 786440 | tf_op jit(solution)/shard_map/ppermute | solution.py:330
  10.9 14.1 %psum.7.parents = s32[1,32]{1,0:T(1,128)S(1)} all-reduce(s32[1,32]{1,0:T(1,128)} %get-tuple-element.34), channel_id=1, replica_groups=mesh['head'=2,'leaf'=16] {'leaf'}, use_global_device_ids=true, to_apply=%region_0.0 | all-reduce | flops 32 | bytes 256 | tf_op jit(solution)/shard_map/psum | solution.py:349
  25.1 0.0 collective-permute-done.4.refs_1_
  25.1 0.0 all-to-all-done
  25.1 0.1 copy.10
  25.1 1.5 %shard_map.77 = (bf16[8,2,16,512]{3,2,1,0:T(8,128)(2,1)S(1)}, s32[16]{0:T(128)S(1)}, s32[1]{0:T(128)}) custom-call(s32[1,32]{1,0:T(1,128)S(1)} %psum.7.parents, bf16[8,2,2,16,512]{4,3,2,1,0:T(8,128)(2,1)S(1)} %bitcast.7), custom_call_target="tpu_custom_call" | custom-call | tf_op jit(solution)/shard_map/pallas_call | solution.py:299
  27.3 5.3 %conditional.2 = (bf16[8,2,16,512]{3,2,1,0:T(8,128)(2,1)S(1)}) conditional(s32[]{:T(128)} %bitcast.3, bf16[8,2,16,512]{3,2,1,0:T(8,128)(2,1)S(1)} %get-tuple-element.42, bf16[8,2,16,512]{3,2,1,0:T(8,128)(2,1)S(1)} %get-tuple-element.42), branch_computations={%region_1.0_spmd, %region_2.0_spmd} | conditional | flops 131072 | bytes 1310768 | solution.py:371
  27.3 0.9 collective-permute-start.2
  28.3 4.3 %collective-permute-done.2 = bf16[2,2,16,512]{3,2,1,0:T(8,128)(2,1)S(1)} collective-permute-done((bf16[2,2,16,512]{3,2,1,0:T(8,128)(2,1)S(1)}, bf16[2,2,16,512]{3,2,1,0:T(8,128)(2,1)S(1)}, u32[]{:S(2)}, u32[]{:S(2)}) %collective-permute-start.2) | collective-permute-done | bytes 65568 | tf_op jit(solution)/shard_map/cond/branch_1_fun/ppermute | solution.py:369
  32.6 0.0 copy-start
  32.6 0.9 shard_map.78
  33.5 17.0 %all_to_all.20.refs_2_ = bf16[8,4,2,16,512]{4,3,2,1,0:T(8,128)(2,1)S(1)} all-to-all(bf16[8,4,2,16,512]{4,3,2,1,0:T(8,128)(2,1)S(1)} %shard_map.78), channel_id=1, replica_groups={{0,1,2,3,4,5,6,7},{8,9,10,11,12,13,14,15},{16,17,18,19,20,21,22,23},{24..., dimensions={0} | all-to-all | bytes 2097152 | tf_op jit(solution)/shard_map/all_to_all | solution.py:324
  50.5 0.0 copy-done
  50.5 12.9 %shard_map.79 = (bf16[2,128,4096]{2,1,0:T(8,128)(2,1)}, bf16[2,2,64,512]{3,2,1,0:T(8,128)(2,1)S(1)}, bf16[2,2,64,512]{3,2,1,0:T(8,128)(2,1)S(1)}, bf16[8,4,2,16,512]{4,3,2,1,0:T(8,128)(2,1)}) custom-call(s32[1,32]{1,0:T(1,128)S(1)} %psum.7.parents, bf16[2,128,4096]{2,1,0:T(8,128)(2,1)} %q_ref.1, bf16[2,128,4096]{2,1,0:T(8,128)(2,1)} %do_ref.1, ...), custom_call_target="tpu_custom_call" | custom-call | flops 4026531840 | bytes 6291456 | tf_op jit(solution)/shard_map/pallas_call | solution.py:125
  63.4 3.6 %all-to-all-start.2 = ((bf16[8,4,2,16,512]{4,3,2,1,0:T(8,128)(2,1)}), bf16[8,4,2,16,512]{4,3,2,1,0:T(8,128)(2,1)S(1)}, u32[]{:S(2)}, u32[]{:S(2)}) async-start(bf16[8,4,2,16,512]{4,3,2,1,0:T(8,128)(2,1)} %get-tuple-element.44), calls=%async_computation.2 | async-start | bytes 2097152 | tf_op jit(solution)/shard_map/all_to_all | solution.py:324
  67.0 1.5 %collective-permute-start.5 = (bf16[2,2,64,512]{3,2,1,0:T(8,128)(2,1)S(1)}, bf16[2,2,64,512]{3,2,1,0:T(8,128)(2,1)S(1)}, u32[]{:S(2)}, u32[]{:S(2)}) collective-permute-start(bf16[2,2,64,512]{3,2,1,0:T(8,128)(2,1)S(1)} %get-tuple-element.45), channel_id=1, source_target_pairs={{0,16},{16,0},{1,17},{17,1},{2,18},{18,2},{3,19},{19,3},{4,20},{20... | collective-permute-start | bytes 786440 | tf_op jit(solution)/shard_map/ppermute | solution.py:330
  68.5 7.1 %collective-permute-done.5.own_got_ref = bf16[2,2,64,512]{3,2,1,0:T(8,128)(2,1)S(1)} collective-permute-done((bf16[2,2,64,512]{3,2,1,0:T(8,128)(2,1)S(1)}, bf16[2,2,64,512]{3,2,1,0:T(8,128)(2,1)S(1)}, u32[]{:S(2)}, u32[]{:S(2)}) %collective-permute-start.5) | collective-permute-done | bytes 262176 | tf_op jit(solution)/shard_map/ppermute | solution.py:330
  75.6 5.8 %all-to-all-done.2.in_ref = bf16[8,4,2,16,512]{4,3,2,1,0:T(8,128)(2,1)S(1)} async-done(((bf16[8,4,2,16,512]{4,3,2,1,0:T(8,128)(2,1)}), bf16[8,4,2,16,512]{4,3,2,1,0:T(8,128)(2,1)S(1)}, u32[]{:S(2)}, u32[]{:S(2)}) %all-to-all-start.2) | async-done | bytes 1048608 | tf_op jit(solution)/shard_map/all_to_all | solution.py:324
  81.4 1.0 shard_map.80
  82.3 6.4 %conditional.3 = (bf16[8,2,16,512]{3,2,1,0:T(8,128)(2,1)S(1)}) conditional(s32[]{:T(128)} %bitcast.3, bf16[8,2,16,512]{3,2,1,0:T(8,128)(2,1)S(1)} %get-tuple-element.48, bf16[8,2,16,512]{3,2,1,0:T(8,128)(2,1)S(1)} %get-tuple-element.48), branch_computations={%region_3.0_spmd, %region_4.0_spmd} | conditional | flops 131072 | bytes 1310768 | solution.py:371
  82.4 3.0 %collective-permute-start.3 = (bf16[2,2,16,512]{3,2,1,0:T(8,128)(2,1)S(1)}, bf16[2,2,16,512]{3,2,1,0:T(8,128)(2,1)S(1)}, u32[]{:S(2)}, u32[]{:S(2)}) collective-permute-start(bf16[2,2,16,512]{3,2,1,0:T(8,128)(2,1)S(1)} %slice.10), channel_id=1, source_target_pairs={{0,8},{1,9},{2,10},{3,11},{4,12},{5,13},{6,14},{7,15},{8,0},{9,1},... | collective-permute-start | bytes 196616 | tf_op jit(solution)/shard_map/cond/branch_1_fun/ppermute | solution.py:369
  85.4 3.3 %collective-permute-done.3 = bf16[2,2,16,512]{3,2,1,0:T(8,128)(2,1)S(1)} collective-permute-done((bf16[2,2,16,512]{3,2,1,0:T(8,128)(2,1)S(1)}, bf16[2,2,16,512]{3,2,1,0:T(8,128)(2,1)S(1)}, u32[]{:S(2)}, u32[]{:S(2)}) %collective-permute-start.3) | collective-permute-done | bytes 65568 | tf_op jit(solution)/shard_map/cond/branch_1_fun/ppermute | solution.py:369
  88.7 0.7 shard_map.81
  89.4 13.8 %all_to_all.21.got_ref = bf16[16,2,16,512]{3,2,1,0:T(8,128)(2,1)S(1)} all-to-all(bf16[16,2,16,512]{3,2,1,0:T(8,128)(2,1)S(1)} %shard_map.81), channel_id=1, replica_groups={{0,1,2,3,4,5,6,7,16,17,18,19,20,21,22,23},{8,9,10,11,12,13,14,15,24,25,..., dimensions={0} | all-to-all | bytes 1048576 | tf_op jit(solution)/shard_map/all_to_all | solution.py:327
  103.1 0.9 shard_map.82
  (6 shorter events, 0.1 us)
Async XLA Ops:
  2.7 22.4 %all-to-all-start = ((bf16[16,2,16,512]{3,2,1,0:T(8,128)(2,1)}), bf16[16,2,16,512]{3,2,1,0:T(8,128)(2,1)S(1)}, u32[]{:S(2)}, u32[]{:S(2)}) async-start(bf16[16,2,16,512]{3,2,1,0:T(8,128)(2,1)} %get-tuple-element.33), calls=%async_computation | async-start | bytes 1048576 | tf_op jit(solution)/shard_map/all_to_all | solution.py:327
  9.0 16.1 %collective-permute-start.4 = (bf16[2,2,64,512]{3,2,1,0:T(8,128)(2,1)}, bf16[2,2,64,512]{3,2,1,0:T(8,128)(2,1)S(1)}, u32[]{:S(2)}, u32[]{:S(2)}) collective-permute-start(bf16[2,2,64,512]{3,2,1,0:T(8,128)(2,1)} %get-tuple-element.35), channel_id=1, source_target_pairs={{0,16},{16,0},{1,17},{17,1},{2,18},{18,2},{3,19},{19,3},{4,20},{20... | collective-permute-start | bytes 786440 | tf_op jit(solution)/shard_map/ppermute | solution.py:330
  27.3 5.2 %collective-permute-start.2 = (bf16[2,2,16,512]{3,2,1,0:T(8,128)(2,1)S(1)}, bf16[2,2,16,512]{3,2,1,0:T(8,128)(2,1)S(1)}, u32[]{:S(2)}, u32[]{:S(2)}) collective-permute-start(bf16[2,2,16,512]{3,2,1,0:T(8,128)(2,1)S(1)} %slice.8), channel_id=1, source_target_pairs={{0,8},{1,9},{2,10},{3,11},{4,12},{5,13},{6,14},{7,15},{8,0},{9,1},... | collective-permute-start | bytes 196616 | tf_op jit(solution)/shard_map/cond/branch_1_fun/ppermute | solution.py:369
  32.6 17.9 %copy-start = (bf16[2,2,64,512]{3,2,1,0:T(8,128)(2,1)S(1)}, bf16[2,2,64,512]{3,2,1,0:T(8,128)(2,1)}, u32[]{:S(2)}) copy-start(bf16[2,2,64,512]{3,2,1,0:T(8,128)(2,1)} %get-tuple-element.37.refs_0_) | copy-start | bytes 786436
  63.4 17.9 %all-to-all-start.2 = ((bf16[8,4,2,16,512]{4,3,2,1,0:T(8,128)(2,1)}), bf16[8,4,2,16,512]{4,3,2,1,0:T(8,128)(2,1)S(1)}, u32[]{:S(2)}, u32[]{:S(2)}) async-start(bf16[8,4,2,16,512]{4,3,2,1,0:T(8,128)(2,1)} %get-tuple-element.44), calls=%async_computation.2 | async-start | bytes 2097152 | tf_op jit(solution)/shard_map/all_to_all | solution.py:324
  67.0 8.6 %collective-permute-start.5 = (bf16[2,2,64,512]{3,2,1,0:T(8,128)(2,1)S(1)}, bf16[2,2,64,512]{3,2,1,0:T(8,128)(2,1)S(1)}, u32[]{:S(2)}, u32[]{:S(2)}) collective-permute-start(bf16[2,2,64,512]{3,2,1,0:T(8,128)(2,1)S(1)} %get-tuple-element.45), channel_id=1, source_target_pairs={{0,16},{16,0},{1,17},{17,1},{2,18},{18,2},{3,19},{19,3},{4,20},{20... | collective-permute-start | bytes 786440 | tf_op jit(solution)/shard_map/ppermute | solution.py:330
  82.4 6.3 %collective-permute-start.3 = (bf16[2,2,16,512]{3,2,1,0:T(8,128)(2,1)S(1)}, bf16[2,2,16,512]{3,2,1,0:T(8,128)(2,1)S(1)}, u32[]{:S(2)}, u32[]{:S(2)}) collective-permute-start(bf16[2,2,16,512]{3,2,1,0:T(8,128)(2,1)S(1)} %slice.10), channel_id=1, source_target_pairs={{0,8},{1,9},{2,10},{3,11},{4,12},{5,13},{6,14},{7,15},{8,0},{9,1},... | collective-permute-start | bytes 196616 | tf_op jit(solution)/shard_map/cond/branch_1_fun/ppermute | solution.py:369

commit v10 on v9

--- a/solution.py
+++ b/solution.py
@@ -23,16 +23,16 @@
     return lax.dot_general(a, b, dims, preferred_element_type=F32)
 
 
-def attend_kernel(parts, parents, q_ref, do_ref, *refs):
-    own_refs, anc_ref, dq_ref = refs[:parts], refs[parts], refs[parts + 1]
-    dself_refs, danc_ref = refs[parts + 2 : 2 * parts + 2], refs[2 * parts + 2]
+def attend_kernel(parts, tree, parents, q_ref, do_ref, *refs):
+    own_refs, anc_ref = refs[:parts], refs[parts]
+    dq_ref, *dself_refs, danc_ref = refs[-parts - 2 :]
     hubs, depth, _, pieces, _ = anc_ref.shape
     rows = q_ref.shape[1]
     step_groups = anc_ref.shape[4] // HEAD_DIM
     heads = q_ref.shape[2] // HEAD_DIM // step_groups
     scale = HEAD_DIM ** (-0.5)
     c = scale * math.log2(math.e)
-    block = 2 * leaf_rank() + pl.program_id(0)
+    block = 2 * leaf_rank() + tree()
     valid = []
     for _ in range(depth):
         block = above(parents, block)
@@ -111,30 +111,37 @@
         stage, ready = following, soft
 
 
-def attend(parents, queries, output_gradient, owns, foreign):
+def attend(parents, queries, output_gradient, owns, foreign, near, half, before):
     trees, rows, width = queries.shape
-    hubs, slots, _, pieces, kv_width = foreign.shape
-    depth = slots // trees
+    hubs, depth, _, pieces, kv_width = foreign.shape
     groups = kv_width // HEAD_DIM
     heads = width // groups // HEAD_DIM
     step = 2 - groups % 2
     lanes = step * HEAD_DIM
-    q_spec = pl.BlockSpec((1, rows, heads * lanes), lambda t, g: (t, 0, g))
-    own_specs = [pl.BlockSpec((2, 1, x.shape[2], lanes), lambda t, g: (0, t, 0, g)) for x in owns]
-    anc_spec = pl.BlockSpec((hubs, depth, 2, pieces, lanes), lambda t, g: (0, t, 0, 0, g))
+
+    def tree():
+        return leaf_rank() // half if near else 1 - leaf_rank() // half
+
+    q_spec = pl.BlockSpec((1, rows, heads * lanes), lambda g: (tree(), 0, g))
+    own_specs = [pl.BlockSpec((2, 1, x.shape[2], lanes), lambda g: (0, tree(), 0, g)) for x in owns]
+    got_spec = pl.BlockSpec((hubs, depth, 2, pieces, lanes), lambda g: (0, 0, 0, 0, g))
+    give_spec = pl.BlockSpec((hubs, depth, 2, pieces, lanes), lambda g: (0, tree(), 0, 0, g))
+    out_shape = [jax.ShapeDtypeStruct(x.shape, BF16) for x in (queries, *owns)]
+    out_shape.append(jax.ShapeDtypeStruct((hubs, trees * depth, 2, pieces, kv_width), BF16))
     return pl.pallas_call(
-        functools.partial(attend_kernel, len(owns)),
-        grid=(trees, groups // step),
-        in_specs=[SMEM, q_spec, q_spec, *own_specs, anc_spec],
-        out_specs=[q_spec, *own_specs, anc_spec],
-        out_shape=[jax.ShapeDtypeStruct(x.shape, BF16) for x in (queries, *owns, foreign)],
+        functools.partial(attend_kernel, len(owns), tree),
+        grid=(groups // step,),
+        in_specs=[SMEM, q_spec, q_spec, *own_specs, got_spec] + [pl.BlockSpec(memory_space=pl.ANY)] * len(before),
+        out_specs=[q_spec, *own_specs, give_spec],
+        out_shape=out_shape,
+        input_output_aliases={4 + len(owns) + i: i for i in range(len(before))},
         compiler_params=pltpu.CompilerParams(vmem_limit_bytes=50 * 1024 * 1024),
         cost_estimate=pl.CostEstimate(
-            flops=10 * trees * groups * heads * (depth + 1) * rows * rows * HEAD_DIM,
-            bytes_accessed=12 * rows * width,
-            transcendentals=trees * groups * heads * (depth + 1) * rows * rows,
+            flops=10 * groups * heads * (depth + 1) * rows * rows * HEAD_DIM,
+            bytes_accessed=6 * rows * width,
+            transcendentals=groups * heads * (depth + 1) * rows * rows,
         ),
-    )(parents, queries, output_gradient, *owns, foreign)
+    )(parents, queries, output_gradient, *owns, foreign, *before)
 
 
 def pack_kernel(parents, keys_ref, values_ref, send_ref, keep_ref, give_ref, table_ref):
@@ -200,17 +207,17 @@
     lax.fori_loop(0, count, step, 0, unroll=count <= 8)
 
 
-def each_need(parents, half, depth, act):
+def each_need(parents, half, depth, trees, act):
     base = (leaf_rank() // half) * half
 
     def leaf(d):
-        for t in range(2):
+        for i, t in enumerate(trees):
             block = 2 * (base + d) + t
             for k in range(depth):
                 block = above(parents, block)
                 p = jnp.maximum(block, 0) // 2
                 here = (p >= base) & (p < base + half)
-                act(d, t * depth + k, block >= 0, here, lax.rem(p, half), t)
+                act(d, i * depth + k, block >= 0, here, lax.rem(p, half), t)
 
     each(half, leaf)
 
@@ -232,12 +239,25 @@
     each(half, copy)
 
 
-def pick_kernel(depth, parents, slots, own_ref, cross_ref, out_ref):
-    def act(d, slot, valid, here, p, t):
-        far = cross_ref[jnp.maximum(slots[p], 0)]
-        out_ref[d, slot] = jnp.where(here | ~valid, own_ref[p, :, t], far)
-
-    each_need(parents, own_ref.shape[0], depth, act)
+def pick_near_kernel(depth, parents, own_ref, out_ref):
+    half = own_ref.shape[0]
+    near = leaf_rank() // half
+
+    def act(d, k, valid, here, p, t):
+        out_ref[d, k] = own_ref[p, :, t]
+
+    each_need(parents, half, depth, (near,), act)
+
+
+def pick_far_kernel(depth, parents, slots, own_ref, cross_ref, out_ref):
+    half = own_ref.shape[0]
+    far = 1 - leaf_rank() // half
+
+    def act(d, k, valid, here, p, t):
+        crossed = cross_ref[jnp.maximum(slots[p], 0)]
+        out_ref[d, k] = jnp.where(here | ~valid, own_ref[p, :, t], crossed)
+
+    each_need(parents, half, depth, (far,), act)
 
 
 def collect_kernel(depth, parents, slots, in_ref, sums, cross_ref):
@@ -248,7 +268,7 @@
         row = jnp.where(here, t * half + p, 2 * half + jnp.maximum(slots[p], 0))
         sums[jnp.where(valid, row, 3 * half)] += in_ref[d, slot].astype(F32)
 
-    each_need(parents, half, depth, act)
+    each_need(parents, half, depth, (0, 1), act)
     cross_ref[...] = sums[2 * half : 3 * half].astype(BF16)
 
 
@@ -370,6 +390,9 @@
 
         return lax.cond(count[0] <= few, short, lambda: lax.ppermute(x, "leaf", swap))
 
+    picked_shape = [like(half, depth, *piece)]
+    (picked_near,) = simple(functools.partial(pick_near_kernel, depth), (all_parents,), (hub_own,), picked_shape)
+    foreign_near = exchange(picked_near)
     crossing, slots, count = simple(
         functools.partial(cross_kernel, depth),
         (all_parents,),
@@ -377,17 +400,18 @@
         [like(half, *piece)],
         slots=(2 * half, 1),
     )
-    (picked,) = simple(
-        functools.partial(pick_kernel, depth),
-        (all_parents, slots),
-        (hub_own, cross(crossing)),
-        [like(half, trees * depth, *piece)],
+    (picked_far,) = simple(
+        functools.partial(pick_far_kernel, depth), (all_parents, slots), (hub_own, cross(crossing)), picked_shape
     )
-    foreign = exchange(picked)
-    if pieces % 16:
-        foreign = foreign.transpose(1, 2, 0, 3, 4).reshape(1, trees * depth, 2, rows, kv_width)
-
-    query_grad, *self_grads, foreign_grad = attend(all_parents, queries, output_gradient, owns, foreign)
+    foreign_near, picked_far = lax.optimization_barrier((foreign_near, picked_far))
+    foreign_far = exchange(picked_far)
+
+    results = ()
+    for near, foreign in ((True, foreign_near), (False, foreign_far)):
+        if pieces % 16:
+            foreign = foreign.transpose(1, 2, 0, 3, 4).reshape(1, depth, 2, rows, kv_width)
+        results = attend(all_parents, queries, output_gradient, owns, foreign, near, half, results)
+    query_grad, *self_grads, foreign_grad = results
     if pieces % 16:
         foreign_grad = foreign_grad.reshape(trees * depth, 2, half, pieces, kv_width).transpose(2, 0, 1, 3, 4)
     back = exchange(foreign_grad)

time: 104 us -> 102 us (0.981)
  blocking collectives: 44.9 us -> 28.2 us
  starting transfers between devices: 17.3 us -> 23.5 us
  Pallas kernels: 19.9 us -> 24.2 us
  waiting for transfers between devices: 20.4 us -> 23.9 us
    all_to_all x1 -> x0, blocking collectives: 17 us -> none  [exchange(): return lax.all_to_all(x, 'leaf', 0, 0, tiled=True, axis_index_groups=sides)]
    all_to_all x1 -> x3, starting transfers between devices: 3.56 us -> 11.9 us  [exchange(): return lax.all_to_all(x, 'leaf', 0, 0, tiled=True, axis_index_groups=sides)]
    pallas_call x1 -> x2, Pallas kernels: 12.9 us -> 15.1 us  [attend(): pl.pallas_call(functools.partial(attend_kernel, len(owns), tree), grid=(g...]
    pallas_call x6 -> x7, Pallas kernels: 7 us -> 9.14 us  [simple(): pl.pallas_call(kernel, grid=(1,), in_specs=[SMEM] * len(scalars) + [whole...]
    all_to_all x1 -> x3, waiting for transfers between devices: 5.76 us -> 7.54 us  [exchange(): return lax.all_to_all(x, 'leaf', 0, 0, tiled=True, axis_index_groups=sides)]
    ppermute x2, starting transfers between devices: 3.96 us -> 2.6 us  [short(): return jnp.concatenate([lax.ppermute(x[:few], 'leaf', swap), x[few:]])]
  transfers between devices with their start and end apart: 6 -> 8, of which waited for: 4 -> 6; matrix products, arithmetic and copies ran while one was open for 0% -> 0% of each run, Pallas kernels for 0% -> 11%
where the time goes in v10:
time: 102 us; the launch traced here: 101 us
  blocking collectives  28.2 us (28%)
  Pallas kernels  24.2 us (24%)
  waiting for transfers between devices  23.9 us (23%)
  starting transfers between devices  23.5 us (23%)
  between operations  1.36 us (1%)
    pallas_call x2, Pallas kernels, attend(): pl.pallas_call(functools.partial(attend_kernel, len(owns), tree), grid=(g...  15.1 us
    psum x1, blocking collectives, body(): lax.psum(table, 'leaf')  14.1 us
    all_to_all x1, blocking collectives, exchange_both(): lax.all_to_all(x, ('head', 'leaf'), 0, 0, tiled=True, axis_index_groups=b...  14 us
    all_to_all x3, starting transfers between devices, exchange(): return lax.all_to_all(x, 'leaf', 0, 0, tiled=True, axis_index_groups=sides)  11.9 us
    pallas_call x7, Pallas kernels, simple(): pl.pallas_call(kernel, grid=(1,), in_specs=[SMEM] * len(scalars) + [whole...  9.14 us
    ppermute x2, waiting for transfers between devices, short(): return jnp.concatenate([lax.ppermute(x[:few], 'leaf', swap), x[few:]])  8.51 us
    ppermute x2, waiting for transfers between devices, to_other_head(): return lax.ppermute(x, 'head', [(0, 1), (1, 0)])  7.83 us
    all_to_all x3, waiting for transfers between devices, exchange(): return lax.all_to_all(x, 'leaf', 0, 0, tiled=True, axis_index_groups=sides)  7.54 us
  transfers between devices with their start and end apart: 8, of which 6 were waited for; matrix products, arithmetic and copies ran while one was open for 0% of the time, Pallas kernels for 11%

profile of v10, /device:TPU:0, one launch (start us, length us, event | category | flops | bytes accessed | tf_op | source)
XLA Modules:
  0.0 101.4 jit_solution(16252577603363906017)
XLA Ops:
  0.6 2.1 %shard_map.76 = (bf16[16,2,16,512]{3,2,1,0:T(8,128)(2,1)}, bf16[2,2,64,512]{3,2,1,0:T(8,128)(2,1)}, bf16[2,2,64,512]{3,2,1,0:T(8,128)(2,1)}, s32[1,32]{1,0:T(1,128)}) custom-call(s32[2]{0:T(128)} %parents.1, bf16[2,64,1024]{2,1,0:T(8,128)(2,1)} %keys_ref.1, bf16[2,64,1024]{2,1,0:T(8,128)(2,1)} %values_ref.1), custom_call_target="tpu_custom_call" | custom-call | tf_op jit(solution)/shard_map/pallas_call | solution.py:319
  2.7 6.3 %all-to-all-start = ((bf16[16,2,16,512]{3,2,1,0:T(8,128)(2,1)}), bf16[16,2,16,512]{3,2,1,0:T(8,128)(2,1)S(1)}, u32[]{:S(2)}, u32[]{:S(2)}) async-start(bf16[16,2,16,512]{3,2,1,0:T(8,128)(2,1)} %get-tuple-element.39), calls=%async_computation | async-start | bytes 1048576 | tf_op jit(solution)/shard_map/all_to_all | solution.py:347
  9.0 1.9 %collective-permute-start.4 = (bf16[2,2,64,512]{3,2,1,0:T(8,128)(2,1)}, bf16[2,2,64,512]{3,2,1,0:T(8,128)(2,1)S(1)}, u32[]{:S(2)}, u32[]{:S(2)}) collective-permute-start(bf16[2,2,64,512]{3,2,1,0:T(8,128)(2,1)} %get-tuple-element.41), channel_id=1, source_target_pairs={{0,16},{16,0},{1,17},{17,1},{2,18},{18,2},{3,19},{19,3},{4,20},{20... | collective-permute-start | bytes 786440 | tf_op jit(solution)/shard_map/ppermute | solution.py:350
  10.9 14.1 %psum.7.parents = s32[1,32]{1,0:T(1,128)S(1)} all-reduce(s32[1,32]{1,0:T(1,128)} %get-tuple-element.40), channel_id=1, replica_groups=mesh['head'=2,'leaf'=16] {'leaf'}, use_global_device_ids=true, to_apply=%region_0.0 | all-reduce | flops 32 | bytes 256 | tf_op jit(solution)/shard_map/psum | solution.py:369
  25.1 0.0 collective-permute-done.4.refs_1_
  25.1 0.0 all-to-all-done
  25.1 0.1 copy.14
  25.1 1.5 %shard_map.77 = bf16[8,2,2,16,512]{4,3,2,1,0:T(8,128)(2,1)} custom-call(s32[1,32]{1,0:T(1,128)S(1)} %psum.7.parents, bf16[8,2,2,16,512]{4,3,2,1,0:T(8,128)(2,1)S(1)} %bitcast.7), custom_call_target="tpu_custom_call" | custom-call | tf_op jit(solution)/shard_map/pallas_call | solution.py:319
  26.6 3.5 %all-to-all-start.1 = ((bf16[8,2,2,16,512]{4,3,2,1,0:T(8,128)(2,1)}), bf16[8,2,2,16,512]{4,3,2,1,0:T(8,128)(2,1)S(1)}, u32[]{:S(2)}, u32[]{:S(2)}) async-start(bf16[8,2,2,16,512]{4,3,2,1,0:T(8,128)(2,1)} %shard_map.77), calls=%async_computation.1 | async-start | bytes 1048576 | tf_op jit(solution)/shard_map/all_to_all | solution.py:344
  30.1 0.0 copy-start
  30.1 1.5 %shard_map.78 = (bf16[8,2,16,512]{3,2,1,0:T(8,128)(2,1)S(1)}, s32[16]{0:T(128)S(1)}, s32[1]{0:T(128)}) custom-call(s32[1,32]{1,0:T(1,128)S(1)} %psum.7.parents, bf16[8,2,2,16,512]{4,3,2,1,0:T(8,128)(2,1)S(1)} %bitcast.8), custom_call_target="tpu_custom_call" | custom-call | tf_op jit(solution)/shard_map/pallas_call | solution.py:319
  32.3 5.9 %conditional.2 = (bf16[8,2,16,512]{3,2,1,0:T(8,128)(2,1)S(1)}) conditional(s32[]{:T(128)} %bitcast.4, bf16[8,2,16,512]{3,2,1,0:T(8,128)(2,1)S(1)} %get-tuple-element.48, bf16[8,2,16,512]{3,2,1,0:T(8,128)(2,1)S(1)} %get-tuple-element.48), branch_computations={%region_1.0_spmd, %region_2.0_spmd} | conditional | flops 131072 | bytes 1310768 | solution.py:391
  32.3 1.1 %collective-permute-start.2 = (bf16[2,2,16,512]{3,2,1,0:T(8,128)(2,1)S(1)}, bf16[2,2,16,512]{3,2,1,0:T(8,128)(2,1)S(1)}, u32[]{:S(2)}, u32[]{:S(2)}) collective-permute-start(bf16[2,2,16,512]{3,2,1,0:T(8,128)(2,1)S(1)} %slice.8), channel_id=1, source_target_pairs={{0,8},{1,9},{2,10},{3,11},{4,12},{5,13},{6,14},{7,15},{8,0},{9,1},... | collective-permute-start | bytes 196616 | tf_op jit(solution)/shard_map/cond/branch_1_fun/ppermute | solution.py:389
  33.4 4.8 %collective-permute-done.2 = bf16[2,2,16,512]{3,2,1,0:T(8,128)(2,1)S(1)} collective-permute-done((bf16[2,2,16,512]{3,2,1,0:T(8,128)(2,1)S(1)}, bf16[2,2,16,512]{3,2,1,0:T(8,128)(2,1)S(1)}, u32[]{:S(2)}, u32[]{:S(2)}) %collective-permute-start.2) | collective-permute-done | bytes 65568 | tf_op jit(solution)/shard_map/cond/branch_1_fun/ppermute | solution.py:389
  38.2 1.5 %shard_map.79 = bf16[8,2,2,16,512]{4,3,2,1,0:T(8,128)(2,1)} custom-call(s32[1,32]{1,0:T(1,128)S(1)} %psum.7.parents, s32[16]{0:T(128)S(1)} %get-tuple-element.46.slots, bf16[8,2,2,16,512]{4,3,2,1,0:T(8,128)(2,1)S(1)} %bitcast.9, bf16[8,2,16,512]{3,2,1,0:T(8,128)(2,1)S(1)} %get-tuple-element.65.cross_ref), custom_call_target="tpu_custom_call" | custom-call | tf_op jit(solution)/shard_map/pallas_call | solution.py:319
  39.7 0.5 all-to-all-done.1.refs_2_
  40.3 4.9 %all-to-all-start.2 = ((bf16[8,2,2,16,512]{4,3,2,1,0:T(8,128)(2,1)}), bf16[8,2,2,16,512]{4,3,2,1,0:T(8,128)(2,1)S(1)}, u32[]{:S(2)}, u32[]{:S(2)}) async-start(bf16[8,2,2,16,512]{4,3,2,1,0:T(8,128)(2,1)} %shard_map.79), calls=%async_computation.2 | async-start | bytes 1048576 | tf_op jit(solution)/shard_map/all_to_all | solution.py:344
  45.1 0.0 copy-done
  45.1 7.6 %shard_map.80 = (bf16[2,128,4096]{2,1,0:T(8,128)(2,1)}, bf16[2,2,64,512]{3,2,1,0:T(8,128)(2,1)S(1)}, bf16[2,2,64,512]{3,2,1,0:T(8,128)(2,1)S(1)}, bf16[8,4,2,16,512]{4,3,2,1,0:T(8,128)(2,1)}) custom-call(s32[1,32]{1,0:T(1,128)S(1)} %psum.7.parents, bf16[2,128,4096]{2,1,0:T(8,128)(2,1)} %q_ref.3, bf16[2,128,4096]{2,1,0:T(8,128)(2,1)} %do_ref.3, ...), custom_call_target="tpu_custom_call" | custom-call | flops 2013265920 | bytes 3145728 | tf_op jit(solution)/shard_map/pallas_call | solution.py:131
  52.7 1.3 %all-to-all-done.2.refs_2_ = bf16[8,2,2,16,512]{4,3,2,1,0:T(8,128)(2,1)S(1)} async-done(((bf16[8,2,2,16,512]{4,3,2,1,0:T(8,128)(2,1)}), bf16[8,2,2,16,512]{4,3,2,1,0:T(8,128)(2,1)S(1)}, u32[]{:S(2)}, u32[]{:S(2)}) %all-to-all-start.2) | async-done | bytes 524320 | tf_op jit(solution)/shard_map/all_to_all | solution.py:344
  54.0 7.5 %shard_map.81 = (bf16[2,128,4096]{2,1,0:T(8,128)(2,1)}, bf16[2,2,64,512]{3,2,1,0:T(8,128)(2,1)S(1)}, bf16[2,2,64,512]{3,2,1,0:T(8,128)(2,1)S(1)}, bf16[8,4,2,16,512]{4,3,2,1,0:T(8,128)(2,1)}) custom-call(s32[1,32]{1,0:T(1,128)S(1)} %psum.7.parents, ...), custom_call_target="tpu_custom_call", output_to_operand_aliasing={{0}: (6, {}), {1}: (7, {}), {2}: (8, {}), {3}: (9, {})} | custom-call | flops 2013265920 | bytes 3145728 | tf_op jit(solution)/shard_map/pallas_call | solution.py:131
  61.4 3.6 %all-to-all-start.3 = ((bf16[8,4,2,16,512]{4,3,2,1,0:T(8,128)(2,1)}), bf16[8,4,2,16,512]{4,3,2,1,0:T(8,128)(2,1)S(1)}, u32[]{:S(2)}, u32[]{:S(2)}) async-start(bf16[8,4,2,16,512]{4,3,2,1,0:T(8,128)(2,1)} %get-tuple-element.56), calls=%async_computation.3 | async-start | bytes 2097152 | tf_op jit(solution)/shard_map/all_to_all | solution.py:344
  65.0 0.8 collective-permute-start.5
  65.8 7.8 %collective-permute-done.5.own_got_ref = bf16[2,2,64,512]{3,2,1,0:T(8,128)(2,1)S(1)} collective-permute-done((bf16[2,2,64,512]{3,2,1,0:T(8,128)(2,1)S(1)}, bf16[2,2,64,512]{3,2,1,0:T(8,128)(2,1)S(1)}, u32[]{:S(2)}, u32[]{:S(2)}) %collective-permute-start.5) | collective-permute-done | bytes 262176 | tf_op jit(solution)/shard_map/ppermute | solution.py:350
  73.6 5.8 %all-to-all-done.3.in_ref = bf16[8,4,2,16,512]{4,3,2,1,0:T(8,128)(2,1)S(1)} async-done(((bf16[8,4,2,16,512]{4,3,2,1,0:T(8,128)(2,1)}), bf16[8,4,2,16,512]{4,3,2,1,0:T(8,128)(2,1)S(1)}, u32[]{:S(2)}, u32[]{:S(2)}) %all-to-all-start.3) | async-done | bytes 1048608 | tf_op jit(solution)/shard_map/all_to_all | solution.py:344
  79.4 1.0 shard_map.82
  80.4 5.4 %conditional.3 = (bf16[8,2,16,512]{3,2,1,0:T(8,128)(2,1)S(1)}) conditional(s32[]{:T(128)} %bitcast.4, bf16[8,2,16,512]{3,2,1,0:T(8,128)(2,1)S(1)} %get-tuple-element.60, bf16[8,2,16,512]{3,2,1,0:T(8,128)(2,1)S(1)} %get-tuple-element.60), branch_computations={%region_3.0_spmd, %region_4.0_spmd} | conditional | flops 131072 | bytes 1310768 | solution.py:391
  80.4 1.5 %collective-permute-start.3 = (bf16[2,2,16,512]{3,2,1,0:T(8,128)(2,1)S(1)}, bf16[2,2,16,512]{3,2,1,0:T(8,128)(2,1)S(1)}, u32[]{:S(2)}, u32[]{:S(2)}) collective-permute-start(bf16[2,2,16,512]{3,2,1,0:T(8,128)(2,1)S(1)} %slice.10), channel_id=1, source_target_pairs={{0,8},{1,9},{2,10},{3,11},{4,12},{5,13},{6,14},{7,15},{8,0},{9,1},... | collective-permute-start | bytes 196616 | tf_op jit(solution)/shard_map/cond/branch_1_fun/ppermute | solution.py:389
  81.9 3.8 %collective-permute-done.3 = bf16[2,2,16,512]{3,2,1,0:T(8,128)(2,1)S(1)} collective-permute-done((bf16[2,2,16,512]{3,2,1,0:T(8,128)(2,1)S(1)}, bf16[2,2,16,512]{3,2,1,0:T(8,128)(2,1)S(1)}, u32[]{:S(2)}, u32[]{:S(2)}) %collective-permute-start.3) | collective-permute-done | bytes 65568 | tf_op jit(solution)/shard_map/cond/branch_1_fun/ppermute | solution.py:389
  85.7 0.7 shard_map.83
  86.4 14.0 %all_to_all.25.got_ref = bf16[16,2,16,512]{3,2,1,0:T(8,128)(2,1)S(1)} all-to-all(bf16[16,2,16,512]{3,2,1,0:T(8,128)(2,1)S(1)} %shard_map.83), channel_id=1, replica_groups={{0,1,2,3,4,5,6,7,16,17,18,19,20,21,22,23},{8,9,10,11,12,13,14,15,24,25,..., dimensions={0} | all-to-all | bytes 1048576 | tf_op jit(solution)/shard_map/all_to_all | solution.py:347
  100.4 0.9 shard_map.84
  (6 shorter events, 0.1 us)
Async XLA Ops:
  2.7 22.4 %all-to-all-start = ((bf16[16,2,16,512]{3,2,1,0:T(8,128)(2,1)}), bf16[16,2,16,512]{3,2,1,0:T(8,128)(2,1)S(1)}, u32[]{:S(2)}, u32[]{:S(2)}) async-start(bf16[16,2,16,512]{3,2,1,0:T(8,128)(2,1)} %get-tuple-element.39), calls=%async_computation | async-start | bytes 1048576 | tf_op jit(solution)/shard_map/all_to_all | solution.py:347
  9.0 16.1 %collective-permute-start.4 = (bf16[2,2,64,512]{3,2,1,0:T(8,128)(2,1)}, bf16[2,2,64,512]{3,2,1,0:T(8,128)(2,1)S(1)}, u32[]{:S(2)}, u32[]{:S(2)}) collective-permute-start(bf16[2,2,64,512]{3,2,1,0:T(8,128)(2,1)} %get-tuple-element.41), channel_id=1, source_target_pairs={{0,16},{16,0},{1,17},{17,1},{2,18},{18,2},{3,19},{19,3},{4,20},{20... | collective-permute-start | bytes 786440 | tf_op jit(solution)/shard_map/ppermute | solution.py:350
  26.6 13.7 %all-to-all-start.1 = ((bf16[8,2,2,16,512]{4,3,2,1,0:T(8,128)(2,1)}), bf16[8,2,2,16,512]{4,3,2,1,0:T(8,128)(2,1)S(1)}, u32[]{:S(2)}, u32[]{:S(2)}) async-start(bf16[8,2,2,16,512]{4,3,2,1,0:T(8,128)(2,1)} %shard_map.77), calls=%async_computation.1 | async-start | bytes 1048576 | tf_op jit(solution)/shard_map/all_to_all | solution.py:344
  30.1 15.0 %copy-start = (bf16[2,2,64,512]{3,2,1,0:T(8,128)(2,1)S(1)}, bf16[2,2,64,512]{3,2,1,0:T(8,128)(2,1)}, u32[]{:S(2)}) copy-start(bf16[2,2,64,512]{3,2,1,0:T(8,128)(2,1)} %get-tuple-element.43.refs_0_) | copy-start | bytes 786436
  32.3 5.8 %collective-permute-start.2 = (bf16[2,2,16,512]{3,2,1,0:T(8,128)(2,1)S(1)}, bf16[2,2,16,512]{3,2,1,0:T(8,128)(2,1)S(1)}, u32[]{:S(2)}, u32[]{:S(2)}) collective-permute-start(bf16[2,2,16,512]{3,2,1,0:T(8,128)(2,1)S(1)} %slice.8), channel_id=1, source_target_pairs={{0,8},{1,9},{2,10},{3,11},{4,12},{5,13},{6,14},{7,15},{8,0},{9,1},... | collective-permute-start | bytes 196616 | tf_op jit(solution)/shard_map/cond/branch_1_fun/ppermute | solution.py:389
  40.3 13.7 %all-to-all-start.2 = ((bf16[8,2,2,16,512]{4,3,2,1,0:T(8,128)(2,1)}), bf16[8,2,2,16,512]{4,3,2,1,0:T(8,128)(2,1)S(1)}, u32[]{:S(2)}, u32[]{:S(2)}) async-start(bf16[8,2,2,16,512]{4,3,2,1,0:T(8,128)(2,1)} %shard_map.79), calls=%async_computation.2 | async-start | bytes 1048576 | tf_op jit(solution)/shard_map/all_to_all | solution.py:344
  61.4 17.9 %all-to-all-start.3 = ((bf16[8,4,2,16,512]{4,3,2,1,0:T(8,128)(2,1)}), bf16[8,4,2,16,512]{4,3,2,1,0:T(8,128)(2,1)S(1)}, u32[]{:S(2)}, u32[]{:S(2)}) async-start(bf16[8,4,2,16,512]{4,3,2,1,0:T(8,128)(2,1)} %get-tuple-element.56), calls=%async_computation.3 | async-start | bytes 2097152 | tf_op jit(solution)/shard_map/all_to_all | solution.py:344
  65.0 8.6 %collective-permute-start.5 = (bf16[2,2,64,512]{3,2,1,0:T(8,128)(2,1)S(1)}, bf16[2,2,64,512]{3,2,1,0:T(8,128)(2,1)S(1)}, u32[]{:S(2)}, u32[]{:S(2)}) collective-permute-start(bf16[2,2,64,512]{3,2,1,0:T(8,128)(2,1)S(1)} %get-tuple-element.57), channel_id=1, source_target_pairs={{0,16},{16,0},{1,17},{17,1},{2,18},{18,2},{3,19},{19,3},{4,20},{20... | collective-permute-start | bytes 786440 | tf_op jit(solution)/shard_map/ppermute | solution.py:350
  80.4 5.3 %collective-permute-start.3 = (bf16[2,2,16,512]{3,2,1,0:T(8,128)(2,1)S(1)}, bf16[2,2,16,512]{3,2,1,0:T(8,128)(2,1)S(1)}, u32[]{:S(2)}, u32[]{:S(2)}) collective-permute-start(bf16[2,2,16,512]{3,2,1,0:T(8,128)(2,1)S(1)} %slice.10), channel_id=1, source_target_pairs={{0,8},{1,9},{2,10},{3,11},{4,12},{5,13},{6,14},{7,15},{8,0},{9,1},... | collective-permute-start | bytes 196616 | tf_op jit(solution)/shard_map/cond/branch_1_fun/ppermute | solution.py:389

commit v11 on v10

--- a/solution.py
+++ b/solution.py
@@ -112,7 +112,7 @@
 
 
 def attend(parents, queries, output_gradient, owns, foreign, near, half, before):
-    trees, rows, width = queries.shape
+    _, rows, width = queries.shape
     hubs, depth, _, pieces, kv_width = foreign.shape
     groups = kv_width // HEAD_DIM
     heads = width // groups // HEAD_DIM
@@ -125,14 +125,12 @@
     q_spec = pl.BlockSpec((1, rows, heads * lanes), lambda g: (tree(), 0, g))
     own_specs = [pl.BlockSpec((2, 1, x.shape[2], lanes), lambda g: (0, tree(), 0, g)) for x in owns]
     got_spec = pl.BlockSpec((hubs, depth, 2, pieces, lanes), lambda g: (0, 0, 0, 0, g))
-    give_spec = pl.BlockSpec((hubs, depth, 2, pieces, lanes), lambda g: (0, tree(), 0, 0, g))
-    out_shape = [jax.ShapeDtypeStruct(x.shape, BF16) for x in (queries, *owns)]
-    out_shape.append(jax.ShapeDtypeStruct((hubs, trees * depth, 2, pieces, kv_width), BF16))
+    out_shape = [jax.ShapeDtypeStruct(x.shape, BF16) for x in (queries, *owns, foreign)]
     return pl.pallas_call(
         functools.partial(attend_kernel, len(owns), tree),
         grid=(groups // step,),
         in_specs=[SMEM, q_spec, q_spec, *own_specs, got_spec] + [pl.BlockSpec(memory_space=pl.ANY)] * len(before),
-        out_specs=[q_spec, *own_specs, give_spec],
+        out_specs=[q_spec, *own_specs, got_spec],
         out_shape=out_shape,
         input_output_aliases={4 + len(owns) + i: i for i in range(len(before))},
         compiler_params=pltpu.CompilerParams(vmem_limit_bytes=50 * 1024 * 1024),
@@ -260,27 +258,39 @@
     each_need(parents, half, depth, (far,), act)
 
 
-def collect_kernel(depth, parents, slots, in_ref, sums, cross_ref):
+def collect_near_kernel(depth, parents, in_ref, sums):
+    half = in_ref.shape[0]
+    sums[...] = jnp.zeros_like(sums)
+
+    def act(d, k, valid, here, p, t):
+        sums[jnp.where(valid, p, half)] += in_ref[d, k].astype(F32)
+
+    each_need(parents, half, depth, (leaf_rank() // half,), act)
+
+
+def collect_far_kernel(depth, parents, slots, in_ref, sums, cross_ref):
     half = cross_ref.shape[0]
     sums[...] = jnp.zeros_like(sums)
 
-    def act(d, slot, valid, here, p, t):
-        row = jnp.where(here, t * half + p, 2 * half + jnp.maximum(slots[p], 0))
-        sums[jnp.where(valid, row, 3 * half)] += in_ref[d, slot].astype(F32)
-
-    each_need(parents, half, depth, (0, 1), act)
-    cross_ref[...] = sums[2 * half : 3 * half].astype(BF16)
-
-
-def merge_kernel(spread, slots, sums_ref, cross_ref, out_ref):
+    def act(d, k, valid, here, p, t):
+        row = jnp.where(here, p, half + jnp.maximum(slots[p], 0))
+        sums[jnp.where(valid, row, 2 * half)] += in_ref[d, k].astype(F32)
+
+    each_need(parents, half, depth, (1 - leaf_rank() // half,), act)
+    cross_ref[...] = sums[half : 2 * half].astype(BF16)
+
+
+def merge_kernel(spread, slots, near_ref, far_ref, cross_ref, out_ref):
     half = cross_ref.shape[0]
-    t = leaf_rank() // half
+    even = leaf_rank() < half
 
     def add(p):
         slot = slots[half + p]
-        far = cross_ref[jnp.maximum(slot, 0)].astype(F32)
+        crossed = cross_ref[jnp.maximum(slot, 0)].astype(F32)
         for kv in range(2):
-            sums = [sums_ref[i * half + p, kv] + jnp.where((slot >= 0) & (i == t), far[kv], 0.0) for i in range(2)]
+            near = near_ref[p, kv] + jnp.where(slot >= 0, crossed[kv], 0.0)
+            far = far_ref[p, kv]
+            sums = [jnp.where(even, near, far), jnp.where(even, far, near)]
             if spread:
                 for h in range(2):
                     tiles = [x[8 * h : 8 * h + 8] for x in sums]
@@ -406,28 +416,44 @@
     foreign_near, picked_far = lax.optimization_barrier((foreign_near, picked_far))
     foreign_far = exchange(picked_far)
 
-    results = ()
-    for near, foreign in ((True, foreign_near), (False, foreign_far)):
-        if pieces % 16:
-            foreign = foreign.transpose(1, 2, 0, 3, 4).reshape(1, depth, 2, rows, kv_width)
-        results = attend(all_parents, queries, output_gradient, owns, foreign, near, half, results)
-    query_grad, *self_grads, foreign_grad = results
-    if pieces % 16:
-        foreign_grad = foreign_grad.reshape(trees * depth, 2, half, pieces, kv_width).transpose(2, 0, 1, 3, 4)
-    back = exchange(foreign_grad)
+    def gather_rows(x):
+        if pieces % 16 == 0:
+            return x
+        return x.transpose(1, 2, 0, 3, 4).reshape(1, depth, 2, rows, kv_width)
+
+    def spread_rows(x):
+        if pieces % 16 == 0:
+            return x
+        return x.reshape(depth, 2, half, pieces, kv_width).transpose(2, 0, 1, 3, 4)
+
+    *results, near_grad = attend(
+        all_parents, queries, output_gradient, owns, gather_rows(foreign_near), True, half, ()
+    )
+    query_grad, *self_grads, far_grad = attend(
+        all_parents, queries, output_gradient, owns, gather_rows(foreign_far), False, half, results
+    )
+    near_back, far_grad = lax.optimization_barrier((exchange(spread_rows(near_grad)), far_grad))
+    far_back = exchange(spread_rows(far_grad))
+    (near_sum,) = simple(
+        functools.partial(collect_near_kernel, depth),
+        (all_parents,),
+        (near_back,),
+        [like(half + 1, *piece, dtype=F32)],
+    )
     if merged:
-        back, own_got = lax.optimization_barrier((back, to_other_head(self_grads[1])))
-
-    sums, cross_sum = simple(
-        functools.partial(collect_kernel, depth),
+        far_back, near_sum, own_got = lax.optimization_barrier((far_back, near_sum, to_other_head(self_grads[1])))
+    else:
+        far_back, near_sum = lax.optimization_barrier((far_back, near_sum))
+    far_sum, cross_sum = simple(
+        functools.partial(collect_far_kernel, depth),
         (all_parents, slots),
-        (back,),
-        [like(3 * half + 1, *piece, dtype=F32), like(half, *piece)],
+        (far_back,),
+        [like(2 * half + 1, *piece, dtype=F32), like(half, *piece)],
     )
     (hub_sum,) = simple(
         functools.partial(merge_kernel, merged),
         (slots,),
-        (sums, cross(cross_sum)),
+        (near_sum, far_sum, cross(cross_sum)),
         [like(2 * half, 2, 16, kv_width) if merged else like(half, 2, trees, pieces, kv_width)],
     )
     if merged:

time: 102 us -> 101 us (level)
  waiting for transfers between devices: 23.9 us -> 18.9 us
  starting transfers between devices: 23.5 us -> 26.9 us
    all_to_all x3 -> x4, waiting for transfers between devices: 7.54 us -> 3.21 us  [exchange(): return lax.all_to_all(x, 'leaf', 0, 0, tiled=True, axis_index_groups=sides)]
    all_to_all x3 -> x4, starting transfers between devices: 11.9 us -> 15.3 us  [exchange(): return lax.all_to_all(x, 'leaf', 0, 0, tiled=True, axis_index_groups=sides)]
    pallas_call x7 -> x8, Pallas kernels: 9.14 us -> 9.65 us  [simple(): pl.pallas_call(kernel, grid=(1,), in_specs=[SMEM] * len(scalars) + [whole...]
  transfers between devices with their start and end apart: 8 -> 9, of which waited for: 6 -> 7; matrix products, arithmetic and copies ran while one was open for 0% -> 0% of each run, Pallas kernels for 11% -> 19%
where the time goes in v11:
time: 101 us; the launch traced here: 100 us
  blocking collectives  28.4 us (28%)
  starting transfers between devices  26.9 us (27%)
  Pallas kernels  24.7 us (24%)
  waiting for transfers between devices  18.9 us (19%)
  between operations  1.38 us (1%)
    all_to_all x4, starting transfers between devices, exchange(): return lax.all_to_all(x, 'leaf', 0, 0, tiled=True, axis_index_groups=sides)  15.3 us
    pallas_call x2, Pallas kernels, attend(): pl.pallas_call(functools.partial(attend_kernel, len(owns), tree), grid=(g...  15.1 us
    all_to_all x1, blocking collectives, exchange_both(): lax.all_to_all(x, ('head', 'leaf'), 0, 0, tiled=True, axis_index_groups=b...  14.3 us
    psum x1, blocking collectives, body(): lax.psum(table, 'leaf')  14.1 us
    pallas_call x8, Pallas kernels, simple(): pl.pallas_call(kernel, grid=(1,), in_specs=[SMEM] * len(scalars) + [whole...  9.65 us
    ppermute x2, waiting for transfers between devices, short(): return jnp.concatenate([lax.ppermute(x[:few], 'leaf', swap), x[few:]])  8.55 us
    ppermute x2, waiting for transfers between devices, to_other_head(): return lax.ppermute(x, 'head', [(0, 1), (1, 0)])  7.1 us
    all_to_all x1, starting transfers between devices, exchange_both(): lax.all_to_all(x, ('head', 'leaf'), 0, 0, tiled=True, axis_index_groups=b...  6.29 us
  transfers between devices with their start and end apart: 9, of which 7 were waited for; matrix products, arithmetic and copies ran while one was open for 0% of the time, Pallas kernels for 19%

profile of v11, /device:TPU:0, one launch (start us, length us, event | category | flops | bytes accessed | tf_op | source)
XLA Modules:
  0.0 100.5 jit_solution(10141879351202492863)
XLA Ops:
  0.6 2.1 %shard_map.76 = (bf16[16,2,16,512]{3,2,1,0:T(8,128)(2,1)}, bf16[2,2,64,512]{3,2,1,0:T(8,128)(2,1)}, bf16[2,2,64,512]{3,2,1,0:T(8,128)(2,1)}, s32[1,32]{1,0:T(1,128)}) custom-call(s32[2]{0:T(128)} %parents.1, bf16[2,64,1024]{2,1,0:T(8,128)(2,1)} %keys_ref.1, bf16[2,64,1024]{2,1,0:T(8,128)(2,1)} %values_ref.1), custom_call_target="tpu_custom_call" | custom-call | tf_op jit(solution)/shard_map/pallas_call | solution.py:329
  2.7 6.3 %all-to-all-start = ((bf16[16,2,16,512]{3,2,1,0:T(8,128)(2,1)}), bf16[16,2,16,512]{3,2,1,0:T(8,128)(2,1)S(1)}, u32[]{:S(2)}, u32[]{:S(2)}) async-start(bf16[16,2,16,512]{3,2,1,0:T(8,128)(2,1)} %get-tuple-element.42), calls=%async_computation | async-start | bytes 1048576 | tf_op jit(solution)/shard_map/all_to_all | solution.py:357
  9.0 1.9 %collective-permute-start.4 = (bf16[2,2,64,512]{3,2,1,0:T(8,128)(2,1)}, bf16[2,2,64,512]{3,2,1,0:T(8,128)(2,1)S(1)}, u32[]{:S(2)}, u32[]{:S(2)}) collective-permute-start(bf16[2,2,64,512]{3,2,1,0:T(8,128)(2,1)} %get-tuple-element.44), channel_id=1, source_target_pairs={{0,16},{16,0},{1,17},{17,1},{2,18},{18,2},{3,19},{19,3},{4,20},{20... | collective-permute-start | bytes 786440 | tf_op jit(solution)/shard_map/ppermute | solution.py:360
  10.9 14.1 %psum.7.parents = s32[1,32]{1,0:T(1,128)S(1)} all-reduce(s32[1,32]{1,0:T(1,128)} %get-tuple-element.43), channel_id=1, replica_groups=mesh['head'=2,'leaf'=16] {'leaf'}, use_global_device_ids=true, to_apply=%region_0.0 | all-reduce | flops 32 | bytes 256 | tf_op jit(solution)/shard_map/psum | solution.py:379
  25.1 0.0 collective-permute-done.4.refs_1_
  25.1 0.0 all-to-all-done
  25.1 0.1 copy.13
  25.1 1.5 %shard_map.77 = bf16[8,2,2,16,512]{4,3,2,1,0:T(8,128)(2,1)} custom-call(s32[1,32]{1,0:T(1,128)S(1)} %psum.7.parents, bf16[8,2,2,16,512]{4,3,2,1,0:T(8,128)(2,1)S(1)} %bitcast.7), custom_call_target="tpu_custom_call" | custom-call | tf_op jit(solution)/shard_map/pallas_call | solution.py:329
  26.6 3.5 %all-to-all-start.1 = ((bf16[8,2,2,16,512]{4,3,2,1,0:T(8,128)(2,1)}), bf16[8,2,2,16,512]{4,3,2,1,0:T(8,128)(2,1)S(1)}, u32[]{:S(2)}, u32[]{:S(2)}) async-start(bf16[8,2,2,16,512]{4,3,2,1,0:T(8,128)(2,1)} %shard_map.77), calls=%async_computation.1 | async-start | bytes 1048576 | tf_op jit(solution)/shard_map/all_to_all | solution.py:354
  30.1 0.0 copy-start
  30.1 1.5 %shard_map.78 = (bf16[8,2,16,512]{3,2,1,0:T(8,128)(2,1)S(1)}, s32[16]{0:T(128)S(1)}, s32[1]{0:T(128)}) custom-call(s32[1,32]{1,0:T(1,128)S(1)} %psum.7.parents, bf16[8,2,2,16,512]{4,3,2,1,0:T(8,128)(2,1)S(1)} %bitcast.8), custom_call_target="tpu_custom_call" | custom-call | tf_op jit(solution)/shard_map/pallas_call | solution.py:329
  32.3 5.9 %conditional.2 = (bf16[8,2,16,512]{3,2,1,0:T(8,128)(2,1)S(1)}) conditional(s32[]{:T(128)} %bitcast.4, bf16[8,2,16,512]{3,2,1,0:T(8,128)(2,1)S(1)} %get-tuple-element.51, bf16[8,2,16,512]{3,2,1,0:T(8,128)(2,1)S(1)} %get-tuple-element.51), branch_computations={%region_1.0_spmd, %region_2.0_spmd} | conditional | flops 131072 | bytes 1310768 | solution.py:401
  32.3 1.1 %collective-permute-start.2 = (bf16[2,2,16,512]{3,2,1,0:T(8,128)(2,1)S(1)}, bf16[2,2,16,512]{3,2,1,0:T(8,128)(2,1)S(1)}, u32[]{:S(2)}, u32[]{:S(2)}) collective-permute-start(bf16[2,2,16,512]{3,2,1,0:T(8,128)(2,1)S(1)} %slice.8), channel_id=1, source_target_pairs={{0,8},{1,9},{2,10},{3,11},{4,12},{5,13},{6,14},{7,15},{8,0},{9,1},... | collective-permute-start | bytes 196616 | tf_op jit(solution)/shard_map/cond/branch_1_fun/ppermute | solution.py:399
  33.4 4.8 %collective-permute-done.2 = bf16[2,2,16,512]{3,2,1,0:T(8,128)(2,1)S(1)} collective-permute-done((bf16[2,2,16,512]{3,2,1,0:T(8,128)(2,1)S(1)}, bf16[2,2,16,512]{3,2,1,0:T(8,128)(2,1)S(1)}, u32[]{:S(2)}, u32[]{:S(2)}) %collective-permute-start.2) | collective-permute-done | bytes 65568 | tf_op jit(solution)/shard_map/cond/branch_1_fun/ppermute | solution.py:399
  38.2 1.5 %shard_map.79 = bf16[8,2,2,16,512]{4,3,2,1,0:T(8,128)(2,1)} custom-call(s32[1,32]{1,0:T(1,128)S(1)} %psum.7.parents, s32[16]{0:T(128)S(1)} %get-tuple-element.49.slots, bf16[8,2,2,16,512]{4,3,2,1,0:T(8,128)(2,1)S(1)} %bitcast.9, bf16[8,2,16,512]{3,2,1,0:T(8,128)(2,1)S(1)} %get-tuple-element.71.cross_ref), custom_call_target="tpu_custom_call" | custom-call | tf_op jit(solution)/shard_map/pallas_call | solution.py:329
  39.7 0.5 all-to-all-done.1.refs_2_
  40.3 4.8 %all-to-all-start.2 = ((bf16[8,2,2,16,512]{4,3,2,1,0:T(8,128)(2,1)}), bf16[8,2,2,16,512]{4,3,2,1,0:T(8,128)(2,1)S(1)}, u32[]{:S(2)}, u32[]{:S(2)}) async-start(bf16[8,2,2,16,512]{4,3,2,1,0:T(8,128)(2,1)} %shard_map.79), calls=%async_computation.2 | async-start | bytes 1048576 | tf_op jit(solution)/shard_map/all_to_all | solution.py:354
  45.1 0.0 copy-done
  45.1 7.5 %shard_map.80 = (bf16[2,128,4096]{2,1,0:T(8,128)(2,1)}, bf16[2,2,64,512]{3,2,1,0:T(8,128)(2,1)S(1)}, bf16[2,2,64,512]{3,2,1,0:T(8,128)(2,1)S(1)}, bf16[8,2,2,16,512]{4,3,2,1,0:T(8,128)(2,1)}) custom-call(s32[1,32]{1,0:T(1,128)S(1)} %psum.7.parents, bf16[2,128,4096]{2,1,0:T(8,128)(2,1)} %q_ref.3, bf16[2,128,4096]{2,1,0:T(8,128)(2,1)} %do_ref.3, ...), custom_call_target="tpu_custom_call" | custom-call | flops 2013265920 | bytes 3145728 | tf_op jit(solution)/shard_map/pallas_call | solution.py:129
  52.6 1.3 %all-to-all-done.2.refs_2_ = bf16[8,2,2,16,512]{4,3,2,1,0:T(8,128)(2,1)S(1)} async-done(((bf16[8,2,2,16,512]{4,3,2,1,0:T(8,128)(2,1)}), bf16[8,2,2,16,512]{4,3,2,1,0:T(8,128)(2,1)S(1)}, u32[]{:S(2)}, u32[]{:S(2)}) %all-to-all-start.2) | async-done | bytes 524320 | tf_op jit(solution)/shard_map/all_to_all | solution.py:354
  53.9 3.5 %all-to-all-start.3 = ((bf16[8,2,2,16,512]{4,3,2,1,0:T(8,128)(2,1)}), bf16[8,2,2,16,512]{4,3,2,1,0:T(8,128)(2,1)S(1)}, u32[]{:S(2)}, u32[]{:S(2)}) async-start(bf16[8,2,2,16,512]{4,3,2,1,0:T(8,128)(2,1)} %get-tuple-element.58), calls=%async_computation.3 | async-start | bytes 1048576 | tf_op jit(solution)/shard_map/all_to_all | solution.py:354
  57.4 7.5 %shard_map.81 = (bf16[2,128,4096]{2,1,0:T(8,128)(2,1)}, bf16[2,2,64,512]{3,2,1,0:T(8,128)(2,1)S(1)}, bf16[2,2,64,512]{3,2,1,0:T(8,128)(2,1)S(1)}, bf16[8,2,2,16,512]{4,3,2,1,0:T(8,128)(2,1)}) custom-call(s32[1,32]{1,0:T(1,128)S(1)} %psum.7.parents, bf16[2,128,4096]{2,1,0:T(8,128)(2,1)} %q_ref.3, ...), custom_call_target="tpu_custom_call", output_to_operand_aliasing={{0}: (6, {}), {1}: (7, {}), {2}: (8, {})} | custom-call | flops 2013265920 | bytes 3145728 | tf_op jit(solution)/shard_map/pallas_call | solution.py:129
  65.0 1.2 %all-to-all-done.3.in_ref = bf16[8,2,2,16,512]{4,3,2,1,0:T(8,128)(2,1)S(1)} async-done(((bf16[8,2,2,16,512]{4,3,2,1,0:T(8,128)(2,1)}), bf16[8,2,2,16,512]{4,3,2,1,0:T(8,128)(2,1)S(1)}, u32[]{:S(2)}, u32[]{:S(2)}) %all-to-all-start.3) | async-done | bytes 524320 | tf_op jit(solution)/shard_map/all_to_all | solution.py:354
  66.2 3.5 %all-to-all-start.4 = ((bf16[8,2,2,16,512]{4,3,2,1,0:T(8,128)(2,1)}), bf16[8,2,2,16,512]{4,3,2,1,0:T(8,128)(2,1)S(1)}, u32[]{:S(2)}, u32[]{:S(2)}) async-start(bf16[8,2,2,16,512]{4,3,2,1,0:T(8,128)(2,1)} %get-tuple-element.60), calls=%async_computation.4 | async-start | bytes 1048576 | tf_op jit(solution)/shard_map/all_to_all | solution.py:354
  69.7 0.8 collective-permute-start.5
  70.5 0.7 shard_map.82.near_ref
  71.2 7.1 %collective-permute-done.5.own_got_ref = bf16[2,2,64,512]{3,2,1,0:T(8,128)(2,1)S(1)} collective-permute-done((bf16[2,2,64,512]{3,2,1,0:T(8,128)(2,1)S(1)}, bf16[2,2,64,512]{3,2,1,0:T(8,128)(2,1)S(1)}, u32[]{:S(2)}, u32[]{:S(2)}) %collective-permute-start.5) | collective-permute-done | bytes 262176 | tf_op jit(solution)/shard_map/ppermute | solution.py:360
  78.3 0.1 all-to-all-done.4.in_ref
  78.5 0.8 shard_map.83
  79.3 5.4 %conditional.3 = (bf16[8,2,16,512]{3,2,1,0:T(8,128)(2,1)S(1)}) conditional(s32[]{:T(128)} %bitcast.4, bf16[8,2,16,512]{3,2,1,0:T(8,128)(2,1)S(1)} %get-tuple-element.66, bf16[8,2,16,512]{3,2,1,0:T(8,128)(2,1)S(1)} %get-tuple-element.66), branch_computations={%region_3.0_spmd, %region_4.0_spmd} | conditional | flops 131072 | bytes 1310768 | solution.py:401
  79.3 1.5 %collective-permute-start.3 = (bf16[2,2,16,512]{3,2,1,0:T(8,128)(2,1)S(1)}, bf16[2,2,16,512]{3,2,1,0:T(8,128)(2,1)S(1)}, u32[]{:S(2)}, u32[]{:S(2)}) collective-permute-start(bf16[2,2,16,512]{3,2,1,0:T(8,128)(2,1)S(1)} %slice.10), channel_id=1, source_target_pairs={{0,8},{1,9},{2,10},{3,11},{4,12},{5,13},{6,14},{7,15},{8,0},{9,1},... | collective-permute-start | bytes 196616 | tf_op jit(solution)/shard_map/cond/branch_1_fun/ppermute | solution.py:399
  80.8 3.8 %collective-permute-done.3 = bf16[2,2,16,512]{3,2,1,0:T(8,128)(2,1)S(1)} collective-permute-done((bf16[2,2,16,512]{3,2,1,0:T(8,128)(2,1)S(1)}, bf16[2,2,16,512]{3,2,1,0:T(8,128)(2,1)S(1)}, u32[]{:S(2)}, u32[]{:S(2)}) %collective-permute-start.3) | collective-permute-done | bytes 65568 | tf_op jit(solution)/shard_map/cond/branch_1_fun/ppermute | solution.py:399
  84.6 0.7 shard_map.84
  85.3 14.3 %all_to_all.30.got_ref = bf16[16,2,16,512]{3,2,1,0:T(8,128)(2,1)S(1)} all-to-all(bf16[16,2,16,512]{3,2,1,0:T(8,128)(2,1)S(1)} %shard_map.84), channel_id=1, replica_groups={{0,1,2,3,4,5,6,7,16,17,18,19,20,21,22,23},{8,9,10,11,12,13,14,15,24,25,..., dimensions={0} | all-to-all | bytes 1048576 | tf_op jit(solution)/shard_map/all_to_all | solution.py:357
  99.6 0.9 shard_map.85
  (6 shorter events, 0.1 us)
Async XLA Ops:
  2.7 22.4 %all-to-all-start = ((bf16[16,2,16,512]{3,2,1,0:T(8,128)(2,1)}), bf16[16,2,16,512]{3,2,1,0:T(8,128)(2,1)S(1)}, u32[]{:S(2)}, u32[]{:S(2)}) async-start(bf16[16,2,16,512]{3,2,1,0:T(8,128)(2,1)} %get-tuple-element.42), calls=%async_computation | async-start | bytes 1048576 | tf_op jit(solution)/shard_map/all_to_all | solution.py:357
  9.0 16.1 %collective-permute-start.4 = (bf16[2,2,64,512]{3,2,1,0:T(8,128)(2,1)}, bf16[2,2,64,512]{3,2,1,0:T(8,128)(2,1)S(1)}, u32[]{:S(2)}, u32[]{:S(2)}) collective-permute-start(bf16[2,2,64,512]{3,2,1,0:T(8,128)(2,1)} %get-tuple-element.44), channel_id=1, source_target_pairs={{0,16},{16,0},{1,17},{17,1},{2,18},{18,2},{3,19},{19,3},{4,20},{20... | collective-permute-start | bytes 786440 | tf_op jit(solution)/shard_map/ppermute | solution.py:360
  26.6 13.7 %all-to-all-start.1 = ((bf16[8,2,2,16,512]{4,3,2,1,0:T(8,128)(2,1)}), bf16[8,2,2,16,512]{4,3,2,1,0:T(8,128)(2,1)S(1)}, u32[]{:S(2)}, u32[]{:S(2)}) async-start(bf16[8,2,2,16,512]{4,3,2,1,0:T(8,128)(2,1)} %shard_map.77), calls=%async_computation.1 | async-start | bytes 1048576 | tf_op jit(solution)/shard_map/all_to_all | solution.py:354
  30.1 15.0 %copy-start = (bf16[2,2,64,512]{3,2,1,0:T(8,128)(2,1)S(1)}, bf16[2,2,64,512]{3,2,1,0:T(8,128)(2,1)}, u32[]{:S(2)}) copy-start(bf16[2,2,64,512]{3,2,1,0:T(8,128)(2,1)} %get-tuple-element.46.refs_0_) | copy-start | bytes 786436
  32.3 5.8 %collective-permute-start.2 = (bf16[2,2,16,512]{3,2,1,0:T(8,128)(2,1)S(1)}, bf16[2,2,16,512]{3,2,1,0:T(8,128)(2,1)S(1)}, u32[]{:S(2)}, u32[]{:S(2)}) collective-permute-start(bf16[2,2,16,512]{3,2,1,0:T(8,128)(2,1)S(1)} %slice.8), channel_id=1, source_target_pairs={{0,8},{1,9},{2,10},{3,11},{4,12},{5,13},{6,14},{7,15},{8,0},{9,1},... | collective-permute-start | bytes 196616 | tf_op jit(solution)/shard_map/cond/branch_1_fun/ppermute | solution.py:399
  40.3 13.7 %all-to-all-start.2 = ((bf16[8,2,2,16,512]{4,3,2,1,0:T(8,128)(2,1)}), bf16[8,2,2,16,512]{4,3,2,1,0:T(8,128)(2,1)S(1)}, u32[]{:S(2)}, u32[]{:S(2)}) async-start(bf16[8,2,2,16,512]{4,3,2,1,0:T(8,128)(2,1)} %shard_map.79), calls=%async_computation.2 | async-start | bytes 1048576 | tf_op jit(solution)/shard_map/all_to_all | solution.py:354
  53.9 12.3 %all-to-all-start.3 = ((bf16[8,2,2,16,512]{4,3,2,1,0:T(8,128)(2,1)}), bf16[8,2,2,16,512]{4,3,2,1,0:T(8,128)(2,1)S(1)}, u32[]{:S(2)}, u32[]{:S(2)}) async-start(bf16[8,2,2,16,512]{4,3,2,1,0:T(8,128)(2,1)} %get-tuple-element.58), calls=%async_computation.3 | async-start | bytes 1048576 | tf_op jit(solution)/shard_map/all_to_all | solution.py:354
  66.2 12.3 %all-to-all-start.4 = ((bf16[8,2,2,16,512]{4,3,2,1,0:T(8,128)(2,1)}), bf16[8,2,2,16,512]{4,3,2,1,0:T(8,128)(2,1)S(1)}, u32[]{:S(2)}, u32[]{:S(2)}) async-start(bf16[8,2,2,16,512]{4,3,2,1,0:T(8,128)(2,1)} %get-tuple-element.60), calls=%async_computation.4 | async-start | bytes 1048576 | tf_op jit(solution)/shard_map/all_to_all | solution.py:354
  69.7 8.6 %collective-permute-start.5 = (bf16[2,2,64,512]{3,2,1,0:T(8,128)(2,1)S(1)}, bf16[2,2,64,512]{3,2,1,0:T(8,128)(2,1)S(1)}, u32[]{:S(2)}, u32[]{:S(2)}) collective-permute-start(bf16[2,2,64,512]{3,2,1,0:T(8,128)(2,1)S(1)} %get-tuple-element.62), channel_id=1, source_target_pairs={{0,16},{16,0},{1,17},{17,1},{2,18},{18,2},{3,19},{19,3},{4,20},{20... | collective-permute-start | bytes 786440 | tf_op jit(solution)/shard_map/ppermute | solution.py:360
  79.3 5.3 %collective-permute-start.3 = (bf16[2,2,16,512]{3,2,1,0:T(8,128)(2,1)S(1)}, bf16[2,2,16,512]{3,2,1,0:T(8,128)(2,1)S(1)}, u32[]{:S(2)}, u32[]{:S(2)}) collective-permute-start(bf16[2,2,16,512]{3,2,1,0:T(8,128)(2,1)S(1)} %slice.10), channel_id=1, source_target_pairs={{0,8},{1,9},{2,10},{3,11},{4,12},{5,13},{6,14},{7,15},{8,0},{9,1},... | collective-permute-start | bytes 196616 | tf_op jit(solution)/shard_map/cond/branch_1_fun/ppermute | solution.py:399

commit v12 on v11

--- a/solution.py
+++ b/solution.py
@@ -205,19 +205,19 @@
     lax.fori_loop(0, count, step, 0, unroll=count <= 8)
 
 
-def each_need(parents, half, depth, trees, act):
+def each_need(parents, half, depth, trees, act, first=0, count=None):
     base = (leaf_rank() // half) * half
 
     def leaf(d):
         for i, t in enumerate(trees):
-            block = 2 * (base + d) + t
+            block = 2 * (base + first + d) + t
             for k in range(depth):
                 block = above(parents, block)
                 p = jnp.maximum(block, 0) // 2
                 here = (p >= base) & (p < base + half)
                 act(d, i * depth + k, block >= 0, here, lax.rem(p, half), t)
 
-    each(half, leaf)
+    each(count or half, leaf)
 
 
 def cross_kernel(depth, parents, own_ref, cross_ref, slots, count):
@@ -244,7 +244,8 @@
     def act(d, k, valid, here, p, t):
         out_ref[d, k] = own_ref[p, :, t]
 
-    each_need(parents, half, depth, (near,), act)
+    count = out_ref.shape[0]
+    each_need(parents, half, depth, (near,), act, pl.program_id(0) * count, count)
 
 
 def pick_far_kernel(depth, parents, slots, own_ref, cross_ref, out_ref):
@@ -255,7 +256,8 @@
         crossed = cross_ref[jnp.maximum(slots[p], 0)]
         out_ref[d, k] = jnp.where(here | ~valid, own_ref[p, :, t], crossed)
 
-    each_need(parents, half, depth, (far,), act)
+    count = out_ref.shape[0]
+    each_need(parents, half, depth, (far,), act, pl.program_id(0) * count, count)
 
 
 def collect_near_kernel(depth, parents, in_ref, sums):
@@ -323,12 +325,14 @@
     return pl.BlockSpec(shape, lambda i: (0,) * len(shape))
 
 
-def simple(kernel, scalars, arrays, outs, slots=(), params=PARAMS):
-    out_specs = [whole(x.shape) for x in outs] + [SMEM] * len(slots)
+def simple(kernel, scalars, arrays, outs, slots=(), steps=1, params=PARAMS):
+    out_specs = [
+        pl.BlockSpec((x.shape[0] // steps,) + x.shape[1:], lambda i, n=len(x.shape): (i,) + (0,) * (n - 1)) for x in outs
+    ] + [SMEM] * len(slots)
     outs = list(outs) + [jax.ShapeDtypeStruct((x,), jnp.int32) for x in slots]
     return pl.pallas_call(
         kernel,
-        grid=(1,),
+        grid=(steps,),
         in_specs=[SMEM] * len(scalars) + [whole(x.shape) for x in arrays],
         out_specs=out_specs,
         out_shape=outs,
@@ -401,7 +405,7 @@
         return lax.cond(count[0] <= few, short, lambda: lax.ppermute(x, "leaf", swap))
 
     picked_shape = [like(half, depth, *piece)]
-    (picked_near,) = simple(functools.partial(pick_near_kernel, depth), (all_parents,), (hub_own,), picked_shape)
+    (picked_near,) = simple(functools.partial(pick_near_kernel, depth), (all_parents,), (hub_own,), picked_shape, steps=2)
     foreign_near = exchange(picked_near)
     crossing, slots, count = simple(
         functools.partial(cross_kernel, depth),
@@ -411,7 +415,7 @@
         slots=(2 * half, 1),
     )
     (picked_far,) = simple(
-        functools.partial(pick_far_kernel, depth), (all_parents, slots), (hub_own, cross(crossing)), picked_shape
+        functools.partial(pick_far_kernel, depth), (all_parents, slots), (hub_own, cross(crossing)), picked_shape, steps=2
     )
     foreign_near, picked_far = lax.optimization_barrier((foreign_near, picked_far))
     foreign_far = exchange(picked_far)

time: 101 us -> 101 us (level)
  no operation moved by 1% of the time
where the time goes in v12:
time: 101 us; the launch traced here: 100 us
  blocking collectives  28.4 us (28%)
  starting transfers between devices  26.9 us (27%)
  Pallas kernels  24.7 us (24%)
  waiting for transfers between devices  18.9 us (19%)
  between operations  1.37 us (1%)
    all_to_all x4, starting transfers between devices, exchange(): return lax.all_to_all(x, 'leaf', 0, 0, tiled=True, axis_index_groups=sides)  15.3 us
    pallas_call x2, Pallas kernels, attend(): pl.pallas_call(functools.partial(attend_kernel, len(owns), tree), grid=(g...  15.1 us
    all_to_all x1, blocking collectives, exchange_both(): lax.all_to_all(x, ('head', 'leaf'), 0, 0, tiled=True, axis_index_groups=b...  14.3 us
    psum x1, blocking collectives, body(): lax.psum(table, 'leaf')  14.1 us
    pallas_call x8, Pallas kernels, simple(): pl.pallas_call(kernel, grid=(steps,), in_specs=[SMEM] * len(scalars) + [w...  9.64 us
    ppermute x2, waiting for transfers between devices, short(): return jnp.concatenate([lax.ppermute(x[:few], 'leaf', swap), x[few:]])  8.55 us
    ppermute x2, waiting for transfers between devices, to_other_head(): return lax.ppermute(x, 'head', [(0, 1), (1, 0)])  7.1 us
    all_to_all x1, starting transfers between devices, exchange_both(): lax.all_to_all(x, ('head', 'leaf'), 0, 0, tiled=True, axis_index_groups=b...  6.29 us
  transfers between devices with their start and end apart: 9, of which 7 were waited for; matrix products, arithmetic and copies ran while one was open for 0% of the time, Pallas kernels for 19%

profile of v12, /device:TPU:0, one launch (start us, length us, event | category | flops | bytes accessed | tf_op | source)
XLA Modules:
  0.0 100.5 jit_solution(11755915359908700132)
XLA Ops:
  0.6 2.1 %shard_map.76 = (bf16[16,2,16,512]{3,2,1,0:T(8,128)(2,1)}, bf16[2,2,64,512]{3,2,1,0:T(8,128)(2,1)}, bf16[2,2,64,512]{3,2,1,0:T(8,128)(2,1)}, s32[1,32]{1,0:T(1,128)}) custom-call(s32[2]{0:T(128)} %parents.1, bf16[2,64,1024]{2,1,0:T(8,128)(2,1)} %keys_ref.1, bf16[2,64,1024]{2,1,0:T(8,128)(2,1)} %values_ref.1), custom_call_target="tpu_custom_call" | custom-call | tf_op jit(solution)/shard_map/pallas_call | solution.py:333
  2.7 6.3 %all-to-all-start = ((bf16[16,2,16,512]{3,2,1,0:T(8,128)(2,1)}), bf16[16,2,16,512]{3,2,1,0:T(8,128)(2,1)S(1)}, u32[]{:S(2)}, u32[]{:S(2)}) async-start(bf16[16,2,16,512]{3,2,1,0:T(8,128)(2,1)} %get-tuple-element.42), calls=%async_computation | async-start | bytes 1048576 | tf_op jit(solution)/shard_map/all_to_all | solution.py:361
  9.0 1.9 %collective-permute-start.4 = (bf16[2,2,64,512]{3,2,1,0:T(8,128)(2,1)}, bf16[2,2,64,512]{3,2,1,0:T(8,128)(2,1)S(1)}, u32[]{:S(2)}, u32[]{:S(2)}) collective-permute-start(bf16[2,2,64,512]{3,2,1,0:T(8,128)(2,1)} %get-tuple-element.44), channel_id=1, source_target_pairs={{0,16},{16,0},{1,17},{17,1},{2,18},{18,2},{3,19},{19,3},{4,20},{20... | collective-permute-start | bytes 786440 | tf_op jit(solution)/shard_map/ppermute | solution.py:364
  10.9 14.1 %psum.7.parents = s32[1,32]{1,0:T(1,128)S(1)} all-reduce(s32[1,32]{1,0:T(1,128)} %get-tuple-element.43), channel_id=1, replica_groups=mesh['head'=2,'leaf'=16] {'leaf'}, use_global_device_ids=true, to_apply=%region_0.0 | all-reduce | flops 32 | bytes 256 | tf_op jit(solution)/shard_map/psum | solution.py:383
  25.1 0.0 collective-permute-done.4.refs_1_
  25.1 0.0 all-to-all-done
  25.1 0.1 copy.13
  25.1 1.5 %shard_map.77 = bf16[8,2,2,16,512]{4,3,2,1,0:T(8,128)(2,1)} custom-call(s32[1,32]{1,0:T(1,128)S(1)} %psum.7.parents, bf16[8,2,2,16,512]{4,3,2,1,0:T(8,128)(2,1)S(1)} %bitcast.7), custom_call_target="tpu_custom_call" | custom-call | tf_op jit(solution)/shard_map/pallas_call | solution.py:333
  26.6 3.5 %all-to-all-start.1 = ((bf16[8,2,2,16,512]{4,3,2,1,0:T(8,128)(2,1)}), bf16[8,2,2,16,512]{4,3,2,1,0:T(8,128)(2,1)S(1)}, u32[]{:S(2)}, u32[]{:S(2)}) async-start(bf16[8,2,2,16,512]{4,3,2,1,0:T(8,128)(2,1)} %shard_map.77), calls=%async_computation.1 | async-start | bytes 1048576 | tf_op jit(solution)/shard_map/all_to_all | solution.py:358
  30.1 0.0 copy-start
  30.1 1.5 %shard_map.78 = (bf16[8,2,16,512]{3,2,1,0:T(8,128)(2,1)S(1)}, s32[16]{0:T(128)S(1)}, s32[1]{0:T(128)}) custom-call(s32[1,32]{1,0:T(1,128)S(1)} %psum.7.parents, bf16[8,2,2,16,512]{4,3,2,1,0:T(8,128)(2,1)S(1)} %bitcast.8), custom_call_target="tpu_custom_call" | custom-call | tf_op jit(solution)/shard_map/pallas_call | solution.py:333
  32.3 5.9 %conditional.2 = (bf16[8,2,16,512]{3,2,1,0:T(8,128)(2,1)S(1)}) conditional(s32[]{:T(128)} %bitcast.4, bf16[8,2,16,512]{3,2,1,0:T(8,128)(2,1)S(1)} %get-tuple-element.51, bf16[8,2,16,512]{3,2,1,0:T(8,128)(2,1)S(1)} %get-tuple-element.51), branch_computations={%region_1.0_spmd, %region_2.0_spmd} | conditional | flops 131072 | bytes 1310768 | solution.py:405
  32.3 1.1 %collective-permute-start.2 = (bf16[2,2,16,512]{3,2,1,0:T(8,128)(2,1)S(1)}, bf16[2,2,16,512]{3,2,1,0:T(8,128)(2,1)S(1)}, u32[]{:S(2)}, u32[]{:S(2)}) collective-permute-start(bf16[2,2,16,512]{3,2,1,0:T(8,128)(2,1)S(1)} %slice.8), channel_id=1, source_target_pairs={{0,8},{1,9},{2,10},{3,11},{4,12},{5,13},{6,14},{7,15},{8,0},{9,1},... | collective-permute-start | bytes 196616 | tf_op jit(solution)/shard_map/cond/branch_1_fun/ppermute | solution.py:403
  33.4 4.8 %collective-permute-done.2 = bf16[2,2,16,512]{3,2,1,0:T(8,128)(2,1)S(1)} collective-permute-done((bf16[2,2,16,512]{3,2,1,0:T(8,128)(2,1)S(1)}, bf16[2,2,16,512]{3,2,1,0:T(8,128)(2,1)S(1)}, u32[]{:S(2)}, u32[]{:S(2)}) %collective-permute-start.2) | collective-permute-done | bytes 65568 | tf_op jit(solution)/shard_map/cond/branch_1_fun/ppermute | solution.py:403
  38.2 1.5 %shard_map.79 = bf16[8,2,2,16,512]{4,3,2,1,0:T(8,128)(2,1)} custom-call(s32[1,32]{1,0:T(1,128)S(1)} %psum.7.parents, s32[16]{0:T(128)S(1)} %get-tuple-element.49.slots, bf16[8,2,2,16,512]{4,3,2,1,0:T(8,128)(2,1)S(1)} %bitcast.9, bf16[8,2,16,512]{3,2,1,0:T(8,128)(2,1)S(1)} %get-tuple-element.71.cross_ref), custom_call_target="tpu_custom_call" | custom-call | tf_op jit(solution)/shard_map/pallas_call | solution.py:333
  39.7 0.5 all-to-all-done.1.refs_2_
  40.2 4.8 %all-to-all-start.2 = ((bf16[8,2,2,16,512]{4,3,2,1,0:T(8,128)(2,1)}), bf16[8,2,2,16,512]{4,3,2,1,0:T(8,128)(2,1)S(1)}, u32[]{:S(2)}, u32[]{:S(2)}) async-start(bf16[8,2,2,16,512]{4,3,2,1,0:T(8,128)(2,1)} %shard_map.79), calls=%async_computation.2 | async-start | bytes 1048576 | tf_op jit(solution)/shard_map/all_to_all | solution.py:358
  45.1 0.0 copy-done
  45.1 7.5 %shard_map.80 = (bf16[2,128,4096]{2,1,0:T(8,128)(2,1)}, bf16[2,2,64,512]{3,2,1,0:T(8,128)(2,1)S(1)}, bf16[2,2,64,512]{3,2,1,0:T(8,128)(2,1)S(1)}, bf16[8,2,2,16,512]{4,3,2,1,0:T(8,128)(2,1)}) custom-call(s32[1,32]{1,0:T(1,128)S(1)} %psum.7.parents, bf16[2,128,4096]{2,1,0:T(8,128)(2,1)} %q_ref.3, bf16[2,128,4096]{2,1,0:T(8,128)(2,1)} %do_ref.3, ...), custom_call_target="tpu_custom_call" | custom-call | flops 2013265920 | bytes 3145728 | tf_op jit(solution)/shard_map/pallas_call | solution.py:129
  52.6 1.3 %all-to-all-done.2.refs_2_ = bf16[8,2,2,16,512]{4,3,2,1,0:T(8,128)(2,1)S(1)} async-done(((bf16[8,2,2,16,512]{4,3,2,1,0:T(8,128)(2,1)}), bf16[8,2,2,16,512]{4,3,2,1,0:T(8,128)(2,1)S(1)}, u32[]{:S(2)}, u32[]{:S(2)}) %all-to-all-start.2) | async-done | bytes 524320 | tf_op jit(solution)/shard_map/all_to_all | solution.py:358
  53.9 3.5 %all-to-all-start.3 = ((bf16[8,2,2,16,512]{4,3,2,1,0:T(8,128)(2,1)}), bf16[8,2,2,16,512]{4,3,2,1,0:T(8,128)(2,1)S(1)}, u32[]{:S(2)}, u32[]{:S(2)}) async-start(bf16[8,2,2,16,512]{4,3,2,1,0:T(8,128)(2,1)} %get-tuple-element.58), calls=%async_computation.3 | async-start | bytes 1048576 | tf_op jit(solution)/shard_map/all_to_all | solution.py:358
  57.4 7.5 %shard_map.81 = (bf16[2,128,4096]{2,1,0:T(8,128)(2,1)}, bf16[2,2,64,512]{3,2,1,0:T(8,128)(2,1)S(1)}, bf16[2,2,64,512]{3,2,1,0:T(8,128)(2,1)S(1)}, bf16[8,2,2,16,512]{4,3,2,1,0:T(8,128)(2,1)}) custom-call(s32[1,32]{1,0:T(1,128)S(1)} %psum.7.parents, bf16[2,128,4096]{2,1,0:T(8,128)(2,1)} %q_ref.3, ...), custom_call_target="tpu_custom_call", output_to_operand_aliasing={{0}: (6, {}), {1}: (7, {}), {2}: (8, {})} | custom-call | flops 2013265920 | bytes 3145728 | tf_op jit(solution)/shard_map/pallas_call | solution.py:129
  65.0 1.2 %all-to-all-done.3.in_ref = bf16[8,2,2,16,512]{4,3,2,1,0:T(8,128)(2,1)S(1)} async-done(((bf16[8,2,2,16,512]{4,3,2,1,0:T(8,128)(2,1)}), bf16[8,2,2,16,512]{4,3,2,1,0:T(8,128)(2,1)S(1)}, u32[]{:S(2)}, u32[]{:S(2)}) %all-to-all-start.3) | async-done | bytes 524320 | tf_op jit(solution)/shard_map/all_to_all | solution.py:358
  66.2 3.5 %all-to-all-start.4 = ((bf16[8,2,2,16,512]{4,3,2,1,0:T(8,128)(2,1)}), bf16[8,2,2,16,512]{4,3,2,1,0:T(8,128)(2,1)S(1)}, u32[]{:S(2)}, u32[]{:S(2)}) async-start(bf16[8,2,2,16,512]{4,3,2,1,0:T(8,128)(2,1)} %get-tuple-element.60), calls=%async_computation.4 | async-start | bytes 1048576 | tf_op jit(solution)/shard_map/all_to_all | solution.py:358
  69.7 0.8 collective-permute-start.5
  70.5 0.7 shard_map.82.near_ref
  71.2 7.1 %collective-permute-done.5.own_got_ref = bf16[2,2,64,512]{3,2,1,0:T(8,128)(2,1)S(1)} collective-permute-done((bf16[2,2,64,512]{3,2,1,0:T(8,128)(2,1)S(1)}, bf16[2,2,64,512]{3,2,1,0:T(8,128)(2,1)S(1)}, u32[]{:S(2)}, u32[]{:S(2)}) %collective-permute-start.5) | collective-permute-done | bytes 262176 | tf_op jit(solution)/shard_map/ppermute | solution.py:364
  78.3 0.1 all-to-all-done.4.in_ref
  78.5 0.8 shard_map.83
  79.3 5.4 %conditional.3 = (bf16[8,2,16,512]{3,2,1,0:T(8,128)(2,1)S(1)}) conditional(s32[]{:T(128)} %bitcast.4, bf16[8,2,16,512]{3,2,1,0:T(8,128)(2,1)S(1)} %get-tuple-element.66, bf16[8,2,16,512]{3,2,1,0:T(8,128)(2,1)S(1)} %get-tuple-element.66), branch_computations={%region_3.0_spmd, %region_4.0_spmd} | conditional | flops 131072 | bytes 1310768 | solution.py:405
  79.3 1.5 %collective-permute-start.3 = (bf16[2,2,16,512]{3,2,1,0:T(8,128)(2,1)S(1)}, bf16[2,2,16,512]{3,2,1,0:T(8,128)(2,1)S(1)}, u32[]{:S(2)}, u32[]{:S(2)}) collective-permute-start(bf16[2,2,16,512]{3,2,1,0:T(8,128)(2,1)S(1)} %slice.10), channel_id=1, source_target_pairs={{0,8},{1,9},{2,10},{3,11},{4,12},{5,13},{6,14},{7,15},{8,0},{9,1},... | collective-permute-start | bytes 196616 | tf_op jit(solution)/shard_map/cond/branch_1_fun/ppermute | solution.py:403
  80.8 3.8 %collective-permute-done.3 = bf16[2,2,16,512]{3,2,1,0:T(8,128)(2,1)S(1)} collective-permute-done((bf16[2,2,16,512]{3,2,1,0:T(8,128)(2,1)S(1)}, bf16[2,2,16,512]{3,2,1,0:T(8,128)(2,1)S(1)}, u32[]{:S(2)}, u32[]{:S(2)}) %collective-permute-start.3) | collective-permute-done | bytes 65568 | tf_op jit(solution)/shard_map/cond/branch_1_fun/ppermute | solution.py:403
  84.6 0.7 shard_map.84
  85.3 14.3 %all_to_all.30.got_ref = bf16[16,2,16,512]{3,2,1,0:T(8,128)(2,1)S(1)} all-to-all(bf16[16,2,16,512]{3,2,1,0:T(8,128)(2,1)S(1)} %shard_map.84), channel_id=1, replica_groups={{0,1,2,3,4,5,6,7,16,17,18,19,20,21,22,23},{8,9,10,11,12,13,14,15,24,25,..., dimensions={0} | all-to-all | bytes 1048576 | tf_op jit(solution)/shard_map/all_to_all | solution.py:361
  99.6 0.9 shard_map.85
  (6 shorter events, 0.1 us)
Async XLA Ops:
  2.7 22.4 %all-to-all-start = ((bf16[16,2,16,512]{3,2,1,0:T(8,128)(2,1)}), bf16[16,2,16,512]{3,2,1,0:T(8,128)(2,1)S(1)}, u32[]{:S(2)}, u32[]{:S(2)}) async-start(bf16[16,2,16,512]{3,2,1,0:T(8,128)(2,1)} %get-tuple-element.42), calls=%async_computation | async-start | bytes 1048576 | tf_op jit(solution)/shard_map/all_to_all | solution.py:361
  9.0 16.1 %collective-permute-start.4 = (bf16[2,2,64,512]{3,2,1,0:T(8,128)(2,1)}, bf16[2,2,64,512]{3,2,1,0:T(8,128)(2,1)S(1)}, u32[]{:S(2)}, u32[]{:S(2)}) collective-permute-start(bf16[2,2,64,512]{3,2,1,0:T(8,128)(2,1)} %get-tuple-element.44), channel_id=1, source_target_pairs={{0,16},{16,0},{1,17},{17,1},{2,18},{18,2},{3,19},{19,3},{4,20},{20... | collective-permute-start | bytes 786440 | tf_op jit(solution)/shard_map/ppermute | solution.py:364
  26.6 13.7 %all-to-all-start.1 = ((bf16[8,2,2,16,512]{4,3,2,1,0:T(8,128)(2,1)}), bf16[8,2,2,16,512]{4,3,2,1,0:T(8,128)(2,1)S(1)}, u32[]{:S(2)}, u32[]{:S(2)}) async-start(bf16[8,2,2,16,512]{4,3,2,1,0:T(8,128)(2,1)} %shard_map.77), calls=%async_computation.1 | async-start | bytes 1048576 | tf_op jit(solution)/shard_map/all_to_all | solution.py:358
  30.1 15.0 %copy-start = (bf16[2,2,64,512]{3,2,1,0:T(8,128)(2,1)S(1)}, bf16[2,2,64,512]{3,2,1,0:T(8,128)(2,1)}, u32[]{:S(2)}) copy-start(bf16[2,2,64,512]{3,2,1,0:T(8,128)(2,1)} %get-tuple-element.46.refs_0_) | copy-start | bytes 786436
  32.3 5.8 %collective-permute-start.2 = (bf16[2,2,16,512]{3,2,1,0:T(8,128)(2,1)S(1)}, bf16[2,2,16,512]{3,2,1,0:T(8,128)(2,1)S(1)}, u32[]{:S(2)}, u32[]{:S(2)}) collective-permute-start(bf16[2,2,16,512]{3,2,1,0:T(8,128)(2,1)S(1)} %slice.8), channel_id=1, source_target_pairs={{0,8},{1,9},{2,10},{3,11},{4,12},{5,13},{6,14},{7,15},{8,0},{9,1},... | collective-permute-start | bytes 196616 | tf_op jit(solution)/shard_map/cond/branch_1_fun/ppermute | solution.py:403
  40.2 13.7 %all-to-all-start.2 = ((bf16[8,2,2,16,512]{4,3,2,1,0:T(8,128)(2,1)}), bf16[8,2,2,16,512]{4,3,2,1,0:T(8,128)(2,1)S(1)}, u32[]{:S(2)}, u32[]{:S(2)}) async-start(bf16[8,2,2,16,512]{4,3,2,1,0:T(8,128)(2,1)} %shard_map.79), calls=%async_computation.2 | async-start | bytes 1048576 | tf_op jit(solution)/shard_map/all_to_all | solution.py:358
  53.9 12.3 %all-to-all-start.3 = ((bf16[8,2,2,16,512]{4,3,2,1,0:T(8,128)(2,1)}), bf16[8,2,2,16,512]{4,3,2,1,0:T(8,128)(2,1)S(1)}, u32[]{:S(2)}, u32[]{:S(2)}) async-start(bf16[8,2,2,16,512]{4,3,2,1,0:T(8,128)(2,1)} %get-tuple-element.58), calls=%async_computation.3 | async-start | bytes 1048576 | tf_op jit(solution)/shard_map/all_to_all | solution.py:358
  66.2 12.3 %all-to-all-start.4 = ((bf16[8,2,2,16,512]{4,3,2,1,0:T(8,128)(2,1)}), bf16[8,2,2,16,512]{4,3,2,1,0:T(8,128)(2,1)S(1)}, u32[]{:S(2)}, u32[]{:S(2)}) async-start(bf16[8,2,2,16,512]{4,3,2,1,0:T(8,128)(2,1)} %get-tuple-element.60), calls=%async_computation.4 | async-start | bytes 1048576 | tf_op jit(solution)/shard_map/all_to_all | solution.py:358
  69.7 8.6 %collective-permute-start.5 = (bf16[2,2,64,512]{3,2,1,0:T(8,128)(2,1)S(1)}, bf16[2,2,64,512]{3,2,1,0:T(8,128)(2,1)S(1)}, u32[]{:S(2)}, u32[]{:S(2)}) collective-permute-start(bf16[2,2,64,512]{3,2,1,0:T(8,128)(2,1)S(1)} %get-tuple-element.62), channel_id=1, source_target_pairs={{0,16},{16,0},{1,17},{17,1},{2,18},{18,2},{3,19},{19,3},{4,20},{20... | collective-permute-start | bytes 786440 | tf_op jit(solution)/shard_map/ppermute | solution.py:364
  79.3 5.3 %collective-permute-start.3 = (bf16[2,2,16,512]{3,2,1,0:T(8,128)(2,1)S(1)}, bf16[2,2,16,512]{3,2,1,0:T(8,128)(2,1)S(1)}, u32[]{:S(2)}, u32[]{:S(2)}) collective-permute-start(bf16[2,2,16,512]{3,2,1,0:T(8,128)(2,1)S(1)} %slice.10), channel_id=1, source_target_pairs={{0,8},{1,9},{2,10},{3,11},{4,12},{5,13},{6,14},{7,15},{8,0},{9,1},... | collective-permute-start | bytes 196616 | tf_op jit(solution)/shard_map/cond/branch_1_fun/ppermute | solution.py:403
